TPU v7x, 32 devices: a whole 2x2x4 slice. The times are simulated.
32 devices in a mesh: ctx: 4 (over y, core), wsh: 8 (over z, x).
Axes of the slice: x: 2, y: 2, z: 4, core: 2. Of those that a mesh axis runs over, the one named last changes fastest.
Arguments:
- stream_in: bfloat16 [8, 1024, 1024], P('wsh', 'ctx'), may hold values from -6 to 6
- doc_lengths: int32 [8, 16], P('wsh'), may hold values from 1 to 768, 1024 in all within a row
- cotangent: bfloat16 [8, 1024, 1024], P('wsh', 'ctx'), may hold values from -6 to 6
- weights: bfloat16 [2, 12, 1024, 1024], P(None, None, 'wsh')
- vec_params: float32 [2, 12288], replicated
- owner_slots: int32 [2, 12], replicated, may hold values from 0 to 23, as said below
- master: float32 [24, 1024, 1024], P('ctx', 'wsh'), may hold values from -1.5 to 1.5
- left_bases: float32 [24, 1024, 1024], P('ctx', 'wsh'), as said below
- right_bases: float32 [24, 1024, 1024], P('ctx'), as said below
- moment1: float32 [24, 1024, 1024], P('ctx', 'wsh'), may hold values from -4 to 4
- moment2: float32 [24, 1024, 1024], P('ctx', 'wsh'), may hold values from 0.01 to 1
- vec_moment1: float32 [2, 12288], replicated, may hold values from -4 to 4
- vec_moment2: float32 [2, 12288], replicated, may hold values from 0.01 to 1
Outputs:
- stream_out: bfloat16 [8, 1024, 1024], P('wsh', 'ctx')
- stream_grad: float32 [8, 1024, 1024], P('wsh', 'ctx')
- block_grads: float32 [24, 1024, 1024], P('ctx', 'wsh')
- new_moment1: float32 [24, 1024, 1024], P('ctx', 'wsh')
- new_moment2: float32 [24, 1024, 1024], P('ctx', 'wsh')
- new_master: float32 [24, 1024, 1024], P('ctx', 'wsh')
- new_weights: bfloat16 [2, 12, 1024, 1024], P(None, None, 'wsh')
- vec_grads: float32 [2, 12288], replicated
- new_vec_params: float32 [2, 12288], replicated
- new_vec_moment1: float32 [2, 12288], replicated
- new_vec_moment2: float32 [2, 12288], replicated
Inputs may be any that keep to these rules, and one draw needn't show every extreme that they name: `doc_lengths`: the 16 lengths of a stream sum to 1024; the longest is exactly 768. `owner_slots`: all entries are distinct; the other 0 slots hold no block. Every left_bases[s] is an orthogonal matrix. Every right_bases[s] is an orthogonal matrix.
All inputs are finite; a program needn't handle non-finite values.
Results may differ from a plain program's by a relative error of at most 0.028.
Values may be sent and summed in bfloat16 or wider, within the bound.
No kernel may reach another device: no remote copies, remote signals or barrier semaphores. Data moves between devices by JAX's collectives and lax.ppermute only.
A program may use at most 448 MiB of HBM per device.

v0:
```python
import jax
import jax.numpy as jnp
import numpy as np
from jax import lax
from jax.sharding import PartitionSpec as P

D = 1024
HEADS = 16
HEAD_DIM = 64
FF = 4096
BLK = 1024
LAYERS = 2


EPS_NORM = 1e-05
EPS_ADAM = 1e-08
LR_BLOCK = 0.1
LR_VEC = 0.25
DECAY_RATE = 0.5
HIGHEST_PREC = lax.Precision.HIGHEST
HEAD_GROUP = 4


def norm_rows(summed, gain_vec, shift_vec):
    average = jnp.mean(summed, axis=-1, keepdims=True)
    centred = summed - average
    variance = jnp.mean(centred * centred, axis=-1, keepdims=True)
    return centred * lax.rsqrt(variance + EPS_NORM) * gain_vec + shift_vec


def gelu_exact(values):
    return jax.nn.gelu(values, approximate=False)


def block_split(full_blocks):
    rows_d = D // BLK
    rows_f = FF // BLK
    end_qkv = 3 * rows_d * rows_d
    end_out = end_qkv + rows_d * rows_d
    end_up = end_out + rows_d * rows_f
    return (
        full_blocks[:end_qkv],
        full_blocks[end_qkv:end_out],
        full_blocks[end_out:end_up],
        full_blocks[end_up:],
    )


def vector_parts(vector):
    pieces = [vector[spot * D : (spot + 1) * D] for spot in range(8)]
    return pieces + [vector[8 * D :]]


def matmul_blocks(activations, blocks, rows_b, cols_b):
    tokens = activations.shape[0]
    block_grid = blocks.reshape(rows_b, cols_b, BLK, BLK)
    result = jnp.einsum(
        "tib,ijbc->tjc",
        activations.reshape(tokens, rows_b, BLK),
        block_grid,
        preferred_element_type=jnp.float32,
    )
    return result.reshape(tokens, cols_b * BLK)


def matmul_blocks_t(gradients, blocks, rows_b, cols_b):
    tokens = gradients.shape[0]
    block_grid = blocks.reshape(rows_b, cols_b, BLK, BLK)
    result = jnp.einsum(
        "tjc,ijbc->tib",
        gradients.reshape(tokens, cols_b, BLK),
        block_grid,
        preferred_element_type=jnp.float32,
    )
    return result.reshape(tokens, rows_b * BLK)


def column_tables():
    rows_d = D // BLK
    rows_f = FF // BLK
    left_cols = []
    right_cols = []
    row_at = 0
    for col_at in range(3 * rows_d):
        left_cols.append(row_at * BLK)
        right_cols.append(col_at * BLK)
    row_at = 0
    col_at = 0
    left_cols.append(D + row_at * BLK)
    right_cols.append(3 * D + col_at * BLK)
    row_at = 0
    for col_at in range(rows_f):
        left_cols.append(2 * D + row_at * BLK)
        right_cols.append(4 * D + col_at * BLK)
    for row_at in range(rows_f):
        col_at = 0
        left_cols.append(3 * D + row_at * BLK)
        right_cols.append(4 * D + FF + col_at * BLK)
    left_all = []
    right_all = []
    for layer_at in range(LAYERS):
        left_all.extend([value + layer_at * (3 * D + FF) for value in left_cols])
        right_all.extend([value + layer_at * (5 * D + FF) for value in right_cols])
    return (np.array(left_all, np.int32), np.array(right_all, np.int32))


def slot_offsets(owner_slots, slot_total):
    left_cols, right_cols = column_tables()
    owner_flat = owner_slots.reshape(-1)
    slot_ids = jnp.arange(slot_total, dtype=jnp.int32)
    matches = owner_flat[None, :] == slot_ids[:, None]
    left_off = jnp.sum(jnp.where(matches, jnp.asarray(left_cols)[None, :], 0), axis=1).astype(
        jnp.int32
    )
    right_off = jnp.sum(jnp.where(matches, jnp.asarray(right_cols)[None, :], 0), axis=1).astype(
        jnp.int32
    )
    used = jnp.sum(matches.astype(jnp.float32), axis=1)
    return (left_off, right_off, used)


def slot_slices(source, offsets):
    return jax.vmap(lambda offset: lax.dynamic_slice_in_dim(source, offset, BLK, 1))(offsets)


def doc_index(lengths, seq_len):
    starts = jnp.cumsum(lengths) - lengths
    position = jnp.arange(seq_len, dtype=jnp.int32)
    return jnp.sum((position[:, None] >= starts[None, :]).astype(jnp.int32), axis=1)


def group_scores(query_g, key_g, same_doc):
    scores = jnp.einsum(
        "thd,shd->hts", query_g, key_g, preferred_element_type=jnp.float32
    ) * HEAD_DIM ** (-0.5)
    return jnp.where(same_doc[None], scores, -1e30)


def attend_forward(queries, key_all, value_all, same_doc):
    tokens = queries.shape[0]
    group_width = HEAD_GROUP * HEAD_DIM
    out_parts = []
    total_parts = []
    for group_at in range(HEADS // HEAD_GROUP):
        low_col = group_at * group_width
        query_g = queries[:, low_col : low_col + group_width].reshape(tokens, HEAD_GROUP, HEAD_DIM)
        key_g = key_all[:, low_col : low_col + group_width].reshape(-1, HEAD_GROUP, HEAD_DIM)
        value_g = value_all[:, low_col : low_col + group_width].reshape(-1, HEAD_GROUP, HEAD_DIM)
        scores = group_scores(query_g, key_g, same_doc)
        row_peak = jnp.max(scores, axis=-1, keepdims=True)
        exp_scores = jnp.exp(scores - row_peak)
        row_total = jnp.sum(exp_scores, axis=-1, keepdims=True)
        probs_low = (exp_scores / row_total).astype(jnp.bfloat16)
        mixture = jnp.einsum("hts,shd->thd", probs_low, value_g, preferred_element_type=jnp.float32)
        out_parts.append(mixture.reshape(tokens, group_width))
        total_parts.append(row_peak + jnp.log(row_total))
    return (jnp.concatenate(out_parts, axis=1), total_parts)


def attend_backward(queries, key_all, value_all, grad_low, log_totals, same_doc):
    tokens = queries.shape[0]
    group_width = HEAD_GROUP * HEAD_DIM
    scale_qk = HEAD_DIM ** (-0.5)
    grad_q_parts = []
    grad_k_parts = []
    grad_v_parts = []
    inner_parts = []
    for group_at in range(HEADS // HEAD_GROUP):
        low_col = group_at * group_width
        query_g = queries[:, low_col : low_col + group_width].reshape(tokens, HEAD_GROUP, HEAD_DIM)
        key_g = key_all[:, low_col : low_col + group_width].reshape(-1, HEAD_GROUP, HEAD_DIM)
        value_g = value_all[:, low_col : low_col + group_width].reshape(-1, HEAD_GROUP, HEAD_DIM)
        grad_g = grad_low[:, low_col : low_col + group_width].reshape(tokens, HEAD_GROUP, HEAD_DIM)
        scores = group_scores(query_g, key_g, same_doc)
        probs = jnp.exp(scores - log_totals[group_at])
        grad_prob = jnp.einsum("thd,shd->hts", grad_g, value_g, preferred_element_type=jnp.float32)
        inner_sum = jnp.sum(probs * grad_prob, axis=-1, keepdims=True)
        grad_score = (probs * (grad_prob - inner_sum)).astype(jnp.bfloat16)
        grad_q = (
            jnp.einsum("hts,shd->thd", grad_score, key_g, preferred_element_type=jnp.float32)
            * scale_qk
        )
        grad_q_parts.append(grad_q.reshape(tokens, group_width))
        inner_parts.append(inner_sum[:, :, 0])
        grad_k = (
            jnp.einsum("hts,thd->shd", grad_score, query_g, preferred_element_type=jnp.float32)
            * scale_qk
        )
        grad_v = jnp.einsum(
            "hts,thd->shd", probs.astype(jnp.bfloat16), grad_g, preferred_element_type=jnp.float32
        )
        grad_k_parts.append(grad_k.reshape(-1, group_width))
        grad_v_parts.append(grad_v.reshape(-1, group_width))
    grad_q_cat = jnp.concatenate(grad_q_parts, axis=1)
    inner_rows = jnp.concatenate(inner_parts, axis=0)
    return (
        grad_q_cat,
        jnp.concatenate(grad_k_parts, axis=1),
        jnp.concatenate(grad_v_parts, axis=1),
        inner_rows,
    )


def layer_forward(activation, full_blocks, vector, same_doc):
    rows_d = D // BLK
    rows_f = FF // BLK
    w_qkv, w_out, w_up, w_down = block_split(full_blocks)
    bias_q, bias_v, bias_o, bias_down, gain_one, shift_one, gain_two, shift_two, bias_up = (
        vector_parts(vector)
    )
    x_low = activation.astype(jnp.bfloat16)
    qkv_vals = matmul_blocks(x_low, w_qkv, rows_d, 3 * rows_d) + jnp.concatenate(
        [bias_q, jnp.zeros((D,), jnp.float32), bias_v]
    )
    qkv_low = qkv_vals.astype(jnp.bfloat16)
    key_mine = qkv_low[:, D : 2 * D]
    value_mine = qkv_low[:, 2 * D :]
    key_all, value_all = (
        lax.all_gather(key_mine, "ctx", axis=0, tiled=True),
        lax.all_gather(value_mine, "ctx", axis=0, tiled=True),
    )
    mixture, log_totals = attend_forward(qkv_low[:, :D], key_all, value_all, same_doc)
    attn_low = mixture.astype(jnp.bfloat16)
    branch = matmul_blocks(attn_low, w_out, rows_d, rows_d) + bias_o
    summed_one = activation + branch
    middle = norm_rows(summed_one, gain_one, shift_one)
    mid_low = middle.astype(jnp.bfloat16)
    hidden = matmul_blocks(mid_low, w_up, rows_d, rows_f) + bias_up
    act_low = gelu_exact(hidden).astype(jnp.bfloat16)
    ffn_out = matmul_blocks(act_low, w_down, rows_f, rows_d) + bias_down
    summed_two = middle + ffn_out
    result = norm_rows(summed_two, gain_two, shift_two)
    saved_vals = (
        x_low,
        qkv_low,
        log_totals,
        attn_low,
        summed_one,
        mid_low,
        hidden,
        act_low,
        summed_two,
    )
    return (result, saved_vals)


def layer_backward(grad_flow, full_blocks, vector, saved_vals, same_doc):
    rows_d = D // BLK
    rows_f = FF // BLK
    w_qkv, w_out, w_up, w_down = block_split(full_blocks)
    bias_q, bias_v, bias_o, bias_down, gain_one, shift_one, gain_two, shift_two, bias_up = (
        vector_parts(vector)
    )
    x_low, qkv_low, log_totals, attn_low, summed_one, mid_low, hidden, act_low, summed_two = (
        saved_vals
    )
    norm_val, norm_pull = jax.vjp(norm_rows, summed_two, gain_two, shift_two)
    grad_s2, grad_g2, grad_e2 = norm_pull(grad_flow)
    ffn_low = grad_s2.astype(jnp.bfloat16)
    grad_act = matmul_blocks_t(ffn_low, w_down, rows_f, rows_d)
    gelu_val, gelu_pull = jax.vjp(gelu_exact, hidden)
    hid_low = gelu_pull(grad_act)[0].astype(jnp.bfloat16)
    grad_mid = grad_s2 + matmul_blocks_t(hid_low, w_up, rows_d, rows_f)
    norm_val_one, norm_pull_one = jax.vjp(norm_rows, summed_one, gain_one, shift_one)
    grad_s1, grad_g1, grad_e1 = norm_pull_one(grad_mid)
    branch_low = grad_s1.astype(jnp.bfloat16)
    attn_grad_low = matmul_blocks_t(branch_low, w_out, rows_d, rows_d).astype(jnp.bfloat16)
    key_mine = qkv_low[:, D : 2 * D]
    value_mine = qkv_low[:, 2 * D :]
    key_all, value_all = (
        lax.all_gather(key_mine, "ctx", axis=0, tiled=True),
        lax.all_gather(value_mine, "ctx", axis=0, tiled=True),
    )
    grad_q, grad_k_all, grad_v_all, inner_rows = attend_backward(
        qkv_low[:, :D], key_all, value_all, attn_grad_low, log_totals, same_doc
    )
    grad_k, grad_v = (
        lax.psum_scatter(
            grad_k_all.astype(jnp.bfloat16), "ctx", scatter_dimension=0, tiled=True
        ).astype(jnp.float32),
        lax.psum_scatter(
            grad_v_all.astype(jnp.bfloat16), "ctx", scatter_dimension=0, tiled=True
        ).astype(jnp.float32),
    )
    qkv_grad_low = jnp.concatenate([grad_q, grad_k, grad_v], axis=1).astype(jnp.bfloat16)
    grad_x = grad_s1 + matmul_blocks_t(qkv_grad_low, w_qkv, rows_d, 3 * rows_d)
    left_ops = jnp.concatenate([x_low, attn_low, mid_low, act_low], axis=1)
    right_ops = jnp.concatenate([qkv_grad_low, branch_low, hid_low, ffn_low], axis=1)
    qkv_sum = jnp.sum(qkv_grad_low, axis=0, dtype=jnp.float32)
    vec_grad = jnp.concatenate(
        [
            qkv_sum[:D],
            qkv_sum[2 * D :],
            jnp.sum(branch_low, axis=0, dtype=jnp.float32),
            jnp.sum(ffn_low, axis=0, dtype=jnp.float32),
            grad_g1,
            grad_e1,
            grad_g2,
            grad_e2,
            jnp.sum(hid_low, axis=0, dtype=jnp.float32),
        ]
    )
    return (grad_x, left_ops, right_ops, vec_grad)


def on_device(
    stream_in,
    doc_lengths,
    cotangent,
    weights,
    vec_params,
    owner_slots,
    master,
    left_bases,
    right_bases,
    moment1,
    moment2,
    vec_moment1,
    vec_moment2,
):
    tokens = stream_in.shape[1]
    ctx_count = lax.axis_size("ctx")
    wsh_count = lax.axis_size("wsh")
    seq_len = tokens * ctx_count
    scaling = (wsh_count * seq_len) ** (-0.5)
    slots_dev = master.shape[0]
    rows_dev = master.shape[1]
    slot_total = ctx_count * slots_dev
    doc_all = doc_index(doc_lengths[0], seq_len)
    doc_mine = lax.dynamic_slice_in_dim(doc_all, lax.axis_index("ctx") * tokens, tokens)
    same_doc = doc_mine[:, None] == doc_all[None, :]
    activation = stream_in[0].astype(jnp.float32)
    kept_vals = []
    kept_blocks = []
    for layer_at in range(LAYERS):
        full_blocks = lax.all_gather(weights[layer_at], "wsh", axis=1, tiled=True)
        activation, saved_vals = layer_forward(
            activation, full_blocks, vec_params[layer_at], same_doc
        )
        kept_vals.append(saved_vals)
        kept_blocks.append(full_blocks)
    stream_out = activation.astype(jnp.bfloat16)[None]
    grad_flow = cotangent[0].astype(jnp.float32)
    left_list = [None] * LAYERS
    right_list = [None] * LAYERS
    vec_terms = [None] * LAYERS
    for layer_at in reversed(range(LAYERS)):
        full_blocks = lax.all_gather(weights[layer_at], "wsh", axis=1, tiled=True)
        grad_flow, left_ops, right_ops, vec_grad = layer_backward(
            grad_flow, full_blocks, vec_params[layer_at], kept_vals[layer_at], same_doc
        )
        vec_terms[layer_at] = vec_grad
        left_list[layer_at] = left_ops
        right_list[layer_at] = right_ops
    left_cat = jnp.concatenate(left_list, axis=1)
    right_cat = jnp.concatenate(right_list, axis=1)
    left_off, right_off, used = slot_offsets(owner_slots, slot_total)
    left_grid = left_off.reshape(ctx_count, slots_dev)
    right_grid = right_off.reshape(ctx_count, slots_dev)
    used_grid = used.reshape(ctx_count, slots_dev)
    slot_rows = []
    for slot_at in range(slots_dev):
        left_slots = slot_slices(left_cat, left_grid[:, slot_at]).reshape(
            ctx_count, tokens, wsh_count, rows_dev
        )
        right_slots = slot_slices(right_cat, right_grid[:, slot_at])
        arranged = jnp.einsum(
            "ctwr,ctb->cwrb", left_slots, right_slots, preferred_element_type=jnp.float32
        )
        arranged = arranged * (scaling * used_grid[:, slot_at])[:, None, None, None]
        slot_rows.append(
            lax.psum_scatter(
                arranged.reshape(ctx_count * wsh_count * rows_dev, BLK),
                ("ctx", "wsh"),
                scatter_dimension=0,
                tiled=True,
            )
        )
    block_grads = jnp.stack(slot_rows)
    stream_grad = grad_flow[None]
    vec_grads = lax.psum(jnp.stack(vec_terms), ("ctx", "wsh")) * scaling
    product = jnp.einsum("krc,kcd->krd", block_grads, right_bases, precision=HIGHEST_PREC)
    col_span = left_bases
    rotated_rows = lax.psum_scatter(
        jnp.einsum("kra,krd->akd", col_span, product, precision=HIGHEST_PREC).astype(jnp.bfloat16),
        "wsh",
        scatter_dimension=0,
        tiled=True,
    ).astype(jnp.float32)
    rotated = rotated_rows.transpose(1, 0, 2)
    new_moment1 = DECAY_RATE * moment1 + (1.0 - DECAY_RATE) * rotated
    new_moment2 = DECAY_RATE * moment2 + (1.0 - DECAY_RATE) * rotated * rotated
    direction = new_moment1 / (jnp.sqrt(new_moment2) + EPS_ADAM)
    back_part = jnp.einsum("krc,kdc->krd", direction, right_bases, precision=HIGHEST_PREC)
    col_span = left_bases
    update = jnp.zeros(back_part.shape, jnp.float32) + jnp.einsum(
        "kra,kad->krd",
        col_span,
        lax.all_gather(back_part.astype(jnp.bfloat16), "wsh", axis=1, tiled=True).astype(
            jnp.float32
        ),
        precision=HIGHEST_PREC,
    )
    new_master = master - LR_BLOCK * update
    slot_all = lax.all_gather(new_master.astype(jnp.bfloat16), "ctx", axis=0, tiled=True)
    new_weights = jnp.take(slot_all, owner_slots.reshape(-1), axis=0).reshape(
        LAYERS, owner_slots.shape[1], rows_dev, BLK
    )
    new_vec_moment1 = DECAY_RATE * vec_moment1 + (1.0 - DECAY_RATE) * vec_grads
    new_vec_moment2 = DECAY_RATE * vec_moment2 + (1.0 - DECAY_RATE) * vec_grads * vec_grads
    new_vec_params = vec_params - LR_VEC * new_vec_moment1 / (jnp.sqrt(new_vec_moment2) + EPS_ADAM)
    return (
        stream_out,
        stream_grad,
        block_grads,
        new_moment1,
        new_moment2,
        new_master,
        new_weights,
        vec_grads,
        new_vec_params,
        new_vec_moment1,
        new_vec_moment2,
    )


def solution(mesh):
    placed = (
        P("wsh", "ctx", None),
        P("wsh", None),
        P("wsh", "ctx", None),
        P(None, None, "wsh", None),
        P(),
        P(),
        P("ctx", "wsh", None),
        P("ctx", "wsh", None),
        P("ctx", None, None),
        P("ctx", "wsh", None),
        P("ctx", "wsh", None),
        P(),
        P(),
    )
    return jax.shard_map(
        on_device,
        mesh=mesh,
        in_specs=placed,
        out_specs=(
            P("wsh", "ctx", None),
            P("wsh", "ctx", None),
            P("ctx", "wsh", None),
            P("ctx", "wsh", None),
            P("ctx", "wsh", None),
            P("ctx", "wsh", None),
            P(None, None, "wsh", None),
            P(),
            P(),
            P(),
            P(),
        ),
        check_vma=False,
    )
```

profile of v0, /device:TPU:0, one launch (start us, length us, event | category | flops | bytes accessed | tf_op | source)
XLA Modules:
  0.0 4421.8 jit_solution(9988648494869185899)
XLA Ops:
  16.2 481.1 %all-gather.23.cloned.1.call-done = bf16[1,12,1024,1024]{3,2,1,0:T(8,128)(2,1)} async-done(((bf16[1,12,128,1024]{3,2,1,0:T(8,128)(2,1)}), bf16[1,12,1024,1024]{3,2,1,0:T(8,128)(2,1)}) %all-gather.23.cloned.1.call-update) | async-done | bytes 25165840 | tf_op jit(solution)/shard_map/all_gather | solution.py:336
  503.5 8.7 copy.358
  530.5 11.7 fusion.246
  542.2 11.4 copy.371
  553.6 426.3 %all-gather.25.cloned.1.call-done = bf16[1,12,1024,1024]{3,2,1,0:T(8,128)(2,1)} async-done(((bf16[1,12,128,1024]{3,2,1,0:T(8,128)(2,1)}), bf16[1,12,1024,1024]{3,2,1,0:T(8,128)(2,1)}) %all-gather.25.cloned.1.call-update) | async-done | bytes 25165840 | tf_op jit(solution)/shard_map/all_gather | solution.py:336
  986.1 8.9 copy.373
  995.0 9.7 all-gather.13.cloned.1.call-done
  1009.6 19.7 all-gather.11.cloned.1.call-done
  1081.8 16.2 constant_dynamic-update-slice_fusion.21
  1109.4 12.0 fusion.247
  1121.4 11.5 copy.386
  1147.3 8.8 all-gather.15.cloned.1.call-done
  1208.4 16.0 constant_dynamic-update-slice_fusion.14
  1346.7 18.2 reduce-scatter.16.cloned.1.call-done
  1474.7 29.4 while.12
  1534.4 16.0 while.13
  1550.3 10.4 convolution_multiply_fusion.5
  1563.0 29.0 while.14
  1593.6 13.3 while.15
  1607.0 10.4 convolution_multiply_fusion.4
  1619.7 29.1 while.16
  1650.4 13.3 while.17
  1663.7 10.4 convolution_multiply_fusion.3
  1676.5 29.0 while.18
  1707.0 13.3 while.19
  1720.3 10.4 convolution_multiply_fusion.2
  1733.1 29.0 while.20
  1763.6 13.3 while.21
  1776.9 10.4 convolution_multiply_fusion.1
  1789.6 29.0 while.22
  1820.2 13.3 while.23
  1833.5 10.4 convolution_multiply_fusion
  1844.0 74.8 %reduce-scatter.22.cloned.1.call-done = f32[128,1024]{1,0:T(8,128)} async-done(((f32[4096,1024]{1,0:T(8,128)}), f32[128,1024]{1,0:T(8,128)}) %reduce-scatter.22.cloned.1.call-update) | async-done | bytes 524304 | tf_op jit(solution)/shard_map/reduce_scatter | solution.py:372
  1920.7 357.7 %reduce-scatter.24.cloned.1.call-done = f32[128,1024]{1,0:T(8,128)} async-done(((f32[4096,1024]{1,0:T(8,128)}), f32[128,1024]{1,0:T(8,128)}) %reduce-scatter.24.cloned.1.call-update) | async-done | bytes 524304 | tf_op jit(solution)/shard_map/reduce_scatter | solution.py:372
  2280.2 357.8 %reduce-scatter.26.cloned.1.call-done = f32[128,1024]{1,0:T(8,128)} async-done(((f32[4096,1024]{1,0:T(8,128)}), f32[128,1024]{1,0:T(8,128)}) %reduce-scatter.26.cloned.1.call-update) | async-done | bytes 524304 | tf_op jit(solution)/shard_map/reduce_scatter | solution.py:372
  2639.9 357.6 %reduce-scatter.28.cloned.1.call-done = f32[128,1024]{1,0:T(8,128)} async-done(((f32[4096,1024]{1,0:T(8,128)}), f32[128,1024]{1,0:T(8,128)}) %reduce-scatter.28.cloned.1.call-update) | async-done | bytes 524304 | tf_op jit(solution)/shard_map/reduce_scatter | solution.py:372
  2999.4 357.6 %reduce-scatter.30.cloned.1.call-done = f32[128,1024]{1,0:T(8,128)} async-done(((f32[4096,1024]{1,0:T(8,128)}), f32[128,1024]{1,0:T(8,128)}) %reduce-scatter.30.cloned.1.call-update) | async-done | bytes 524304 | tf_op jit(solution)/shard_map/reduce_scatter | solution.py:372
  3358.9 357.6 %reduce-scatter.32.cloned.1.call-done = f32[128,1024]{1,0:T(8,128)} async-done(((f32[4096,1024]{1,0:T(8,128)}), f32[128,1024]{1,0:T(8,128)}) %reduce-scatter.32.cloned.1.call-update) | async-done | bytes 524304 | tf_op jit(solution)/shard_map/reduce_scatter | solution.py:372
  3718.4 43.7 fusion.270
  3762.1 22.0 convolution_convert_fusion
  3784.1 16.6 copy.481
  3808.2 199.2 %reduce-scatter.34.cloned.1.call-done = bf16[128,6144]{1,0:T(8,128)(2,1)} async-done(((bf16[1024,6144]{1,0:T(8,128)(2,1)}), bf16[128,6144]{1,0:T(8,128)(2,1)}) %reduce-scatter.34.cloned.1.call-update) | async-done | bytes 1572880
  4016.9 34.9 fusion.101
  4061.5 166.0 %all-gather.19.cloned.1.call-done = bf16[6,1024,1024]{2,1,0:T(8,128)(2,1)} async-done(((bf16[6,128,1024]{2,1,0:T(8,128)(2,1)}), bf16[6,1024,1024]{2,1,0:T(8,128)(2,1)}) %all-gather.19.cloned.1.call-update) | async-done | bytes 12582928 | tf_op jit(solution)/shard_map/all_gather | solution.py:399
  4227.5 16.5 fusion.269
  4254.1 10.3 fusion.120
  4264.4 88.0 %all-reduce.14.cloned.1.call-done = f32[2,12288]{1,0:T(2,128)} async-done(((f32[2,12288]{1,0:T(2,128)}), f32[2,12288]{1,0:T(2,128)}) %all-reduce.14.cloned.1.call-update) | async-done | bytes 98320 | tf_op jit(solution)/shard_map/psum | solution.py:381
  4365.7 35.4 all-gather.21.cloned.1.call-done
  (939 shorter events, 785.9 us)
Async XLA Ops:
  7.2 3754.9 %copy-start = (f32[6,128,1024]{2,1,0:T(8,128)S(1)}, f32[6,128,1024]{2,1,0:T(8,128)}, u32[]{:S(2)}) copy-start(f32[6,128,1024]{2,1,0:T(8,128)} %param.22) | copy-start | bytes 9437188
  7.2 490.1 %all-gather.23.cloned.1.call-start = ((), (), s32[]{:S(2)}) async-start(), calls=%async_computation.28 | async-start | bytes 28311552 | tf_op jit(solution)/shard_map/all_gather | solution.py:336
  14.0 965.8 %all-gather.25.cloned.1.call-start = ((), (), s32[]{:S(2)}) async-start(), calls=%async_computation.29 | async-start | bytes 28311552 | tf_op jit(solution)/shard_map/all_gather | solution.py:336
  14.8 989.8 %all-gather.13.cloned.1.call-start = ((), (), s32[]{:S(2)}) async-start(), calls=%async_computation.12 | async-start | bytes 2621440 | tf_op jit(solution)/shard_map/all_gather | solution.py:219
  15.5 1082.5 %copy-start.84 = (f32[1,1024]{1,0:T(1,128)}, f32[1,1024]{1,0:T(1,128)S(1)}, u32[]{:S(2)}) copy-start(f32[1,1024]{1,0:T(1,128)S(1)} %get-tuple-element.554) | copy-start | bytes 12292
  15.5 1082.5 %copy-start.91 = (f32[1,1024]{1,0:T(1,128)}, f32[1,1024]{1,0:T(1,128)S(1)}, u32[]{:S(2)}) copy-start(f32[1,1024]{1,0:T(1,128)S(1)} %get-tuple-element.553) | copy-start | bytes 12292
  15.5 1124.4 %copy-start.81 = (f32[1,1024]{1,0:T(1,128)}, f32[1,1024]{1,0:T(1,128)S(1)}, u32[]{:S(2)}) copy-start(f32[1,1024]{1,0:T(1,128)S(1)} %get-tuple-element.551) | copy-start | bytes 12292
  15.6 1124.4 %copy-start.89 = (f32[1,1024]{1,0:T(1,128)}, f32[1,1024]{1,0:T(1,128)S(1)}, u32[]{:S(2)}) copy-start(f32[1,1024]{1,0:T(1,128)S(1)} %get-tuple-element.550) | copy-start | bytes 12292
  519.2 510.0 %all-gather.11.cloned.1.call-start = ((), (), s32[]{:S(2)}) async-start(), calls=%async_computation.11 | async-start | bytes 2621440 | tf_op jit(solution)/shard_map/all_gather | solution.py:220
  521.6 620.8 %all-gather.17.cloned.1.call-start = ((), (), s32[]{:S(2)}) async-start(), calls=%async_computation.14 | async-start | bytes 2621440 | tf_op jit(solution)/shard_map/all_gather | solution.py:219
  525.4 508.7 %copy-start.52 = (bf16[256,256]{0,1:T(8,128)(2,1)}, bf16[256,256]{0,1:T(8,128)(2,1)S(1)}, u32[]{:S(2)}) copy-start(bf16[256,256]{0,1:T(8,128)(2,1)S(1)} %copy.360) | copy-start | bytes 393220
  1077.7 20.4 copy-start.26
  1077.7 20.4 copy-start.103
  1077.7 27.6 slice-start.4
  1078.0 20.1 copy-start.113
  1081.8 16.3 copy-start.165
  1081.8 23.5 slice-start.5
  1105.0 35.0 copy-start.106
  1105.3 34.7 copy-start.116
  1108.8 47.4 %all-gather.15.cloned.1.call-start = ((), (), s32[]{:S(2)}) async-start(), calls=%async_computation.13 | async-start | bytes 2621440 | tf_op jit(solution)/shard_map/all_gather | solution.py:220
  1109.4 235.4 %reduce-scatter.14.cloned.1.call-start = ((), (), s32[]{:S(2)}) async-start(), calls=%async_computation.15 | async-start | bytes 2621440 | tf_op jit(solution)/shard_map/reduce_scatter | solution.py:278
  1139.9 53.4 %copy-start.60 = (bf16[256,256]{0,1:T(8,128)(2,1)}, bf16[256,256]{0,1:T(8,128)(2,1)S(1)}, u32[]{:S(2)}) copy-start(bf16[256,256]{0,1:T(8,128)(2,1)S(1)} %copy.384) | copy-start | bytes 393220
  1204.3 46.1 %copy-start.109 = (f32[256]{0:T(256)}, f32[256]{0:T(256)S(1)}, u32[]{:S(2)}) copy-start(f32[256]{0:T(256)S(1)} %broadcast_multiply_fusion.2) | copy-start | bytes 3076
  1204.5 45.8 %copy-start.119 = (f32[256]{0:T(256)}, f32[256]{0:T(256)S(1)}, u32[]{:S(2)}) copy-start(f32[256]{0:T(256)S(1)} %fusion.222) | copy-start | bytes 3076
  1208.4 16.0 copy-start.164
  1231.4 10.5 copy-start.101
  1299.1 65.8 %reduce-scatter.16.cloned.1.call-start = ((), (), s32[]{:S(2)}) async-start(), calls=%async_computation.16 | async-start | bytes 2621440 | tf_op jit(solution)/shard_map/reduce_scatter | solution.py:281
  1326.6 195.5 %reduce-scatter.18.cloned.1.call-start = ((), (), s32[]{:S(2)}) async-start(), calls=%async_computation.17 | async-start | bytes 2621440 | tf_op jit(solution)/shard_map/reduce_scatter | solution.py:278
  1343.4 26.0 copy-start.82
  1343.4 26.0 copy-start.107
  1343.4 26.0 copy-start.117
  1343.4 26.0 copy-start.175
  1442.4 81.5 %reduce-scatter.20.cloned.1.call-start = ((), (), s32[]{:S(2)}) async-start(), calls=%async_computation.18 | async-start | bytes 2621440 | tf_op jit(solution)/shard_map/reduce_scatter | solution.py:281
  1469.8 449.0 %reduce-scatter.22.cloned.1.call-start = ((), (), s32[]{:S(2)}) async-start(), calls=%async_computation.19 | async-start | bytes 17301504 | tf_op jit(solution)/shard_map/reduce_scatter | solution.py:372
  1530.0 20.3 copy-start.140
  1560.8 717.6 %reduce-scatter.24.cloned.1.call-start = ((), (), s32[]{:S(2)}) async-start(), calls=%async_computation.20 | async-start | bytes 17301504 | tf_op jit(solution)/shard_map/reduce_scatter | solution.py:372
  1592.1 14.9 copy-start.139
  1617.5 1020.5 %reduce-scatter.26.cloned.1.call-start = ((), (), s32[]{:S(2)}) async-start(), calls=%async_computation.21 | async-start | bytes 17301504 | tf_op jit(solution)/shard_map/reduce_scatter | solution.py:372
  1674.2 1323.3 %reduce-scatter.28.cloned.1.call-start = ((), (), s32[]{:S(2)}) async-start(), calls=%async_computation.22 | async-start | bytes 17301504 | tf_op jit(solution)/shard_map/reduce_scatter | solution.py:372
  1730.8 1626.2 %reduce-scatter.30.cloned.1.call-start = ((), (), s32[]{:S(2)}) async-start(), calls=%async_computation.23 | async-start | bytes 17301504 | tf_op jit(solution)/shard_map/reduce_scatter | solution.py:372
  1787.4 1929.1 %reduce-scatter.32.cloned.1.call-start = ((), (), s32[]{:S(2)}) async-start(), calls=%async_computation.24 | async-start | bytes 17301504 | tf_op jit(solution)/shard_map/reduce_scatter | solution.py:372
  1844.0 2163.5 %reduce-scatter.34.cloned.1.call-start = ((), (), s32[]{:S(2)}) async-start(), calls=%async_computation.30 | async-start | bytes 14155776
  3800.7 426.7 %all-gather.19.cloned.1.call-start = ((), (), s32[]{:S(2)}) async-start(), calls=%async_computation.25 | async-start | bytes 14155776 | tf_op jit(solution)/shard_map/all_gather | solution.py:399
  4051.9 300.5 %all-reduce.14.cloned.1.call-start = ((), (), s32[]{:S(2)}) async-start(), calls=%async_computation.27 | async-start | bytes 196608 | tf_op jit(solution)/shard_map/psum | solution.py:381
  4061.4 339.6 %all-gather.21.cloned.1.call-start = ((), (), s32[]{:S(2)}) async-start(), calls=%async_computation.26 | async-start | bytes 7864320 | tf_op jit(solution)/shard_map/all_gather | solution.py:405
  4254.1 98.3 %copy-start.74 = (f32[2,12288]{1,0:T(2,128)S(1)}, f32[2,12288]{1,0:T(2,128)}, u32[]{:S(2)}) copy-start(f32[2,12288]{1,0:T(2,128)} %param.19) | copy-start | bytes 294916
  4254.1 98.3 %copy-start.75 = (f32[2,12288]{1,0:T(2,128)S(1)}, f32[2,12288]{1,0:T(2,128)}, u32[]{:S(2)}) copy-start(f32[2,12288]{1,0:T(2,128)} %param.26) | copy-start | bytes 294916
  4254.1 98.3 %copy-start.76 = (f32[2,12288]{1,0:T(2,128)S(1)}, f32[2,12288]{1,0:T(2,128)}, u32[]{:S(2)}) copy-start(f32[2,12288]{1,0:T(2,128)} %param.27) | copy-start | bytes 294916
  (164 other events, 738.5 us)
Sparse Core Ops, SparseCore 0:
  14.2 483.1 all-gather.22
  499.4 480.3 all-gather.24
  982.0 22.5 all-gather.12
  1006.6 22.5 all-gather.10
  1108.9 22.5 all-gather.16
  1133.5 22.5 all-gather.14
  1299.2 31.4 reduce-scatter.13
  1333.4 31.4 reduce-scatter.15
  1442.5 31.4 reduce-scatter.17
  1476.5 31.4 reduce-scatter.19
  1560.9 357.8 reduce-scatter.21
  1920.9 357.3 reduce-scatter.23
  2280.6 357.3 reduce-scatter.25
  2640.1 357.3 reduce-scatter.27
  2999.6 357.3 reduce-scatter.29
  3359.1 357.3 reduce-scatter.31
  3800.9 206.5 reduce-scatter.33
  4051.9 175.5 all-gather.18
  4233.6 118.7 all-reduce.13
  4353.8 47.2 all-gather.20
where the time goes:
time: 4440 us; the launch traced here: 4420 us
  waiting for transfers between devices  3320 us (75%)
  local copies, waits for them, and re-layouts  589 us (13%)
  matrix products  420 us (9%)
  other arithmetic  77.5 us (2%)
    reduce_scatter x6, waiting for transfers between devices, on_device(): lax.psum_scatter(arranged.reshape(ctx_count * wsh_count * rows_dev, BLK),...  1860 us
    all_gather x2, waiting for transfers between devices, on_device(): full_blocks = lax.all_gather(weights[layer_at], 'wsh', axis=1, tiled=True)  907 us
    gather x192, local copies, waits for them, and re-layouts  257 us
    unnamed x21, waiting for transfers between devices  201 us
    all_gather x1, waiting for transfers between devices, on_device(): lax.all_gather(back_part.astype(jnp.bfloat16), 'wsh', axis=1, tiled=True)  166 us
    unnamed x449, local copies, waits for them, and re-layouts  110 us
  transfers between devices with their start and end apart: 20, of which 16 were waited for; matrix products, arithmetic and copies ran while one was open for 14% of the time, Pallas kernels for 0%

commit v1 on v0

v1 whole, which is shorter than its diff:
```python
import functools

import jax
import jax.numpy as jnp
import numpy as np
from jax import lax
from jax.experimental import pallas as pl
from jax.experimental.pallas import tpu as pltpu
from jax.sharding import PartitionSpec as P

D = 1024
HEADS = 16
HEAD_DIM = 64
FF = 4096
BLK = 1024
LAYERS = 2
NBLK = 12
CORES = 2
DEPTH_Z = 4

EPS_NORM = 1e-05
EPS_ADAM = 1e-08
LR_BLOCK = 0.1
LR_VEC = 0.25
DECAY_RATE = 0.5
HEAD_GROUP = 4
BF16 = jnp.bfloat16
F32 = jnp.float32


class Place:
    def __init__(self, ctx_count, wsh_count):
        self.size = {
            "core": CORES,
            "y": ctx_count // CORES,
            "z": DEPTH_Z,
            "x": wsh_count // DEPTH_Z,
        }
        ctx_at = lax.axis_index("ctx")
        wsh_at = lax.axis_index("wsh")
        self.at = {
            "core": ctx_at % CORES,
            "y": ctx_at // CORES,
            "z": wsh_at // self.size["x"],
            "x": wsh_at % self.size["x"],
        }

    def take(self, value, axis, step):
        name, slow, fast = {
            "core": ("ctx", "y", "core"),
            "y": ("ctx", "y", "core"),
            "z": ("wsh", "z", "x"),
            "x": ("wsh", "z", "x"),
        }[axis]
        extent = self.size[axis]
        pairs = []
        for slow_at in range(self.size[slow]):
            for fast_at in range(self.size[fast]):
                if axis == fast:
                    other = (slow_at, (fast_at + step) % extent)
                else:
                    other = ((slow_at + step) % extent, fast_at)
                pairs.append(
                    (
                        other[0] * self.size[fast] + other[1],
                        slow_at * self.size[fast] + fast_at,
                    )
                )
        return lax.ppermute(value, name, pairs)

    def gather(self, value, axis):
        steps = range(1, self.size[axis])
        return jnp.stack([value] + [self.take(value, axis, step) for step in steps])

    def scatter(self, values, axis):
        total = values[0].astype(F32)
        for step in range(1, self.size[axis]):
            total = total + self.take(values[step], axis, -step).astype(F32)
        return total


def norm_rows(summed, gain_vec, shift_vec):
    average = jnp.mean(summed, axis=-1, keepdims=True)
    centred = summed - average
    variance = jnp.mean(centred * centred, axis=-1, keepdims=True)
    return centred * lax.rsqrt(variance + EPS_NORM) * gain_vec + shift_vec


def gelu_exact(values):
    return jax.nn.gelu(values, approximate=False)


def vector_parts(vector):
    pieces = [vector[spot * D : (spot + 1) * D] for spot in range(8)]
    return pieces + [vector[8 * D :]]


def dot(left, right):
    return jnp.dot(left, right, preferred_element_type=F32)


def dot_t(left, right):
    return lax.dot_general(left, right, (((1,), (1,)), ((), ())), preferred_element_type=F32)


def assemble_kernel(split_count, whole_count, has_y, where, *refs):
    if has_y:
        mine, other_y, core_mine, core_other_y, out = refs
    else:
        mine, core_mine, out = refs
    half_rows = mine.shape[3]
    half_cols = mine.shape[4]
    core_at = where[3]
    y_at = where[2]

    def put(block, rows, cols, value):
        out[block, 0, pl.ds(rows * half_rows, half_rows), pl.ds(cols * half_cols, half_cols)] = value

    for core in range(2):

        @pl.when(core_at == core)
        def _():
            if has_y:
                for y in range(2):

                    @pl.when(y_at == y)
                    def _():
                        for block in range(split_count):
                            put(block, core, y, mine[0, 0, block])
                            put(block, core, 1 - y, other_y[0, 0, block])
                            put(block, 1 - core, y, core_mine[0, 0, block])
                            put(block, 1 - core, 1 - y, core_other_y[0, 0, block])

            for block in range(whole_count):
                for cols in range(2):
                    entry = split_count + 2 * block + cols
                    put(split_count + block, core, cols, mine[0, 0, entry])
                    put(split_count + block, 1 - core, cols, core_mine[0, 0, entry])


def gather_blocks(place, shard):
    count, rows, _ = shard.shape
    half_rows, half_cols = rows // 2, BLK // 2
    has_y = place.size["y"] == 2
    split_count = count - 1 if has_y else 0
    whole_count = count - split_count
    mine = lax.dynamic_slice_in_dim(shard, place.at["core"] * half_rows, half_rows, 1)
    whole = mine[split_count:]
    pieces = [
        part for block in range(whole_count) for part in (whole[block, :, :half_cols], whole[block, :, half_cols:])
    ]
    piece = jnp.stack(pieces)
    if has_y:
        parts = lax.dynamic_slice_in_dim(
            mine[:split_count], place.at["y"] * half_cols, half_cols, 2
        )
        piece = jnp.concatenate([parts, piece])
    held = place.gather(place.gather(piece, "z"), "x")
    operands = [held]
    if has_y:
        other_y = place.take(held[:, :, :split_count], "y", 1)
        operands.append(other_y)
    operands += [place.take(value, "core", 1) for value in list(operands)]
    count_z, count_x = place.size["z"], place.size["x"]
    where = jnp.stack([place.at[name] for name in ("z", "x", "y", "core")]).astype(jnp.int32)

    def piece_at(z, x, where):
        return (
            lax.rem(x - where[1] + count_x, count_x),
            lax.rem(z - where[0] + count_z, count_z),
            0,
            0,
            0,
        )

    out = pl.pallas_call(
        functools.partial(assemble_kernel, split_count, whole_count, has_y),
        grid_spec=pltpu.PrefetchScalarGridSpec(
            num_scalar_prefetch=1,
            grid=(count_z, count_x),
            in_specs=[pl.BlockSpec((1, 1) + value.shape[2:], piece_at) for value in operands],
            out_specs=pl.BlockSpec(
                (count, 1, rows, BLK), lambda z, x, where: (0, z * count_x + x, 0, 0)
            ),
        ),
        out_shape=jax.ShapeDtypeStruct((count, count_z * count_x, rows, BLK), BF16),
        cost_estimate=pl.CostEstimate(
            flops=0, bytes_accessed=4 * count * BLK * BLK, transcendentals=0
        ),
        name="assemble",
    )(where, *operands)
    return out.reshape(count, BLK, BLK)


def group_scores(query_g, key_g, same_doc):
    scores = jnp.einsum(
        "thd,shd->hts", query_g, key_g, preferred_element_type=jnp.float32
    ) * HEAD_DIM ** (-0.5)
    return jnp.where(same_doc[None], scores, -1e30)


def attend_forward(queries, key_all, value_all, same_doc):
    tokens = queries.shape[0]
    group_width = HEAD_GROUP * HEAD_DIM
    out_parts = []
    total_parts = []
    for group_at in range(HEADS // HEAD_GROUP):
        low_col = group_at * group_width
        query_g = queries[:, low_col : low_col + group_width].reshape(tokens, HEAD_GROUP, HEAD_DIM)
        key_g = key_all[:, low_col : low_col + group_width].reshape(-1, HEAD_GROUP, HEAD_DIM)
        value_g = value_all[:, low_col : low_col + group_width].reshape(-1, HEAD_GROUP, HEAD_DIM)
        scores = group_scores(query_g, key_g, same_doc)
        row_peak = jnp.max(scores, axis=-1, keepdims=True)
        exp_scores = jnp.exp(scores - row_peak)
        row_total = jnp.sum(exp_scores, axis=-1, keepdims=True)
        probs_low = (exp_scores / row_total).astype(jnp.bfloat16)
        mixture = jnp.einsum("hts,shd->thd", probs_low, value_g, preferred_element_type=jnp.float32)
        out_parts.append(mixture.reshape(tokens, group_width))
        total_parts.append(row_peak + jnp.log(row_total))
    return (jnp.concatenate(out_parts, axis=1), total_parts)


def attend_backward(queries, key_all, value_all, grad_low, log_totals, same_doc):
    tokens = queries.shape[0]
    group_width = HEAD_GROUP * HEAD_DIM
    scale_qk = HEAD_DIM ** (-0.5)
    grad_q_parts = []
    grad_k_parts = []
    grad_v_parts = []
    for group_at in range(HEADS // HEAD_GROUP):
        low_col = group_at * group_width
        query_g = queries[:, low_col : low_col + group_width].reshape(tokens, HEAD_GROUP, HEAD_DIM)
        key_g = key_all[:, low_col : low_col + group_width].reshape(-1, HEAD_GROUP, HEAD_DIM)
        value_g = value_all[:, low_col : low_col + group_width].reshape(-1, HEAD_GROUP, HEAD_DIM)
        grad_g = grad_low[:, low_col : low_col + group_width].reshape(tokens, HEAD_GROUP, HEAD_DIM)
        scores = group_scores(query_g, key_g, same_doc)
        probs = jnp.exp(scores - log_totals[group_at])
        grad_prob = jnp.einsum("thd,shd->hts", grad_g, value_g, preferred_element_type=jnp.float32)
        inner_sum = jnp.sum(probs * grad_prob, axis=-1, keepdims=True)
        grad_score = (probs * (grad_prob - inner_sum)).astype(jnp.bfloat16)
        grad_q = (
            jnp.einsum("hts,shd->thd", grad_score, key_g, preferred_element_type=jnp.float32)
            * scale_qk
        )
        grad_q_parts.append(grad_q.reshape(tokens, group_width))
        grad_k = (
            jnp.einsum("hts,thd->shd", grad_score, query_g, preferred_element_type=jnp.float32)
            * scale_qk
        )
        grad_v = jnp.einsum(
            "hts,thd->shd", probs.astype(jnp.bfloat16), grad_g, preferred_element_type=jnp.float32
        )
        grad_k_parts.append(grad_k.reshape(-1, group_width))
        grad_v_parts.append(grad_v.reshape(-1, group_width))
    return (
        jnp.concatenate(grad_q_parts, axis=1),
        jnp.concatenate(grad_k_parts, axis=1),
        jnp.concatenate(grad_v_parts, axis=1),
    )


def layer_forward(place, activation, blocks, vector, same_doc):
    w_in, w_up, w_down = blocks
    bias_q, bias_v, bias_o, bias_down, gain_one, shift_one, gain_two, shift_two, bias_up = (
        vector_parts(vector)
    )
    x_low = activation.astype(BF16)
    query = (dot(x_low, w_in[0]) + bias_q).astype(BF16)
    keyval = jnp.concatenate([dot(x_low, w_in[1]), dot(x_low, w_in[2]) + bias_v], axis=1).astype(
        BF16
    )
    keyval_all = place.gather(place.gather(keyval, "y"), "core").reshape(-1, 2 * D)
    mixture, log_totals = attend_forward(
        query, keyval_all[:, :D], keyval_all[:, D:], same_doc
    )
    attn_low = mixture.astype(BF16)
    summed_one = activation + dot(attn_low, w_in[3]) + bias_o
    middle = norm_rows(summed_one, gain_one, shift_one)
    mid_low = middle.astype(BF16)
    hidden = (
        jnp.concatenate([dot(mid_low, w_up[spot]) for spot in range(FF // BLK)], axis=1) + bias_up
    )
    act_low = gelu_exact(hidden).astype(BF16)
    ffn_out = bias_down
    for spot in range(FF // BLK):
        ffn_out = ffn_out + dot(act_low[:, spot * BLK : (spot + 1) * BLK], w_down[spot])
    summed_two = middle + ffn_out
    result = norm_rows(summed_two, gain_two, shift_two)
    saved = (x_low, query, keyval_all, log_totals, attn_low, summed_one, mid_low, hidden, act_low, summed_two)
    return (result, saved)


def left_order(place, left):
    tokens, cols = left.shape
    count_z, count_x = place.size["z"], place.size["x"]
    blocks = cols // BLK
    rows = BLK // (count_z * count_x)
    value = left.reshape(tokens, blocks, count_z, count_x, rows)
    value = jnp.roll(value, (-place.at["z"], -place.at["x"]), axis=(2, 3))
    return value.transpose(0, 3, 2, 1, 4).reshape(tokens, cols)


def right_halves(place, right):
    tokens, cols = right.shape
    count_y = place.size["y"]
    width = BLK // (CORES * count_y)
    value = right.reshape(tokens, cols // BLK, CORES, count_y, width)
    halves = []
    for step in range(CORES):
        half = lax.dynamic_index_in_dim(value, (place.at["core"] + step) % CORES, 2, False)
        half = jnp.roll(half, -place.at["y"], axis=2)
        halves.append(half.transpose(2, 0, 1, 3).reshape(count_y, tokens, -1))
    return halves


def sum_job(place, left, right, first):
    count_z, count_x, count_y = place.size["z"], place.size["x"], place.size["y"]
    left = left_order(place, left)
    right_mine, right_other = right_halves(place, right)
    left_both = jnp.concatenate([left, place.take(left, "core", 1)], axis=0)
    right_both = jnp.concatenate([right_mine, place.take(right_other, "core", 1)], axis=1)
    partial = [
        lax.dot_general(left_both, right_both[step], (((0,), (0,)), ((), ())), preferred_element_type=F32)
        .astype(BF16)
        .reshape(count_x, count_z, -1, right_both.shape[2])
        for step in range(count_y)
    ]
    if first == "y":
        total = place.scatter(partial, "y").astype(BF16)
        total = place.scatter(total, "x").astype(BF16)
    else:
        parts = [[value[step] for value in partial] for step in range(count_x)]
        parts = [jnp.stack(part) for part in parts]
        total = place.scatter(parts, "x").astype(BF16)
        total = place.scatter(total, "y").astype(BF16)
    total = place.scatter(total, "z")
    rows = BLK // (count_z * count_x)
    width = BLK // (CORES * count_y)
    if left.shape[1] > BLK:
        return total.reshape(-1, rows, width)
    return total.reshape(rows, -1, width).transpose(1, 0, 2)


def layer_backward(place, grad_flow, blocks, vector, saved, same_doc):
    w_in, w_up, w_down = blocks
    bias_q, bias_v, bias_o, bias_down, gain_one, shift_one, gain_two, shift_two, bias_up = (
        vector_parts(vector)
    )
    x_low, query, keyval_all, log_totals, attn_low, summed_one, mid_low, hidden, act_low, summed_two = saved
    tokens = x_low.shape[0]
    norm_val, norm_pull = jax.vjp(norm_rows, summed_two, gain_two, shift_two)
    grad_s2, grad_g2, grad_e2 = norm_pull(grad_flow)
    ffn_low = grad_s2.astype(BF16)
    sum_down = sum_job(place, act_low, ffn_low, "y")
    grad_act = jnp.concatenate([dot_t(ffn_low, w_down[spot]) for spot in range(FF // BLK)], axis=1)
    gelu_val, gelu_pull = jax.vjp(gelu_exact, hidden)
    hid_low = gelu_pull(grad_act)[0].astype(BF16)
    sum_up = sum_job(place, mid_low, hid_low, "x")
    grad_mid = grad_s2
    for spot in range(FF // BLK):
        grad_mid = grad_mid + dot_t(hid_low[:, spot * BLK : (spot + 1) * BLK], w_up[spot])
    norm_val_one, norm_pull_one = jax.vjp(norm_rows, summed_one, gain_one, shift_one)
    grad_s1, grad_g1, grad_e1 = norm_pull_one(grad_mid)
    branch_low = grad_s1.astype(BF16)
    sum_out = sum_job(place, attn_low, branch_low, "y")
    attn_grad_low = dot_t(branch_low, w_in[3]).astype(BF16)
    grad_q, grad_k_all, grad_v_all = attend_backward(
        query, keyval_all[:, :D], keyval_all[:, D:], attn_grad_low, log_totals, same_doc
    )
    grad_kv = jnp.concatenate([grad_k_all, grad_v_all], axis=1).astype(BF16)
    grad_kv = grad_kv.reshape(CORES, -1, tokens, 2 * D)
    grad_kv = place.scatter(place.scatter(grad_kv, "core").astype(BF16), "y")
    qkv_grad_low = jnp.concatenate([grad_q, grad_kv], axis=1).astype(BF16)
    grad_x = grad_s1
    for spot in range(3):
        grad_x = grad_x + dot_t(qkv_grad_low[:, spot * D : (spot + 1) * D], w_in[spot])
    sum_in = sum_job(place, x_low, qkv_grad_low, "x")
    sums = jnp.concatenate([sum_in, sum_out, sum_up, sum_down])
    qkv_sum = jnp.sum(qkv_grad_low, axis=0, dtype=F32)
    vec_grad = jnp.concatenate(
        [
            qkv_sum[:D],
            qkv_sum[2 * D :],
            jnp.sum(branch_low, axis=0, dtype=F32),
            jnp.sum(ffn_low, axis=0, dtype=F32),
            grad_g1,
            grad_e1,
            grad_g2,
            grad_e2,
            jnp.sum(hid_low, axis=0, dtype=F32),
        ]
    )
    return (grad_x, sums, vec_grad)


def sum_everywhere(place, value):
    if place.size["y"] != 2 or place.size["x"] != 2:
        return lax.psum(value, ("ctx", "wsh"))
    for axis in ("core", "y", "x"):
        value = value + place.take(value, axis, 1)
    pairs = place.size["x"]
    for bit in (1, 2):
        swap = [
            (z * pairs + x, (z ^ bit) * pairs + x) for z in range(DEPTH_Z) for x in range(pairs)
        ]
        value = value + lax.ppermute(value, "wsh", swap)
    return value


def doc_ids(lengths, position):
    starts = jnp.cumsum(lengths) - lengths
    return jnp.sum((position[:, None] >= starts[None, :]).astype(jnp.int32), axis=1)


def to_owner(rows_value, wsh_count):
    slots = rows_value.shape[0]
    padded = jnp.pad(rows_value.astype(BF16), ((0, wsh_count - slots), (0, 0), (0, 0)))
    return lax.all_to_all(padded, "wsh", 0, 0, tiled=True).reshape(BLK, BLK)


def from_owner(whole, wsh_count, slots):
    cut = whole.astype(BF16).reshape(wsh_count, BLK // wsh_count, BLK)
    return lax.all_to_all(cut, "wsh", 0, 0, tiled=True)[:slots]


def on_device(
    stream_in,
    doc_lengths,
    cotangent,
    weights,
    vec_params,
    owner_slots,
    master,
    left_bases,
    right_bases,
    moment1,
    moment2,
    vec_moment1,
    vec_moment2,
):
    tokens = stream_in.shape[1]
    ctx_count = lax.axis_size("ctx")
    wsh_count = lax.axis_size("wsh")
    place = Place(ctx_count, wsh_count)
    seq_len = tokens * ctx_count
    scaling = (wsh_count * seq_len) ** (-0.5)
    slots_dev, rows_dev = master.shape[0], master.shape[1]
    slot_total = ctx_count * slots_dev
    count_y = place.size["y"]
    width = BLK // ctx_count

    core_of = (place.at["core"] + jnp.arange(CORES)) % CORES
    y_of = (place.at["y"] + jnp.arange(count_y)) % count_y
    ctx_of = (y_of[None, :] * CORES + core_of[:, None]).reshape(-1)
    key_pos = (ctx_of[:, None] * tokens + jnp.arange(tokens)[None, :]).reshape(-1)
    doc_keys = doc_ids(doc_lengths[0], key_pos)
    same_doc = doc_keys[:tokens, None] == doc_keys[None, :]

    blocks = []
    for layer_at in range(LAYERS):
        blocks.append(
            [
                gather_blocks(place, weights[layer_at, first : first + 4])
                for first in range(0, NBLK, 4)
            ]
        )
    activation = stream_in[0].astype(F32)
    kept = []
    for layer_at in range(LAYERS):
        activation, saved = layer_forward(
            place, activation, blocks[layer_at], vec_params[layer_at], same_doc
        )
        kept.append(saved)
    stream_out = activation.astype(BF16)[None]

    ahead, activation = lax.optimization_barrier(((left_bases, moment1, moment2), activation))
    left_own = to_owner(ahead[0], wsh_count)
    first_own = to_owner(ahead[1], wsh_count)
    second_own = to_owner(ahead[2], wsh_count)

    grad_flow = cotangent[0].astype(F32)
    sums = [None] * LAYERS
    vec_terms = [None] * LAYERS
    for layer_at in reversed(range(LAYERS)):
        grad_flow, sums[layer_at], vec_terms[layer_at] = layer_backward(
            place, grad_flow, blocks[layer_at], vec_params[layer_at], kept[layer_at], same_doc
        )
    stream_grad = grad_flow[None]
    vec_grads = sum_everywhere(place, jnp.stack(vec_terms)) * scaling

    all_sums = (jnp.concatenate(sums) * scaling).astype(BF16)
    owner_flat = owner_slots.reshape(-1)
    picks = (owner_flat[None, :] == jnp.arange(slot_total, dtype=jnp.int32)[:, None]).astype(BF16)
    by_slot = dot(picks, all_sums.reshape(LAYERS * NBLK, -1)).astype(BF16)
    by_slot = by_slot.reshape(ctx_count, slots_dev, rows_dev, width)

    quarters = lax.all_to_all(by_slot, "ctx", 0, 0, tiled=True)
    quarters = quarters.reshape(count_y, CORES, slots_dev, rows_dev, width)
    block_grads = quarters.transpose(2, 3, 1, 0, 4).reshape(slots_dev, rows_dev, BLK).astype(F32)

    padded = jnp.pad(by_slot, ((0, 0), (0, wsh_count - slots_dev), (0, 0), (0, 0)))
    arrived = lax.all_to_all(
        padded.reshape(ctx_count * wsh_count, rows_dev, width), ("ctx", "wsh"), 0, 0, tiled=True
    )
    arrived = arrived.reshape(count_y, CORES, wsh_count, rows_dev, width)
    grad_own = arrived.transpose(2, 3, 1, 0, 4).reshape(BLK, BLK)
    slot_own = jnp.minimum(lax.axis_index("wsh"), slots_dev - 1)
    right_own = lax.dynamic_index_in_dim(right_bases, slot_own, 0, False).astype(BF16)
    product = dot(grad_own, right_own).astype(BF16)
    rotated_own = lax.dot_general(
        left_own, product, (((0,), (0,)), ((), ())), preferred_element_type=F32
    )
    rotated = from_owner(rotated_own, wsh_count, slots_dev).astype(F32)
    first_new = DECAY_RATE * first_own.astype(F32) + (1.0 - DECAY_RATE) * rotated_own
    second_new = (
        DECAY_RATE * second_own.astype(F32) + (1.0 - DECAY_RATE) * rotated_own * rotated_own
    )
    direction = (first_new / (jnp.sqrt(second_new) + EPS_ADAM)).astype(BF16)
    back = dot_t(direction, right_own).astype(BF16)
    update = from_owner(dot(left_own, back), wsh_count, slots_dev).astype(F32)

    new_moment1 = DECAY_RATE * moment1 + (1.0 - DECAY_RATE) * rotated
    new_moment2 = DECAY_RATE * moment2 + (1.0 - DECAY_RATE) * rotated * rotated
    new_master = master - LR_BLOCK * update
    slot_rows = place.gather(place.gather(new_master.astype(BF16), "y"), "core")
    slot_rows = slot_rows.reshape(slot_total, rows_dev, BLK)
    owner_ctx, owner_at = owner_flat // slots_dev, owner_flat % slots_dev
    step_y = (owner_ctx // CORES - place.at["y"]) % count_y
    step_core = (owner_ctx % CORES - place.at["core"]) % CORES
    spot = (step_core * count_y + step_y) * slots_dev + owner_at
    new_weights = jnp.take(slot_rows, spot, axis=0).reshape(LAYERS, NBLK, rows_dev, BLK)

    new_vec_moment1 = DECAY_RATE * vec_moment1 + (1.0 - DECAY_RATE) * vec_grads
    new_vec_moment2 = DECAY_RATE * vec_moment2 + (1.0 - DECAY_RATE) * vec_grads * vec_grads
    new_vec_params = vec_params - LR_VEC * new_vec_moment1 / (jnp.sqrt(new_vec_moment2) + EPS_ADAM)
    return (
        stream_out,
        stream_grad,
        block_grads,
        new_moment1,
        new_moment2,
        new_master,
        new_weights,
        vec_grads,
        new_vec_params,
        new_vec_moment1,
        new_vec_moment2,
    )


def solution(mesh):
    rows = P("ctx", "wsh", None)
    placed = (
        P("wsh", "ctx", None),
        P("wsh", None),
        P("wsh", "ctx", None),
        P(None, None, "wsh", None),
        P(),
        P(),
        rows,
        rows,
        P("ctx", None, None),
        rows,
        rows,
        P(),
        P(),
    )
    return jax.shard_map(
        on_device,
        mesh=mesh,
        in_specs=placed,
        out_specs=(
            P("wsh", "ctx", None),
            P("wsh", "ctx", None),
            rows,
            rows,
            rows,
            rows,
            P(None, None, "wsh", None),
            P(),
            P(),
            P(),
            P(),
        ),
        check_vma=False,
    )
```

time: 4440 us -> 1770 us (0.40)
  waiting for transfers between devices: 3320 us -> 641 us
  matrix products: 420 us -> 200 us
  starting transfers between devices: 0.82 us -> 218 us
  local copies, waits for them, and re-layouts: 589 us -> 375 us
  other arithmetic: 77.5 us -> 259 us
  Pallas kernels: 0 us -> 57.6 us
    reduce_scatter x10 -> x0, waiting for transfers between devices: 1880 us -> none  [the longest x6 1860 us: on_device(): lax.psum_scatter(arranged.reshape(ctx_count * wsh_count * rows_dev, BLK),...]
    all_gather x8 -> x0, waiting for transfers between devices: 1150 us -> none  [the longest x2 907 us: on_device(): full_blocks = lax.all_gather(weights[layer_at], 'wsh', axis=1, tiled=True)]
    ppermute x0 -> x113, waiting for transfers between devices: none -> 505 us  [the longest x111 485 us: take(): return lax.ppermute(value, name, pairs)]
    gather x193 -> x1, local copies, waits for them, and re-layouts: 264 us -> 7.21 us  [on_device(): jnp.take(slot_rows, spot, axis=0).reshape(LAYERS, NBLK, rows_dev, BLK)]
    unnamed x21 -> x0, waiting for transfers between devices: 201 us -> none
    dot_general x26 -> x67, matrix products: 294 us -> 117 us  [the longest x16 45.9 us: sum_job(): lax.dot_general(left_both, right_both[step], (((0,), (0,)), ((), ())), pr...]
    ppermute x0 -> x113, starting transfers between devices: none -> 177 us  [the longest x111 172 us: take(): return lax.ppermute(value, name, pairs)]
    all_to_all x0 -> x7, waiting for transfers between devices: none -> 136 us  [the longest x1 46.3 us: on_device(): lax.all_to_all(padded.reshape(ctx_count * wsh_count, rows_dev, width), ('...]
  transfers between devices with their start and end apart: 20 -> 120, of which waited for: 16 -> 40; matrix products, arithmetic and copies ran while one was open for 14% -> 31% of each run, Pallas kernels for 0% -> 3%
where the time goes in v1:
time: 1770 us; the launch traced here: 1760 us
  waiting for transfers between devices  641 us (36%)
  local copies, waits for them, and re-layouts  375 us (21%)
  other arithmetic  259 us (15%)
  starting transfers between devices  218 us (12%)
  matrix products  200 us (11%)
  Pallas kernels  57.6 us (3%)
    ppermute x111, waiting for transfers between devices, take(): return lax.ppermute(value, name, pairs)  485 us
    ppermute x111, starting transfers between devices, take(): return lax.ppermute(value, name, pairs)  172 us
    pallas_call x6, Pallas kernels, gather_blocks(): pl.pallas_call(functools.partial(assemble_kernel, split_count, whole_coun...  57.6 us
    concatenate x24, local copies, waits for them, and re-layouts, layer_forward(): jnp.concatenate([dot(mid_low, w_up[spot]) for spot in range(FF // BLK)],...  50.6 us
    all_to_all x1, waiting for transfers between devices, on_device(): lax.all_to_all(padded.reshape(ctx_count * wsh_count, rows_dev, width), ('...  46.3 us
    dot_general x16, matrix products, sum_job(): lax.dot_general(left_both, right_both[step], (((0,), (0,)), ((), ())), pr...  45.9 us
    unnamed x717, local copies, waits for them, and re-layouts  44.8 us
    convert_element_type x4, other arithmetic, layer_forward(): act_low = gelu_exact(hidden).astype(BF16)  44.5 us
  transfers between devices with their start and end apart: 120, of which 40 were waited for; matrix products, arithmetic and copies ran while one was open for 31% of the time, Pallas kernels for 3%

profile of v1, /device:TPU:0, one launch (start us, length us, event | category | flops | bytes accessed | tf_op | source)
XLA Modules:
  0.0 1756.9 jit_solution(15935011072495610022)
XLA Ops:
  24.1 11.6 collective-permute-done.40
  35.7 19.6 %collective-permute-start.18 = (bf16[5,64,512]{2,1,0:T(8,128)(2,1)S(1)}, bf16[5,64,512]{2,1,0:T(8,128)(2,1)S(1)}, u32[]{:S(2)}, u32[]{:S(2)}) collective-permute-start(bf16[5,64,512]{2,1,0:T(8,128)(2,1)S(1)} %get-tuple-element.213), channel_id=1, source_target_pairs={{6,0},{7,1},{0,2},{1,3},{2,4},{3,5},{4,6},{5,7},{14,8},{15,9},{8,1... | collective-permute-start | bytes 983048 | tf_op jit(solution)/shard_map/ppermute | solution.py:69
  59.8 17.2 collective-permute-done.24
  87.6 17.6 collective-permute-done.17
  113.5 7.4 collective-permute-start.10
  121.1 12.1 collective-permute-done.1
  137.4 9.7 collective-permute-start.34
  147.3 6.9 collective-permute-done.10
  164.3 11.9 collective-permute-done.33
  182.3 17.6 collective-permute-done.19
  201.5 26.4 %collective-permute-done.3 = bf16[4,5,64,512]{3,2,1,0:T(8,128)(2,1)S(1)} collective-permute-done((bf16[4,5,64,512]{3,2,1,0:T(8,128)(2,1)S(1)}, bf16[4,5,64,512]{3,2,1,0:T(8,128)(2,1)S(1)}, u32[]{:S(2)}, u32[]{:S(2)}) %collective-permute-start.3) | collective-permute-done | bytes 1310752 | tf_op jit(solution)/shard_map/ppermute | solution.py:69
  229.6 26.4 %collective-permute-done.12 = bf16[4,5,64,512]{3,2,1,0:T(8,128)(2,1)S(1)} collective-permute-done((bf16[4,5,64,512]{3,2,1,0:T(8,128)(2,1)S(1)}, bf16[4,5,64,512]{3,2,1,0:T(8,128)(2,1)S(1)}, u32[]{:S(2)}, u32[]{:S(2)}) %collective-permute-start.12) | collective-permute-done | bytes 1310752 | tf_op jit(solution)/shard_map/ppermute | solution.py:69
  257.7 22.9 %collective-permute-done.35 = bf16[4,5,64,512]{3,2,1,0:T(8,128)(2,1)S(1)} collective-permute-done((bf16[4,5,64,512]{3,2,1,0:T(8,128)(2,1)S(1)}, bf16[4,5,64,512]{3,2,1,0:T(8,128)(2,1)S(1)}, u32[]{:S(2)}, u32[]{:S(2)}) %collective-permute-start.35) | collective-permute-done | bytes 1310752 | tf_op jit(solution)/shard_map/ppermute | solution.py:69
  289.9 29.1 %collective-permute-done.4.refs_1_ = bf16[2,4,3,64,512]{4,3,2,1,0:T(8,128)(2,1)S(1)} collective-permute-done((bf16[2,4,3,64,512]{4,3,2,1,0:T(8,128)(2,1)S(1)}, bf16[2,4,3,64,512]{4,3,2,1,0:T(8,128)(2,1)S(1)}, u32[]{:S(2)}, u32[]{:S(2)}) %collective-permute-start.4) | collective-permute-done | bytes 1572896 | tf_op jit(solution)/shard_map/ppermute | solution.py:69
  320.5 29.4 %collective-permute-done.13.refs_1_ = bf16[2,4,3,64,512]{4,3,2,1,0:T(8,128)(2,1)} collective-permute-done((bf16[2,4,3,64,512]{4,3,2,1,0:T(8,128)(2,1)S(1)}, bf16[2,4,3,64,512]{4,3,2,1,0:T(8,128)(2,1)}, u32[]{:S(2)}, u32[]{:S(2)}) %collective-permute-start.13) | collective-permute-done | bytes 1572896 | tf_op jit(solution)/shard_map/ppermute | solution.py:69
  351.4 32.2 %collective-permute-done.36.refs_1_ = bf16[2,4,3,64,512]{4,3,2,1,0:T(8,128)(2,1)} collective-permute-done((bf16[2,4,3,64,512]{4,3,2,1,0:T(8,128)(2,1)}, bf16[2,4,3,64,512]{4,3,2,1,0:T(8,128)(2,1)}, u32[]{:S(2)}, u32[]{:S(2)}) %collective-permute-start.36) | collective-permute-done | bytes 1572896 | tf_op jit(solution)/shard_map/ppermute | solution.py:69
  394.4 9.7 assemble.6
  419.6 9.6 assemble.11
  429.2 9.5 assemble.9
  438.8 9.6 assemble.8
  448.3 9.5 assemble.7
  457.9 9.6 assemble.10
  553.5 11.2 multiply_convert_fusion.9
  582.4 12.4 fusion.14
  669.2 9.1 multiply_convert_fusion.8
  800.4 11.3 fusion.19
  824.7 11.9 fusion.22
  847.3 13.1 all-to-all-start.5
  884.6 12.9 collective-permute-done.88
  1045.5 10.1 fusion.11
  1111.8 28.5 %collective-permute-done.59 = bf16[2,4,128,256]{3,2,1,0:T(8,128)(2,1)} collective-permute-done((bf16[2,4,128,256]{3,2,1,0:T(8,128)(2,1)}, bf16[2,4,128,256]{3,2,1,0:T(8,128)(2,1)}, u32[]{:S(2)}, u32[]{:S(2)}) %collective-permute-start.59) | collective-permute-done | bytes 524320 | tf_op jit(solution)/shard_map/ppermute | solution.py:69
  1173.6 17.9 %collective-permute-done.97 = bf16[128,1024]{1,0:T(8,128)(2,1)S(1)} collective-permute-done((bf16[128,1024]{1,0:T(8,128)(2,1)S(1)}, bf16[128,1024]{1,0:T(8,128)(2,1)S(1)}, u32[]{:S(2)}, u32[]{:S(2)}) %collective-permute-start.97) | collective-permute-done | bytes 262176 | tf_op jit(solution)/shard_map/ppermute | solution.py:69
  1201.8 31.9 %collective-permute-done.102 = bf16[4,512,256]{2,1,0:T(8,128)(2,1)} collective-permute-done((bf16[4,512,256]{2,1,0:T(8,128)(2,1)}, bf16[4,512,256]{2,1,0:T(8,128)(2,1)}, u32[]{:S(2)}, u32[]{:S(2)}) %collective-permute-start.102) | collective-permute-done | bytes 1048608 | tf_op jit(solution)/shard_map/ppermute | solution.py:69
  1239.5 12.4 collective-permute-start.104
  1319.5 13.8 collective-permute-done.83
  1343.6 14.1 collective-permute-done.52
  1363.4 31.7 %collective-permute-done.76 = bf16[512,256]{1,0:T(8,128)(2,1)} collective-permute-done((bf16[512,256]{1,0:T(8,128)(2,1)}, bf16[512,256]{1,0:T(8,128)(2,1)}, u32[]{:S(2)}, u32[]{:S(2)}) %collective-permute-start.76) | collective-permute-done | bytes 262176 | tf_op jit(solution)/shard_map/ppermute | solution.py:69
  1408.7 23.7 %collective-permute-done.69 = bf16[128,1024]{1,0:T(8,128)(2,1)S(1)} collective-permute-done((bf16[128,1024]{1,0:T(8,128)(2,1)S(1)}, bf16[128,1024]{1,0:T(8,128)(2,1)S(1)}, u32[]{:S(2)}, u32[]{:S(2)}) %collective-permute-start.69) | collective-permute-done | bytes 262176 | tf_op jit(solution)/shard_map/ppermute | solution.py:69
  1442.0 10.5 concatenate.382
  1465.3 46.3 %all-to-all-done.2 = bf16[32,128,256]{2,1,0:T(8,128)(2,1)} async-done(((bf16[32,128,256]{2,1,0:T(8,128)(2,1)}), bf16[32,128,256]{2,1,0:T(8,128)(2,1)}, u32[]{:S(2)}, u32[]{:S(2)}) %all-to-all-start.2) | async-done | bytes 2097184 | tf_op jit(solution)/shard_map/all_to_all | solution.py:502
  1532.0 32.4 %all-to-all-done.1 = bf16[8,128,1024]{2,1,0:T(8,128)(2,1)} async-done(((bf16[8,128,1024]{2,1,0:T(8,128)(2,1)}), bf16[8,128,1024]{2,1,0:T(8,128)(2,1)}, u32[]{:S(2)}, u32[]{:S(2)}) %all-to-all-start.1) | async-done | bytes 2097184 | tf_op jit(solution)/shard_map/all_to_all | solution.py:418
  1564.5 12.4 fusion.1
  1576.9 9.3 fusion.130
  1594.7 43.8 %all-to-all-done.6 = bf16[8,128,1024]{2,1,0:T(8,128)(2,1)} async-done(((bf16[8,128,1024]{2,1,0:T(8,128)(2,1)}), bf16[8,128,1024]{2,1,0:T(8,128)(2,1)}, u32[]{:S(2)}, u32[]{:S(2)}) %all-to-all-start.6) | async-done | bytes 2097184 | tf_op jit(solution)/shard_map/all_to_all | solution.py:423
  1650.4 13.0 all-to-all-done
  1672.7 15.1 collective-permute-done.110
  1690.5 13.8 collective-permute-done.111
  1743.1 7.2 gather_fusion
  (1442 shorter events, 924.9 us)
Async XLA Ops:
  17.6 59.4 %collective-permute-start.24 = (bf16[5,64,512]{2,1,0:T(8,128)(2,1)S(1)}, bf16[5,64,512]{2,1,0:T(8,128)(2,1)S(1)}, u32[]{:S(2)}, u32[]{:S(2)}) collective-permute-start(bf16[5,64,512]{2,1,0:T(8,128)(2,1)S(1)} %get-tuple-element.215), channel_id=1, source_target_pairs={{4,0},{5,1},{6,2},{7,3},{0,4},{1,5},{2,6},{3,7},{12,8},{13,9},{14,... | collective-permute-start | bytes 983048 | tf_op jit(solution)/shard_map/ppermute | solution.py:69
  21.6 62.4 %collective-permute-start.23 = (bf16[5,64,512]{2,1,0:T(8,128)(2,1)S(1)}, bf16[5,64,512]{2,1,0:T(8,128)(2,1)S(1)}, u32[]{:S(2)}, u32[]{:S(2)}) collective-permute-start(bf16[5,64,512]{2,1,0:T(8,128)(2,1)S(1)} %get-tuple-element.215), channel_id=1, source_target_pairs={{2,0},{3,1},{4,2},{5,3},{6,4},{7,5},{0,6},{1,7},{10,8},{11,9},{12,... | collective-permute-start | bytes 983048 | tf_op jit(solution)/shard_map/ppermute | solution.py:69
  59.2 52.8 %collective-permute-start.16 = (bf16[5,64,512]{2,1,0:T(8,128)(2,1)S(1)}, bf16[5,64,512]{2,1,0:T(8,128)(2,1)S(1)}, u32[]{:S(2)}, u32[]{:S(2)}) collective-permute-start(bf16[5,64,512]{2,1,0:T(8,128)(2,1)S(1)} %get-tuple-element.213), channel_id=1, source_target_pairs={{2,0},{3,1},{4,2},{5,3},{6,4},{7,5},{0,6},{1,7},{10,8},{11,9},{12,... | collective-permute-start | bytes 983048 | tf_op jit(solution)/shard_map/ppermute | solution.py:69
  112.0 66.9 %collective-permute-start.42 = (bf16[4,5,64,512]{3,2,1,0:T(8,128)(2,1)S(1)}, bf16[4,5,64,512]{3,2,1,0:T(8,128)(2,1)S(1)}, u32[]{:S(2)}, u32[]{:S(2)}) collective-permute-start(bf16[4,5,64,512]{3,2,1,0:T(8,128)(2,1)S(1)} %get-tuple-element.163), channel_id=1, source_target_pairs={{1,0},{0,1},{3,2},{2,3},{5,4},{4,5},{7,6},{6,7},{9,8},{8,9},{11,10... | collective-permute-start | bytes 3932168 | tf_op jit(solution)/shard_map/ppermute | solution.py:69
  178.0 78.0 %collective-permute-start.12 = (bf16[4,5,64,512]{3,2,1,0:T(8,128)(2,1)S(1)}, bf16[4,5,64,512]{3,2,1,0:T(8,128)(2,1)S(1)}, u32[]{:S(2)}, u32[]{:S(2)}) collective-permute-start(bf16[4,5,64,512]{3,2,1,0:T(8,128)(2,1)S(1)} %get-tuple-element.155), channel_id=1, source_target_pairs={{1,0},{0,1},{3,2},{2,3},{5,4},{4,5},{7,6},{6,7},{9,8},{8,9},{11,10... | collective-permute-start | bytes 3932168 | tf_op jit(solution)/shard_map/ppermute | solution.py:69
  178.9 101.8 %collective-permute-start.35 = (bf16[4,5,64,512]{3,2,1,0:T(8,128)(2,1)S(1)}, bf16[4,5,64,512]{3,2,1,0:T(8,128)(2,1)S(1)}, u32[]{:S(2)}, u32[]{:S(2)}) collective-permute-start(bf16[4,5,64,512]{3,2,1,0:T(8,128)(2,1)S(1)} %get-tuple-element.153), channel_id=1, source_target_pairs={{1,0},{0,1},{3,2},{2,3},{5,4},{4,5},{7,6},{6,7},{9,8},{8,9},{11,10... | collective-permute-start | bytes 3932168 | tf_op jit(solution)/shard_map/ppermute | solution.py:69
  180.6 105.0 %collective-permute-start.43 = (bf16[2,4,3,64,512]{4,3,2,1,0:T(8,128)(2,1)S(1)}, bf16[2,4,3,64,512]{4,3,2,1,0:T(8,128)(2,1)S(1)}, u32[]{:S(2)}, u32[]{:S(2)}) collective-permute-start(bf16[2,4,3,64,512]{4,3,2,1,0:T(8,128)(2,1)S(1)} %fusion.133), channel_id=1, source_target_pairs={{16,0},{24,8},{0,16},{8,24},{17,1},{25,9},{1,17},{9,25},{18,2},{26... | collective-permute-start | bytes 4718600 | tf_op jit(solution)/shard_map/ppermute | solution.py:69
  199.9 85.7 %collective-permute-start.27 = (bf16[2,4,3,64,512]{4,3,2,1,0:T(8,128)(2,1)S(1)}, bf16[2,4,3,64,512]{4,3,2,1,0:T(8,128)(2,1)S(1)}, u32[]{:S(2)}, u32[]{:S(2)}) collective-permute-start(bf16[2,4,3,64,512]{4,3,2,1,0:T(8,128)(2,1)S(1)} %fusion.135), channel_id=1, source_target_pairs={{16,0},{24,8},{0,16},{8,24},{17,1},{25,9},{1,17},{9,25},{18,2},{26... | collective-permute-start | bytes 4718600 | tf_op jit(solution)/shard_map/ppermute | solution.py:69
  227.9 61.9 %collective-permute-start.20 = (bf16[2,4,3,64,512]{4,3,2,1,0:T(8,128)(2,1)S(1)}, bf16[2,4,3,64,512]{4,3,2,1,0:T(8,128)(2,1)S(1)}, u32[]{:S(2)}, u32[]{:S(2)}) collective-permute-start(bf16[2,4,3,64,512]{4,3,2,1,0:T(8,128)(2,1)S(1)} %fusion.136), channel_id=1, source_target_pairs={{16,0},{24,8},{0,16},{8,24},{17,1},{25,9},{1,17},{9,25},{18,2},{26... | collective-permute-start | bytes 4718600 | tf_op jit(solution)/shard_map/ppermute | solution.py:69
  256.0 63.0 %collective-permute-start.4 = (bf16[2,4,3,64,512]{4,3,2,1,0:T(8,128)(2,1)S(1)}, bf16[2,4,3,64,512]{4,3,2,1,0:T(8,128)(2,1)S(1)}, u32[]{:S(2)}, u32[]{:S(2)}) collective-permute-start(bf16[2,4,3,64,512]{4,3,2,1,0:T(8,128)(2,1)S(1)} %fusion.138), channel_id=1, source_target_pairs={{16,0},{24,8},{0,16},{8,24},{17,1},{25,9},{1,17},{9,25},{18,2},{26... | collective-permute-start | bytes 4718600 | tf_op jit(solution)/shard_map/ppermute | solution.py:69
  280.6 69.3 %collective-permute-start.13 = (bf16[2,4,3,64,512]{4,3,2,1,0:T(8,128)(2,1)S(1)}, bf16[2,4,3,64,512]{4,3,2,1,0:T(8,128)(2,1)}, u32[]{:S(2)}, u32[]{:S(2)}) collective-permute-start(bf16[2,4,3,64,512]{4,3,2,1,0:T(8,128)(2,1)S(1)} %fusion.137), channel_id=1, source_target_pairs={{16,0},{24,8},{0,16},{8,24},{17,1},{25,9},{1,17},{9,25},{18,2},{26... | collective-permute-start | bytes 4718600 | tf_op jit(solution)/shard_map/ppermute | solution.py:69
  285.6 99.5 %collective-permute-start.44 = (bf16[2,4,5,64,512]{4,3,2,1,0:T(8,128)(2,1)}, bf16[2,4,5,64,512]{4,3,2,1,0:T(8,128)(2,1)}, u32[]{:S(2)}, u32[]{:S(2)}) collective-permute-start(bf16[2,4,5,64,512]{4,3,2,1,0:T(8,128)(2,1)} %pad_maximum_fusion.15.refs_0_), channel_id=1, source_target_pairs={{8,0},{0,8},{24,16},{16,24},{9,1},{1,9},{25,17},{17,25},{10,2},{2,... | collective-permute-start | bytes 7864328 | tf_op jit(solution)/shard_map/ppermute | solution.py:69
  285.6 100.0 %collective-permute-start.28 = (bf16[2,4,5,64,512]{4,3,2,1,0:T(8,128)(2,1)}, bf16[2,4,5,64,512]{4,3,2,1,0:T(8,128)(2,1)}, u32[]{:S(2)}, u32[]{:S(2)}) collective-permute-start(bf16[2,4,5,64,512]{4,3,2,1,0:T(8,128)(2,1)} %pad_maximum_fusion.13.refs_0_), channel_id=1, source_target_pairs={{8,0},{0,8},{24,16},{16,24},{9,1},{1,9},{25,17},{17,25},{10,2},{2,... | collective-permute-start | bytes 7864328 | tf_op jit(solution)/shard_map/ppermute | solution.py:69
  289.9 100.7 %collective-permute-start.21 = (bf16[2,4,5,64,512]{4,3,2,1,0:T(8,128)(2,1)}, bf16[2,4,5,64,512]{4,3,2,1,0:T(8,128)(2,1)}, u32[]{:S(2)}, u32[]{:S(2)}) collective-permute-start(bf16[2,4,5,64,512]{4,3,2,1,0:T(8,128)(2,1)} %pad_maximum_fusion.12.refs_0_), channel_id=1, source_target_pairs={{8,0},{0,8},{24,16},{16,24},{9,1},{1,9},{25,17},{17,25},{10,2},{2,... | collective-permute-start | bytes 7864328 | tf_op jit(solution)/shard_map/ppermute | solution.py:69
  319.1 71.9 %collective-permute-start.5 = (bf16[2,4,5,64,512]{4,3,2,1,0:T(8,128)(2,1)}, bf16[2,4,5,64,512]{4,3,2,1,0:T(8,128)(2,1)}, u32[]{:S(2)}, u32[]{:S(2)}) collective-permute-start(bf16[2,4,5,64,512]{4,3,2,1,0:T(8,128)(2,1)} %pad_maximum_fusion.10.refs_0_), channel_id=1, source_target_pairs={{8,0},{0,8},{24,16},{16,24},{9,1},{1,9},{25,17},{17,25},{10,2},{2,... | collective-permute-start | bytes 7864328 | tf_op jit(solution)/shard_map/ppermute | solution.py:69
  390.6 57.7 %collective-permute-start.14 = (bf16[2,4,5,64,512]{4,3,2,1,0:T(8,128)(2,1)}, bf16[2,4,5,64,512]{4,3,2,1,0:T(8,128)(2,1)}, u32[]{:S(2)}, u32[]{:S(2)}) collective-permute-start(bf16[2,4,5,64,512]{4,3,2,1,0:T(8,128)(2,1)} %pad_maximum_fusion.11.refs_0_), channel_id=1, source_target_pairs={{8,0},{0,8},{24,16},{16,24},{9,1},{1,9},{25,17},{17,25},{10,2},{2,... | collective-permute-start | bytes 7864328 | tf_op jit(solution)/shard_map/ppermute | solution.py:69
  391.0 66.9 %collective-permute-start.37 = (bf16[2,4,5,64,512]{4,3,2,1,0:T(8,128)(2,1)}, bf16[2,4,5,64,512]{4,3,2,1,0:T(8,128)(2,1)}, u32[]{:S(2)}, u32[]{:S(2)}) collective-permute-start(bf16[2,4,5,64,512]{4,3,2,1,0:T(8,128)(2,1)} %pad_maximum_fusion.14.refs_0_), channel_id=1, source_target_pairs={{8,0},{0,8},{24,16},{16,24},{9,1},{1,9},{25,17},{17,25},{10,2},{2,... | collective-permute-start | bytes 7864328 | tf_op jit(solution)/shard_map/ppermute | solution.py:69
  404.3 53.6 %collective-permute-start.38 = (bf16[2,4,3,64,512]{4,3,2,1,0:T(8,128)(2,1)}, bf16[2,4,3,64,512]{4,3,2,1,0:T(8,128)(2,1)}, u32[]{:S(2)}, u32[]{:S(2)}) collective-permute-start(bf16[2,4,3,64,512]{4,3,2,1,0:T(8,128)(2,1)} %collective-permute-done.36.refs_1_), channel_id=1, source_target_pairs={{8,0},{0,8},{24,16},{16,24},{9,1},{1,9},{25,17},{17,25},{10,2},{2,... | collective-permute-start | bytes 4718600 | tf_op jit(solution)/shard_map/ppermute | solution.py:69
  412.7 63.3 %collective-permute-start.7 = (bf16[256,2048]{0,1:T(8,128)(2,1)}, bf16[256,2048]{0,1:T(8,128)(2,1)}, u32[]{:S(2)}, u32[]{:S(2)}) collective-permute-start(bf16[256,2048]{0,1:T(8,128)(2,1)} %pad_maximum_fusion.34), channel_id=1, source_target_pairs={{16,0},{24,8},{0,16},{8,24},{17,1},{25,9},{1,17},{9,25},{18,2},{26... | collective-permute-start | bytes 3145736 | tf_op jit(solution)/shard_map/ppermute | solution.py:69
  778.1 121.5 %collective-permute-start.46 = (bf16[2,256,2048]{2,1,0:T(8,128)(2,1)}, bf16[2,256,2048]{2,1,0:T(8,128)(2,1)}, u32[]{:S(2)}, u32[]{:S(2)}) collective-permute-start(bf16[2,256,2048]{2,1,0:T(8,128)(2,1)} %bitcast.1085), channel_id=1, source_target_pairs={{8,0},{0,8},{24,16},{16,24},{9,1},{1,9},{25,17},{17,25},{10,2},{2,... | collective-permute-start | bytes 6291464 | tf_op jit(solution)/shard_map/ppermute | solution.py:69
  781.3 79.3 %collective-permute-start.85 = (bf16[256,1024]{0,1:T(8,128)(2,1)}, bf16[256,1024]{0,1:T(8,128)(2,1)}, u32[]{:S(2)}, u32[]{:S(2)}) collective-permute-start(bf16[256,1024]{0,1:T(8,128)(2,1)} %bitcast.353), channel_id=1, source_target_pairs={{8,0},{0,8},{24,16},{16,24},{9,1},{1,9},{25,17},{17,25},{10,2},{2,... | collective-permute-start | bytes 1572872 | tf_op jit(solution)/shard_map/ppermute | solution.py:69
  783.6 76.9 %collective-permute-start.86 = (bf16[2,256,256]{2,1,0:T(8,128)(2,1)}, bf16[2,256,256]{2,1,0:T(8,128)(2,1)}, u32[]{:S(2)}, u32[]{:S(2)}) collective-permute-start(bf16[2,256,256]{2,1,0:T(8,128)(2,1)} %fusion.370), channel_id=1, source_target_pairs={{8,0},{0,8},{24,16},{16,24},{9,1},{1,9},{25,17},{17,25},{10,2},{2,... | collective-permute-start | bytes 786440 | tf_op jit(solution)/shard_map/ppermute | solution.py:69
  813.6 62.2 %collective-permute-start.93 = (bf16[2,256,1024]{1,2,0:T(8,128)(2,1)}, bf16[2,256,1024]{1,2,0:T(8,128)(2,1)}, u32[]{:S(2)}, u32[]{:S(2)}) collective-permute-start(bf16[2,256,1024]{1,2,0:T(8,128)(2,1)} %bitcast.387), channel_id=1, source_target_pairs={{8,0},{0,8},{24,16},{16,24},{9,1},{1,9},{25,17},{17,25},{10,2},{2,... | collective-permute-start | bytes 3145736 | tf_op jit(solution)/shard_map/ppermute | solution.py:69
  818.4 57.2 %collective-permute-start.92 = (bf16[256,1024]{0,1:T(8,128)(2,1)}, bf16[256,1024]{0,1:T(8,128)(2,1)}, u32[]{:S(2)}, u32[]{:S(2)}) collective-permute-start(bf16[256,1024]{0,1:T(8,128)(2,1)} %bitcast.372), channel_id=1, source_target_pairs={{8,0},{0,8},{24,16},{16,24},{9,1},{1,9},{25,17},{17,25},{10,2},{2,... | collective-permute-start | bytes 1572872 | tf_op jit(solution)/shard_map/ppermute | solution.py:69
  847.3 462.7 %all-to-all-start.5 = ((bf16[8,128,1024]{2,1,0:T(8,128)(2,1)}), bf16[8,128,1024]{2,1,0:T(8,128)(2,1)}, u32[]{:S(2)}, u32[]{:S(2)}) async-start(bf16[8,128,1024]{2,1,0:T(8,128)(2,1)} %pad.17), calls=%async_computation.5 | async-start | bytes 4194304 | tf_op jit(solution)/shard_map/all_to_all | solution.py:418
  860.5 55.8 %collective-permute-start.99 = (bf16[256,4096]{0,1:T(8,128)(2,1)}, bf16[256,4096]{0,1:T(8,128)(2,1)}, u32[]{:S(2)}, u32[]{:S(2)}) collective-permute-start(bf16[256,4096]{0,1:T(8,128)(2,1)} %bitcast.1087), channel_id=1, source_target_pairs={{8,0},{0,8},{24,16},{16,24},{9,1},{1,9},{25,17},{17,25},{10,2},{2,... | collective-permute-start | bytes 6291464 | tf_op jit(solution)/shard_map/ppermute | solution.py:69
  914.5 166.1 %collective-permute-start.57 = (bf16[256,1024]{0,1:T(8,128)(2,1)}, bf16[256,1024]{0,1:T(8,128)(2,1)}, u32[]{:S(2)}, u32[]{:S(2)}) collective-permute-start(bf16[256,1024]{0,1:T(8,128)(2,1)} %bitcast.252), channel_id=1, source_target_pairs={{8,0},{0,8},{24,16},{16,24},{9,1},{1,9},{25,17},{17,25},{10,2},{2,... | collective-permute-start | bytes 1572872 | tf_op jit(solution)/shard_map/ppermute | solution.py:69
  914.9 235.8 %collective-permute-start.64 = (bf16[256,1024]{0,1:T(8,128)(2,1)}, bf16[256,1024]{0,1:T(8,128)(2,1)}, u32[]{:S(2)}, u32[]{:S(2)}) collective-permute-start(bf16[256,1024]{0,1:T(8,128)(2,1)} %bitcast.271), channel_id=1, source_target_pairs={{8,0},{0,8},{24,16},{16,24},{9,1},{1,9},{25,17},{17,25},{10,2},{2,... | collective-permute-start | bytes 1572872 | tf_op jit(solution)/shard_map/ppermute | solution.py:69
  915.9 170.4 %collective-permute-start.71 = (bf16[256,4096]{0,1:T(8,128)(2,1)}, bf16[256,4096]{0,1:T(8,128)(2,1)}, u32[]{:S(2)}, u32[]{:S(2)}) collective-permute-start(bf16[256,4096]{0,1:T(8,128)(2,1)} %bitcast.303), channel_id=1, source_target_pairs={{8,0},{0,8},{24,16},{16,24},{9,1},{1,9},{25,17},{17,25},{10,2},{2,... | collective-permute-start | bytes 6291464 | tf_op jit(solution)/shard_map/ppermute | solution.py:69
  916.3 139.5 %collective-permute-start.94 = (bf16[2,4,128,1024]{3,2,1,0:T(8,128)(2,1)}, bf16[2,4,128,1024]{3,2,1,0:T(8,128)(2,1)}, u32[]{:S(2)}, u32[]{:S(2)}) collective-permute-start(bf16[2,4,128,1024]{3,2,1,0:T(8,128)(2,1)} %pad_maximum_fusion.23), channel_id=1, source_target_pairs={{1,0},{0,1},{3,2},{2,3},{5,4},{4,5},{7,6},{6,7},{9,8},{8,9},{11,10... | collective-permute-start | bytes 6291464 | tf_op jit(solution)/shard_map/ppermute | solution.py:69
  1012.8 68.3 %collective-permute-start.58 = (bf16[2,256,256]{2,1,0:T(8,128)(2,1)}, bf16[2,256,256]{2,1,0:T(8,128)(2,1)}, u32[]{:S(2)}, u32[]{:S(2)}) collective-permute-start(bf16[2,256,256]{2,1,0:T(8,128)(2,1)} %fusion.384), channel_id=1, source_target_pairs={{8,0},{0,8},{24,16},{16,24},{9,1},{1,9},{25,17},{17,25},{10,2},{2,... | collective-permute-start | bytes 786440 | tf_op jit(solution)/shard_map/ppermute | solution.py:69
  1080.6 61.5 %collective-permute-start.101 = (bf16[2,4,512,256]{3,2,1,0:T(8,128)(2,1)}, bf16[2,4,512,256]{3,2,1,0:T(8,128)(2,1)}, u32[]{:S(2)}, u32[]{:S(2)}) collective-permute-start(bf16[2,4,512,256]{3,2,1,0:T(8,128)(2,1)} %bitcast.1265), channel_id=1, source_target_pairs={{16,0},{24,8},{0,16},{8,24},{17,1},{25,9},{1,17},{9,25},{18,2},{26... | collective-permute-start | bytes 6291464 | tf_op jit(solution)/shard_map/ppermute | solution.py:69
  1086.6 110.0 %collective-permute-start.48 = (bf16[2,256,2048]{2,1,0:T(8,128)(2,1)}, bf16[2,256,2048]{2,1,0:T(8,128)(2,1)}, u32[]{:S(2)}, u32[]{:S(2)}) collective-permute-start(bf16[2,256,2048]{2,1,0:T(8,128)(2,1)} %bitcast.214), channel_id=1, source_target_pairs={{8,0},{0,8},{24,16},{16,24},{9,1},{1,9},{25,17},{17,25},{10,2},{2,... | collective-permute-start | bytes 6291464 | tf_op jit(solution)/shard_map/ppermute | solution.py:69
  1096.5 57.3 %collective-permute-start.65 = (bf16[2,256,1024]{1,2,0:T(8,128)(2,1)}, bf16[2,256,1024]{1,2,0:T(8,128)(2,1)}, u32[]{:S(2)}, u32[]{:S(2)}) collective-permute-start(bf16[2,256,1024]{1,2,0:T(8,128)(2,1)} %bitcast.286), channel_id=1, source_target_pairs={{8,0},{0,8},{24,16},{16,24},{9,1},{1,9},{25,17},{17,25},{10,2},{2,... | collective-permute-start | bytes 3145736 | tf_op jit(solution)/shard_map/ppermute | solution.py:69
  1171.5 67.9 %collective-permute-start.73 = (bf16[2,4,512,256]{3,2,1,0:T(8,128)(2,1)}, bf16[2,4,512,256]{3,2,1,0:T(8,128)(2,1)}, u32[]{:S(2)}, u32[]{:S(2)}) collective-permute-start(bf16[2,4,512,256]{3,2,1,0:T(8,128)(2,1)} %bitcast.314), channel_id=1, source_target_pairs={{16,0},{24,8},{0,16},{8,24},{17,1},{25,9},{1,17},{9,25},{18,2},{26... | collective-permute-start | bytes 6291464 | tf_op jit(solution)/shard_map/ppermute | solution.py:69
  1173.6 107.4 %collective-permute-start.80 = (bf16[2,4,128,768]{2,3,1,0:T(8,128)(2,1)}, bf16[2,4,128,768]{2,3,1,0:T(8,128)(2,1)}, u32[]{:S(2)}, u32[]{:S(2)}) collective-permute-start(bf16[2,4,128,768]{2,3,1,0:T(8,128)(2,1)} %pad_maximum_fusion.25), channel_id=1, source_target_pairs={{1,0},{0,1},{3,2},{2,3},{5,4},{4,5},{7,6},{6,7},{9,8},{8,9},{11,10... | collective-permute-start | bytes 4718600 | tf_op jit(solution)/shard_map/ppermute | solution.py:69
  1191.5 96.6 %collective-permute-start.66 = (bf16[2,4,128,1024]{3,2,1,0:T(8,128)(2,1)}, bf16[2,4,128,1024]{3,2,1,0:T(8,128)(2,1)}, u32[]{:S(2)}, u32[]{:S(2)}) collective-permute-start(bf16[2,4,128,1024]{3,2,1,0:T(8,128)(2,1)} %pad_maximum_fusion.22), channel_id=1, source_target_pairs={{1,0},{0,1},{3,2},{2,3},{5,4},{4,5},{7,6},{6,7},{9,8},{8,9},{11,10... | collective-permute-start | bytes 6291464 | tf_op jit(solution)/shard_map/ppermute | solution.py:69
  1201.4 66.3 %collective-permute-start.49 = (bf16[256,2048]{1,0:T(8,128)(2,1)}, bf16[256,2048]{1,0:T(8,128)(2,1)}, u32[]{:S(2)}, u32[]{:S(2)}) collective-permute-start(bf16[256,2048]{1,0:T(8,128)(2,1)} %slice_bitcast_fusion.8), channel_id=1, source_target_pairs={{16,0},{24,8},{0,16},{8,24},{17,1},{25,9},{1,17},{9,25},{18,2},{26... | collective-permute-start | bytes 3145736 | tf_op jit(solution)/shard_map/ppermute | solution.py:69
  1264.6 70.0 %collective-permute-start.74 = (bf16[4,512,256]{2,1,0:T(8,128)(2,1)}, bf16[4,512,256]{2,1,0:T(8,128)(2,1)}, u32[]{:S(2)}, u32[]{:S(2)}) collective-permute-start(bf16[4,512,256]{2,1,0:T(8,128)(2,1)} %slice_bitcast_fusion.4), channel_id=1, source_target_pairs={{1,0},{0,1},{3,2},{2,3},{5,4},{4,5},{7,6},{6,7},{9,8},{8,9},{11,10... | collective-permute-start | bytes 3145736 | tf_op jit(solution)/shard_map/ppermute | solution.py:69
  1303.3 54.4 %collective-permute-start.52 = (bf16[2,4,128,768]{2,3,1,0:T(8,128)(2,1)}, bf16[2,4,128,768]{2,3,1,0:T(8,128)(2,1)}, u32[]{:S(2)}, u32[]{:S(2)}) collective-permute-start(bf16[2,4,128,768]{2,3,1,0:T(8,128)(2,1)} %pad_maximum_fusion.24), channel_id=1, source_target_pairs={{1,0},{0,1},{3,2},{2,3},{5,4},{4,5},{7,6},{6,7},{9,8},{8,9},{11,10... | collective-permute-start | bytes 4718600 | tf_op jit(solution)/shard_map/ppermute | solution.py:69
  1310.0 148.1 %all-to-all-start.4 = ((bf16[8,128,1024]{2,1,0:T(8,128)(2,1)}), bf16[8,128,1024]{2,1,0:T(8,128)(2,1)}, u32[]{:S(2)}, u32[]{:S(2)}) async-start(bf16[8,128,1024]{2,1,0:T(8,128)(2,1)} %pad.16), calls=%async_computation.4 | async-start | bytes 4194304 | tf_op jit(solution)/shard_map/all_to_all | solution.py:418
  1319.0 78.3 %collective-permute-start.67 = (bf16[4,128,1024]{2,1,0:T(8,128)(2,1)}, bf16[4,128,1024]{2,1,0:T(8,128)(2,1)}, u32[]{:S(2)}, u32[]{:S(2)}) collective-permute-start(bf16[4,128,1024]{2,1,0:T(8,128)(2,1)} %slice_bitcast_fusion.6), channel_id=1, source_target_pairs={{16,0},{24,8},{0,16},{8,24},{17,1},{25,9},{1,17},{9,25},{18,2},{26... | collective-permute-start | bytes 3145736 | tf_op jit(solution)/shard_map/ppermute | solution.py:69
  1337.3 57.7 %collective-permute-start.76 = (bf16[512,256]{1,0:T(8,128)(2,1)}, bf16[512,256]{1,0:T(8,128)(2,1)}, u32[]{:S(2)}, u32[]{:S(2)}) collective-permute-start(bf16[512,256]{1,0:T(8,128)(2,1)} %get-tuple-element.172), channel_id=1, source_target_pairs={{4,0},{5,1},{6,2},{7,3},{0,4},{1,5},{2,6},{3,7},{12,8},{13,9},{14,... | collective-permute-start | bytes 786440 | tf_op jit(solution)/shard_map/ppermute | solution.py:69
  1337.8 57.3 %collective-permute-start.75 = (bf16[512,256]{1,0:T(8,128)(2,1)}, bf16[512,256]{1,0:T(8,128)(2,1)}, u32[]{:S(2)}, u32[]{:S(2)}) collective-permute-start(bf16[512,256]{1,0:T(8,128)(2,1)} %get-tuple-element.170), channel_id=1, source_target_pairs={{6,0},{7,1},{0,2},{1,3},{2,4},{3,5},{4,6},{5,7},{14,8},{15,9},{8,1... | collective-permute-start | bytes 786440 | tf_op jit(solution)/shard_map/ppermute | solution.py:69
  1458.1 53.5 %all-to-all-start.2 = ((bf16[32,128,256]{2,1,0:T(8,128)(2,1)}), bf16[32,128,256]{2,1,0:T(8,128)(2,1)}, u32[]{:S(2)}, u32[]{:S(2)}) async-start(bf16[32,128,256]{2,1,0:T(8,128)(2,1)} %bitcast.985), calls=%async_computation.2 | async-start | bytes 4194304 | tf_op jit(solution)/shard_map/all_to_all | solution.py:502
  1511.6 52.9 %all-to-all-start.1 = ((bf16[8,128,1024]{2,1,0:T(8,128)(2,1)}), bf16[8,128,1024]{2,1,0:T(8,128)(2,1)}, u32[]{:S(2)}, u32[]{:S(2)}) async-start(bf16[8,128,1024]{2,1,0:T(8,128)(2,1)} %pad.14), calls=%async_computation.1 | async-start | bytes 4194304 | tf_op jit(solution)/shard_map/all_to_all | solution.py:418
  1650.3 58.1 %collective-permute-start.106 = (bf16[6,128,1024]{2,1,0:T(8,128)(2,1)}, bf16[6,128,1024]{2,1,0:T(8,128)(2,1)}, u32[]{:S(2)}, u32[]{:S(2)}) collective-permute-start(bf16[6,128,1024]{2,1,0:T(8,128)(2,1)} %get-tuple-element.54), channel_id=1, source_target_pairs={{16,0},{24,8},{0,16},{8,24},{17,1},{25,9},{1,17},{9,25},{18,2},{26... | collective-permute-start | bytes 4718600 | tf_op jit(solution)/shard_map/ppermute | solution.py:69
  1663.4 68.1 %all-to-all-start.3 = ((bf16[8,128,1024]{2,1,0:T(8,128)(2,1)}), bf16[8,128,1024]{2,1,0:T(8,128)(2,1)}, u32[]{:S(2)}, u32[]{:S(2)}) async-start(bf16[8,128,1024]{2,1,0:T(8,128)(2,1)} %bitcast.1086), calls=%async_computation.3 | async-start | bytes 4194304 | tf_op jit(solution)/shard_map/all_to_all | solution.py:423
  (408 other events, 5031.5 us)

commit v2 on v1

v2 whole, which is shorter than its diff:
```python
import functools

import jax
import jax.numpy as jnp
import numpy as np
from jax import lax
from jax.experimental import pallas as pl
from jax.experimental.pallas import tpu as pltpu
from jax.sharding import PartitionSpec as P

D = 1024
HEADS = 16
HEAD_DIM = 64
FF = 4096
BLK = 1024
LAYERS = 2
NBLK = 12
CORES = 2
DEPTH_Z = 4

EPS_NORM = 1e-05
EPS_ADAM = 1e-08
LR_BLOCK = 0.1
LR_VEC = 0.25
DECAY_RATE = 0.5
VMEM_BYTES = 56 * 1024 * 1024
BF16 = jnp.bfloat16
F32 = jnp.float32


class Place:
    def __init__(self, ctx_count, wsh_count):
        self.size = {
            "core": CORES,
            "y": ctx_count // CORES,
            "z": DEPTH_Z,
            "x": wsh_count // DEPTH_Z,
        }
        ctx_at = lax.axis_index("ctx")
        wsh_at = lax.axis_index("wsh")
        self.at = {
            "core": ctx_at % CORES,
            "y": ctx_at // CORES,
            "z": wsh_at // self.size["x"],
            "x": wsh_at % self.size["x"],
        }

    def take(self, value, axis, step):
        name, slow, fast = {
            "core": ("ctx", "y", "core"),
            "y": ("ctx", "y", "core"),
            "z": ("wsh", "z", "x"),
            "x": ("wsh", "z", "x"),
        }[axis]
        extent = self.size[axis]
        pairs = []
        for slow_at in range(self.size[slow]):
            for fast_at in range(self.size[fast]):
                if axis == fast:
                    other = (slow_at, (fast_at + step) % extent)
                else:
                    other = ((slow_at + step) % extent, fast_at)
                pairs.append(
                    (
                        other[0] * self.size[fast] + other[1],
                        slow_at * self.size[fast] + fast_at,
                    )
                )
        return lax.ppermute(value, name, pairs)

    def gather(self, value, axis):
        steps = range(1, self.size[axis])
        return jnp.stack([value] + [self.take(value, axis, step) for step in steps])

    def collect(self, values, axis):
        steps = range(1, self.size[axis])
        return [values[0]] + [self.take(values[step], axis, -step) for step in steps]

    def scatter(self, values, axis):
        total = values[0].astype(F32)
        for step in range(1, self.size[axis]):
            total = total + self.take(values[step], axis, -step).astype(F32)
        return total


def vector_parts(vector):
    pieces = [vector[spot * D : (spot + 1) * D] for spot in range(8)]
    return pieces + [vector[8 * D :]]


def dot(left, right):
    return jnp.dot(left, right, preferred_element_type=F32)


def dot_t(left, right):
    return lax.dot_general(left, right, (((1,), (1,)), ((), ())), preferred_element_type=F32)


def assemble_kernel(split_count, whole_count, has_y, where, *refs):
    if has_y:
        mine, other_y, core_mine, core_other_y, out = refs
    else:
        mine, core_mine, out = refs
    half_rows = mine.shape[3]
    half_cols = mine.shape[4]
    core_at = where[3]
    y_at = where[2]

    def put(block, rows, cols, value):
        out[block, 0, pl.ds(rows * half_rows, half_rows), pl.ds(cols * half_cols, half_cols)] = value

    for core in range(2):

        @pl.when(core_at == core)
        def _():
            if has_y:
                for y in range(2):

                    @pl.when(y_at == y)
                    def _():
                        for block in range(split_count):
                            put(block, core, y, mine[0, 0, block])
                            put(block, core, 1 - y, other_y[0, 0, block])
                            put(block, 1 - core, y, core_mine[0, 0, block])
                            put(block, 1 - core, 1 - y, core_other_y[0, 0, block])

            for block in range(whole_count):
                for cols in range(2):
                    entry = split_count + 2 * block + cols
                    put(split_count + block, core, cols, mine[0, 0, entry])
                    put(split_count + block, 1 - core, cols, core_mine[0, 0, entry])


def after(value, *others):
    return lax.optimization_barrier((value,) + others)[0]


def together(*values):
    return lax.optimization_barrier(values)


def add_up(values):
    return sum(value.astype(F32) for value in values)


class Gathering:
    def __init__(self, place, shard):
        self.place = place
        self.count, self.rows, _ = shard.shape
        half_rows, half_cols = self.rows // 2, BLK // 2
        has_y = place.size["y"] == 2
        self.split_count = self.count // 2 if has_y else 0
        whole_count = self.count - self.split_count
        mine = lax.dynamic_slice_in_dim(shard, place.at["core"] * half_rows, half_rows, 1)
        whole = mine[self.split_count :]
        pieces = [
            part
            for block in range(whole_count)
            for part in (whole[block, :, :half_cols], whole[block, :, half_cols:])
        ]
        piece = jnp.stack(pieces)
        if has_y:
            parts = lax.dynamic_slice_in_dim(
                mine[: self.split_count], place.at["y"] * half_cols, half_cols, 2
            )
            piece = jnp.concatenate([parts, piece])
        self.held = [piece]
        self.crossed = []

    def step_z(self):
        self.held = gather_list(self.place, self.held[0], "z")

    def step_x(self):
        self.held = gather_list(self.place, jnp.stack(self.held), "x")

    def step_y(self):
        self.held = [jnp.stack(self.held)]
        if self.split_count:
            value = self.held[0][:, :, : self.split_count]
            self.held.append(self.place.take(value, "y", 1))
        self.crossed = [self.place.take(self.held[0], "core", 1)]

    def step_core(self):
        if self.split_count:
            self.crossed.append(self.place.take(self.held[1], "core", 1))

    def whole(self):
        place, operands = self.place, self.held + self.crossed
        count_z, count_x = place.size["z"], place.size["x"]
        where = jnp.stack([place.at[name] for name in ("z", "x", "y", "core")]).astype(jnp.int32)

        def piece_at(z, x, where):
            return (
                lax.rem(x - where[1] + count_x, count_x),
                lax.rem(z - where[0] + count_z, count_z),
                0,
                0,
                0,
            )

        out = call(
            functools.partial(
                assemble_kernel, self.split_count, self.count - self.split_count, self.split_count > 0
            ),
            (count_z, count_x),
            [pl.BlockSpec((1, 1) + value.shape[2:], piece_at) for value in operands],
            pl.BlockSpec(
                (self.count, 1, self.rows, BLK), lambda z, x, where: (0, z * count_x + x, 0, 0)
            ),
            shaped((self.count, count_z * count_x, self.rows, BLK), BF16),
            prefetch=1,
            cost=9.0,
            name="assemble",
        )(where, *operands)
        return out.reshape(self.count, BLK, BLK)


def call(body, grid, in_specs, out_specs, out_shape, scratch=(), prefetch=0, cost=1.0, name=None):
    return pl.pallas_call(
        body,
        grid_spec=pltpu.PrefetchScalarGridSpec(
            num_scalar_prefetch=prefetch,
            grid=grid,
            in_specs=in_specs,
            out_specs=out_specs,
            scratch_shapes=list(scratch),
        ),
        out_shape=out_shape,
        compiler_params=pltpu.CompilerParams(vmem_limit_bytes=VMEM_BYTES),
        cost_estimate=pl.CostEstimate(flops=int(cost * 1e9), bytes_accessed=0, transcendentals=0),
        name=name,
    )


def shaped(shape, dtype):
    return jax.ShapeDtypeStruct(shape, dtype)


def fixed(shape):
    return pl.BlockSpec(shape, lambda *at: (0,) * len(shape))


def norm_stats(summed):
    average = jnp.mean(summed, axis=-1, keepdims=True)
    centred = summed - average
    variance = jnp.mean(centred * centred, axis=-1, keepdims=True)
    scale = lax.rsqrt(variance + EPS_NORM)
    return centred * scale, scale


def norm_back(grad, normed, scale, gain):
    flow = grad * gain
    return (
        flow
        - jnp.mean(flow, axis=-1, keepdims=True)
        - normed * jnp.mean(flow * normed, axis=-1, keepdims=True)
    ) * scale


def project_kernel(x_low, weight, bias, query, keyval):
    value = (dot(x_low[...], weight[0]) + bias[0]).astype(BF16)

    @pl.when(pl.program_id(0) == 0)
    def _():
        query[...] = value

    @pl.when(pl.program_id(0) > 0)
    def _():
        keyval[...] = value


def project(x_low, w_in, bias):
    tokens = x_low.shape[0]
    return call(
        project_kernel,
        (3,),
        [
            fixed((tokens, D)),
            pl.BlockSpec((1, BLK, BLK), lambda i: (i, 0, 0)),
            pl.BlockSpec((1, 1, D), lambda i: (i, 0, 0)),
        ],
        [fixed((tokens, D)), pl.BlockSpec((tokens, D), lambda i: (0, jnp.maximum(i - 1, 0)))],
        [shaped((tokens, D), BF16), shaped((tokens, 2 * D), BF16)],
        cost=6.0,
        name="project",
    )(x_low, w_in, bias)


def head_probs(query_h, keys_h, masks):
    scores = [
        dot_t(key, query_h) * HEAD_DIM ** (-0.5) + mask for key, mask in zip(keys_h, masks)
    ]
    peak = functools.reduce(
        jnp.maximum, [jnp.max(score, axis=0, keepdims=True) for score in scores]
    )
    scores = [jnp.exp(score - peak) for score in scores]
    total = sum(jnp.sum(score, axis=0, keepdims=True) for score in scores)
    inverse = 1.0 / total
    return [score * inverse for score in scores]


def dot_tt(left, right):
    return lax.dot_general(left, right, (((0,), (0,)), ((), ())), preferred_element_type=F32)


def head_of(ref, head):
    return ref[:, pl.ds(head * HEAD_DIM, HEAD_DIM)]


def attend_kernel(count, tokens, query, mask, *refs):
    keys, values, out = refs[:count], refs[count : 2 * count], refs[-1]
    masks = [mask[pl.ds(spot * tokens, tokens), :] for spot in range(count)]
    mixed = []
    for head in range(2):
        probs = head_probs(head_of(query, head), [head_of(key, head) for key in keys], masks)
        mixed.append(
            sum(dot_tt(head_of(value, head), prob.astype(BF16)) for value, prob in zip(values, probs))
        )
    out[...] = jnp.concatenate(mixed, axis=0).T.astype(BF16)


def pair_specs(tokens, count):
    pair = 2 * HEAD_DIM
    half = D // pair
    return (
        [pl.BlockSpec((tokens, pair), lambda i: (0, i))] * count
        + [pl.BlockSpec((tokens, pair), lambda i: (0, half + i))] * count
    )


def attend(query, keyvals, mask):
    tokens = query.shape[0]
    count = len(keyvals)
    pair = 2 * HEAD_DIM
    return call(
        functools.partial(attend_kernel, count, tokens),
        (D // pair,),
        [pl.BlockSpec((tokens, pair), lambda i: (0, i)), fixed(mask.shape)]
        + pair_specs(tokens, count),
        pl.BlockSpec((tokens, pair), lambda i: (0, i)),
        shaped((tokens, D), BF16),
        cost=14.0,
        name="attend",
    )(query, mask, *keyvals, *keyvals)


def attend_back_kernel(count, count_y, tokens, query, grad, mask, *refs):
    keys, values = refs[:count], refs[count : 2 * count]
    grad_q, mine, other = refs[2 * count :]
    masks = [mask[pl.ds(spot * tokens, tokens), :] for spot in range(count)]
    scale = HEAD_DIM ** (-0.5)
    grads_q = []
    grads_k = [[] for _ in range(count)]
    grads_v = [[] for _ in range(count)]
    for head in range(2):
        query_h = head_of(query, head)
        grad_h = head_of(grad, head)
        keys_h = [head_of(key, head) for key in keys]
        probs = head_probs(query_h, keys_h, masks)
        grad_probs = [dot_t(head_of(value, head), grad_h) for value in values]
        inner = sum(
            jnp.sum(prob * grad_prob, axis=0, keepdims=True)
            for prob, grad_prob in zip(probs, grad_probs)
        )
        flow_q = 0.0
        for spot in range(count):
            grad_score = (probs[spot] * (grad_probs[spot] - inner)).astype(BF16)
            flow_q = flow_q + dot_tt(keys_h[spot], grad_score)
            grads_k[spot].append(dot(grad_score, query_h) * scale)
            grads_v[spot].append(dot(probs[spot].astype(BF16), grad_h))
        grads_q.append(flow_q * scale)
    grad_q[...] = jnp.concatenate(grads_q, axis=0).T.astype(BF16)
    for spot in range(count):
        out = mine if spot < count_y else other
        out[0, spot % count_y] = jnp.concatenate(grads_k[spot], axis=1).astype(BF16)
        out[1, spot % count_y] = jnp.concatenate(grads_v[spot], axis=1).astype(BF16)


def attend_back(query, keyvals, grad, mask):
    tokens = query.shape[0]
    count = len(keyvals)
    count_y = count // CORES
    pair = 2 * HEAD_DIM
    part = pl.BlockSpec((2, count_y, tokens, pair), lambda i: (0, 0, 0, i))
    return call(
        functools.partial(attend_back_kernel, count, count_y, tokens),
        (D // pair,),
        [pl.BlockSpec((tokens, pair), lambda i: (0, i))] * 2
        + [fixed(mask.shape)]
        + pair_specs(tokens, count),
        [pl.BlockSpec((tokens, pair), lambda i: (0, i)), part, part],
        [shaped((tokens, D), BF16)] + [shaped((2, count_y, tokens, D), BF16)] * 2,
        cost=21.0,
        name="attend_back",
    )(query, grad, mask, *keyvals, *keyvals)


def mix_kernel(attn, weight, carried, vecs, summed, middle, middle_low):
    value = carried[...].astype(F32) + (dot(attn[...], weight[0]) + vecs[0:1, :])
    summed[...] = value
    normed, _ = norm_stats(value)
    value = normed * vecs[1:2, :] + vecs[2:3, :]
    middle[...] = value
    middle_low[...] = value.astype(BF16)


def mix(attn, w_in, carried, vecs):
    tokens = attn.shape[0]
    full = fixed((tokens, D))
    return call(
        mix_kernel,
        (1,),
        [full, pl.BlockSpec((1, BLK, BLK), lambda i: (3, 0, 0)), full, fixed(vecs.shape)],
        [full, full, full],
        [shaped((tokens, D), F32), shaped((tokens, D), F32), shaped((tokens, D), BF16)],
        cost=4.0,
        name="mix",
    )(attn, w_in, carried, vecs)


def erf_part(hidden):
    return (1.0 + lax.erf(hidden * (0.5**0.5))) * 0.5


def up_kernel(middle_low, weight, bias, hidden, act):
    value = dot(middle_low[...], weight[0]) + bias[0]
    hidden[...] = value
    act[...] = (value * erf_part(value)).astype(BF16)


def up(middle_low, w_up, bias):
    tokens = middle_low.shape[0]
    part = pl.BlockSpec((tokens, BLK), lambda i: (0, i))
    return call(
        up_kernel,
        (FF // BLK,),
        [
            fixed((tokens, D)),
            pl.BlockSpec((1, BLK, BLK), lambda i: (i, 0, 0)),
            pl.BlockSpec((1, 1, BLK), lambda i: (i, 0, 0)),
        ],
        [part, part],
        [shaped((tokens, FF), F32), shaped((tokens, FF), BF16)],
        cost=8.0,
        name="up",
    )(middle_low, w_up, bias)


def down_kernel(act, weight, middle, vecs, summed, result, result_low, total):
    spot = pl.program_id(0)
    value = dot(act[...], weight[0])

    @pl.when(spot == 0)
    def _():
        total[...] = value

    @pl.when(spot > 0)
    def _():
        total[...] += value

    @pl.when(spot == pl.num_programs(0) - 1)
    def _():
        value = middle[...] + (total[...] + vecs[0:1, :])
        summed[...] = value
        normed, _ = norm_stats(value)
        value = normed * vecs[1:2, :] + vecs[2:3, :]
        result[...] = value
        result_low[...] = value.astype(BF16)


def down(act, w_down, middle, vecs):
    tokens = act.shape[0]
    full = fixed((tokens, D))
    return call(
        down_kernel,
        (FF // BLK,),
        [
            pl.BlockSpec((tokens, BLK), lambda i: (0, i)),
            pl.BlockSpec((1, BLK, BLK), lambda i: (i, 0, 0)),
            full,
            fixed(vecs.shape),
        ],
        [full, full, full],
        [shaped((tokens, D), F32), shaped((tokens, D), F32), shaped((tokens, D), BF16)],
        scratch=[pltpu.VMEM((tokens, D), F32)],
        cost=8.0,
        name="down",
    )(act, w_down, middle, vecs)


def column_sum(value):
    return jnp.sum(value, axis=0, keepdims=True)


def close_kernel(flow, summed, gain, back_out, low_out, sums):
    grad = flow[...].astype(F32)
    normed, scale = norm_stats(summed[...])
    back = norm_back(grad, normed, scale, gain[...])
    back_out[...] = back
    low = back.astype(BF16)
    low_out[...] = low
    sums[0:1, :] = column_sum(low.astype(F32))
    sums[1:2, :] = column_sum(grad * normed)
    sums[2:3, :] = column_sum(grad)
    sums[3:8, :] = jnp.zeros((5, D), F32)


def close(flow, summed, gain):
    tokens = flow.shape[0]
    full = fixed((tokens, D))
    return call(
        close_kernel,
        (1,),
        [full, full, fixed((1, D))],
        [full, full, fixed((8, D))],
        [shaped((tokens, D), F32), shaped((tokens, D), BF16), shaped((8, D), F32)],
        cost=3.0,
        name="close",
    )(flow, summed, gain)


def feed_back_kernel(
    grad_two, ffn_low, summed_one, hidden, w_down, w_up, w_out, gain,
    hid_low, branch_low, attn_grad, grad_one, sums, bias_sums, total,
):
    spot = pl.program_id(0)

    @pl.when(spot == 0)
    def _():
        total[...] = grad_two[...]

    value = hidden[...]
    slope = erf_part(value) + value * jnp.exp(-0.5 * value * value) * ((2.0 * np.pi) ** -0.5)
    low = (dot_t(ffn_low[...], w_down[0]) * slope).astype(BF16)
    hid_low[...] = low
    bias_sums[0] = column_sum(low.astype(F32))
    total[...] += dot_t(low, w_up[0])

    @pl.when(spot == pl.num_programs(0) - 1)
    def _():
        grad = total[...]
        normed, scale = norm_stats(summed_one[...])
        back = norm_back(grad, normed, scale, gain[...])
        grad_one[...] = back
        low = back.astype(BF16)
        branch_low[...] = low
        sums[0:1, :] = column_sum(low.astype(F32))
        sums[1:2, :] = column_sum(grad * normed)
        sums[2:3, :] = column_sum(grad)
        sums[3:8, :] = jnp.zeros((5, D), F32)
        attn_grad[...] = dot_t(low, w_out[0]).astype(BF16)


def feed_back(grad_two, ffn_low, summed_one, hidden, w_down, w_up, w_in, gain):
    tokens = ffn_low.shape[0]
    full = fixed((tokens, D))
    part = pl.BlockSpec((tokens, BLK), lambda i: (0, i))
    weight = pl.BlockSpec((1, BLK, BLK), lambda i: (i, 0, 0))
    return call(
        feed_back_kernel,
        (FF // BLK,),
        [full, full, full, part, weight, weight, pl.BlockSpec((1, BLK, BLK), lambda i: (3, 0, 0)), fixed((1, D))],
        [part, full, full, full, fixed((8, D)), pl.BlockSpec((1, 1, BLK), lambda i: (i, 0, 0))],
        [
            shaped((tokens, FF), BF16),
            shaped((tokens, D), BF16),
            shaped((tokens, D), BF16),
            shaped((tokens, D), F32),
            shaped((8, D), F32),
            shaped((FF // BLK, 1, BLK), F32),
        ],
        scratch=[pltpu.VMEM((tokens, D), F32)],
        cost=15.0,
        name="feed_back",
    )(grad_two, ffn_low, summed_one, hidden, w_down, w_up, w_in, gain)


def input_back_kernel(count, grad_q, grad_one, weight, *refs):
    parts, (joined, result, sums, total) = refs[:count], refs[count:]
    spot = pl.program_id(0)

    @pl.when(spot == 0)
    def _():
        joined[...] = grad_q[...]
        total[...] = grad_one[...]

    @pl.when(spot > 0)
    def _():
        joined[...] = sum(part[0].astype(F32) for part in parts).astype(BF16)

    low = joined[...]
    sums[0] = column_sum(low.astype(F32))
    total[...] += dot_t(low, weight[0])

    @pl.when(spot == pl.num_programs(0) - 1)
    def _():
        result[...] = total[...]


def input_back(grad_q, parts, grad_one, w_in):
    tokens = grad_q.shape[0]
    full = fixed((tokens, D))
    return call(
        functools.partial(input_back_kernel, len(parts)),
        (3,),
        [full, full, pl.BlockSpec((1, BLK, BLK), lambda i: (i, 0, 0))]
        + [pl.BlockSpec((1, tokens, D), lambda i: (jnp.maximum(i - 1, 0), 0, 0))] * len(parts),
        [pl.BlockSpec((tokens, D), lambda i: (0, i)), full, pl.BlockSpec((1, 1, D), lambda i: (i, 0, 0))],
        [shaped((tokens, 3 * D), BF16), shaped((tokens, D), F32), shaped((3, 1, D), F32)],
        scratch=[pltpu.VMEM((tokens, D), F32)],
        cost=8.0,
        name="input_back",
    )(grad_q, grad_one, w_in, *parts)


def gather_list(place, value, axis):
    return [value] + [place.take(value, axis, step) for step in range(1, place.size[axis])]


def project_step(place, carried_low, w_in, vector):
    parts = vector_parts(vector)
    bias_in = jnp.stack([parts[0], jnp.zeros((D,), F32), parts[1]])[:, None]
    query, keyval = project(carried_low, w_in, bias_in)
    return query, gather_list(place, keyval, "y")


def mix_step(query, keyvals, carried, w_in, vector, mask):
    parts = vector_parts(vector)
    attn_low = attend(query, keyvals, mask)
    return attn_low, *mix(attn_low, w_in, carried, jnp.stack([parts[2], parts[4], parts[5]]))


def up_step(mid_low, w_up, vector):
    return up(mid_low, w_up, vector[8 * D :].reshape(FF // BLK, 1, BLK))


def down_step(act_low, w_down, middle, vector):
    parts = vector_parts(vector)
    return down(act_low, w_down, middle, jnp.stack([parts[3], parts[6], parts[7]]))


def sum_kernel(count_one, first_half, sizes, where, *refs):
    sets = (refs[:4], refs[4:8]) if count_one is not None else (refs[:4],)
    outs, product = refs[4 * len(sets) : -1], refs[-1]
    z_at, x_at, y_at = where[0], where[1], where[2]
    extent_z, extent_x, extent_y, rows = sizes
    spot = pl.program_id(0)

    def multiply(left_mine, left_other, right_mine, right_other):
        left = jnp.concatenate([left_mine[...], left_other[...]], axis=0)
        right = jnp.concatenate([right_mine[...], right_other[...]], axis=0)
        product[...] = dot_tt(left, right)

    if len(sets) == 1:
        multiply(*sets[0])
    else:
        pl.when(spot < count_one)(lambda: multiply(*sets[0]))
        pl.when(spot >= count_one)(lambda: multiply(*sets[1]))
    cols = product.shape[1] // extent_y

    def put(y_first):
        for step_y in range(extent_y):
            from_col = pl.multiple_of(lax.rem(y_at + step_y, extent_y) * cols, cols)
            for step_x in range(extent_x):
                for step_z in range(extent_z):
                    row_block = lax.rem(z_at + step_z, extent_z) * extent_x + lax.rem(
                        x_at + step_x, extent_x
                    )
                    from_row = pl.multiple_of(row_block * rows, rows)
                    value = product[pl.ds(from_row, rows), pl.ds(from_col, cols)].astype(BF16)
                    if y_first:
                        outs[step_y][step_x, step_z, 0] = value
                    else:
                        outs[extent_y + step_x][step_y, step_z, 0] = value

    pl.when(spot < first_half)(lambda: put(True))
    pl.when(spot >= first_half)(lambda: put(False))


def partial_sums(place, sets):
    tokens = sets[0][0].shape[0]
    extent_z, extent_x, extent_y = (place.size[name] for name in ("z", "x", "y"))
    rows = BLK // (extent_z * extent_x)
    half = BLK // CORES
    cols = half // extent_y
    where = jnp.stack([place.at[name] for name in ("z", "x", "y", "core")]).astype(jnp.int32)
    counts = [max(one[0].shape[1], one[2].shape[1]) // BLK for one in sets]
    count = sum(counts)
    first_half = count // 2
    specs = []
    start = 0
    for one, amount in zip(sets, counts):

        def at(i, start=start, amount=amount):
            return jnp.clip(i - start, 0, amount - 1)

        many_left, many_right = one[0].shape[1] > BLK, one[2].shape[1] > BLK
        specs += [
            pl.BlockSpec((tokens, BLK), lambda i, where, at=at, many=many_left: (0, at(i) if many else 0))
        ] * 2
        specs += [
            pl.BlockSpec(
                (tokens, half),
                lambda i, where, at=at, many=many_right: (0, (at(i) * CORES if many else 0) + where[3]),
            )
        ] * 2
        start += amount
    part_y = (extent_x, extent_z, 1, rows, cols)
    part_x = (extent_y, extent_z, 1, rows, cols)
    spec_y = pl.BlockSpec(part_y, lambda i, where: (0, 0, jnp.minimum(i, first_half - 1), 0, 0))
    spec_x = pl.BlockSpec(part_x, lambda i, where: (0, 0, jnp.maximum(i - first_half, 0), 0, 0))
    outs = call(
        functools.partial(
            sum_kernel,
            counts[0] if len(sets) > 1 else None,
            first_half,
            (extent_z, extent_x, extent_y, rows),
        ),
        (count,),
        specs,
        [spec_y] * extent_y + [spec_x] * extent_x,
        [shaped((extent_x, extent_z, first_half, rows, cols), BF16)] * extent_y
        + [shaped((extent_y, extent_z, count - first_half, rows, cols), BF16)] * extent_x,
        scratch=[pltpu.VMEM((BLK, half), F32)],
        prefetch=1,
        cost=8.0,
        name="partial_sums",
    )(where, *[value for one in sets for value in one])
    return outs[:extent_y], outs[extent_y:]


class Summing:
    def __init__(self, place, sets):
        self.place = place
        if (BLK // (CORES * place.size["y"])) % 128:
            self.plain = True
            self.parts = self.by_y = self.by_x = ()
            self.groups = [[sum_job_plain(place, one[0], one[2], "y")] for one in sets]
        else:
            self.plain = False
            sets = [(one[0], one[1], one[2], place.take(one[2], "core", 1)) for one in sets]
            self.parts = partial_sums(place, sets)
            self.by_y = self.by_x = ()
            self.groups = ()

    def first_y(self):
        if not self.plain:
            self.by_y = self.place.collect(self.parts[0], "y")

    def first_x(self):
        if not self.plain:
            self.by_x = self.place.collect(self.parts[1], "x")

    def second_x(self):
        if not self.plain:
            total = add_up(self.by_y)
            parts = [total[step].astype(BF16) for step in range(self.place.size["x"])]
            self.by_y = self.place.collect(parts, "x")

    def second_y(self):
        if not self.plain:
            total = add_up(self.by_x)
            parts = [total[step].astype(BF16) for step in range(self.place.size["y"])]
            self.by_x = self.place.collect(parts, "y")

    def third(self):
        if not self.plain:
            by_y, by_x = add_up(self.by_y), add_up(self.by_x)
            both = [
                jnp.concatenate([by_y[step], by_x[step]]).astype(BF16)
                for step in range(self.place.size["z"])
            ]
            self.groups = [self.place.collect(both, "z")]


def route_kernel(groups, slots, scaling, spots, *refs):
    out, total = refs[-2:]
    refs = list(refs[:-2])
    at = 0
    for addends in groups:
        parts = [refs.pop(0) for _ in range(addends)]
        for block in range(parts[0].shape[0]):
            value = sum(part[block].astype(F32) for part in parts)
            total[at] = (value * scaling).astype(BF16)
            at += 1
    total[at] = jnp.zeros(total.shape[1:], BF16)
    for ctx in range(out.shape[0]):
        for spot in range(out.shape[1]):
            if spot < slots:
                out[ctx, spot] = total[spots[ctx * slots + spot]]
            else:
                out[ctx, spot] = total[at]


def route(groups, spots, slots, wsh_count, scaling):
    rows, cols = groups[0][0].shape[1:]
    blocks = sum(addends[0].shape[0] for addends in groups)
    flat = [value for addends in groups for value in addends]
    shape = (spots.shape[0] // slots, wsh_count, rows, cols)
    return call(
        functools.partial(route_kernel, [len(addends) for addends in groups], slots, scaling),
        (1,),
        [fixed(value.shape) for value in flat],
        fixed(shape),
        shaped(shape, BF16),
        scratch=[pltpu.VMEM((blocks + 1, rows, cols), BF16)],
        prefetch=1,
        cost=6.0,
        name="route",
    )(spots, *flat)


def rotate_kernel(quarters, where, grads, right, left, first, second, rotated, update, total, low, right_low):
    step = BLK // 4
    right_low[...] = right[0].astype(BF16)
    for at in range(4):
        rows = pl.ds(at * step, step)
        product = 0.0
        for source, quarter in enumerate(quarters):
            width = grads.shape[2]
            product = product + dot(
                grads[source, rows, :], right_low[pl.ds(quarter * width, width), :]
            )
        value = dot_tt(left[rows, :], product.astype(BF16))
        if at:
            total[...] += value
        else:
            total[...] = value
    for at in range(4):
        rows = pl.ds(at * step, step)
        turned = total[rows, :]
        rotated[rows, :] = turned.astype(BF16)
        first_new = DECAY_RATE * first[rows, :].astype(F32) + (1.0 - DECAY_RATE) * turned
        second_new = DECAY_RATE * second[rows, :].astype(F32) + (1.0 - DECAY_RATE) * turned * turned
        direction = first_new / (jnp.sqrt(second_new) + EPS_ADAM)
        low[rows, :] = dot_t(direction.astype(BF16), right_low[...]).astype(BF16)
    for at in range(4):
        rows = pl.ds(at * step, step)
        update[rows, :] = dot(left[rows, :], low[...]).astype(BF16)


def rotate(grads, quarters, right_bases, slot, left, first, second):
    full = fixed((BLK, BLK))
    return call(
        functools.partial(rotate_kernel, quarters),
        (1,),
        [
            fixed(grads.shape),
            pl.BlockSpec((1, BLK, BLK), lambda i, where: (where[0], 0, 0)),
            full,
            full,
            full,
        ],
        [full, full],
        [shaped((BLK, BLK), BF16)] * 2,
        scratch=[pltpu.VMEM((BLK, BLK), F32), pltpu.VMEM((BLK, BLK), BF16), pltpu.VMEM((BLK, BLK), BF16)],
        prefetch=1,
        cost=16.0,
        name="rotate",
    )(slot, grads, right_bases, left, first, second)


def pick_kernel(count, table, *refs):
    parts, out = refs[:count], refs[count]
    block = pl.program_id(0)

    def put(part):
        out[0] = parts[part][table[1, block]]

    for part in range(count):
        pl.when(table[0, block] == part)(functools.partial(put, part))


def pick(parts, table):
    blocks = table.shape[1]
    shape = (blocks,) + parts[0].shape[1:]
    return call(
        functools.partial(pick_kernel, len(parts)),
        (blocks,),
        [fixed(value.shape) for value in parts],
        pl.BlockSpec((1,) + shape[1:], lambda i, table: (i, 0, 0)),
        shaped(shape, BF16),
        prefetch=1,
        cost=12.0,
        name="pick",
    )(table, *parts)


def left_order(place, left):
    tokens, cols = left.shape
    count_z, count_x = place.size["z"], place.size["x"]
    blocks = cols // BLK
    rows = BLK // (count_z * count_x)
    value = left.reshape(tokens, blocks, count_z, count_x, rows)
    value = jnp.roll(value, (-place.at["z"], -place.at["x"]), axis=(2, 3))
    return value.transpose(0, 3, 2, 1, 4).reshape(tokens, cols)


def right_halves(place, right):
    tokens, cols = right.shape
    count_y = place.size["y"]
    width = BLK // (CORES * count_y)
    value = right.reshape(tokens, cols // BLK, CORES, count_y, width)
    halves = []
    for step in range(CORES):
        half = lax.dynamic_index_in_dim(value, (place.at["core"] + step) % CORES, 2, False)
        half = jnp.roll(half, -place.at["y"], axis=2)
        halves.append(half.transpose(2, 0, 1, 3).reshape(count_y, tokens, -1))
    return halves


def sum_job_plain(place, left, right, first):
    count_z, count_x, count_y = place.size["z"], place.size["x"], place.size["y"]
    left = left_order(place, left)
    right_mine, right_other = right_halves(place, right)
    left_both = jnp.concatenate([left, place.take(left, "core", 1)], axis=0)
    right_both = jnp.concatenate([right_mine, place.take(right_other, "core", 1)], axis=1)
    partial = [
        lax.dot_general(left_both, right_both[step], (((0,), (0,)), ((), ())), preferred_element_type=F32)
        .astype(BF16)
        .reshape(count_x, count_z, -1, right_both.shape[2])
        for step in range(count_y)
    ]
    if first == "y":
        total = place.scatter(partial, "y").astype(BF16)
        total = place.scatter(total, "x").astype(BF16)
    else:
        parts = [[value[step] for value in partial] for step in range(count_x)]
        parts = [jnp.stack(part) for part in parts]
        total = place.scatter(parts, "x").astype(BF16)
        total = place.scatter(total, "y").astype(BF16)
    total = place.scatter(total, "z")
    rows = BLK // (count_z * count_x)
    width = BLK // (CORES * count_y)
    if left.shape[1] > BLK:
        return total.reshape(-1, rows, width)
    return total.reshape(rows, -1, width).transpose(1, 0, 2)


def sum_everywhere(place, value):
    if place.size["y"] != 2 or place.size["x"] != 2:
        return lax.psum(value, ("ctx", "wsh"))
    for axis in ("core", "y", "x"):
        value = value + place.take(value, axis, 1)
    pairs = place.size["x"]
    for bit in (1, 2):
        swap = [
            (z * pairs + x, (z ^ bit) * pairs + x) for z in range(DEPTH_Z) for x in range(pairs)
        ]
        value = value + lax.ppermute(value, "wsh", swap)
    return value


def doc_ids(lengths, position):
    starts = jnp.cumsum(lengths) - lengths
    return jnp.sum((position[:, None] >= starts[None, :]).astype(jnp.int32), axis=1)


def to_owner(rows_value, wsh_count):
    slots = rows_value.shape[0]
    padded = jnp.pad(rows_value.astype(BF16), ((0, wsh_count - slots), (0, 0), (0, 0)))
    return lax.all_to_all(padded, "wsh", 0, 0, tiled=True).reshape(BLK, BLK)


def from_owner(whole, wsh_count, slots):
    cut = whole.astype(BF16).reshape(wsh_count, BLK // wsh_count, BLK)
    return lax.all_to_all(cut, "wsh", 0, 0, tiled=True)[:slots]


def on_device(
    stream_in,
    doc_lengths,
    cotangent,
    weights,
    vec_params,
    owner_slots,
    master,
    left_bases,
    right_bases,
    moment1,
    moment2,
    vec_moment1,
    vec_moment2,
):
    tokens = stream_in.shape[1]
    ctx_count = lax.axis_size("ctx")
    wsh_count = lax.axis_size("wsh")
    place = Place(ctx_count, wsh_count)
    seq_len = tokens * ctx_count
    scaling = (wsh_count * seq_len) ** (-0.5)
    slots_dev, rows_dev = master.shape[0], master.shape[1]
    slot_total = ctx_count * slots_dev
    count_y = place.size["y"]
    width = BLK // ctx_count

    core_of = (place.at["core"] + jnp.arange(CORES)) % CORES
    y_of = (place.at["y"] + jnp.arange(count_y)) % count_y
    ctx_of = (y_of[None, :] * CORES + core_of[:, None]).reshape(-1)
    key_pos = (ctx_of[:, None] * tokens + jnp.arange(tokens)[None, :]).reshape(-1)
    doc_keys = doc_ids(doc_lengths[0], key_pos)
    mask = jnp.where(doc_keys[:, None] == doc_keys[None, :tokens], 0.0, -1e30).astype(F32)

    chunks = [
        Gathering(place, weights[layer_at, first : first + 4])
        for layer_at in range(LAYERS)
        for first in range(0, NBLK, 4)
    ]

    live = {}

    def settle():
        state = [(chunk.held, chunk.crossed) for chunk in chunks]
        state, values = together(state, {name: live[name] for name in live})
        for chunk, (held, crossed) in zip(chunks, state):
            chunk.held, chunk.crossed = held, crossed
        live.update(values)

    def finish(spot):
        chunks[spot].step_core()
        whole = chunks[spot].whole()
        chunks[spot].held = chunks[spot].crossed = []
        return whole

    def keyvals_of(layer_at):
        keyvals = live[f"keyvals{layer_at}"]
        return keyvals + [place.take(value, "core", 1) for value in keyvals]

    kept = [{}, {}]
    chunks[0].step_z()
    settle()
    chunks[0].step_x()
    chunks[1].step_z()
    settle()
    chunks[0].step_y()
    chunks[1].step_x()
    chunks[2].step_z()
    settle()
    chunks[1].step_y()
    chunks[2].step_x()
    chunks[3].step_z()
    w_in_0 = finish(0)
    query_0, live["keyvals0"] = project_step(place, stream_in[0], w_in_0, vec_params[0])
    live["query"] = query_0
    settle()
    chunks[2].step_y()
    chunks[3].step_x()
    chunks[4].step_z()
    keyvals_0 = keyvals_of(0)
    query_0 = live["query"]
    attn_0, summed_one_0, middle_0, mid_low_0 = mix_step(
        query_0, keyvals_0, stream_in[0], w_in_0, vec_params[0], mask
    )
    w_up_0 = finish(1)
    hidden_0, live["act"] = up_step(mid_low_0, w_up_0, vec_params[0])
    settle()
    chunks[3].step_y()
    chunks[4].step_x()
    chunks[5].step_z()
    act_0 = live["act"]
    w_down_0 = finish(2)
    summed_two_0, live["result"], live["result_low"] = down_step(
        act_0, w_down_0, middle_0, vec_params[0]
    )
    settle()
    chunks[4].step_y()
    chunks[5].step_x()
    result_0, result_low_0 = live["result"], live["result_low"]
    w_in_1 = finish(3)
    query_1, live["keyvals1"] = project_step(place, result_low_0, w_in_1, vec_params[1])
    live["query"] = query_1
    live["own"] = left_bases
    settle()
    chunks[5].step_y()
    live["own"] = to_owner(live["own"], wsh_count)
    keyvals_1 = keyvals_of(1)
    query_1 = live["query"]
    attn_1, summed_one_1, middle_1, mid_low_1 = mix_step(
        query_1, keyvals_1, result_0, w_in_1, vec_params[1], mask
    )
    w_up_1 = finish(4)
    hidden_1, live["act"] = up_step(mid_low_1, w_up_1, vec_params[1])
    live["first"] = moment1
    settle()
    left_own = live["own"]
    first_own = to_owner(live["first"], wsh_count)
    act_1 = live["act"]
    w_down_1 = finish(5)
    summed_two_1, _, result_low_1 = down_step(act_1, w_down_1, middle_1, vec_params[1])
    stream_out = result_low_1[None]

    blocks = [(w_in_0, w_up_0, w_down_0), (w_in_1, w_up_1, w_down_1)]
    lefts = [
        (stream_in[0], attn_0, mid_low_0, act_0),
        (result_low_0, attn_1, mid_low_1, act_1),
    ]
    crossed = [[place.take(value, "core", 1) for value in values] for values in lefts]
    summed = [(summed_one_0, summed_two_0), (summed_one_1, summed_two_1)]
    hidden = [hidden_0, hidden_1]
    queries = [query_0, query_1]
    keyvals_all = [keyvals_0, keyvals_1]
    gains = [
        (vec_params[layer_at][None, 4 * D : 5 * D], vec_params[layer_at][None, 6 * D : 7 * D])
        for layer_at in range(LAYERS)
    ]
    live = {}
    jobs = []
    vec_terms = [None] * LAYERS

    def settle_back():
        state = [(job.parts, job.by_y, job.by_x, job.groups) for job in jobs]
        state, values = together(state, dict(live))
        for job, fields in zip(jobs, state):
            job.parts, job.by_y, job.by_x, job.groups = fields
        live.update(values)

    def begin(layer_at, *sets):
        jobs.append(
            Summing(place, [(lefts[layer_at][spot], crossed[layer_at][spot], right) for spot, right in sets])
        )
        return jobs[-1]

    def close_step(layer_at, flow):
        live["two"], live["ffn"], live["sums_two"] = close(flow, summed[layer_at][1], gains[layer_at][1])
        return begin(layer_at, (3, live["ffn"]))

    def feed_step(layer_at):
        w_in, w_up, w_down = blocks[layer_at]
        hid_low, live["branch"], attn_grad, live["one"], live["sums_one"], live["sums_up"] = feed_back(
            live["two"], live["ffn"], summed[layer_at][0], hidden[layer_at], w_down, w_up, w_in, gains[layer_at][0]
        )
        live["attn_grad"] = attn_grad
        return begin(layer_at, (2, hid_low))

    def attend_step(layer_at):
        live["grad_q"], mine, other = attend_back(
            queries[layer_at], keyvals_all[layer_at], live["attn_grad"], mask
        )
        live["pair"] = [mine, place.take(other, "core", 1)]

    def send_step():
        mine, arrived = live["pair"]
        sums = [mine[:, step].astype(F32) + arrived[:, step].astype(F32) for step in range(count_y)]
        live["kv"] = [sums[0]] + [
            place.take(sums[step].astype(BF16), "y", -step) for step in range(1, count_y)
        ]

    def input_step(layer_at):
        joined, grad_x, in_sums = input_back(live["grad_q"], live["kv"], live["one"], blocks[layer_at][0])
        sums_two, sums_one = live["sums_two"], live["sums_one"]
        vec_terms[layer_at] = jnp.concatenate(
            [
                in_sums[0, 0],
                in_sums[2, 0],
                sums_one[0],
                sums_two[0],
                sums_one[1:3].reshape(-1),
                sums_two[1:3].reshape(-1),
                live["sums_up"].reshape(-1),
            ]
        )
        return grad_x, begin(layer_at, (0, joined), (1, live["branch"]))

    down_1 = close_step(1, cotangent[0])
    settle_back()
    down_1.first_y()
    down_1.first_x()
    live["first"] = first_own
    live["second"] = moment2
    up_1 = feed_step(1)
    settle_back()
    live["second"] = to_owner(live["second"], wsh_count)
    down_1.second_x()
    down_1.second_y()
    up_1.first_y()
    up_1.first_x()
    attend_step(1)
    settle_back()
    down_1.third()
    send_step()
    up_1.second_x()
    settle_back()
    up_1.second_y()
    grad_flow, in_1 = input_step(1)
    down_0 = close_step(0, grad_flow)
    settle_back()
    up_1.third()
    in_1.first_y()
    in_1.first_x()
    down_0.first_y()
    down_0.first_x()
    up_0 = feed_step(0)
    attend_step(0)
    settle_back()
    send_step()
    in_1.second_x()
    in_1.second_y()
    down_0.second_x()
    down_0.second_y()
    up_0.first_x()
    settle_back()
    in_1.third()
    down_0.third()
    up_0.first_y()
    up_0.second_y()
    grad_flow, in_0 = input_step(0)
    settle_back()
    in_0.first_y()
    in_0.first_x()
    up_0.second_x()
    settle_back()
    in_0.second_x()
    in_0.second_y()
    up_0.third()
    settle_back()
    in_0.third()
    stream_grad = grad_flow[None]
    vec_grads = sum_everywhere(place, jnp.stack(vec_terms)) * scaling
    groups = [
        group for layer_jobs in ((in_0, up_0, down_0), (in_1, up_1, down_1)) for job in layer_jobs for group in job.groups
    ]

    owner_flat = owner_slots.reshape(-1)
    block_count = LAYERS * NBLK
    picks = owner_flat[None, :] == jnp.arange(slot_total, dtype=jnp.int32)[:, None]
    spots = jnp.where(
        jnp.any(picks, axis=1), jnp.argmax(picks, axis=1).astype(jnp.int32), block_count
    )
    by_slot = route(groups, spots, slots_dev, wsh_count, scaling)

    arrived = lax.all_to_all(
        by_slot.reshape(ctx_count * wsh_count, rows_dev, width), ("ctx", "wsh"), 0, 0, tiled=True
    )
    quarters = [(source % CORES) * count_y + source // CORES for source in range(ctx_count)]
    slot_own = jnp.minimum(lax.axis_index("wsh"), slots_dev - 1).reshape(1)
    rotated_own, update_own = rotate(
        arrived.reshape(ctx_count, BLK, width), quarters, right_bases, slot_own, left_own, live["first"], live["second"]
    )

    by_rows = after(by_slot[:, :slots_dev], arrived)
    by_rows = lax.all_to_all(by_rows, "ctx", 0, 0, tiled=True)
    update_own, rotated_own, by_rows = together(update_own, rotated_own, by_rows)
    update = from_owner(update_own, wsh_count, slots_dev)
    update, rotated_own = together(update, rotated_own)
    update = update.astype(F32)
    by_rows = by_rows.reshape(count_y, CORES, slots_dev, rows_dev, width)
    block_grads = by_rows.transpose(2, 3, 1, 0, 4).reshape(slots_dev, rows_dev, BLK).astype(F32)

    new_master = master - LR_BLOCK * update
    master_low = new_master.astype(BF16)
    parts = gather_list(place, master_low, "y")
    rotated = from_owner(rotated_own, wsh_count, slots_dev)
    parts, rotated = together(parts, rotated)
    rotated = rotated.astype(F32)
    parts = parts + [place.take(value, "core", 1) for value in parts]
    owner_ctx, owner_at = owner_flat // slots_dev, owner_flat % slots_dev
    step_y = (owner_ctx // CORES - place.at["y"]) % count_y
    step_core = (owner_ctx % CORES - place.at["core"]) % CORES
    table = jnp.stack([step_core * count_y + step_y, owner_at]).astype(jnp.int32)
    new_weights = pick(parts, table).reshape(LAYERS, NBLK, rows_dev, BLK)

    new_moment1 = DECAY_RATE * moment1 + (1.0 - DECAY_RATE) * rotated
    new_moment2 = DECAY_RATE * moment2 + (1.0 - DECAY_RATE) * rotated * rotated

    new_vec_moment1 = DECAY_RATE * vec_moment1 + (1.0 - DECAY_RATE) * vec_grads
    new_vec_moment2 = DECAY_RATE * vec_moment2 + (1.0 - DECAY_RATE) * vec_grads * vec_grads
    new_vec_params = vec_params - LR_VEC * new_vec_moment1 / (jnp.sqrt(new_vec_moment2) + EPS_ADAM)
    return (
        stream_out,
        stream_grad,
        block_grads,
        new_moment1,
        new_moment2,
        new_master,
        new_weights,
        vec_grads,
        new_vec_params,
        new_vec_moment1,
        new_vec_moment2,
    )


def solution(mesh):
    rows = P("ctx", "wsh", None)
    placed = (
        P("wsh", "ctx", None),
        P("wsh", None),
        P("wsh", "ctx", None),
        P(None, None, "wsh", None),
        P(),
        P(),
        rows,
        rows,
        P("ctx", None, None),
        rows,
        rows,
        P(),
        P(),
    )
    return jax.shard_map(
        on_device,
        mesh=mesh,
        in_specs=placed,
        out_specs=(
            P("wsh", "ctx", None),
            P("wsh", "ctx", None),
            rows,
            rows,
            rows,
            rows,
            P(None, None, "wsh", None),
            P(),
            P(),
            P(),
            P(),
        ),
        check_vma=False,
    )
```

time: 1770 us -> 1180 us (0.67)
  local copies, waits for them, and re-layouts: 375 us -> 65 us
  Pallas kernels: 57.6 us -> 316 us
  matrix products: 200 us -> 0 us
  other arithmetic: 259 us -> 66.9 us
  starting transfers between devices: 218 us -> 143 us
  waiting for transfers between devices: 641 us -> 574 us
    pallas_call x6 -> x33, Pallas kernels: 57.6 us -> 316 us  [the longest x6 57.3 us: whole(): call(functools.partial(assemble_kernel, self.split_count, self.count - se...]
    dot_general x115 -> x0, matrix products: 200 us -> none  [the longest x16 45.9 us: sum_job(): lax.dot_general(left_both, right_both[step], (((0,), (0,)), ((), ())), pr...]
    convert_element_type x36 -> x4, other arithmetic: 111 us -> 11.7 us  [the longest x2 6 us: send_step(): sums[step].astype(BF16)]
    slice x69 -> x15, local copies, waits for them, and re-layouts: 94 us -> 10.4 us  [the longest x2 2.52 us: from_owner(): return lax.all_to_all(cut, 'wsh', 0, 0, tiled=True)[:slots]]
    concatenate x39 -> x8, local copies, waits for them, and re-layouts: 81.3 us -> 0.05 us  [the longest x6 0.04 us: __init__(): piece = jnp.concatenate([parts, piece])]
    ppermute x111 -> x116, starting transfers between devices: 172 us -> 107 us  [take(): return lax.ppermute(value, name, pairs)]
    ppermute x111 -> x116, waiting for transfers between devices: 485 us -> 447 us  [take(): return lax.ppermute(value, name, pairs)]
    dot_general x16 -> x0, local copies, waits for them, and re-layouts: 29 us -> none  [the longest x8 18 us: dot_t(): lax.dot_general(left, right, (((1,), (1,)), ((), ())), preferred_element_...]
  transfers between devices with their start and end apart: 120 -> 125, of which waited for: 40 -> 50; matrix products, arithmetic and copies ran while one was open for 31% -> 8% of each run, Pallas kernels for 3% -> 26%
where the time goes in v2:
time: 1180 us; the launch traced here: 1170 us
  waiting for transfers between devices  574 us (49%)
  Pallas kernels  316 us (27%)
  starting transfers between devices  143 us (12%)
  other arithmetic  66.9 us (6%)
  local copies, waits for them, and re-layouts  65 us (6%)
    ppermute x116, waiting for transfers between devices, take(): return lax.ppermute(value, name, pairs)  447 us
    ppermute x116, starting transfers between devices, take(): return lax.ppermute(value, name, pairs)  107 us
    pallas_call x6, Pallas kernels, whole(): call(functools.partial(assemble_kernel, self.split_count, self.count - se...  57.3 us
    all_to_all x2, waiting for transfers between devices, from_owner(): return lax.all_to_all(cut, 'wsh', 0, 0, tiled=True)[:slots]  56.3 us
    pallas_call x6, Pallas kernels, partial_sums(): call(functools.partial(sum_kernel, counts[0] if len(sets) > 1 else None,...  47.4 us
    all_to_all x1, waiting for transfers between devices, on_device(): lax.all_to_all(by_slot.reshape(ctx_count * wsh_count, rows_dev, width), (...  42.5 us
    pallas_call x2, Pallas kernels, attend_back(): call(functools.partial(attend_back_kernel, count, count_y, tokens), (D //...  42.2 us
    pallas_call x2, Pallas kernels, feed_back(): call(feed_back_kernel, (FF // BLK,), [full, full, full, part, weight, wei...  30.5 us
  transfers between devices with their start and end apart: 125, of which 50 were waited for; matrix products, arithmetic and copies ran while one was open for 8% of the time, Pallas kernels for 26%

profile of v2, /device:TPU:0, one launch (start us, length us, event | category | flops | bytes accessed | tf_op | source)
XLA Modules:
  0.0 1168.9 jit_solution(3161984100074674016)
XLA Ops:
  22.3 24.0 %collective-permute-done.1 = bf16[6,64,512]{2,1,0:T(8,128)(2,1)S(1)} collective-permute-done((bf16[6,64,512]{2,1,0:T(8,128)(2,1)S(1)}, bf16[6,64,512]{2,1,0:T(8,128)(2,1)S(1)}, u32[]{:S(2)}, u32[]{:S(2)}) %collective-permute-start.1) | collective-permute-done | bytes 393248 | tf_op jit(solution)/shard_map/ppermute | solution.py:69
  58.3 26.1 %collective-permute-done.5 = bf16[6,64,512]{2,1,0:T(8,128)(2,1)S(1)} collective-permute-done((bf16[6,64,512]{2,1,0:T(8,128)(2,1)S(1)}, bf16[6,64,512]{2,1,0:T(8,128)(2,1)S(1)}, u32[]{:S(2)}, u32[]{:S(2)}) %collective-permute-start.5) | collective-permute-done | bytes 393248 | tf_op jit(solution)/shard_map/ppermute | solution.py:69
  88.8 10.1 collective-permute-done.10
  99.9 23.4 %collective-permute-done.11 = bf16[6,64,512]{2,1,0:T(8,128)(2,1)S(1)} collective-permute-done((bf16[6,64,512]{2,1,0:T(8,128)(2,1)S(1)}, bf16[6,64,512]{2,1,0:T(8,128)(2,1)S(1)}, u32[]{:S(2)}, u32[]{:S(2)}) %collective-permute-start.11) | collective-permute-done | bytes 393248 | tf_op jit(solution)/shard_map/ppermute | solution.py:69
  135.8 9.5 assemble.6
  158.1 12.3 %collective-permute-done.18 = bf16[6,64,512]{2,1,0:T(8,128)(2,1)S(1)} collective-permute-done((bf16[6,64,512]{2,1,0:T(8,128)(2,1)S(1)}, bf16[6,64,512]{2,1,0:T(8,128)(2,1)S(1)}, u32[]{:S(2)}, u32[]{:S(2)}) %collective-permute-start.18) | collective-permute-done | bytes 393248 | tf_op jit(solution)/shard_map/ppermute | solution.py:69
  170.5 12.9 %collective-permute-done.20.refs_1_.refs_5_ = bf16[256,2048]{1,0:T(8,128)(2,1)} collective-permute-done((bf16[256,2048]{1,0:T(8,128)(2,1)}, bf16[256,2048]{1,0:T(8,128)(2,1)}, u32[]{:S(2)}, u32[]{:S(2)}) %collective-permute-start.20) | collective-permute-done | bytes 1048608 | tf_op jit(solution)/shard_map/ppermute | solution.py:69
  195.6 14.3 %attend.2.attn.refs_4_ = bf16[256,1024]{1,0:T(8,128)(2,1)} custom-call(bf16[256,1024]{1,0:T(8,128)(2,1)} %get-tuple-element.437.query, f32[1024,256]{1,0:T(8,128)} %compare_select_fusion.mask, bf16[256,2048]{1,0:T(8,128)(2,1)} %get-tuple-element.438.refs_0_.refs_4_, bf16[256,2048]{1,0:T(8,128)(2,1)} %collective-permute-done.20.refs_1_.refs_5_, ...), custom_call_target="tpu_custom_call" | custom-call | flops 14000000000 | tf_op jit(solution)/shard_map/attend/pallas_call | solution.py:335
  210.5 9.6 assemble.7
  224.1 8.2 up.2
  247.9 9.5 assemble.8
  257.5 8.4 down.2
  265.9 9.0 collective-permute-done.34
  283.8 9.6 assemble.9
  300.0 8.7 collective-permute-done.37.refs_1_
  308.8 8.7 collective-permute-done.39
  317.5 12.3 %collective-permute-done.41.refs_1_.refs_5_ = bf16[256,2048]{1,0:T(8,128)(2,1)S(1)} collective-permute-done((bf16[256,2048]{1,0:T(8,128)(2,1)}, bf16[256,2048]{1,0:T(8,128)(2,1)S(1)}, u32[]{:S(2)}, u32[]{:S(2)}) %collective-permute-start.41) | collective-permute-done | bytes 1048608 | tf_op jit(solution)/shard_map/ppermute | solution.py:69
  344.6 9.5 assemble.10
  354.1 14.3 %attend.3.attn.refs_4_ = bf16[256,1024]{1,0:T(8,128)(2,1)} custom-call(bf16[256,1024]{1,0:T(8,128)(2,1)} %get-tuple-element.474.query, f32[1024,256]{1,0:T(8,128)} %compare_select_fusion.mask, bf16[256,2048]{1,0:T(8,128)(2,1)} %get-tuple-element.475.refs_0_.refs_4_, bf16[256,2048]{1,0:T(8,128)(2,1)} %copy-done.78, ...), custom_call_target="tpu_custom_call" | custom-call | flops 14000000000 | tf_op jit(solution)/shard_map/attend/pallas_call | solution.py:335
  380.9 8.1 all-to-all-done
  392.6 9.6 assemble.11
  402.2 8.4 down.3
  430.5 15.3 %feed_back.2 = (bf16[256,4096]{1,0:T(8,128)(2,1)}, bf16[256,1024]{1,0:T(8,128)(2,1)}, bf16[256,1024]{1,0:T(8,128)(2,1)}, f32[256,1024]{1,0:T(8,128)}, f32[8,1024]{1,0:T(8,128)}, /*index=5*/f32[4,1,1024]{2,1,0:T(1,128)}) custom-call(f32[256,1024]{1,0:T(8,128)} %get-tuple-element.501.grad_two, bf16[256,1024]{1,0:T(8,128)(2,1)} %get-tuple-element.502.refs_2_.ffn_low, ...), custom_call_target="tpu_custom_call" | custom-call | flops 15000000512 | tf_op jit(solution)/shard_map/feed_back/pallas_call | solution.py:559
  460.8 11.2 collective-permute-done.50
  486.1 21.1 %attend_back.2 = (bf16[256,1024]{1,0:T(8,128)(2,1)}, bf16[2,2,256,1024]{3,2,1,0:T(8,128)(2,1)}, bf16[2,2,256,1024]{3,2,1,0:T(8,128)(2,1)}) custom-call(bf16[256,1024]{1,0:T(8,128)(2,1)} %get-tuple-element.474.query, bf16[256,1024]{1,0:T(8,128)(2,1)} %get-tuple-element.525.grad, f32[1024,256]{1,0:T(8,128)} %compare_select_fusion.mask, ...), custom_call_target="tpu_custom_call" | custom-call | flops 20999999488 | tf_op jit(solution)/shard_map/attend_back/pallas_call | solution.py:385
  516.8 9.1 collective-permute-done.55
  525.9 26.7 %collective-permute-done.54 = bf16[4,2,128,256]{3,2,1,0:T(8,128)(2,1)} collective-permute-done((bf16[4,2,128,256]{3,2,1,0:T(8,128)(2,1)S(1)}, bf16[4,2,128,256]{3,2,1,0:T(8,128)(2,1)}, u32[]{:S(2)}, u32[]{:S(2)}) %collective-permute-start.54) | collective-permute-done | bytes 524320 | tf_op jit(solution)/shard_map/ppermute | solution.py:69
  570.0 13.4 %collective-permute-start.59 = (bf16[4,128,256]{2,1,0:T(8,128)(2,1)S(1)}, bf16[4,128,256]{2,1,0:T(8,128)(2,1)S(1)}, u32[]{:S(2)}, u32[]{:S(2)}) collective-permute-start(bf16[4,128,256]{2,1,0:T(8,128)(2,1)S(1)} %pad_maximum_fusion.13), channel_id=1, source_target_pairs={{6,0},{7,1},{0,2},{1,3},{2,4},{3,5},{4,6},{5,7},{14,8},{15,9},{8,1... | collective-permute-start | bytes 786440 | tf_op jit(solution)/shard_map/ppermute | solution.py:69
  614.6 8.1 partial_sums.8
  626.3 15.2 %feed_back.3 = (bf16[256,4096]{1,0:T(8,128)(2,1)}, bf16[256,1024]{1,0:T(8,128)(2,1)}, bf16[256,1024]{1,0:T(8,128)(2,1)}, f32[256,1024]{1,0:T(8,128)}, f32[8,1024]{1,0:T(8,128)}, /*index=5*/f32[4,1,1024]{2,1,0:T(1,128)}) custom-call(f32[256,1024]{1,0:T(8,128)} %get-tuple-element.601.grad_two, bf16[256,1024]{1,0:T(8,128)(2,1)} %get-tuple-element.602.refs_2_.ffn_low, ...), custom_call_target="tpu_custom_call" | custom-call | flops 15000000512 | tf_op jit(solution)/shard_map/feed_back/pallas_call | solution.py:559
  641.6 21.1 %attend_back.3 = (bf16[256,1024]{1,0:T(8,128)(2,1)}, bf16[2,2,256,1024]{3,2,1,0:T(8,128)(2,1)}, bf16[2,2,256,1024]{3,2,1,0:T(8,128)(2,1)}) custom-call(bf16[256,1024]{1,0:T(8,128)(2,1)} %get-tuple-element.437.query, bf16[256,1024]{1,0:T(8,128)(2,1)} %get-tuple-element.610.grad, f32[1024,256]{1,0:T(8,128)} %compare_select_fusion.mask, ...), custom_call_target="tpu_custom_call" | custom-call | flops 20999999488 | tf_op jit(solution)/shard_map/attend_back/pallas_call | solution.py:385
  675.4 16.2 %collective-permute-done.72.refs_18_ = bf16[4,128,256]{2,1,0:T(8,128)(2,1)S(1)} collective-permute-done((bf16[4,128,256]{2,1,0:T(8,128)(2,1)S(1)}, bf16[4,128,256]{2,1,0:T(8,128)(2,1)S(1)}, u32[]{:S(2)}, u32[]{:S(2)}) %collective-permute-start.72) | collective-permute-done | bytes 262176 | tf_op jit(solution)/shard_map/ppermute | solution.py:69
  702.3 15.7 %collective-permute-done.75 = bf16[2,4,2,128,256]{4,3,2,1,0:T(8,128)(2,1)} collective-permute-done((bf16[2,4,2,128,256]{4,3,2,1,0:T(8,128)(2,1)}, bf16[2,4,2,128,256]{4,3,2,1,0:T(8,128)(2,1)}, u32[]{:S(2)}, u32[]{:S(2)}) %collective-permute-start.75) | collective-permute-done | bytes 1048608 | tf_op jit(solution)/shard_map/ppermute | solution.py:69
  720.7 17.9 %collective-permute-done.77 = bf16[2,4,2,128,256]{4,3,2,1,0:T(8,128)(2,1)} collective-permute-done((bf16[2,4,2,128,256]{4,3,2,1,0:T(8,128)(2,1)}, bf16[2,4,2,128,256]{4,3,2,1,0:T(8,128)(2,1)}, u32[]{:S(2)}, u32[]{:S(2)}) %collective-permute-start.77) | collective-permute-done | bytes 1048608 | tf_op jit(solution)/shard_map/ppermute | solution.py:69
  751.5 26.7 %collective-permute-done.84 = bf16[4,2,128,256]{3,2,1,0:T(8,128)(2,1)S(1)} collective-permute-done((bf16[4,2,128,256]{3,2,1,0:T(8,128)(2,1)S(1)}, bf16[4,2,128,256]{3,2,1,0:T(8,128)(2,1)S(1)}, u32[]{:S(2)}, u32[]{:S(2)}) %collective-permute-start.84) | collective-permute-done | bytes 524320 | tf_op jit(solution)/shard_map/ppermute | solution.py:69
  811.0 15.3 %collective-permute-done.91.refs_10_ = bf16[4,128,256]{2,1,0:T(8,128)(2,1)S(1)} collective-permute-done((bf16[4,128,256]{2,1,0:T(8,128)(2,1)S(1)}, bf16[4,128,256]{2,1,0:T(8,128)(2,1)S(1)}, u32[]{:S(2)}, u32[]{:S(2)}) %collective-permute-start.91) | collective-permute-done | bytes 262176 | tf_op jit(solution)/shard_map/ppermute | solution.py:69
  830.6 8.1 partial_sums.11
  838.8 12.3 %collective-permute-done.88.refs_14_ = bf16[4,128,256]{2,1,0:T(8,128)(2,1)S(1)} collective-permute-done((bf16[4,128,256]{2,1,0:T(8,128)(2,1)S(1)}, bf16[4,128,256]{2,1,0:T(8,128)(2,1)S(1)}, u32[]{:S(2)}, u32[]{:S(2)}) %collective-permute-start.88) | collective-permute-done | bytes 262176 | tf_op jit(solution)/shard_map/ppermute | solution.py:69
  856.0 32.4 %collective-permute-done.99 = bf16[4,2,128,256]{3,2,1,0:T(8,128)(2,1)} collective-permute-done((bf16[4,2,128,256]{3,2,1,0:T(8,128)(2,1)}, bf16[4,2,128,256]{3,2,1,0:T(8,128)(2,1)}, u32[]{:S(2)}, u32[]{:S(2)}) %collective-permute-start.99) | collective-permute-done | bytes 524320 | tf_op jit(solution)/shard_map/ppermute | solution.py:69
  901.7 16.4 %collective-permute-done.103.refs_6_ = bf16[4,128,256]{2,1,0:T(8,128)(2,1)S(1)} collective-permute-done((bf16[4,128,256]{2,1,0:T(8,128)(2,1)S(1)}, bf16[4,128,256]{2,1,0:T(8,128)(2,1)S(1)}, u32[]{:S(2)}, u32[]{:S(2)}) %collective-permute-start.103) | collective-permute-done | bytes 262176 | tf_op jit(solution)/shard_map/ppermute | solution.py:69
  925.8 16.7 %collective-permute-done.108.refs_2_ = bf16[4,128,256]{2,1,0:T(8,128)(2,1)S(1)} collective-permute-done((bf16[4,128,256]{2,1,0:T(8,128)(2,1)S(1)}, bf16[4,128,256]{2,1,0:T(8,128)(2,1)S(1)}, u32[]{:S(2)}, u32[]{:S(2)}) %collective-permute-start.108) | collective-permute-done | bytes 262176 | tf_op jit(solution)/shard_map/ppermute | solution.py:69
  961.0 42.5 %all-to-all-done.3 = bf16[32,128,256]{2,1,0:T(8,128)(2,1)} async-done(((bf16[32,128,256]{2,1,0:T(8,128)(2,1)}), bf16[32,128,256]{2,1,0:T(8,128)(2,1)}, u32[]{:S(2)}, u32[]{:S(2)}) %all-to-all-start.3) | async-done | bytes 2097184 | tf_op jit(solution)/shard_map/all_to_all | solution.py:1230
  1007.1 16.3 %rotate.1 = (bf16[1024,1024]{1,0:T(8,128)(2,1)}, bf16[1024,1024]{1,0:T(8,128)(2,1)}) custom-call(s32[1]{0:T(128)} %bitcast.105.where, bf16[4,1024,256]{2,1,0:T(8,128)(2,1)} %bitcast.147.grads, f32[6,1024,1024]{2,1,0:T(8,128)} %right.1, bf16[1024,1024]{1,0:T(8,128)(2,1)} %bitcast.62.left, bf16[1024,1024]{1,0:T(8,128)(2,1)} %bitcast.66.first, ...), custom_call_target="tpu_custom_call" | custom-call | flops 16000000000 | tf_op jit(solution)/shard_map/rotate/pallas_call | solution.py:844
  1034.1 46.2 %all-to-all-done.5 = bf16[8,128,1024]{2,1,0:T(8,128)(2,1)S(1)} async-done(((bf16[8,128,1024]{2,1,0:T(8,128)(2,1)}), bf16[8,128,1024]{2,1,0:T(8,128)(2,1)S(1)}, u32[]{:S(2)}, u32[]{:S(2)}) %all-to-all-start.5) | async-done | bytes 2097184 | tf_op jit(solution)/shard_map/all_to_all | solution.py:967
  1093.8 11.4 collective-permute-done.115
  1106.4 16.2 %collective-permute-done.116 = f32[2,12288]{1,0:T(2,128)S(1)} collective-permute-done((f32[2,12288]{1,0:T(2,128)S(1)}, f32[2,12288]{1,0:T(2,128)S(1)}, u32[]{:S(2)}, u32[]{:S(2)}) %collective-permute-start.116) | collective-permute-done | bytes 98336 | tf_op jit(solution)/shard_map/ppermute | solution.py:950
  1126.8 10.1 all-to-all-done.6
  1156.0 12.4 %pick.1 = bf16[24,128,1024]{2,1,0:T(8,128)(2,1)} custom-call(s32[2,24]{1,0:T(2,128)} %pad_add_fusion.table, bf16[6,128,1024]{2,1,0:T(8,128)(2,1)} %get-tuple-element.776.refs_0_, bf16[6,128,1024]{2,1,0:T(8,128)(2,1)} %collective-permute-done.110.refs_1_, bf16[6,128,1024]{2,1,0:T(8,128)(2,1)} %collective-permute-done.111.refs_2_, ...), custom_call_target="tpu_custom_call" | custom-call | flops 12000000000 | tf_op jit(solution)/shard_map/pick/pallas_call | solution.py:877
  (668 shorter events, 424.9 us)
Async XLA Ops:
  12.8 33.5 %collective-permute-start.1 = (bf16[6,64,512]{2,1,0:T(8,128)(2,1)S(1)}, bf16[6,64,512]{2,1,0:T(8,128)(2,1)S(1)}, u32[]{:S(2)}, u32[]{:S(2)}) collective-permute-start(bf16[6,64,512]{2,1,0:T(8,128)(2,1)S(1)} %constant_dynamic-update-slice_fusion), channel_id=1, source_target_pairs={{4,0},{5,1},{6,2},{7,3},{0,4},{1,5},{2,6},{3,7},{12,8},{13,9},{14,... | collective-permute-start | bytes 1179656 | tf_op jit(solution)/shard_map/ppermute | solution.py:69
  12.8 33.5 %collective-permute-start.2 = (bf16[6,64,512]{2,1,0:T(8,128)(2,1)S(1)}, bf16[6,64,512]{2,1,0:T(8,128)(2,1)S(1)}, u32[]{:S(2)}, u32[]{:S(2)}) collective-permute-start(bf16[6,64,512]{2,1,0:T(8,128)(2,1)S(1)} %constant_dynamic-update-slice_fusion), channel_id=1, source_target_pairs={{6,0},{7,1},{0,2},{1,3},{2,4},{3,5},{4,6},{5,7},{14,8},{15,9},{8,1... | collective-permute-start | bytes 1179656 | tf_op jit(solution)/shard_map/ppermute | solution.py:69
  46.6 37.9 %collective-permute-start.3 = (bf16[4,6,64,512]{3,2,1,0:T(8,128)(2,1)S(1)}, bf16[4,6,64,512]{3,2,1,0:T(8,128)(2,1)S(1)}, u32[]{:S(2)}, u32[]{:S(2)}) collective-permute-start(bf16[4,6,64,512]{3,2,1,0:T(8,128)(2,1)S(1)} %pad_maximum_fusion.6), channel_id=1, source_target_pairs={{1,0},{0,1},{3,2},{2,3},{5,4},{4,5},{7,6},{6,7},{9,8},{8,9},{11,10... | collective-permute-start | bytes 4718600 | tf_op jit(solution)/shard_map/ppermute | solution.py:69
  48.1 36.3 %collective-permute-start.5 = (bf16[6,64,512]{2,1,0:T(8,128)(2,1)S(1)}, bf16[6,64,512]{2,1,0:T(8,128)(2,1)S(1)}, u32[]{:S(2)}, u32[]{:S(2)}) collective-permute-start(bf16[6,64,512]{2,1,0:T(8,128)(2,1)S(1)} %constant_dynamic-update-slice_fusion.4), channel_id=1, source_target_pairs={{4,0},{5,1},{6,2},{7,3},{0,4},{1,5},{2,6},{3,7},{12,8},{13,9},{14,... | collective-permute-start | bytes 1179656 | tf_op jit(solution)/shard_map/ppermute | solution.py:69
  50.9 33.5 %collective-permute-start.6 = (bf16[6,64,512]{2,1,0:T(8,128)(2,1)S(1)}, bf16[6,64,512]{2,1,0:T(8,128)(2,1)S(1)}, u32[]{:S(2)}, u32[]{:S(2)}) collective-permute-start(bf16[6,64,512]{2,1,0:T(8,128)(2,1)S(1)} %constant_dynamic-update-slice_fusion.4), channel_id=1, source_target_pairs={{6,0},{7,1},{0,2},{1,3},{2,4},{3,5},{4,6},{5,7},{14,8},{15,9},{8,1... | collective-permute-start | bytes 1179656 | tf_op jit(solution)/shard_map/ppermute | solution.py:69
  84.7 38.6 %collective-permute-start.8 = (bf16[2,4,6,64,512]{4,3,2,1,0:T(8,128)(2,1)S(1)}, bf16[2,4,6,64,512]{4,3,2,1,0:T(8,128)(2,1)S(1)}, u32[]{:S(2)}, u32[]{:S(2)}) collective-permute-start(bf16[2,4,6,64,512]{4,3,2,1,0:T(8,128)(2,1)S(1)} %pad_maximum_fusion.refs_0_), channel_id=1, source_target_pairs={{8,0},{0,8},{24,16},{16,24},{9,1},{1,9},{25,17},{17,25},{10,2},{2,... | collective-permute-start | bytes 9437192 | tf_op jit(solution)/shard_map/ppermute | solution.py:69
  85.0 38.3 %collective-permute-start.9 = (bf16[4,6,64,512]{3,2,1,0:T(8,128)(2,1)S(1)}, bf16[4,6,64,512]{3,2,1,0:T(8,128)(2,1)S(1)}, u32[]{:S(2)}, u32[]{:S(2)}) collective-permute-start(bf16[4,6,64,512]{3,2,1,0:T(8,128)(2,1)S(1)} %pad_maximum_fusion.7), channel_id=1, source_target_pairs={{1,0},{0,1},{3,2},{2,3},{5,4},{4,5},{7,6},{6,7},{9,8},{8,9},{11,10... | collective-permute-start | bytes 4718600 | tf_op jit(solution)/shard_map/ppermute | solution.py:69
  86.4 36.9 %collective-permute-start.7 = (bf16[2,4,2,64,512]{4,3,2,1,0:T(8,128)(2,1)S(1)}, bf16[2,4,2,64,512]{4,3,2,1,0:T(8,128)(2,1)}, u32[]{:S(2)}, u32[]{:S(2)}) collective-permute-start(bf16[2,4,2,64,512]{4,3,2,1,0:T(8,128)(2,1)S(1)} %fusion.8), channel_id=1, source_target_pairs={{16,0},{24,8},{0,16},{8,24},{17,1},{25,9},{1,17},{9,25},{18,2},{26... | collective-permute-start | bytes 3145736 | tf_op jit(solution)/shard_map/ppermute | solution.py:69
  87.9 35.4 %collective-permute-start.11 = (bf16[6,64,512]{2,1,0:T(8,128)(2,1)S(1)}, bf16[6,64,512]{2,1,0:T(8,128)(2,1)S(1)}, u32[]{:S(2)}, u32[]{:S(2)}) collective-permute-start(bf16[6,64,512]{2,1,0:T(8,128)(2,1)S(1)} %constant_dynamic-update-slice_fusion.8), channel_id=1, source_target_pairs={{4,0},{5,1},{6,2},{7,3},{0,4},{1,5},{2,6},{3,7},{12,8},{13,9},{14,... | collective-permute-start | bytes 1179656 | tf_op jit(solution)/shard_map/ppermute | solution.py:69
  132.1 51.2 %collective-permute-start.14 = (bf16[2,4,6,64,512]{4,3,2,1,0:T(8,128)(2,1)}, bf16[2,4,6,64,512]{4,3,2,1,0:T(8,128)(2,1)}, u32[]{:S(2)}, u32[]{:S(2)}) collective-permute-start(bf16[2,4,6,64,512]{4,3,2,1,0:T(8,128)(2,1)} %pad_maximum_fusion.1.refs_0_), channel_id=1, source_target_pairs={{8,0},{0,8},{24,16},{16,24},{9,1},{1,9},{25,17},{17,25},{10,2},{2,... | collective-permute-start | bytes 9437192 | tf_op jit(solution)/shard_map/ppermute | solution.py:69
  132.5 37.9 %collective-permute-start.15 = (bf16[4,6,64,512]{3,2,1,0:T(8,128)(2,1)S(1)}, bf16[4,6,64,512]{3,2,1,0:T(8,128)(2,1)}, u32[]{:S(2)}, u32[]{:S(2)}) collective-permute-start(bf16[4,6,64,512]{3,2,1,0:T(8,128)(2,1)S(1)} %pad_maximum_fusion.8), channel_id=1, source_target_pairs={{1,0},{0,1},{3,2},{2,3},{5,4},{4,5},{7,6},{6,7},{9,8},{8,9},{11,10... | collective-permute-start | bytes 4718600 | tf_op jit(solution)/shard_map/ppermute | solution.py:69
  135.3 35.2 %collective-permute-start.13 = (bf16[2,4,2,64,512]{4,3,2,1,0:T(8,128)(2,1)}, bf16[2,4,2,64,512]{4,3,2,1,0:T(8,128)(2,1)}, u32[]{:S(2)}, u32[]{:S(2)}) collective-permute-start(bf16[2,4,2,64,512]{4,3,2,1,0:T(8,128)(2,1)} %fusion.7), channel_id=1, source_target_pairs={{16,0},{24,8},{0,16},{8,24},{17,1},{25,9},{1,17},{9,25},{18,2},{26... | collective-permute-start | bytes 3145736 | tf_op jit(solution)/shard_map/ppermute | solution.py:69
  185.8 38.2 %collective-permute-start.24 = (bf16[6,64,512]{2,1,0:T(8,128)(2,1)S(1)}, bf16[6,64,512]{2,1,0:T(8,128)(2,1)S(1)}, u32[]{:S(2)}, u32[]{:S(2)}) collective-permute-start(bf16[6,64,512]{2,1,0:T(8,128)(2,1)S(1)} %copy-done.29), channel_id=1, source_target_pairs={{2,0},{3,1},{4,2},{5,3},{6,4},{7,5},{0,6},{1,7},{10,8},{11,9},{12,... | collective-permute-start | bytes 1179656 | tf_op jit(solution)/shard_map/ppermute | solution.py:69
  188.4 43.9 %collective-permute-start.25 = (bf16[6,64,512]{2,1,0:T(8,128)(2,1)S(1)}, bf16[6,64,512]{2,1,0:T(8,128)(2,1)S(1)}, u32[]{:S(2)}, u32[]{:S(2)}) collective-permute-start(bf16[6,64,512]{2,1,0:T(8,128)(2,1)S(1)} %copy-done.29), channel_id=1, source_target_pairs={{4,0},{5,1},{6,2},{7,3},{0,4},{1,5},{2,6},{3,7},{12,8},{13,9},{14,... | collective-permute-start | bytes 1179656 | tf_op jit(solution)/shard_map/ppermute | solution.py:69
  194.0 42.9 %collective-permute-start.23 = (bf16[4,6,64,512]{3,2,1,0:T(8,128)(2,1)S(1)}, bf16[4,6,64,512]{3,2,1,0:T(8,128)(2,1)S(1)}, u32[]{:S(2)}, u32[]{:S(2)}) collective-permute-start(bf16[4,6,64,512]{3,2,1,0:T(8,128)(2,1)S(1)} %pad_maximum_fusion.9), channel_id=1, source_target_pairs={{1,0},{0,1},{3,2},{2,3},{5,4},{4,5},{7,6},{6,7},{9,8},{8,9},{11,10... | collective-permute-start | bytes 4718600 | tf_op jit(solution)/shard_map/ppermute | solution.py:69
  195.4 41.5 %collective-permute-start.22 = (bf16[2,4,6,64,512]{4,3,2,1,0:T(8,128)(2,1)}, bf16[2,4,6,64,512]{4,3,2,1,0:T(8,128)(2,1)}, u32[]{:S(2)}, u32[]{:S(2)}) collective-permute-start(bf16[2,4,6,64,512]{4,3,2,1,0:T(8,128)(2,1)} %pad_maximum_fusion.2.refs_0_), channel_id=1, source_target_pairs={{8,0},{0,8},{24,16},{16,24},{9,1},{1,9},{25,17},{17,25},{10,2},{2,... | collective-permute-start | bytes 9437192 | tf_op jit(solution)/shard_map/ppermute | solution.py:69
  238.9 38.0 %collective-permute-start.31 = (bf16[2,4,6,64,512]{4,3,2,1,0:T(8,128)(2,1)}, bf16[2,4,6,64,512]{4,3,2,1,0:T(8,128)(2,1)}, u32[]{:S(2)}, u32[]{:S(2)}) collective-permute-start(bf16[2,4,6,64,512]{4,3,2,1,0:T(8,128)(2,1)} %pad_maximum_fusion.3.refs_0_), channel_id=1, source_target_pairs={{8,0},{0,8},{24,16},{16,24},{9,1},{1,9},{25,17},{17,25},{10,2},{2,... | collective-permute-start | bytes 9437192 | tf_op jit(solution)/shard_map/ppermute | solution.py:69
  240.2 34.8 %collective-permute-start.34 = (bf16[6,64,512]{2,1,0:T(8,128)(2,1)S(1)}, bf16[6,64,512]{2,1,0:T(8,128)(2,1)}, u32[]{:S(2)}, u32[]{:S(2)}) collective-permute-start(bf16[6,64,512]{2,1,0:T(8,128)(2,1)S(1)} %copy-done.31), channel_id=1, source_target_pairs={{4,0},{5,1},{6,2},{7,3},{0,4},{1,5},{2,6},{3,7},{12,8},{13,9},{14,... | collective-permute-start | bytes 1179656 | tf_op jit(solution)/shard_map/ppermute | solution.py:69
  240.6 36.3 %collective-permute-start.32 = (bf16[4,6,64,512]{3,2,1,0:T(8,128)(2,1)S(1)}, bf16[4,6,64,512]{3,2,1,0:T(8,128)(2,1)S(1)}, u32[]{:S(2)}, u32[]{:S(2)}) collective-permute-start(bf16[4,6,64,512]{3,2,1,0:T(8,128)(2,1)S(1)} %pad_maximum_fusion.10), channel_id=1, source_target_pairs={{1,0},{0,1},{3,2},{2,3},{5,4},{4,5},{7,6},{6,7},{9,8},{8,9},{11,10... | collective-permute-start | bytes 4718600 | tf_op jit(solution)/shard_map/ppermute | solution.py:69
  278.8 51.0 %collective-permute-start.38 = (bf16[2,4,6,64,512]{4,3,2,1,0:T(8,128)(2,1)}, bf16[2,4,6,64,512]{4,3,2,1,0:T(8,128)(2,1)}, u32[]{:S(2)}, u32[]{:S(2)}) collective-permute-start(bf16[2,4,6,64,512]{4,3,2,1,0:T(8,128)(2,1)} %pad_maximum_fusion.4.refs_0_), channel_id=1, source_target_pairs={{8,0},{0,8},{24,16},{16,24},{9,1},{1,9},{25,17},{17,25},{10,2},{2,... | collective-permute-start | bytes 9437192 | tf_op jit(solution)/shard_map/ppermute | solution.py:69
  281.1 36.4 %collective-permute-start.39 = (bf16[4,6,64,512]{3,2,1,0:T(8,128)(2,1)S(1)}, bf16[4,6,64,512]{3,2,1,0:T(8,128)(2,1)S(1)}, u32[]{:S(2)}, u32[]{:S(2)}) collective-permute-start(bf16[4,6,64,512]{3,2,1,0:T(8,128)(2,1)S(1)} %pad_maximum_fusion.11), channel_id=1, source_target_pairs={{1,0},{0,1},{3,2},{2,3},{5,4},{4,5},{7,6},{6,7},{9,8},{8,9},{11,10... | collective-permute-start | bytes 4718600 | tf_op jit(solution)/shard_map/ppermute | solution.py:69
  334.6 54.4 %all-to-all-start = ((bf16[8,128,1024]{2,1,0:T(8,128)(2,1)}), bf16[8,128,1024]{2,1,0:T(8,128)(2,1)}, u32[]{:S(2)}, u32[]{:S(2)}) async-start(bf16[8,128,1024]{2,1,0:T(8,128)(2,1)} %pad.10), calls=%async_computation | async-start | bytes 4194304 | tf_op jit(solution)/shard_map/all_to_all | solution.py:962
  341.4 39.4 %collective-permute-start.43 = (bf16[2,4,6,64,512]{4,3,2,1,0:T(8,128)(2,1)S(1)}, bf16[2,4,6,64,512]{4,3,2,1,0:T(8,128)(2,1)}, u32[]{:S(2)}, u32[]{:S(2)}) collective-permute-start(bf16[2,4,6,64,512]{4,3,2,1,0:T(8,128)(2,1)S(1)} %pad_maximum_fusion.5.refs_0_), channel_id=1, source_target_pairs={{8,0},{0,8},{24,16},{16,24},{9,1},{1,9},{25,17},{17,25},{10,2},{2,... | collective-permute-start | bytes 9437192 | tf_op jit(solution)/shard_map/ppermute | solution.py:69
  343.1 37.8 %collective-permute-start.42 = (bf16[2,4,2,64,512]{4,3,2,1,0:T(8,128)(2,1)S(1)}, bf16[2,4,2,64,512]{4,3,2,1,0:T(8,128)(2,1)S(1)}, u32[]{:S(2)}, u32[]{:S(2)}) collective-permute-start(bf16[2,4,2,64,512]{4,3,2,1,0:T(8,128)(2,1)S(1)} %fusion.3), channel_id=1, source_target_pairs={{16,0},{24,8},{0,16},{8,24},{17,1},{25,9},{1,17},{9,25},{18,2},{26... | collective-permute-start | bytes 3145736 | tf_op jit(solution)/shard_map/ppermute | solution.py:69
  416.0 61.2 %all-to-all-start.1 = ((bf16[8,128,1024]{2,1,0:T(8,128)(2,1)}), bf16[8,128,1024]{2,1,0:T(8,128)(2,1)}, u32[]{:S(2)}, u32[]{:S(2)}) async-start(bf16[8,128,1024]{2,1,0:T(8,128)(2,1)} %pad.11), calls=%async_computation.1 | async-start | bytes 4194304 | tf_op jit(solution)/shard_map/all_to_all | solution.py:962
  479.0 73.6 %all-to-all-start.2 = ((bf16[8,128,1024]{2,1,0:T(8,128)(2,1)}), bf16[8,128,1024]{2,1,0:T(8,128)(2,1)}, u32[]{:S(2)}, u32[]{:S(2)}) async-start(bf16[8,128,1024]{2,1,0:T(8,128)(2,1)} %pad.12), calls=%async_computation.2 | async-start | bytes 4194304 | tf_op jit(solution)/shard_map/all_to_all | solution.py:962
  509.0 43.5 %collective-permute-start.58 = (bf16[2,2,256,1024]{3,2,0,1:T(8,128)(2,1)S(1)}, bf16[2,2,256,1024]{3,2,0,1:T(8,128)(2,1)}, u32[]{:S(2)}, u32[]{:S(2)}) collective-permute-start(bf16[2,2,256,1024]{3,2,0,1:T(8,128)(2,1)S(1)} %copy.33), channel_id=1, source_target_pairs={{8,0},{0,8},{24,16},{16,24},{9,1},{1,9},{25,17},{17,25},{10,2},{2,... | collective-permute-start | bytes 6291464 | tf_op jit(solution)/shard_map/ppermute | solution.py:69
  511.6 41.0 %collective-permute-start.56 = (bf16[2,4,2,128,256]{4,3,2,1,0:T(8,128)(2,1)S(1)}, bf16[2,4,2,128,256]{4,3,2,1,0:T(8,128)(2,1)}, u32[]{:S(2)}, u32[]{:S(2)}) collective-permute-start(bf16[2,4,2,128,256]{4,3,2,1,0:T(8,128)(2,1)S(1)} %copy-done.83), channel_id=1, source_target_pairs={{16,0},{24,8},{0,16},{8,24},{17,1},{25,9},{1,17},{9,25},{18,2},{26... | collective-permute-start | bytes 3145736 | tf_op jit(solution)/shard_map/ppermute | solution.py:69
  513.1 39.5 %collective-permute-start.57 = (bf16[2,4,2,128,256]{4,3,2,1,0:T(8,128)(2,1)S(1)}, bf16[2,4,2,128,256]{4,3,2,1,0:T(8,128)(2,1)}, u32[]{:S(2)}, u32[]{:S(2)}) collective-permute-start(bf16[2,4,2,128,256]{4,3,2,1,0:T(8,128)(2,1)S(1)} %copy-done.82), channel_id=1, source_target_pairs={{1,0},{0,1},{3,2},{2,3},{5,4},{4,5},{7,6},{6,7},{9,8},{8,9},{11,10... | collective-permute-start | bytes 3145736 | tf_op jit(solution)/shard_map/ppermute | solution.py:69
  516.7 35.8 %collective-permute-start.54 = (bf16[4,2,128,256]{3,2,1,0:T(8,128)(2,1)S(1)}, bf16[4,2,128,256]{3,2,1,0:T(8,128)(2,1)}, u32[]{:S(2)}, u32[]{:S(2)}) collective-permute-start(bf16[4,2,128,256]{3,2,1,0:T(8,128)(2,1)S(1)} %get-tuple-element.821), channel_id=1, source_target_pairs={{1,0},{0,1},{3,2},{2,3},{5,4},{4,5},{7,6},{6,7},{9,8},{8,9},{11,10... | collective-permute-start | bytes 1572872 | tf_op jit(solution)/shard_map/ppermute | solution.py:69
  568.8 34.4 %collective-permute-start.69 = (bf16[256,4096]{1,0:T(8,128)(2,1)S(1)}, bf16[256,4096]{1,0:T(8,128)(2,1)S(1)}, u32[]{:S(2)}, u32[]{:S(2)}) collective-permute-start(bf16[256,4096]{1,0:T(8,128)(2,1)S(1)} %copy-done.73), channel_id=1, source_target_pairs={{8,0},{0,8},{24,16},{16,24},{9,1},{1,9},{25,17},{17,25},{10,2},{2,... | collective-permute-start | bytes 6291464 | tf_op jit(solution)/shard_map/ppermute | solution.py:69
  588.1 80.6 %collective-permute-start.78 = (bf16[256,1024]{1,0:T(8,128)(2,1)S(1)}, bf16[256,1024]{1,0:T(8,128)(2,1)}, u32[]{:S(2)}, u32[]{:S(2)}) collective-permute-start(bf16[256,1024]{1,0:T(8,128)(2,1)S(1)} %copy-done.88), channel_id=1, source_target_pairs={{8,0},{0,8},{24,16},{16,24},{9,1},{1,9},{25,17},{17,25},{10,2},{2,... | collective-permute-start | bytes 1572872 | tf_op jit(solution)/shard_map/ppermute | solution.py:69
  641.5 52.3 %collective-permute-start.79 = (bf16[256,4096]{1,0:T(8,128)(2,1)}, bf16[256,4096]{1,0:T(8,128)(2,1)}, u32[]{:S(2)}, u32[]{:S(2)}) collective-permute-start(bf16[256,4096]{1,0:T(8,128)(2,1)} %get-tuple-element.605.refs_2_), channel_id=1, source_target_pairs={{8,0},{0,8},{24,16},{16,24},{9,1},{1,9},{25,17},{17,25},{10,2},{2,... | collective-permute-start | bytes 6291464 | tf_op jit(solution)/shard_map/ppermute | solution.py:69
  664.4 74.2 %collective-permute-start.80 = (bf16[2,2,256,1024]{3,2,0,1:T(8,128)(2,1)S(1)}, bf16[2,2,256,1024]{3,2,0,1:T(8,128)(2,1)S(1)}, u32[]{:S(2)}, u32[]{:S(2)}) collective-permute-start(bf16[2,2,256,1024]{3,2,0,1:T(8,128)(2,1)S(1)} %copy.36), channel_id=1, source_target_pairs={{8,0},{0,8},{24,16},{16,24},{9,1},{1,9},{25,17},{17,25},{10,2},{2,... | collective-permute-start | bytes 6291464 | tf_op jit(solution)/shard_map/ppermute | solution.py:69
  693.8 44.8 %collective-permute-start.77 = (bf16[2,4,2,128,256]{4,3,2,1,0:T(8,128)(2,1)}, bf16[2,4,2,128,256]{4,3,2,1,0:T(8,128)(2,1)}, u32[]{:S(2)}, u32[]{:S(2)}) collective-permute-start(bf16[2,4,2,128,256]{4,3,2,1,0:T(8,128)(2,1)} %get-tuple-element.598), channel_id=1, source_target_pairs={{1,0},{0,1},{3,2},{2,3},{5,4},{4,5},{7,6},{6,7},{9,8},{8,9},{11,10... | collective-permute-start | bytes 3145736 | tf_op jit(solution)/shard_map/ppermute | solution.py:69
  740.9 50.7 %collective-permute-start.86 = (bf16[2,256,1024]{2,1,0:T(8,128)(2,1)S(1)}, bf16[2,256,1024]{2,1,0:T(8,128)(2,1)S(1)}, u32[]{:S(2)}, u32[]{:S(2)}) collective-permute-start(bf16[2,256,1024]{2,1,0:T(8,128)(2,1)S(1)} %get-tuple-element.793), channel_id=1, source_target_pairs={{16,0},{24,8},{0,16},{8,24},{17,1},{25,9},{1,17},{9,25},{18,2},{26... | collective-permute-start | bytes 3145736 | tf_op jit(solution)/shard_map/ppermute | solution.py:69
  743.3 34.9 %collective-permute-start.84 = (bf16[4,2,128,256]{3,2,1,0:T(8,128)(2,1)S(1)}, bf16[4,2,128,256]{3,2,1,0:T(8,128)(2,1)S(1)}, u32[]{:S(2)}, u32[]{:S(2)}) collective-permute-start(bf16[4,2,128,256]{3,2,1,0:T(8,128)(2,1)S(1)} %get-tuple-element.807), channel_id=1, source_target_pairs={{16,0},{24,8},{0,16},{8,24},{17,1},{25,9},{1,17},{9,25},{18,2},{26... | collective-permute-start | bytes 1572872 | tf_op jit(solution)/shard_map/ppermute | solution.py:69
  749.1 37.6 %collective-permute-start.82 = (bf16[4,2,128,256]{3,2,1,0:T(8,128)(2,1)S(1)}, bf16[4,2,128,256]{3,2,1,0:T(8,128)(2,1)S(1)}, u32[]{:S(2)}, u32[]{:S(2)}) collective-permute-start(bf16[4,2,128,256]{3,2,1,0:T(8,128)(2,1)S(1)} %get-tuple-element.811), channel_id=1, source_target_pairs={{16,0},{24,8},{0,16},{8,24},{17,1},{25,9},{1,17},{9,25},{18,2},{26... | collective-permute-start | bytes 1572872 | tf_op jit(solution)/shard_map/ppermute | solution.py:69
  750.6 41.0 %collective-permute-start.85 = (bf16[2,4,2,128,256]{4,3,2,1,0:T(8,128)(2,1)S(1)}, bf16[2,4,2,128,256]{4,3,2,1,0:T(8,128)(2,1)S(1)}, u32[]{:S(2)}, u32[]{:S(2)}) collective-permute-start(bf16[2,4,2,128,256]{4,3,2,1,0:T(8,128)(2,1)S(1)} %copy-done.79), channel_id=1, source_target_pairs={{1,0},{0,1},{3,2},{2,3},{5,4},{4,5},{7,6},{6,7},{9,8},{8,9},{11,10... | collective-permute-start | bytes 3145736 | tf_op jit(solution)/shard_map/ppermute | solution.py:69
  804.0 47.2 %collective-permute-start.93 = (bf16[2,4,2,128,256]{4,3,2,1,0:T(8,128)(2,1)}, bf16[2,4,2,128,256]{4,3,2,1,0:T(8,128)(2,1)S(1)}, u32[]{:S(2)}, u32[]{:S(2)}) collective-permute-start(bf16[2,4,2,128,256]{4,3,2,1,0:T(8,128)(2,1)} %get-tuple-element.673), channel_id=1, source_target_pairs={{16,0},{24,8},{0,16},{8,24},{17,1},{25,9},{1,17},{9,25},{18,2},{26... | collective-permute-start | bytes 3145736 | tf_op jit(solution)/shard_map/ppermute | solution.py:69
  851.2 37.2 %collective-permute-start.100 = (bf16[2,4,2,128,256]{4,3,2,1,0:T(8,128)(2,1)}, bf16[2,4,2,128,256]{4,3,2,1,0:T(8,128)(2,1)S(1)}, u32[]{:S(2)}, u32[]{:S(2)}) collective-permute-start(bf16[2,4,2,128,256]{4,3,2,1,0:T(8,128)(2,1)} %get-tuple-element.708), channel_id=1, source_target_pairs={{16,0},{24,8},{0,16},{8,24},{17,1},{25,9},{1,17},{9,25},{18,2},{26... | collective-permute-start | bytes 3145736 | tf_op jit(solution)/shard_map/ppermute | solution.py:69
  852.6 35.8 %collective-permute-start.101 = (bf16[2,4,2,128,256]{4,3,2,1,0:T(8,128)(2,1)}, bf16[2,4,2,128,256]{4,3,2,1,0:T(8,128)(2,1)}, u32[]{:S(2)}, u32[]{:S(2)}) collective-permute-start(bf16[2,4,2,128,256]{4,3,2,1,0:T(8,128)(2,1)} %get-tuple-element.709), channel_id=1, source_target_pairs={{1,0},{0,1},{3,2},{2,3},{5,4},{4,5},{7,6},{6,7},{9,8},{8,9},{11,10... | collective-permute-start | bytes 3145736 | tf_op jit(solution)/shard_map/ppermute | solution.py:69
  855.3 33.1 %collective-permute-start.99 = (bf16[4,2,128,256]{3,2,1,0:T(8,128)(2,1)}, bf16[4,2,128,256]{3,2,1,0:T(8,128)(2,1)}, u32[]{:S(2)}, u32[]{:S(2)}) collective-permute-start(bf16[4,2,128,256]{3,2,1,0:T(8,128)(2,1)} %get-tuple-element.803), channel_id=1, source_target_pairs={{1,0},{0,1},{3,2},{2,3},{5,4},{4,5},{7,6},{6,7},{9,8},{8,9},{11,10... | collective-permute-start | bytes 1572872 | tf_op jit(solution)/shard_map/ppermute | solution.py:69
  949.8 53.7 %all-to-all-start.3 = ((bf16[32,128,256]{2,1,0:T(8,128)(2,1)}), bf16[32,128,256]{2,1,0:T(8,128)(2,1)}, u32[]{:S(2)}, u32[]{:S(2)}) async-start(bf16[32,128,256]{2,1,0:T(8,128)(2,1)} %bitcast.301), calls=%async_computation.3 | async-start | bytes 4194304 | tf_op jit(solution)/shard_map/all_to_all | solution.py:1230
  1028.3 52.1 %all-to-all-start.5 = ((bf16[8,128,1024]{2,1,0:T(8,128)(2,1)}), bf16[8,128,1024]{2,1,0:T(8,128)(2,1)S(1)}, u32[]{:S(2)}, u32[]{:S(2)}) async-start(bf16[8,128,1024]{2,1,0:T(8,128)(2,1)} %bitcast.314), calls=%async_computation.5 | async-start | bytes 4194304 | tf_op jit(solution)/shard_map/all_to_all | solution.py:967
  1033.7 57.6 %collective-permute-start.114 = (f32[2,12288]{1,0:T(2,128)S(1)}, f32[2,12288]{1,0:T(2,128)S(1)}, u32[]{:S(2)}, u32[]{:S(2)}) collective-permute-start(f32[2,12288]{1,0:T(2,128)S(1)} %fusion.24), channel_id=1, source_target_pairs={{16,0},{24,8},{0,16},{8,24},{17,1},{25,9},{1,17},{9,25},{18,2},{26... | collective-permute-start | bytes 294920 | tf_op jit(solution)/shard_map/ppermute | solution.py:69
  1081.6 55.2 %all-to-all-start.6 = ((bf16[8,128,1024]{2,1,0:T(8,128)(2,1)}), bf16[8,128,1024]{2,1,0:T(8,128)(2,1)S(1)}, u32[]{:S(2)}, u32[]{:S(2)}) async-start(bf16[8,128,1024]{2,1,0:T(8,128)(2,1)} %bitcast.313), calls=%async_computation.6 | async-start | bytes 4194304 | tf_op jit(solution)/shard_map/all_to_all | solution.py:967
  1090.6 47.5 %collective-permute-start.110 = (bf16[6,128,1024]{2,1,0:T(8,128)(2,1)}, bf16[6,128,1024]{2,1,0:T(8,128)(2,1)}, u32[]{:S(2)}, u32[]{:S(2)}) collective-permute-start(bf16[6,128,1024]{2,1,0:T(8,128)(2,1)} %get-tuple-element.776.refs_0_), channel_id=1, source_target_pairs={{16,0},{24,8},{0,16},{8,24},{17,1},{25,9},{1,17},{9,25},{18,2},{26... | collective-permute-start | bytes 4718600 | tf_op jit(solution)/shard_map/ppermute | solution.py:69
  (192 other events, 2611.5 us)

commit v3 on v2

--- a/solution.py
+++ b/solution.py
@@ -76,6 +76,11 @@
         steps = range(1, self.size[axis])
         return [values[0]] + [self.take(values[step], axis, -step) for step in steps]
 
+    def swap_z(self, values):
+        count_x = self.size["x"]
+        lines = [[z * count_x + x for z in range(self.size["z"])] for x in range(count_x)]
+        return lax.all_to_all(values, "wsh", 0, 0, tiled=True, axis_index_groups=lines)
+
     def scatter(self, values, axis):
         total = values[0].astype(F32)
         for step in range(1, self.size[axis]):
@@ -94,41 +99,6 @@
 
 def dot_t(left, right):
     return lax.dot_general(left, right, (((1,), (1,)), ((), ())), preferred_element_type=F32)
-
-
-def assemble_kernel(split_count, whole_count, has_y, where, *refs):
-    if has_y:
-        mine, other_y, core_mine, core_other_y, out = refs
-    else:
-        mine, core_mine, out = refs
-    half_rows = mine.shape[3]
-    half_cols = mine.shape[4]
-    core_at = where[3]
-    y_at = where[2]
-
-    def put(block, rows, cols, value):
-        out[block, 0, pl.ds(rows * half_rows, half_rows), pl.ds(cols * half_cols, half_cols)] = value
-
-    for core in range(2):
-
-        @pl.when(core_at == core)
-        def _():
-            if has_y:
-                for y in range(2):
-
-                    @pl.when(y_at == y)
-                    def _():
-                        for block in range(split_count):
-                            put(block, core, y, mine[0, 0, block])
-                            put(block, core, 1 - y, other_y[0, 0, block])
-                            put(block, 1 - core, y, core_mine[0, 0, block])
-                            put(block, 1 - core, 1 - y, core_other_y[0, 0, block])
-
-            for block in range(whole_count):
-                for cols in range(2):
-                    entry = split_count + 2 * block + cols
-                    put(split_count + block, core, cols, mine[0, 0, entry])
-                    put(split_count + block, 1 - core, cols, core_mine[0, 0, entry])
 
 
 def after(value, *others):
@@ -168,10 +138,12 @@
         self.crossed = []
 
     def step_z(self):
-        self.held = gather_list(self.place, self.held[0], "z")
+        piece = self.held[0]
+        copies = jnp.broadcast_to(piece[None], (self.place.size["z"],) + piece.shape)
+        self.held = [self.place.swap_z(copies)]
 
     def step_x(self):
-        self.held = gather_list(self.place, jnp.stack(self.held), "x")
+        self.held = gather_list(self.place, self.held[0], "x")
 
     def step_y(self):
         self.held = [jnp.stack(self.held)]
@@ -184,35 +156,49 @@
         if self.split_count:
             self.crossed.append(self.place.take(self.held[1], "core", 1))
 
-    def whole(self):
-        place, operands = self.place, self.held + self.crossed
-        count_z, count_x = place.size["z"], place.size["x"]
-        where = jnp.stack([place.at[name] for name in ("z", "x", "y", "core")]).astype(jnp.int32)
-
-        def piece_at(z, x, where):
-            return (
-                lax.rem(x - where[1] + count_x, count_x),
-                lax.rem(z - where[0] + count_z, count_z),
-                0,
-                0,
-                0,
-            )
-
-        out = call(
-            functools.partial(
-                assemble_kernel, self.split_count, self.count - self.split_count, self.split_count > 0
-            ),
-            (count_z, count_x),
-            [pl.BlockSpec((1, 1) + value.shape[2:], piece_at) for value in operands],
-            pl.BlockSpec(
-                (self.count, 1, self.rows, BLK), lambda z, x, where: (0, z * count_x + x, 0, 0)
-            ),
-            shaped((self.count, count_z * count_x, self.rows, BLK), BF16),
-            prefetch=1,
-            cost=9.0,
-            name="assemble",
-        )(where, *operands)
-        return out.reshape(self.count, BLK, BLK)
+    def pieces(self):
+        split, mine, crossed = self.split_count, self.held, self.crossed
+        part = (mine[0].shape[:2]) + (1,) + mine[0].shape[3:]
+
+        def spec(place_of):
+            return pl.BlockSpec(part, lambda i, where: (0, 0, place_of(i), 0, 0))
+
+        low = spec(lambda i: jnp.where(i < split, i, 2 * i - split))
+        high = spec(lambda i: jnp.where(i < split, split + 1, 2 * i - split + 1))
+        operands = [mine[0], crossed[0], mine[0], crossed[0]]
+        specs = [low, low, high, high]
+        if split:
+            operands += [mine[1], crossed[1]]
+            specs += [spec(lambda i: jnp.minimum(i, split - 1))] * 2
+        return operands, specs
+
+    def where(self):
+        return jnp.stack([self.place.at[name] for name in ("x", "y", "core")]).astype(jnp.int32)
+
+
+def open_block(split, where, pieces, out):
+    spot = pl.program_id(0)
+    extent_x, extent_z, _, half_rows, half_cols = pieces[0].shape
+    x_at, y_at, core_at = where[0], where[1], where[2]
+
+    def put(first_col, sources):
+        low_col = pl.ds(pl.multiple_of(first_col * half_cols, half_cols), half_cols)
+        high_col = pl.ds(pl.multiple_of((1 - first_col) * half_cols, half_cols), half_cols)
+        for step_x in range(extent_x):
+            for z in range(extent_z):
+                base = (z * extent_x + lax.rem(x_at + step_x, extent_x)) * 2
+                mine = pl.ds(pl.multiple_of((base + core_at) * half_rows, half_rows), half_rows)
+                other = pl.ds(pl.multiple_of((base + 1 - core_at) * half_rows, half_rows), half_rows)
+                out[0, mine, low_col] = sources[0][step_x, z, 0]
+                out[0, other, low_col] = sources[1][step_x, z, 0]
+                out[0, mine, high_col] = sources[2][step_x, z, 0]
+                out[0, other, high_col] = sources[3][step_x, z, 0]
+
+    if split:
+        pl.when(spot < split)(lambda: put(y_at, list(pieces[:2]) + list(pieces[4:])))
+        pl.when(spot >= split)(lambda: put(0, pieces[:4]))
+    else:
+        put(0, pieces[:4])
 
 
 def call(body, grid, in_specs, out_specs, out_shape, scratch=(), prefetch=0, cost=1.0, name=None):
@@ -227,7 +213,7 @@
         ),
         out_shape=out_shape,
         compiler_params=pltpu.CompilerParams(vmem_limit_bytes=VMEM_BYTES),
-        cost_estimate=pl.CostEstimate(flops=int(cost * 1e9), bytes_accessed=0, transcendentals=0),
+        cost_estimate=pl.CostEstimate(flops=int(cost * 2e7), bytes_accessed=0, transcendentals=0),
         name=name,
     )
 
@@ -257,33 +243,43 @@
     ) * scale
 
 
-def project_kernel(x_low, weight, bias, query, keyval):
-    value = (dot(x_low[...], weight[0]) + bias[0]).astype(BF16)
+BLOCK = pl.BlockSpec((1, BLK, BLK), lambda i, *at: (i, 0, 0))
+BLOCKS = jax.ShapeDtypeStruct((4, BLK, BLK), BF16)
+
+
+def project_kernel(split, where, x_low, bias, *refs):
+    pieces, (query, keyval, weight) = refs[:-3], refs[-3:]
+    open_block(split, where, pieces, weight)
+
+    def value():
+        return (dot(x_low[...], weight[0]) + bias[0]).astype(BF16)
 
     @pl.when(pl.program_id(0) == 0)
     def _():
-        query[...] = value
-
-    @pl.when(pl.program_id(0) > 0)
+        query[...] = value()
+
+    @pl.when((pl.program_id(0) > 0) & (pl.program_id(0) < 3))
     def _():
-        keyval[...] = value
-
-
-def project(x_low, w_in, bias):
+        keyval[...] = value()
+
+
+def project(x_low, chunk, bias):
     tokens = x_low.shape[0]
+    pieces, specs = chunk.pieces()
     return call(
-        project_kernel,
-        (3,),
+        functools.partial(project_kernel, chunk.split_count),
+        (4,),
+        [fixed((tokens, D)), pl.BlockSpec((1, 1, D), lambda i, where: (jnp.minimum(i, 2), 0, 0))] + specs,
         [
             fixed((tokens, D)),
-            pl.BlockSpec((1, BLK, BLK), lambda i: (i, 0, 0)),
-            pl.BlockSpec((1, 1, D), lambda i: (i, 0, 0)),
+            pl.BlockSpec((tokens, D), lambda i, where: (0, jnp.clip(i - 1, 0, 1))),
+            BLOCK,
         ],
-        [fixed((tokens, D)), pl.BlockSpec((tokens, D), lambda i: (0, jnp.maximum(i - 1, 0)))],
-        [shaped((tokens, D), BF16), shaped((tokens, 2 * D), BF16)],
-        cost=6.0,
+        [shaped((tokens, D), BF16), shaped((tokens, 2 * D), BF16), BLOCKS],
+        prefetch=1,
+        cost=8.0,
         name="project",
-    )(x_low, w_in, bias)
+    )(chunk.where(), x_low, bias, *pieces)
 
 
 def head_probs(query_h, keys_h, masks):
@@ -422,31 +418,33 @@
     return (1.0 + lax.erf(hidden * (0.5**0.5))) * 0.5
 
 
-def up_kernel(middle_low, weight, bias, hidden, act):
+def up_kernel(split, where, middle_low, bias, *refs):
+    pieces, (hidden, act, weight) = refs[:-3], refs[-3:]
+    open_block(split, where, pieces, weight)
     value = dot(middle_low[...], weight[0]) + bias[0]
     hidden[...] = value
     act[...] = (value * erf_part(value)).astype(BF16)
 
 
-def up(middle_low, w_up, bias):
+def up(middle_low, chunk, bias):
     tokens = middle_low.shape[0]
-    part = pl.BlockSpec((tokens, BLK), lambda i: (0, i))
+    pieces, specs = chunk.pieces()
+    part = pl.BlockSpec((tokens, BLK), lambda i, where: (0, i))
     return call(
-        up_kernel,
+        functools.partial(up_kernel, chunk.split_count),
         (FF // BLK,),
-        [
-            fixed((tokens, D)),
-            pl.BlockSpec((1, BLK, BLK), lambda i: (i, 0, 0)),
-            pl.BlockSpec((1, 1, BLK), lambda i: (i, 0, 0)),
-        ],
-        [part, part],
-        [shaped((tokens, FF), F32), shaped((tokens, FF), BF16)],
+        [fixed((tokens, D)), pl.BlockSpec((1, 1, BLK), lambda i, where: (i, 0, 0))] + specs,
+        [part, part, BLOCK],
+        [shaped((tokens, FF), F32), shaped((tokens, FF), BF16), BLOCKS],
+        prefetch=1,
         cost=8.0,
         name="up",
-    )(middle_low, w_up, bias)
-
-
-def down_kernel(act, weight, middle, vecs, summed, result, result_low, total):
+    )(chunk.where(), middle_low, bias, *pieces)
+
+
+def down_kernel(split, where, act, middle, vecs, *refs):
+    pieces, (summed, result, result_low, weight, total) = refs[:-5], refs[-5:]
+    open_block(split, where, pieces, weight)
     spot = pl.program_id(0)
     value = dot(act[...], weight[0])
 
@@ -468,24 +466,21 @@
         result_low[...] = value.astype(BF16)
 
 
-def down(act, w_down, middle, vecs):
+def down(act, chunk, middle, vecs):
     tokens = act.shape[0]
     full = fixed((tokens, D))
+    pieces, specs = chunk.pieces()
     return call(
-        down_kernel,
+        functools.partial(down_kernel, chunk.split_count),
         (FF // BLK,),
-        [
-            pl.BlockSpec((tokens, BLK), lambda i: (0, i)),
-            pl.BlockSpec((1, BLK, BLK), lambda i: (i, 0, 0)),
-            full,
-            fixed(vecs.shape),
-        ],
-        [full, full, full],
-        [shaped((tokens, D), F32), shaped((tokens, D), F32), shaped((tokens, D), BF16)],
+        [pl.BlockSpec((tokens, BLK), lambda i, where: (0, i)), full, fixed(vecs.shape)] + specs,
+        [full, full, full, BLOCK],
+        [shaped((tokens, D), F32), shaped((tokens, D), F32), shaped((tokens, D), BF16), BLOCKS],
         scratch=[pltpu.VMEM((tokens, D), F32)],
+        prefetch=1,
         cost=8.0,
         name="down",
-    )(act, w_down, middle, vecs)
+    )(chunk.where(), act, middle, vecs, *pieces)
 
 
 def column_sum(value):
@@ -617,11 +612,12 @@
     return [value] + [place.take(value, axis, step) for step in range(1, place.size[axis])]
 
 
-def project_step(place, carried_low, w_in, vector):
+def project_step(place, carried_low, chunk, vector):
     parts = vector_parts(vector)
     bias_in = jnp.stack([parts[0], jnp.zeros((D,), F32), parts[1]])[:, None]
-    query, keyval = project(carried_low, w_in, bias_in)
-    return query, gather_list(place, keyval, "y")
+    query, keyval, w_in = project(carried_low, chunk, bias_in)
+    keyvals = [keyval, *gather_list(place, keyval, "y")[1:], place.take(keyval, "core", 1)]
+    return query, keyvals, w_in
 
 
 def mix_step(query, keyvals, carried, w_in, vector, mask):
@@ -630,19 +626,19 @@
     return attn_low, *mix(attn_low, w_in, carried, jnp.stack([parts[2], parts[4], parts[5]]))
 
 
-def up_step(mid_low, w_up, vector):
-    return up(mid_low, w_up, vector[8 * D :].reshape(FF // BLK, 1, BLK))
-
-
-def down_step(act_low, w_down, middle, vector):
+def up_step(mid_low, chunk, vector):
+    return up(mid_low, chunk, vector[8 * D :].reshape(FF // BLK, 1, BLK))
+
+
+def down_step(act_low, chunk, middle, vector):
     parts = vector_parts(vector)
-    return down(act_low, w_down, middle, jnp.stack([parts[3], parts[6], parts[7]]))
+    return down(act_low, chunk, middle, jnp.stack([parts[3], parts[6], parts[7]]))
 
 
 def sum_kernel(count_one, first_half, sizes, where, *refs):
     sets = (refs[:4], refs[4:8]) if count_one is not None else (refs[:4],)
     outs, product = refs[4 * len(sets) : -1], refs[-1]
-    z_at, x_at, y_at = where[0], where[1], where[2]
+    x_at, y_at = where[1], where[2]
     extent_z, extent_x, extent_y, rows = sizes
     spot = pl.program_id(0)
 
@@ -663,9 +659,7 @@
             from_col = pl.multiple_of(lax.rem(y_at + step_y, extent_y) * cols, cols)
             for step_x in range(extent_x):
                 for step_z in range(extent_z):
-                    row_block = lax.rem(z_at + step_z, extent_z) * extent_x + lax.rem(
-                        x_at + step_x, extent_x
-                    )
+                    row_block = step_z * extent_x + lax.rem(x_at + step_x, extent_x)
                     from_row = pl.multiple_of(row_block * rows, rows)
                     value = product[pl.ds(from_row, rows), pl.ds(from_col, cols)].astype(BF16)
                     if y_first:
@@ -695,9 +689,13 @@
             return jnp.clip(i - start, 0, amount - 1)
 
         many_left, many_right = one[0].shape[1] > BLK, one[2].shape[1] > BLK
-        specs += [
-            pl.BlockSpec((tokens, BLK), lambda i, where, at=at, many=many_left: (0, at(i) if many else 0))
-        ] * 2
+        for first in (0, one[4]):
+            specs.append(
+                pl.BlockSpec(
+                    (tokens, BLK),
+                    lambda i, where, at=at, many=many_left, first=first: (0, first + (at(i) if many else 0)),
+                )
+            )
         specs += [
             pl.BlockSpec(
                 (tokens, half),
@@ -725,20 +723,21 @@
         prefetch=1,
         cost=8.0,
         name="partial_sums",
-    )(where, *[value for one in sets for value in one])
+    )(where, *[value for one in sets for value in one[:4]])
     return outs[:extent_y], outs[extent_y:]
 
 
 class Summing:
-    def __init__(self, place, sets):
+    def __init__(self, place, ids, sets):
         self.place = place
+        self.ids = ids
         if (BLK // (CORES * place.size["y"])) % 128:
             self.plain = True
             self.parts = self.by_y = self.by_x = ()
-            self.groups = [[sum_job_plain(place, one[0], one[2], "y")] for one in sets]
+            self.groups = [sum_job_plain(place, one[0], one[2], "y")[None] for one in sets]
         else:
             self.plain = False
-            sets = [(one[0], one[1], one[2], place.take(one[2], "core", 1)) for one in sets]
+            sets = [(one[0], one[1], one[2], place.take(one[2], "core", 1), one[3]) for one in sets]
             self.parts = partial_sums(place, sets)
             self.by_y = self.by_x = ()
             self.groups = ()
@@ -765,22 +764,16 @@
 
     def third(self):
         if not self.plain:
-            by_y, by_x = add_up(self.by_y), add_up(self.by_x)
-            both = [
-                jnp.concatenate([by_y[step], by_x[step]]).astype(BF16)
-                for step in range(self.place.size["z"])
-            ]
-            self.groups = [self.place.collect(both, "z")]
-
-
-def route_kernel(groups, slots, scaling, spots, *refs):
-    out, total = refs[-2:]
-    refs = list(refs[:-2])
+            both = jnp.concatenate([add_up(self.by_y), add_up(self.by_x)], axis=1)
+            self.groups = [self.place.swap_z(both.astype(BF16))]
+
+
+def route_kernel(count, slots, scaling, spots, *refs):
+    parts, (out, total) = refs[:count], refs[count:]
     at = 0
-    for addends in groups:
-        parts = [refs.pop(0) for _ in range(addends)]
-        for block in range(parts[0].shape[0]):
-            value = sum(part[block].astype(F32) for part in parts)
+    for part in parts:
+        for block in range(part.shape[1]):
+            value = sum(part[addend, block].astype(F32) for addend in range(part.shape[0]))
             total[at] = (value * scaling).astype(BF16)
             at += 1
     total[at] = jnp.zeros(total.shape[1:], BF16)
@@ -793,21 +786,20 @@
 
 
 def route(groups, spots, slots, wsh_count, scaling):
-    rows, cols = groups[0][0].shape[1:]
-    blocks = sum(addends[0].shape[0] for addends in groups)
-    flat = [value for addends in groups for value in addends]
+    rows, cols = groups[0].shape[2:]
+    blocks = sum(group.shape[1] for group in groups)
     shape = (spots.shape[0] // slots, wsh_count, rows, cols)
     return call(
-        functools.partial(route_kernel, [len(addends) for addends in groups], slots, scaling),
+        functools.partial(route_kernel, len(groups), slots, scaling),
         (1,),
-        [fixed(value.shape) for value in flat],
+        [fixed(group.shape) for group in groups],
         fixed(shape),
         shaped(shape, BF16),
         scratch=[pltpu.VMEM((blocks + 1, rows, cols), BF16)],
         prefetch=1,
         cost=6.0,
         name="route",
-    )(spots, *flat)
+    )(spots, *groups)
 
 
 def rotate_kernel(quarters, where, grads, right, left, first, second, rotated, update, total, low, right_low):
@@ -860,25 +852,27 @@
     )(slot, grads, right_bases, left, first, second)
 
 
-def pick_kernel(count, table, *refs):
+def pick_kernel(count, amount, table, *refs):
     parts, out = refs[:count], refs[count]
-    block = pl.program_id(0)
-
-    def put(part):
-        out[0] = parts[part][table[1, block]]
-
-    for part in range(count):
-        pl.when(table[0, block] == part)(functools.partial(put, part))
+    first = pl.program_id(0) * amount
+
+    def put(spot, part):
+        out[spot] = parts[part][table[1, first + spot]]
+
+    for spot in range(amount):
+        for part in range(count):
+            pl.when(table[0, first + spot] == part)(functools.partial(put, spot, part))
 
 
 def pick(parts, table):
     blocks = table.shape[1]
+    amount = 4
     shape = (blocks,) + parts[0].shape[1:]
     return call(
-        functools.partial(pick_kernel, len(parts)),
-        (blocks,),
+        functools.partial(pick_kernel, len(parts), amount),
+        (blocks // amount,),
         [fixed(value.shape) for value in parts],
-        pl.BlockSpec((1,) + shape[1:], lambda i, table: (i, 0, 0)),
+        pl.BlockSpec((amount,) + shape[1:], lambda i, table: (i, 0, 0)),
         shaped(shape, BF16),
         prefetch=1,
         cost=12.0,
@@ -1009,21 +1003,22 @@
     live = {}
 
     def settle():
-        state = [(chunk.held, chunk.crossed) for chunk in chunks]
+        going = [chunk for chunk in chunks if chunk]
+        state = [(chunk.held, chunk.crossed) for chunk in going]
         state, values = together(state, {name: live[name] for name in live})
-        for chunk, (held, crossed) in zip(chunks, state):
+        for chunk, (held, crossed) in zip(going, state):
             chunk.held, chunk.crossed = held, crossed
         live.update(values)
 
     def finish(spot):
-        chunks[spot].step_core()
-        whole = chunks[spot].whole()
-        chunks[spot].held = chunks[spot].crossed = []
-        return whole
+        chunk = chunks[spot]
+        chunk.step_core()
+        chunks[spot] = None
+        return chunk
 
     def keyvals_of(layer_at):
         keyvals = live[f"keyvals{layer_at}"]
-        return keyvals + [place.take(value, "core", 1) for value in keyvals]
+        return keyvals + [place.take(value, "core", 1) for value in keyvals[1:count_y]]
 
     kept = [{}, {}]
     chunks[0].step_z()
@@ -1038,8 +1033,7 @@
     chunks[1].step_y()
     chunks[2].step_x()
     chunks[3].step_z()
-    w_in_0 = finish(0)
-    query_0, live["keyvals0"] = project_step(place, stream_in[0], w_in_0, vec_params[0])
+    query_0, live["keyvals0"], w_in_0 = project_step(place, stream_in[0], finish(0), vec_params[0])
     live["query"] = query_0
     settle()
     chunks[2].step_y()
@@ -1050,42 +1044,34 @@
     attn_0, summed_one_0, middle_0, mid_low_0 = mix_step(
         query_0, keyvals_0, stream_in[0], w_in_0, vec_params[0], mask
     )
-    w_up_0 = finish(1)
-    hidden_0, live["act"] = up_step(mid_low_0, w_up_0, vec_params[0])
+    hidden_0, live["act"], w_up_0 = up_step(mid_low_0, finish(1), vec_params[0])
     settle()
     chunks[3].step_y()
     chunks[4].step_x()
     chunks[5].step_z()
     act_0 = live["act"]
-    w_down_0 = finish(2)
-    summed_two_0, live["result"], live["result_low"] = down_step(
-        act_0, w_down_0, middle_0, vec_params[0]
+    summed_two_0, live["result"], live["result_low"], w_down_0 = down_step(
+        act_0, finish(2), middle_0, vec_params[0]
     )
     settle()
     chunks[4].step_y()
     chunks[5].step_x()
     result_0, result_low_0 = live["result"], live["result_low"]
-    w_in_1 = finish(3)
-    query_1, live["keyvals1"] = project_step(place, result_low_0, w_in_1, vec_params[1])
+    query_1, live["keyvals1"], w_in_1 = project_step(place, result_low_0, finish(3), vec_params[1])
     live["query"] = query_1
     live["own"] = left_bases
     settle()
     chunks[5].step_y()
-    live["own"] = to_owner(live["own"], wsh_count)
+    left_own = to_owner(live.pop("own"), wsh_count)
     keyvals_1 = keyvals_of(1)
     query_1 = live["query"]
     attn_1, summed_one_1, middle_1, mid_low_1 = mix_step(
         query_1, keyvals_1, result_0, w_in_1, vec_params[1], mask
     )
-    w_up_1 = finish(4)
-    hidden_1, live["act"] = up_step(mid_low_1, w_up_1, vec_params[1])
-    live["first"] = moment1
+    hidden_1, live["act"], w_up_1 = up_step(mid_low_1, finish(4), vec_params[1])
     settle()
-    left_own = live["own"]
-    first_own = to_owner(live["first"], wsh_count)
     act_1 = live["act"]
-    w_down_1 = finish(5)
-    summed_two_1, _, result_low_1 = down_step(act_1, w_down_1, middle_1, vec_params[1])
+    summed_two_1, _, result_low_1, w_down_1 = down_step(act_1, finish(5), middle_1, vec_params[1])
     stream_out = result_low_1[None]
 
     blocks = [(w_in_0, w_up_0, w_down_0), (w_in_1, w_up_1, w_down_1)]
@@ -1093,7 +1079,10 @@
         (stream_in[0], attn_0, mid_low_0, act_0),
         (result_low_0, attn_1, mid_low_1, act_1),
     ]
-    crossed = [[place.take(value, "core", 1) for value in values] for values in lefts]
+    crossed = [
+        (place.take(jnp.concatenate(values[:3], axis=1), "core", 1), place.take(values[3], "core", 1))
+        for values in lefts
+    ]
     summed = [(summed_one_0, summed_two_0), (summed_one_1, summed_two_1)]
     hidden = [hidden_0, hidden_1]
     queries = [query_0, query_1]
@@ -1102,7 +1091,7 @@
         (vec_params[layer_at][None, 4 * D : 5 * D], vec_params[layer_at][None, 6 * D : 7 * D])
         for layer_at in range(LAYERS)
     ]
-    live = {}
+    live = {"crossed": crossed}
     jobs = []
     vec_terms = [None] * LAYERS
 
@@ -1113,39 +1102,55 @@
             job.parts, job.by_y, job.by_x, job.groups = fields
         live.update(values)
 
-    def begin(layer_at, *sets):
+    def begin(layer_at, first_block, *sets):
+        ids = [layer_at * NBLK + first_block + spot for spot in range(4)]
         jobs.append(
-            Summing(place, [(lefts[layer_at][spot], crossed[layer_at][spot], right) for spot, right in sets])
+            Summing(
+                place,
+                ids,
+                [
+                    (lefts[layer_at][spot], live["crossed"][layer_at][spot // 3], right, spot % 3)
+                    for spot, right in sets
+                ],
+            )
         )
         return jobs[-1]
 
     def close_step(layer_at, flow):
         live["two"], live["ffn"], live["sums_two"] = close(flow, summed[layer_at][1], gains[layer_at][1])
-        return begin(layer_at, (3, live["ffn"]))
+
+    def down_job(layer_at):
+        return begin(layer_at, 8, (3, live["ffn"]))
+
+    def in_job(layer_at):
+        return begin(layer_at, 0, (0, live["joined"]), (1, live["branch_in"]))
+
+    def up_job(layer_at):
+        return begin(layer_at, 4, (2, live["hid"]))
 
     def feed_step(layer_at):
         w_in, w_up, w_down = blocks[layer_at]
-        hid_low, live["branch"], attn_grad, live["one"], live["sums_one"], live["sums_up"] = feed_back(
+        live["hid"], live["branch"], attn_grad, live["one"], live["sums_one"], live["sums_up"] = feed_back(
             live["two"], live["ffn"], summed[layer_at][0], hidden[layer_at], w_down, w_up, w_in, gains[layer_at][0]
         )
         live["attn_grad"] = attn_grad
-        return begin(layer_at, (2, hid_low))
 
     def attend_step(layer_at):
         live["grad_q"], mine, other = attend_back(
             queries[layer_at], keyvals_all[layer_at], live["attn_grad"], mask
         )
-        live["pair"] = [mine, place.take(other, "core", 1)]
+        live["pair"] = [mine, other]
 
     def send_step():
-        mine, arrived = live["pair"]
+        mine, other = live["pair"]
+        arrived = place.take(other, "core", 1)
         sums = [mine[:, step].astype(F32) + arrived[:, step].astype(F32) for step in range(count_y)]
         live["kv"] = [sums[0]] + [
             place.take(sums[step].astype(BF16), "y", -step) for step in range(1, count_y)
         ]
 
     def input_step(layer_at):
-        joined, grad_x, in_sums = input_back(live["grad_q"], live["kv"], live["one"], blocks[layer_at][0])
+        live["joined"], grad_x, in_sums = input_back(live["grad_q"], live["kv"], live["one"], blocks[layer_at][0])
         sums_two, sums_one = live["sums_two"], live["sums_one"]
         vec_terms[layer_at] = jnp.concatenate(
             [
@@ -1158,70 +1163,84 @@
                 live["sums_up"].reshape(-1),
             ]
         )
-        return grad_x, begin(layer_at, (0, joined), (1, live["branch"]))
-
-    down_1 = close_step(1, cotangent[0])
+        live["branch_in"] = live["branch"]
+        return grad_x
+
+    close_step(1, cotangent[0])
+    down_1 = down_job(1)
+    live["left"] = left_own
+    live["first"] = moment1
     settle_back()
     down_1.first_y()
     down_1.first_x()
-    live["first"] = first_own
-    live["second"] = moment2
-    up_1 = feed_step(1)
+    background = to_owner(live["first"], wsh_count)
+    feed_step(1)
     settle_back()
-    live["second"] = to_owner(live["second"], wsh_count)
     down_1.second_x()
     down_1.second_y()
+    up_1 = up_job(1)
+    live["first"] = background
+    settle_back()
+    down_1.third()
     up_1.first_y()
     up_1.first_x()
     attend_step(1)
+    live["second"] = moment2
     settle_back()
-    down_1.third()
     send_step()
     up_1.second_x()
+    up_1.second_y()
+    live["second"] = to_owner(live["second"], wsh_count)
     settle_back()
-    up_1.second_y()
-    grad_flow, in_1 = input_step(1)
-    down_0 = close_step(0, grad_flow)
+    grad_flow = input_step(1)
+    close_step(0, grad_flow)
+    settle_back()
+    in_1 = in_job(1)
+    down_0 = down_job(0)
     settle_back()
     up_1.third()
     in_1.first_y()
     in_1.first_x()
+    feed_step(0)
+    settle_back()
+    in_1.second_x()
+    in_1.second_y()
     down_0.first_y()
     down_0.first_x()
-    up_0 = feed_step(0)
     attend_step(0)
     settle_back()
     send_step()
-    in_1.second_x()
-    in_1.second_y()
+    in_1.third()
     down_0.second_x()
     down_0.second_y()
-    up_0.first_x()
+    up_0 = up_job(0)
     settle_back()
-    in_1.third()
     down_0.third()
     up_0.first_y()
+    up_0.first_x()
+    grad_flow = input_step(0)
+    settle_back()
+    up_0.second_x()
     up_0.second_y()
-    grad_flow, in_0 = input_step(0)
+    in_0 = in_job(0)
     settle_back()
+    up_0.third()
     in_0.first_y()
     in_0.first_x()
-    up_0.second_x()
     settle_back()
     in_0.second_x()
     in_0.second_y()
-    up_0.third()
     settle_back()
     in_0.third()
     stream_grad = grad_flow[None]
     vec_grads = sum_everywhere(place, jnp.stack(vec_terms)) * scaling
-    groups = [
-        group for layer_jobs in ((in_0, up_0, down_0), (in_1, up_1, down_1)) for job in layer_jobs for group in job.groups
-    ]
+    groups = [group for job in jobs for group in job.groups]
+    ids = [block for job in jobs for block in job.ids]
 
     owner_flat = owner_slots.reshape(-1)
     block_count = LAYERS * NBLK
-    picks = owner_flat[None, :] == jnp.arange(slot_total, dtype=jnp.int32)[:, None]
+    owner_sorted = jnp.stack([owner_flat[block] for block in ids])
+    picks = owner_sorted[None, :] == jnp.arange(slot_total, dtype=jnp.int32)[:, None]
     spots = jnp.where(
         jnp.any(picks, axis=1), jnp.argmax(picks, axis=1).astype(jnp.int32), block_count
     )
@@ -1233,17 +1252,17 @@
     quarters = [(source % CORES) * count_y + source // CORES for source in range(ctx_count)]
     slot_own = jnp.minimum(lax.axis_index("wsh"), slots_dev - 1).reshape(1)
     rotated_own, update_own = rotate(
-        arrived.reshape(ctx_count, BLK, width), quarters, right_bases, slot_own, left_own, live["first"], live["second"]
+        arrived.reshape(ctx_count, BLK, width), quarters, right_bases, slot_own, live["left"], live["first"], live["second"]
     )
 
     by_rows = after(by_slot[:, :slots_dev], arrived)
     by_rows = lax.all_to_all(by_rows, "ctx", 0, 0, tiled=True)
     update_own, rotated_own, by_rows = together(update_own, rotated_own, by_rows)
     update = from_owner(update_own, wsh_count, slots_dev)
-    update, rotated_own = together(update, rotated_own)
-    update = update.astype(F32)
     by_rows = by_rows.reshape(count_y, CORES, slots_dev, rows_dev, width)
     block_grads = by_rows.transpose(2, 3, 1, 0, 4).reshape(slots_dev, rows_dev, BLK).astype(F32)
+    update, rotated_own, block_grads = together(update, rotated_own, block_grads)
+    update = update.astype(F32)
 
     new_master = master - LR_BLOCK * update
     master_low = new_master.astype(BF16)

time: 1180 us -> 1100 us (0.932)
  waiting for transfers between devices: 574 us -> 504 us
  Pallas kernels: 316 us -> 273 us
  other arithmetic: 66.9 us -> 83.6 us
  local copies, waits for them, and re-layouts: 65 us -> 78.7 us
    ppermute x116 -> x76, waiting for transfers between devices: 447 us -> 328 us  [take(): return lax.ppermute(value, name, pairs)]
    all_to_all x0 -> x12, waiting for transfers between devices: none -> 59 us  [swap_z(): lax.all_to_all(values, 'wsh', 0, 0, tiled=True, axis_index_groups=lines)]
    all_to_all x0 -> x12, starting transfers between devices: none -> 54.6 us  [swap_z(): lax.all_to_all(values, 'wsh', 0, 0, tiled=True, axis_index_groups=lines)]
    ppermute x116 -> x76, starting transfers between devices: 107 us -> 56.8 us  [take(): return lax.ppermute(value, name, pairs)]
    pallas_call x14 -> x8, Pallas kernels: 120 us -> 77.2 us  [the longest x2 23.1 us: up(): call(functools.partial(up_kernel, chunk.split_count), (FF // BLK,), [fixe...]
    unnamed x269 -> x232, local copies, waits for them, and re-layouts: 26 us -> 33.4 us
  transfers between devices with their start and end apart: 125 -> 97, of which waited for: 50 -> 54; matrix products, arithmetic and copies ran while one was open for 8% -> 8% of each run, Pallas kernels for 26% -> 22%
where the time goes in v3:
time: 1100 us; the launch traced here: 1090 us
  waiting for transfers between devices  504 us (46%)
  Pallas kernels  273 us (25%)
  starting transfers between devices  148 us (13%)
  other arithmetic  83.6 us (8%)
  local copies, waits for them, and re-layouts  78.7 us (7%)
    ppermute x76, waiting for transfers between devices, take(): return lax.ppermute(value, name, pairs)  328 us
    all_to_all x12, waiting for transfers between devices, swap_z(): lax.all_to_all(values, 'wsh', 0, 0, tiled=True, axis_index_groups=lines)  59 us
    ppermute x76, starting transfers between devices, take(): return lax.ppermute(value, name, pairs)  56.8 us
    all_to_all x12, starting transfers between devices, swap_z(): lax.all_to_all(values, 'wsh', 0, 0, tiled=True, axis_index_groups=lines)  54.6 us
    all_to_all x2, waiting for transfers between devices, from_owner(): return lax.all_to_all(cut, 'wsh', 0, 0, tiled=True)[:slots]  49.2 us
    pallas_call x6, Pallas kernels, partial_sums(): call(functools.partial(sum_kernel, counts[0] if len(sets) > 1 else None,...  47 us
    all_to_all x1, waiting for transfers between devices, on_device(): lax.all_to_all(by_slot.reshape(ctx_count * wsh_count, rows_dev, width), (...  44.9 us
    pallas_call x2, Pallas kernels, attend_back(): call(functools.partial(attend_back_kernel, count, count_y, tokens), (D //...  42.3 us
  transfers between devices with their start and end apart: 97, of which 54 were waited for; matrix products, arithmetic and copies ran while one was open for 8% of the time, Pallas kernels for 22%

profile of v3, /device:TPU:0, one launch (start us, length us, event | category | flops | bytes accessed | tf_op | source)
XLA Modules:
  0.0 1090.8 jit_solution(16477099421856326703)
XLA Ops:
  7.5 6.3 all-to-all-start
  19.2 31.6 %all-to-all-done = bf16[4,6,64,512]{3,2,1,0:T(8,128)(2,1)S(1)} async-done(((bf16[4,6,64,512]{3,2,1,0:T(8,128)(2,1)}), bf16[4,6,64,512]{3,2,1,0:T(8,128)(2,1)S(1)}, u32[]{:S(2)}, u32[]{:S(2)}) %all-to-all-start) | async-done | bytes 1572896 | tf_op jit(solution)/shard_map/all_to_all | solution.py:82
  57.3 34.0 %collective-permute-done = bf16[4,6,64,512]{3,2,1,0:T(8,128)(2,1)} collective-permute-done((bf16[4,6,64,512]{3,2,1,0:T(8,128)(2,1)S(1)}, bf16[4,6,64,512]{3,2,1,0:T(8,128)(2,1)}, u32[]{:S(2)}, u32[]{:S(2)}) %collective-permute-start) | collective-permute-done | bytes 1572896 | tf_op jit(solution)/shard_map/ppermute | solution.py:69
  106.6 23.1 %collective-permute-done.1.refs_4_ = bf16[2,4,2,64,512]{4,3,2,1,0:T(8,128)(2,1)} collective-permute-done((bf16[2,4,2,64,512]{4,3,2,1,0:T(8,128)(2,1)S(1)}, bf16[2,4,2,64,512]{4,3,2,1,0:T(8,128)(2,1)}, u32[]{:S(2)}, u32[]{:S(2)}) %collective-permute-start.1) | collective-permute-done | bytes 1048608 | tf_op jit(solution)/shard_map/ppermute | solution.py:69
  129.7 8.9 collective-permute-done.3
  154.2 9.1 project.2
  163.8 14.8 %collective-permute-done.4.refs_4_ = bf16[2,4,2,64,512]{4,3,2,1,0:T(8,128)(2,1)S(1)} collective-permute-done((bf16[2,4,2,64,512]{4,3,2,1,0:T(8,128)(2,1)S(1)}, bf16[2,4,2,64,512]{4,3,2,1,0:T(8,128)(2,1)S(1)}, u32[]{:S(2)}, u32[]{:S(2)}) %collective-permute-start.4) | collective-permute-done | bytes 1048608 | tf_op jit(solution)/shard_map/ppermute | solution.py:69
  185.3 15.1 %collective-permute-done.8.refs_1_.refs_5_ = bf16[256,2048]{1,0:T(8,128)(2,1)} collective-permute-done((bf16[256,2048]{1,0:T(8,128)(2,1)}, bf16[256,2048]{1,0:T(8,128)(2,1)}, u32[]{:S(2)}, u32[]{:S(2)}) %collective-permute-start.8) | collective-permute-done | bytes 1048608 | tf_op jit(solution)/shard_map/ppermute | solution.py:69
  217.7 14.3 %attend.2.attn.refs_4_ = bf16[256,1024]{1,0:T(8,128)(2,1)} custom-call(bf16[256,1024]{1,0:T(8,128)(2,1)} %get-tuple-element.436.query, f32[1024,256]{1,0:T(8,128)} %compare_select_fusion.mask, bf16[256,2048]{1,0:T(8,128)(2,1)} %get-tuple-element.437.refs_0_.refs_4_, bf16[256,2048]{1,0:T(8,128)(2,1)} %collective-permute-done.8.refs_1_.refs_5_, ...), custom_call_target="tpu_custom_call" | custom-call | flops 280000000 | tf_op jit(solution)/shard_map/attend/pallas_call | solution.py:331
  237.1 11.5 %up.2 = (f32[256,4096]{1,0:T(8,128)}, bf16[256,4096]{1,0:T(8,128)(2,1)}, bf16[4,1024,1024]{2,1,0:T(8,128)(2,1)}) custom-call(s32[3]{0:T(128)} %pad_add_fusion.1.where, bf16[256,1024]{1,0:T(8,128)(2,1)} %get-tuple-element.441.middle_low.refs_0_, f32[4,1,1024]{2,1,0:T(1,128)} %bitcast.188, bf16[2,4,6,64,512]{4,3,2,1,0:T(8,128)(2,1)} %copy-done.2, ...), custom_call_target="tpu_custom_call" | custom-call | flops 160000000 | tf_op jit(solution)/shard_map/up/pallas_call | solution.py:433
  263.8 11.3 %down.2 = (f32[256,1024]{1,0:T(8,128)}, f32[256,1024]{1,0:T(8,128)}, bf16[256,1024]{1,0:T(8,128)(2,1)}, bf16[4,1024,1024]{2,1,0:T(8,128)(2,1)}) custom-call(s32[3]{0:T(128)} %pad_add_fusion.1.where, bf16[256,4096]{1,0:T(8,128)(2,1)} %get-tuple-element.450.act.refs_0_, f32[256,1024]{1,0:T(8,128)} %get-tuple-element.451.middle, ...), custom_call_target="tpu_custom_call" | custom-call | flops 160000000 | tf_op jit(solution)/shard_map/down/pallas_call | solution.py:473
  275.1 11.8 %collective-permute-done.15.refs_4_ = bf16[2,4,2,64,512]{4,3,2,1,0:T(8,128)(2,1)} collective-permute-done((bf16[2,4,2,64,512]{4,3,2,1,0:T(8,128)(2,1)S(1)}, bf16[2,4,2,64,512]{4,3,2,1,0:T(8,128)(2,1)}, u32[]{:S(2)}, u32[]{:S(2)}) %collective-permute-start.15) | collective-permute-done | bytes 1048608 | tf_op jit(solution)/shard_map/ppermute | solution.py:69
  286.9 7.5 collective-permute-done.17
  304.6 9.1 project.3
  314.3 14.4 %collective-permute-done.19.refs_4_ = bf16[2,4,2,64,512]{4,3,2,1,0:T(8,128)(2,1)} collective-permute-done((bf16[2,4,2,64,512]{4,3,2,1,0:T(8,128)(2,1)}, bf16[2,4,2,64,512]{4,3,2,1,0:T(8,128)(2,1)}, u32[]{:S(2)}, u32[]{:S(2)}) %collective-permute-start.19) | collective-permute-done | bytes 1048608 | tf_op jit(solution)/shard_map/ppermute | solution.py:69
  334.6 15.3 %collective-permute-done.23.refs_1_.refs_5_ = bf16[256,2048]{1,0:T(8,128)(2,1)S(1)} collective-permute-done((bf16[256,2048]{1,0:T(8,128)(2,1)}, bf16[256,2048]{1,0:T(8,128)(2,1)S(1)}, u32[]{:S(2)}, u32[]{:S(2)}) %collective-permute-start.23) | collective-permute-done | bytes 1048608 | tf_op jit(solution)/shard_map/ppermute | solution.py:69
  367.3 14.3 %attend.3.attn.refs_4_ = bf16[256,1024]{1,0:T(8,128)(2,1)} custom-call(bf16[256,1024]{1,0:T(8,128)(2,1)} %get-tuple-element.469.query, f32[1024,256]{1,0:T(8,128)} %compare_select_fusion.mask, bf16[256,2048]{1,0:T(8,128)(2,1)} %get-tuple-element.470.refs_0_.refs_4_, bf16[256,2048]{1,0:T(8,128)(2,1)} %copy-done.7, bf16[256,2048]{1,0:T(8,128)(2,1)} %copy-done.8, ...), custom_call_target="tpu_custom_call" | custom-call | flops 280000000 | tf_op jit(solution)/shard_map/attend/pallas_call | solution.py:331
  386.8 11.6 %up.3 = (f32[256,4096]{1,0:T(8,128)}, bf16[256,4096]{1,0:T(8,128)(2,1)}, bf16[4,1024,1024]{2,1,0:T(8,128)(2,1)}) custom-call(s32[3]{0:T(128)} %pad_add_fusion.1.where, bf16[256,1024]{1,0:T(8,128)(2,1)} %get-tuple-element.474.middle_low.refs_0_, f32[4,1,1024]{2,1,0:T(1,128)} %bitcast.187, bf16[2,4,6,64,512]{4,3,2,1,0:T(8,128)(2,1)} %copy-done.4, ...), custom_call_target="tpu_custom_call" | custom-call | flops 160000000 | tf_op jit(solution)/shard_map/up/pallas_call | solution.py:433
  406.9 11.4 %down.3 = (f32[256,1024]{1,0:T(8,128)}, f32[256,1024]{1,0:T(8,128)}, bf16[256,1024]{1,0:T(8,128)(2,1)}, bf16[4,1024,1024]{2,1,0:T(8,128)(2,1)}) custom-call(s32[3]{0:T(128)} %pad_add_fusion.1.where, bf16[256,4096]{1,0:T(8,128)(2,1)} %get-tuple-element.479.act.refs_0_, f32[256,1024]{1,0:T(8,128)} %get-tuple-element.480.middle, ...), custom_call_target="tpu_custom_call" | custom-call | flops 160000000 | tf_op jit(solution)/shard_map/down/pallas_call | solution.py:473
  423.9 7.7 partial_sums.6
  446.2 15.2 %feed_back.2 = (bf16[256,4096]{1,0:T(8,128)(2,1)}, bf16[256,1024]{1,0:T(8,128)(2,1)}, bf16[256,1024]{1,0:T(8,128)(2,1)}, f32[256,1024]{1,0:T(8,128)}, f32[8,1024]{1,0:T(8,128)}, /*index=5*/f32[4,1,1024]{2,1,0:T(1,128)}) custom-call(f32[256,1024]{1,0:T(8,128)} %get-tuple-element.498.grad_two, bf16[256,1024]{1,0:T(8,128)(2,1)} %get-tuple-element.499.refs_2_.ffn_low, ...), custom_call_target="tpu_custom_call" | custom-call | flops 300000000 | tf_op jit(solution)/shard_map/feed_back/pallas_call | solution.py:554
  461.5 6.6 collective-permute-done.35
  468.0 22.3 %collective-permute-done.36 = bf16[2,4,2,128,256]{4,3,2,1,0:T(8,128)(2,1)S(1)} collective-permute-done((bf16[2,4,2,128,256]{4,3,2,1,0:T(8,128)(2,1)}, bf16[2,4,2,128,256]{4,3,2,1,0:T(8,128)(2,1)S(1)}, u32[]{:S(2)}, u32[]{:S(2)}) %collective-permute-start.36) | collective-permute-done | bytes 1048608 | tf_op jit(solution)/shard_map/ppermute | solution.py:69
  496.1 7.6 partial_sums.7
  516.5 21.2 %attend_back.2 = (bf16[256,1024]{1,0:T(8,128)(2,1)}, bf16[2,2,256,1024]{3,2,1,0:T(8,128)(2,1)}, bf16[2,2,256,1024]{3,2,1,0:T(8,128)(2,1)}) custom-call(bf16[256,1024]{1,0:T(8,128)(2,1)} %get-tuple-element.469.query, bf16[256,1024]{1,0:T(8,128)(2,1)} %get-tuple-element.543.grad, f32[1024,256]{1,0:T(8,128)} %compare_select_fusion.mask, ...), custom_call_target="tpu_custom_call" | custom-call | flops 420000000 | tf_op jit(solution)/shard_map/attend_back/pallas_call | solution.py:381
  566.1 17.4 %collective-permute-done.42 = bf16[4,2,128,256]{3,2,1,0:T(8,128)(2,1)S(1)} collective-permute-done((bf16[4,2,128,256]{3,2,1,0:T(8,128)(2,1)S(1)}, bf16[4,2,128,256]{3,2,1,0:T(8,128)(2,1)S(1)}, u32[]{:S(2)}, u32[]{:S(2)}) %collective-permute-start.42) | collective-permute-done | bytes 524320 | tf_op jit(solution)/shard_map/ppermute | solution.py:69
  594.2 8.6 input_back.2
  611.9 7.8 partial_sums.9
  621.7 8.1 partial_sums.8
  637.2 15.2 %feed_back.3 = (bf16[256,4096]{1,0:T(8,128)(2,1)}, bf16[256,1024]{1,0:T(8,128)(2,1)}, bf16[256,1024]{1,0:T(8,128)(2,1)}, f32[256,1024]{1,0:T(8,128)}, f32[8,1024]{1,0:T(8,128)}, /*index=5*/f32[4,1,1024]{2,1,0:T(1,128)}) custom-call(f32[256,1024]{1,0:T(8,128)} %get-tuple-element.637.grad_two, bf16[256,1024]{1,0:T(8,128)(2,1)} %get-tuple-element.638.refs_2_.ffn_low, ...), custom_call_target="tpu_custom_call" | custom-call | flops 300000000 | tf_op jit(solution)/shard_map/feed_back/pallas_call | solution.py:554
  652.5 8.1 collective-permute-done.49
  668.0 21.1 %attend_back.3 = (bf16[256,1024]{1,0:T(8,128)(2,1)}, bf16[2,2,256,1024]{3,2,1,0:T(8,128)(2,1)}, bf16[2,2,256,1024]{3,2,1,0:T(8,128)(2,1)}) custom-call(bf16[256,1024]{1,0:T(8,128)(2,1)} %get-tuple-element.436.query, bf16[256,1024]{1,0:T(8,128)(2,1)} %get-tuple-element.664.grad, f32[1024,256]{1,0:T(8,128)} %compare_select_fusion.mask, ...), custom_call_target="tpu_custom_call" | custom-call | flops 420000000 | tf_op jit(solution)/shard_map/attend_back/pallas_call | solution.py:381
  689.1 11.9 %collective-permute-done.51 = bf16[4,2,128,256]{3,2,1,0:T(8,128)(2,1)S(1)} collective-permute-done((bf16[4,2,128,256]{3,2,1,0:T(8,128)(2,1)S(1)}, bf16[4,2,128,256]{3,2,1,0:T(8,128)(2,1)S(1)}, u32[]{:S(2)}, u32[]{:S(2)}) %collective-permute-start.51) | collective-permute-done | bytes 524320 | tf_op jit(solution)/shard_map/ppermute | solution.py:69
  722.5 7.6 partial_sums.10
  736.9 13.1 %collective-permute-done.59.refs_1_ = bf16[2,256,1024]{2,1,0:T(8,128)(2,1)} collective-permute-done((bf16[2,256,1024]{2,1,0:T(8,128)(2,1)}, bf16[2,256,1024]{2,1,0:T(8,128)(2,1)}, u32[]{:S(2)}, u32[]{:S(2)}) %collective-permute-start.59) | collective-permute-done | bytes 1048608 | tf_op jit(solution)/shard_map/ppermute | solution.py:69
  761.3 7.8 input_back.3
  769.1 13.4 %collective-permute-done.60 = bf16[2,4,2,128,256]{4,3,2,1,0:T(8,128)(2,1)S(1)} collective-permute-done((bf16[2,4,2,128,256]{4,3,2,1,0:T(8,128)(2,1)}, bf16[2,4,2,128,256]{4,3,2,1,0:T(8,128)(2,1)S(1)}, u32[]{:S(2)}, u32[]{:S(2)}) %collective-permute-start.60) | collective-permute-done | bytes 1048608 | tf_op jit(solution)/shard_map/ppermute | solution.py:69
  790.5 8.2 partial_sums.11
  809.2 21.4 %collective-permute-done.66 = bf16[2,4,2,128,256]{4,3,2,1,0:T(8,128)(2,1)S(1)} collective-permute-done((bf16[2,4,2,128,256]{4,3,2,1,0:T(8,128)(2,1)}, bf16[2,4,2,128,256]{4,3,2,1,0:T(8,128)(2,1)S(1)}, u32[]{:S(2)}, u32[]{:S(2)}) %collective-permute-start.66) | collective-permute-done | bytes 1048608 | tf_op jit(solution)/shard_map/ppermute | solution.py:69
  836.7 9.8 collective-permute-done.69
  854.3 22.2 %all-to-all-done.14.refs_5_ = bf16[4,4,128,256]{3,2,1,0:T(8,128)(2,1)S(1)} async-done(((bf16[4,4,128,256]{3,2,1,0:T(8,128)(2,1)}), bf16[4,4,128,256]{3,2,1,0:T(8,128)(2,1)S(1)}, u32[]{:S(2)}, u32[]{:S(2)}) %all-to-all-start.14) | async-done | bytes 1048608 | tf_op jit(solution)/shard_map/all_to_all | solution.py:82
  892.1 44.9 %all-to-all-done.15 = bf16[32,128,256]{2,1,0:T(8,128)(2,1)} async-done(((bf16[32,128,256]{2,1,0:T(8,128)(2,1)}), bf16[32,128,256]{2,1,0:T(8,128)(2,1)}, u32[]{:S(2)}, u32[]{:S(2)}) %all-to-all-start.15) | async-done | bytes 2097184 | tf_op jit(solution)/shard_map/all_to_all | solution.py:1249
  943.2 16.3 %rotate.1 = (bf16[1024,1024]{1,0:T(8,128)(2,1)}, bf16[1024,1024]{1,0:T(8,128)(2,1)}) custom-call(s32[1]{0:T(128)} %bitcast.59.where, bf16[4,1024,256]{2,1,0:T(8,128)(2,1)} %bitcast.69.grads, f32[6,1024,1024]{2,1,0:T(8,128)} %right.1, bf16[1024,1024]{1,0:T(8,128)(2,1)} %bitcast.35.left, bf16[1024,1024]{1,0:T(8,128)(2,1)} %bitcast.168, ...), custom_call_target="tpu_custom_call" | custom-call | flops 320000000 | tf_op jit(solution)/shard_map/rotate/pallas_call | solution.py:836
  974.7 39.1 %all-to-all-done.17 = bf16[8,128,1024]{2,1,0:T(8,128)(2,1)} async-done(((bf16[8,128,1024]{2,1,0:T(8,128)(2,1)}), bf16[8,128,1024]{2,1,0:T(8,128)(2,1)}, u32[]{:S(2)}, u32[]{:S(2)}) %all-to-all-start.17) | async-done | bytes 2097184 | tf_op jit(solution)/shard_map/all_to_all | solution.py:961
  1029.0 10.2 collective-permute-done.75
  1040.2 15.6 %collective-permute-done.76 = f32[2,12288]{1,0:T(2,128)S(1)} collective-permute-done((f32[2,12288]{1,0:T(2,128)S(1)}, f32[2,12288]{1,0:T(2,128)S(1)}, u32[]{:S(2)}, u32[]{:S(2)}) %collective-permute-start.76) | collective-permute-done | bytes 98336 | tf_op jit(solution)/shard_map/ppermute | solution.py:944
  1060.5 10.1 all-to-all-done.18
  1083.0 7.4 pick.1
  (544 shorter events, 387.0 us)
Async XLA Ops:
  7.5 43.3 %all-to-all-start = ((bf16[4,6,64,512]{3,2,1,0:T(8,128)(2,1)}), bf16[4,6,64,512]{3,2,1,0:T(8,128)(2,1)S(1)}, u32[]{:S(2)}, u32[]{:S(2)}) async-start(bf16[4,6,64,512]{3,2,1,0:T(8,128)(2,1)} %broadcast_in_dim.31), calls=%async_computation | async-start | bytes 3145728 | tf_op jit(solution)/shard_map/all_to_all | solution.py:82
  52.2 40.0 %all-to-all-start.1 = ((bf16[4,6,64,512]{3,2,1,0:T(8,128)(2,1)}), bf16[4,6,64,512]{3,2,1,0:T(8,128)(2,1)S(1)}, u32[]{:S(2)}, u32[]{:S(2)}) async-start(bf16[4,6,64,512]{3,2,1,0:T(8,128)(2,1)} %broadcast_in_dim.32), calls=%async_computation.1 | async-start | bytes 3145728 | tf_op jit(solution)/shard_map/all_to_all | solution.py:82
  55.8 35.5 %collective-permute-start = (bf16[4,6,64,512]{3,2,1,0:T(8,128)(2,1)S(1)}, bf16[4,6,64,512]{3,2,1,0:T(8,128)(2,1)}, u32[]{:S(2)}, u32[]{:S(2)}) collective-permute-start(bf16[4,6,64,512]{3,2,1,0:T(8,128)(2,1)S(1)} %all-to-all-done), channel_id=1, source_target_pairs={{1,0},{0,1},{3,2},{2,3},{5,4},{4,5},{7,6},{6,7},{9,8},{8,9},{11,10... | collective-permute-start | bytes 4718600 | tf_op jit(solution)/shard_map/ppermute | solution.py:69
  95.6 43.7 %collective-permute-start.2 = (bf16[2,4,6,64,512]{4,3,2,1,0:T(8,128)(2,1)S(1)}, bf16[2,4,6,64,512]{4,3,2,1,0:T(8,128)(2,1)}, u32[]{:S(2)}, u32[]{:S(2)}) collective-permute-start(bf16[2,4,6,64,512]{4,3,2,1,0:T(8,128)(2,1)S(1)} %pad_maximum_fusion.refs_0_.refs_2_), channel_id=1, source_target_pairs={{8,0},{0,8},{24,16},{16,24},{9,1},{1,9},{25,17},{17,25},{10,2},{2,... | collective-permute-start | bytes 9437192 | tf_op jit(solution)/shard_map/ppermute | solution.py:69
  97.8 41.5 %all-to-all-start.2 = ((bf16[4,6,64,512]{3,2,1,0:T(8,128)(2,1)}), bf16[4,6,64,512]{3,2,1,0:T(8,128)(2,1)}, u32[]{:S(2)}, u32[]{:S(2)}) async-start(bf16[4,6,64,512]{3,2,1,0:T(8,128)(2,1)} %broadcast_in_dim.33), calls=%async_computation.2 | async-start | bytes 3145728 | tf_op jit(solution)/shard_map/all_to_all | solution.py:82
  102.1 36.4 %collective-permute-start.3 = (bf16[4,6,64,512]{3,2,1,0:T(8,128)(2,1)}, bf16[4,6,64,512]{3,2,1,0:T(8,128)(2,1)}, u32[]{:S(2)}, u32[]{:S(2)}) collective-permute-start(bf16[4,6,64,512]{3,2,1,0:T(8,128)(2,1)} %copy-done.13), channel_id=1, source_target_pairs={{1,0},{0,1},{3,2},{2,3},{5,4},{4,5},{7,6},{6,7},{9,8},{8,9},{11,10... | collective-permute-start | bytes 4718600 | tf_op jit(solution)/shard_map/ppermute | solution.py:69
  141.6 58.9 %collective-permute-start.5 = (bf16[2,4,6,64,512]{4,3,2,1,0:T(8,128)(2,1)S(1)}, bf16[2,4,6,64,512]{4,3,2,1,0:T(8,128)(2,1)}, u32[]{:S(2)}, u32[]{:S(2)}) collective-permute-start(bf16[2,4,6,64,512]{4,3,2,1,0:T(8,128)(2,1)S(1)} %pad_maximum_fusion.1.refs_0_.refs_2_), channel_id=1, source_target_pairs={{8,0},{0,8},{24,16},{16,24},{9,1},{1,9},{25,17},{17,25},{10,2},{2,... | collective-permute-start | bytes 9437192 | tf_op jit(solution)/shard_map/ppermute | solution.py:69
  143.7 56.7 %all-to-all-start.3 = ((bf16[4,6,64,512]{3,2,1,0:T(8,128)(2,1)}), bf16[4,6,64,512]{3,2,1,0:T(8,128)(2,1)}, u32[]{:S(2)}, u32[]{:S(2)}) async-start(bf16[4,6,64,512]{3,2,1,0:T(8,128)(2,1)} %broadcast_in_dim.34), calls=%async_computation.3 | async-start | bytes 3145728 | tf_op jit(solution)/shard_map/all_to_all | solution.py:82
  148.2 37.1 %collective-permute-start.6 = (bf16[4,6,64,512]{3,2,1,0:T(8,128)(2,1)}, bf16[4,6,64,512]{3,2,1,0:T(8,128)(2,1)}, u32[]{:S(2)}, u32[]{:S(2)}) collective-permute-start(bf16[4,6,64,512]{3,2,1,0:T(8,128)(2,1)} %all-to-all-done.2), channel_id=1, source_target_pairs={{1,0},{0,1},{3,2},{2,3},{5,4},{4,5},{7,6},{6,7},{9,8},{8,9},{11,10... | collective-permute-start | bytes 4718600 | tf_op jit(solution)/shard_map/ppermute | solution.py:69
  163.2 37.2 %collective-permute-start.8 = (bf16[256,2048]{1,0:T(8,128)(2,1)}, bf16[256,2048]{1,0:T(8,128)(2,1)}, u32[]{:S(2)}, u32[]{:S(2)}) collective-permute-start(bf16[256,2048]{1,0:T(8,128)(2,1)} %get-tuple-element.437.refs_0_.refs_4_), channel_id=1, source_target_pairs={{16,0},{24,8},{0,16},{8,24},{17,1},{25,9},{1,17},{9,25},{18,2},{26... | collective-permute-start | bytes 3145736 | tf_op jit(solution)/shard_map/ppermute | solution.py:69
  163.8 36.7 %collective-permute-start.9 = (bf16[256,2048]{1,0:T(8,128)(2,1)}, bf16[256,2048]{1,0:T(8,128)(2,1)}, u32[]{:S(2)}, u32[]{:S(2)}) collective-permute-start(bf16[256,2048]{1,0:T(8,128)(2,1)} %get-tuple-element.437.refs_0_.refs_4_), channel_id=1, source_target_pairs={{8,0},{0,8},{24,16},{16,24},{9,1},{1,9},{25,17},{17,25},{10,2},{2,... | collective-permute-start | bytes 3145736 | tf_op jit(solution)/shard_map/ppermute | solution.py:69
  202.7 45.9 %collective-permute-start.11 = (bf16[2,4,6,64,512]{4,3,2,1,0:T(8,128)(2,1)S(1)}, bf16[2,4,6,64,512]{4,3,2,1,0:T(8,128)(2,1)}, u32[]{:S(2)}, u32[]{:S(2)}) collective-permute-start(bf16[2,4,6,64,512]{4,3,2,1,0:T(8,128)(2,1)S(1)} %pad_maximum_fusion.2.refs_0_.refs_2_), channel_id=1, source_target_pairs={{8,0},{0,8},{24,16},{16,24},{9,1},{1,9},{25,17},{17,25},{10,2},{2,... | collective-permute-start | bytes 9437192 | tf_op jit(solution)/shard_map/ppermute | solution.py:69
  204.9 43.7 %all-to-all-start.4 = ((bf16[4,6,64,512]{3,2,1,0:T(8,128)(2,1)}), bf16[4,6,64,512]{3,2,1,0:T(8,128)(2,1)}, u32[]{:S(2)}, u32[]{:S(2)}) async-start(bf16[4,6,64,512]{3,2,1,0:T(8,128)(2,1)} %broadcast_in_dim.36), calls=%async_computation.4 | async-start | bytes 3145728 | tf_op jit(solution)/shard_map/all_to_all | solution.py:82
  210.3 38.3 %collective-permute-start.12 = (bf16[4,6,64,512]{3,2,1,0:T(8,128)(2,1)}, bf16[4,6,64,512]{3,2,1,0:T(8,128)(2,1)}, u32[]{:S(2)}, u32[]{:S(2)}) collective-permute-start(bf16[4,6,64,512]{3,2,1,0:T(8,128)(2,1)} %all-to-all-done.3), channel_id=1, source_target_pairs={{1,0},{0,1},{3,2},{2,3},{5,4},{4,5},{7,6},{6,7},{9,8},{8,9},{11,10... | collective-permute-start | bytes 4718600 | tf_op jit(solution)/shard_map/ppermute | solution.py:69
  213.9 34.7 %collective-permute-start.10 = (bf16[2,4,2,64,512]{4,3,2,1,0:T(8,128)(2,1)S(1)}, bf16[2,4,2,64,512]{4,3,2,1,0:T(8,128)(2,1)}, u32[]{:S(2)}, u32[]{:S(2)}) collective-permute-start(bf16[2,4,2,64,512]{4,3,2,1,0:T(8,128)(2,1)S(1)} %fusion.6), channel_id=1, source_target_pairs={{16,0},{24,8},{0,16},{8,24},{17,1},{25,9},{1,17},{9,25},{18,2},{26... | collective-permute-start | bytes 3145736 | tf_op jit(solution)/shard_map/ppermute | solution.py:69
  250.8 44.4 %collective-permute-start.16 = (bf16[2,4,6,64,512]{4,3,2,1,0:T(8,128)(2,1)S(1)}, bf16[2,4,6,64,512]{4,3,2,1,0:T(8,128)(2,1)}, u32[]{:S(2)}, u32[]{:S(2)}) collective-permute-start(bf16[2,4,6,64,512]{4,3,2,1,0:T(8,128)(2,1)S(1)} %pad_maximum_fusion.3.refs_0_.refs_2_), channel_id=1, source_target_pairs={{8,0},{0,8},{24,16},{16,24},{9,1},{1,9},{25,17},{17,25},{10,2},{2,... | collective-permute-start | bytes 9437192 | tf_op jit(solution)/shard_map/ppermute | solution.py:69
  253.0 42.2 %all-to-all-start.5 = ((bf16[4,6,64,512]{3,2,1,0:T(8,128)(2,1)}), bf16[4,6,64,512]{3,2,1,0:T(8,128)(2,1)}, u32[]{:S(2)}, u32[]{:S(2)}) async-start(bf16[4,6,64,512]{3,2,1,0:T(8,128)(2,1)} %broadcast_in_dim.39), calls=%async_computation.5 | async-start | bytes 3145728 | tf_op jit(solution)/shard_map/all_to_all | solution.py:82
  258.3 36.1 %collective-permute-start.17 = (bf16[4,6,64,512]{3,2,1,0:T(8,128)(2,1)}, bf16[4,6,64,512]{3,2,1,0:T(8,128)(2,1)}, u32[]{:S(2)}, u32[]{:S(2)}) collective-permute-start(bf16[4,6,64,512]{3,2,1,0:T(8,128)(2,1)} %all-to-all-done.4), channel_id=1, source_target_pairs={{1,0},{0,1},{3,2},{2,3},{5,4},{4,5},{7,6},{6,7},{9,8},{8,9},{11,10... | collective-permute-start | bytes 4718600 | tf_op jit(solution)/shard_map/ppermute | solution.py:69
  297.4 52.5 %collective-permute-start.20 = (bf16[2,4,6,64,512]{4,3,2,1,0:T(8,128)(2,1)S(1)}, bf16[2,4,6,64,512]{4,3,2,1,0:T(8,128)(2,1)S(1)}, u32[]{:S(2)}, u32[]{:S(2)}) collective-permute-start(bf16[2,4,6,64,512]{4,3,2,1,0:T(8,128)(2,1)S(1)} %pad_maximum_fusion.4.refs_0_.refs_2_), channel_id=1, source_target_pairs={{8,0},{0,8},{24,16},{16,24},{9,1},{1,9},{25,17},{17,25},{10,2},{2,... | collective-permute-start | bytes 9437192 | tf_op jit(solution)/shard_map/ppermute | solution.py:69
  298.0 36.6 %collective-permute-start.21 = (bf16[4,6,64,512]{3,2,1,0:T(8,128)(2,1)}, bf16[4,6,64,512]{3,2,1,0:T(8,128)(2,1)S(1)}, u32[]{:S(2)}, u32[]{:S(2)}) collective-permute-start(bf16[4,6,64,512]{3,2,1,0:T(8,128)(2,1)} %all-to-all-done.5), channel_id=1, source_target_pairs={{1,0},{0,1},{3,2},{2,3},{5,4},{4,5},{7,6},{6,7},{9,8},{8,9},{11,10... | collective-permute-start | bytes 4718600 | tf_op jit(solution)/shard_map/ppermute | solution.py:69
  302.4 26.4 %collective-permute-start.19 = (bf16[2,4,2,64,512]{4,3,2,1,0:T(8,128)(2,1)}, bf16[2,4,2,64,512]{4,3,2,1,0:T(8,128)(2,1)}, u32[]{:S(2)}, u32[]{:S(2)}) collective-permute-start(bf16[2,4,2,64,512]{4,3,2,1,0:T(8,128)(2,1)} %fusion.4), channel_id=1, source_target_pairs={{16,0},{24,8},{0,16},{8,24},{17,1},{25,9},{1,17},{9,25},{18,2},{26... | collective-permute-start | bytes 3145736 | tf_op jit(solution)/shard_map/ppermute | solution.py:69
  313.7 36.2 %collective-permute-start.23 = (bf16[256,2048]{1,0:T(8,128)(2,1)}, bf16[256,2048]{1,0:T(8,128)(2,1)S(1)}, u32[]{:S(2)}, u32[]{:S(2)}) collective-permute-start(bf16[256,2048]{1,0:T(8,128)(2,1)} %get-tuple-element.470.refs_0_.refs_4_), channel_id=1, source_target_pairs={{16,0},{24,8},{0,16},{8,24},{17,1},{25,9},{1,17},{9,25},{18,2},{26... | collective-permute-start | bytes 3145736 | tf_op jit(solution)/shard_map/ppermute | solution.py:69
  314.3 35.6 %collective-permute-start.24 = (bf16[256,2048]{1,0:T(8,128)(2,1)}, bf16[256,2048]{1,0:T(8,128)(2,1)S(1)}, u32[]{:S(2)}, u32[]{:S(2)}) collective-permute-start(bf16[256,2048]{1,0:T(8,128)(2,1)} %get-tuple-element.470.refs_0_.refs_4_), channel_id=1, source_target_pairs={{8,0},{0,8},{24,16},{16,24},{9,1},{1,9},{25,17},{17,25},{10,2},{2,... | collective-permute-start | bytes 3145736 | tf_op jit(solution)/shard_map/ppermute | solution.py:69
  354.6 43.9 %collective-permute-start.26 = (bf16[2,4,6,64,512]{4,3,2,1,0:T(8,128)(2,1)S(1)}, bf16[2,4,6,64,512]{4,3,2,1,0:T(8,128)(2,1)}, u32[]{:S(2)}, u32[]{:S(2)}) collective-permute-start(bf16[2,4,6,64,512]{4,3,2,1,0:T(8,128)(2,1)S(1)} %pad_maximum_fusion.5.refs_0_.refs_2_), channel_id=1, source_target_pairs={{8,0},{0,8},{24,16},{16,24},{9,1},{1,9},{25,17},{17,25},{10,2},{2,... | collective-permute-start | bytes 9437192 | tf_op jit(solution)/shard_map/ppermute | solution.py:69
  357.8 73.8 %all-to-all-start.6 = ((bf16[8,128,1024]{2,1,0:T(8,128)(2,1)}), bf16[8,128,1024]{2,1,0:T(8,128)(2,1)}, u32[]{:S(2)}, u32[]{:S(2)}) async-start(bf16[8,128,1024]{2,1,0:T(8,128)(2,1)} %pad.10), calls=%async_computation.6 | async-start | bytes 4194304 | tf_op jit(solution)/shard_map/all_to_all | solution.py:956
  365.1 33.4 %collective-permute-start.25 = (bf16[2,4,2,64,512]{4,3,2,1,0:T(8,128)(2,1)}, bf16[2,4,2,64,512]{4,3,2,1,0:T(8,128)(2,1)S(1)}, u32[]{:S(2)}, u32[]{:S(2)}) collective-permute-start(bf16[2,4,2,64,512]{4,3,2,1,0:T(8,128)(2,1)} %fusion.3), channel_id=1, source_target_pairs={{16,0},{24,8},{0,16},{8,24},{17,1},{25,9},{1,17},{9,25},{18,2},{26... | collective-permute-start | bytes 3145736 | tf_op jit(solution)/shard_map/ppermute | solution.py:69
  366.2 65.4 %collective-permute-start.33 = (bf16[256,4096]{1,0:T(8,128)(2,1)}, bf16[256,4096]{1,0:T(8,128)(2,1)}, u32[]{:S(2)}, u32[]{:S(2)}) collective-permute-start(bf16[256,4096]{1,0:T(8,128)(2,1)} %get-tuple-element.450.act.refs_0_), channel_id=1, source_target_pairs={{8,0},{0,8},{24,16},{16,24},{9,1},{1,9},{25,17},{17,25},{10,2},{2,... | collective-permute-start | bytes 6291464 | tf_op jit(solution)/shard_map/ppermute | solution.py:69
  400.3 31.3 %collective-permute-start.32 = (bf16[256,3072]{1,0:T(8,128)(2,1)}, bf16[256,3072]{1,0:T(8,128)(2,1)S(1)}, u32[]{:S(2)}, u32[]{:S(2)}) collective-permute-start(bf16[256,3072]{1,0:T(8,128)(2,1)} %pad_maximum_fusion.6), channel_id=1, source_target_pairs={{8,0},{0,8},{24,16},{16,24},{9,1},{1,9},{25,17},{17,25},{10,2},{2,... | collective-permute-start | bytes 4718600 | tf_op jit(solution)/shard_map/ppermute | solution.py:69
  402.1 29.6 %collective-permute-start.34 = (bf16[256,3072]{1,0:T(8,128)(2,1)}, bf16[256,3072]{1,0:T(8,128)(2,1)S(1)}, u32[]{:S(2)}, u32[]{:S(2)}) collective-permute-start(bf16[256,3072]{1,0:T(8,128)(2,1)} %pad_maximum_fusion.7), channel_id=1, source_target_pairs={{8,0},{0,8},{24,16},{16,24},{9,1},{1,9},{25,17},{17,25},{10,2},{2,... | collective-permute-start | bytes 4718600 | tf_op jit(solution)/shard_map/ppermute | solution.py:69
  436.5 70.5 %all-to-all-start.7 = ((bf16[8,128,1024]{2,1,0:T(8,128)(2,1)}), bf16[8,128,1024]{2,1,0:T(8,128)(2,1)S(1)}, u32[]{:S(2)}, u32[]{:S(2)}) async-start(bf16[8,128,1024]{2,1,0:T(8,128)(2,1)} %pad.11), calls=%async_computation.7 | async-start | bytes 4194304 | tf_op jit(solution)/shard_map/all_to_all | solution.py:956
  444.2 46.2 %collective-permute-start.36 = (bf16[2,4,2,128,256]{4,3,2,1,0:T(8,128)(2,1)}, bf16[2,4,2,128,256]{4,3,2,1,0:T(8,128)(2,1)S(1)}, u32[]{:S(2)}, u32[]{:S(2)}) collective-permute-start(bf16[2,4,2,128,256]{4,3,2,1,0:T(8,128)(2,1)} %get-tuple-element.495), channel_id=1, source_target_pairs={{1,0},{0,1},{3,2},{2,3},{5,4},{4,5},{7,6},{6,7},{9,8},{8,9},{11,10... | collective-permute-start | bytes 3145736 | tf_op jit(solution)/shard_map/ppermute | solution.py:69
  510.8 29.9 %all-to-all-start.8 = ((bf16[4,4,128,256]{3,2,1,0:T(8,128)(2,1)}), bf16[4,4,128,256]{3,2,1,0:T(8,128)(2,1)}, u32[]{:S(2)}, u32[]{:S(2)}) async-start(bf16[4,4,128,256]{3,2,1,0:T(8,128)(2,1)} %pad_maximum_fusion.8), calls=%async_computation.8 | async-start | bytes 2097152 | tf_op jit(solution)/shard_map/all_to_all | solution.py:82
  542.5 51.7 %all-to-all-start.9 = ((bf16[8,128,1024]{2,1,0:T(8,128)(2,1)}), bf16[8,128,1024]{2,1,0:T(8,128)(2,1)S(1)}, u32[]{:S(2)}, u32[]{:S(2)}) async-start(bf16[8,128,1024]{2,1,0:T(8,128)(2,1)} %pad.12), calls=%async_computation.9 | async-start | bytes 4194304 | tf_op jit(solution)/shard_map/all_to_all | solution.py:956
  555.9 32.2 %collective-permute-start.45 = (bf16[2,256,1024]{2,1,0:T(8,128)(2,1)S(1)}, bf16[2,256,1024]{2,1,0:T(8,128)(2,1)}, u32[]{:S(2)}, u32[]{:S(2)}) collective-permute-start(bf16[2,256,1024]{2,1,0:T(8,128)(2,1)S(1)} %get-tuple-element.817), channel_id=1, source_target_pairs={{16,0},{24,8},{0,16},{8,24},{17,1},{25,9},{1,17},{9,25},{18,2},{26... | collective-permute-start | bytes 3145736 | tf_op jit(solution)/shard_map/ppermute | solution.py:69
  631.1 30.3 %all-to-all-start.10 = ((bf16[4,4,128,256]{3,2,1,0:T(8,128)(2,1)}), bf16[4,4,128,256]{3,2,1,0:T(8,128)(2,1)S(1)}, u32[]{:S(2)}, u32[]{:S(2)}) async-start(bf16[4,4,128,256]{3,2,1,0:T(8,128)(2,1)} %pad_maximum_fusion.9), calls=%async_computation.10 | async-start | bytes 2097152 | tf_op jit(solution)/shard_map/all_to_all | solution.py:82
  664.5 36.5 %collective-permute-start.53 = (bf16[2,4,2,128,256]{4,3,2,1,0:T(8,128)(2,1)}, bf16[2,4,2,128,256]{4,3,2,1,0:T(8,128)(2,1)S(1)}, u32[]{:S(2)}, u32[]{:S(2)}) collective-permute-start(bf16[2,4,2,128,256]{4,3,2,1,0:T(8,128)(2,1)} %get-tuple-element.660), channel_id=1, source_target_pairs={{16,0},{24,8},{0,16},{8,24},{17,1},{25,9},{1,17},{9,25},{18,2},{26... | collective-permute-start | bytes 3145736 | tf_op jit(solution)/shard_map/ppermute | solution.py:69
  665.5 35.5 %collective-permute-start.54 = (bf16[2,4,2,128,256]{4,3,2,1,0:T(8,128)(2,1)}, bf16[2,4,2,128,256]{4,3,2,1,0:T(8,128)(2,1)S(1)}, u32[]{:S(2)}, u32[]{:S(2)}) collective-permute-start(bf16[2,4,2,128,256]{4,3,2,1,0:T(8,128)(2,1)} %get-tuple-element.661), channel_id=1, source_target_pairs={{1,0},{0,1},{3,2},{2,3},{5,4},{4,5},{7,6},{6,7},{9,8},{8,9},{11,10... | collective-permute-start | bytes 3145736 | tf_op jit(solution)/shard_map/ppermute | solution.py:69
  667.3 33.7 %collective-permute-start.51 = (bf16[4,2,128,256]{3,2,1,0:T(8,128)(2,1)S(1)}, bf16[4,2,128,256]{3,2,1,0:T(8,128)(2,1)S(1)}, u32[]{:S(2)}, u32[]{:S(2)}) collective-permute-start(bf16[4,2,128,256]{3,2,1,0:T(8,128)(2,1)S(1)} %get-tuple-element.835), channel_id=1, source_target_pairs={{1,0},{0,1},{3,2},{2,3},{5,4},{4,5},{7,6},{6,7},{9,8},{8,9},{11,10... | collective-permute-start | bytes 1572872 | tf_op jit(solution)/shard_map/ppermute | solution.py:69
  706.7 30.2 %all-to-all-start.11 = ((bf16[4,4,128,256]{3,2,1,0:T(8,128)(2,1)}), bf16[4,4,128,256]{3,2,1,0:T(8,128)(2,1)S(1)}, u32[]{:S(2)}, u32[]{:S(2)}) async-start(bf16[4,4,128,256]{3,2,1,0:T(8,128)(2,1)} %pad_maximum_fusion.10), calls=%async_computation.11 | async-start | bytes 2097152 | tf_op jit(solution)/shard_map/all_to_all | solution.py:82
  718.9 31.1 %collective-permute-start.59 = (bf16[2,256,1024]{2,1,0:T(8,128)(2,1)}, bf16[2,256,1024]{2,1,0:T(8,128)(2,1)}, u32[]{:S(2)}, u32[]{:S(2)}) collective-permute-start(bf16[2,256,1024]{2,1,0:T(8,128)(2,1)} %get-tuple-element.815), channel_id=1, source_target_pairs={{16,0},{24,8},{0,16},{8,24},{17,1},{25,9},{1,17},{9,25},{18,2},{26... | collective-permute-start | bytes 3145736 | tf_op jit(solution)/shard_map/ppermute | solution.py:69
  753.7 29.5 %all-to-all-start.12 = ((bf16[4,4,128,256]{3,2,1,0:T(8,128)(2,1)}), bf16[4,4,128,256]{3,2,1,0:T(8,128)(2,1)S(1)}, u32[]{:S(2)}, u32[]{:S(2)}) async-start(bf16[4,4,128,256]{3,2,1,0:T(8,128)(2,1)} %pad_maximum_fusion.11), calls=%async_computation.12 | async-start | bytes 2097152 | tf_op jit(solution)/shard_map/all_to_all | solution.py:82
  802.0 29.7 %all-to-all-start.13 = ((bf16[4,4,128,256]{3,2,1,0:T(8,128)(2,1)}), bf16[4,4,128,256]{3,2,1,0:T(8,128)(2,1)S(1)}, u32[]{:S(2)}, u32[]{:S(2)}) async-start(bf16[4,4,128,256]{3,2,1,0:T(8,128)(2,1)} %pad_maximum_fusion.12), calls=%async_computation.13 | async-start | bytes 2097152 | tf_op jit(solution)/shard_map/all_to_all | solution.py:82
  849.1 27.3 %all-to-all-start.14 = ((bf16[4,4,128,256]{3,2,1,0:T(8,128)(2,1)}), bf16[4,4,128,256]{3,2,1,0:T(8,128)(2,1)S(1)}, u32[]{:S(2)}, u32[]{:S(2)}) async-start(bf16[4,4,128,256]{3,2,1,0:T(8,128)(2,1)} %pad_maximum_fusion.13), calls=%async_computation.14 | async-start | bytes 2097152 | tf_op jit(solution)/shard_map/all_to_all | solution.py:82
  883.3 53.7 %all-to-all-start.15 = ((bf16[32,128,256]{2,1,0:T(8,128)(2,1)}), bf16[32,128,256]{2,1,0:T(8,128)(2,1)}, u32[]{:S(2)}, u32[]{:S(2)}) async-start(bf16[32,128,256]{2,1,0:T(8,128)(2,1)} %bitcast.163), calls=%async_computation.15 | async-start | bytes 4194304 | tf_op jit(solution)/shard_map/all_to_all | solution.py:1249
  960.9 52.9 %all-to-all-start.17 = ((bf16[8,128,1024]{2,1,0:T(8,128)(2,1)}), bf16[8,128,1024]{2,1,0:T(8,128)(2,1)}, u32[]{:S(2)}, u32[]{:S(2)}) async-start(bf16[8,128,1024]{2,1,0:T(8,128)(2,1)} %bitcast.179), calls=%async_computation.17 | async-start | bytes 4194304 | tf_op jit(solution)/shard_map/all_to_all | solution.py:961
  967.7 58.0 %collective-permute-start.74 = (f32[2,12288]{1,0:T(2,128)}, f32[2,12288]{1,0:T(2,128)}, u32[]{:S(2)}, u32[]{:S(2)}) collective-permute-start(f32[2,12288]{1,0:T(2,128)} %fusion.24), channel_id=1, source_target_pairs={{16,0},{24,8},{0,16},{8,24},{17,1},{25,9},{1,17},{9,25},{18,2},{26... | collective-permute-start | bytes 294920 | tf_op jit(solution)/shard_map/ppermute | solution.py:69
  1015.3 55.3 %all-to-all-start.18 = ((bf16[8,128,1024]{2,1,0:T(8,128)(2,1)}), bf16[8,128,1024]{2,1,0:T(8,128)(2,1)}, u32[]{:S(2)}, u32[]{:S(2)}) async-start(bf16[8,128,1024]{2,1,0:T(8,128)(2,1)} %bitcast.178), calls=%async_computation.18 | async-start | bytes 4194304 | tf_op jit(solution)/shard_map/all_to_all | solution.py:961
  1024.6 47.6 %collective-permute-start.70 = (bf16[6,128,1024]{2,1,0:T(8,128)(2,1)}, bf16[6,128,1024]{2,1,0:T(8,128)(2,1)}, u32[]{:S(2)}, u32[]{:S(2)}) collective-permute-start(bf16[6,128,1024]{2,1,0:T(8,128)(2,1)} %get-tuple-element.798.refs_0_), channel_id=1, source_target_pairs={{16,0},{24,8},{0,16},{8,24},{17,1},{25,9},{1,17},{9,25},{18,2},{26... | collective-permute-start | bytes 4718600 | tf_op jit(solution)/shard_map/ppermute | solution.py:69
  (146 other events, 2085.8 us)

commit v4 on v3

--- a/solution.py
+++ b/solution.py
@@ -114,12 +114,12 @@
 
 
 class Gathering:
-    def __init__(self, place, shard):
+    def __init__(self, place, shard, split_count):
         self.place = place
         self.count, self.rows, _ = shard.shape
         half_rows, half_cols = self.rows // 2, BLK // 2
         has_y = place.size["y"] == 2
-        self.split_count = self.count // 2 if has_y else 0
+        self.split_count = split_count if has_y else 0
         whole_count = self.count - self.split_count
         mine = lax.dynamic_slice_in_dim(shard, place.at["core"] * half_rows, half_rows, 1)
         whole = mine[self.split_count :]
@@ -128,13 +128,17 @@
             for block in range(whole_count)
             for part in (whole[block, :, :half_cols], whole[block, :, half_cols:])
         ]
-        piece = jnp.stack(pieces)
+        parts = []
+        if pieces:
+            parts.append(jnp.stack(pieces))
         if has_y:
-            parts = lax.dynamic_slice_in_dim(
-                mine[: self.split_count], place.at["y"] * half_cols, half_cols, 2
+            parts.insert(
+                0,
+                lax.dynamic_slice_in_dim(
+                    mine[: self.split_count], place.at["y"] * half_cols, half_cols, 2
+                ),
             )
-            piece = jnp.concatenate([parts, piece])
-        self.held = [piece]
+        self.held = [jnp.concatenate(parts)]
         self.crossed = []
 
     def step_z(self):
@@ -163,8 +167,9 @@
         def spec(place_of):
             return pl.BlockSpec(part, lambda i, where: (0, 0, place_of(i), 0, 0))
 
+        last = mine[0].shape[2] - 1
         low = spec(lambda i: jnp.where(i < split, i, 2 * i - split))
-        high = spec(lambda i: jnp.where(i < split, split + 1, 2 * i - split + 1))
+        high = spec(lambda i: jnp.minimum(jnp.where(i < split, split + 1, 2 * i - split + 1), last))
         operands = [mine[0], crossed[0], mine[0], crossed[0]]
         specs = [low, low, high, high]
         if split:
@@ -931,18 +936,29 @@
     return total.reshape(rows, -1, width).transpose(1, 0, 2)
 
 
-def sum_everywhere(place, value):
-    if place.size["y"] != 2 or place.size["x"] != 2:
-        return lax.psum(value, ("ctx", "wsh"))
-    for axis in ("core", "y", "x"):
-        value = value + place.take(value, axis, 1)
-    pairs = place.size["x"]
-    for bit in (1, 2):
-        swap = [
-            (z * pairs + x, (z ^ bit) * pairs + x) for z in range(DEPTH_Z) for x in range(pairs)
-        ]
-        value = value + lax.ppermute(value, "wsh", swap)
-    return value
+class EverySum:
+    def __init__(self, place, value):
+        self.place = place
+        self.terms = [value]
+        self.plain = place.size["y"] != 2 or place.size["x"] != 2
+
+    def step(self, axis, bit=0):
+        if self.plain:
+            return
+        value = sum(self.terms)
+        if axis == "z":
+            pairs = self.place.size["x"]
+            swap = [
+                (z * pairs + x, (z ^ bit) * pairs + x) for z in range(DEPTH_Z) for x in range(pairs)
+            ]
+            self.terms = [value, lax.ppermute(value, "wsh", swap)]
+        else:
+            self.terms = [value, self.place.take(value, axis, 1)]
+
+    def total(self):
+        if self.plain:
+            return lax.psum(self.terms[0], ("ctx", "wsh"))
+        return sum(self.terms)
 
 
 def doc_ids(lengths, position):
@@ -995,9 +1011,15 @@
     mask = jnp.where(doc_keys[:, None] == doc_keys[None, :tokens], 0.0, -1e30).astype(F32)
 
     chunks = [
-        Gathering(place, weights[layer_at, first : first + 4])
-        for layer_at in range(LAYERS)
-        for first in range(0, NBLK, 4)
+        Gathering(place, weights[layer_at, first : first + 4], split_count)
+        for layer_at, first, split_count in (
+            (0, 0, 2),
+            (0, 4, 2),
+            (0, 8, 2),
+            (1, 0, 2),
+            (1, 4, 2),
+            (1, 8, 4),
+        )
     ]
 
     live = {}
@@ -1053,16 +1075,19 @@
     summed_two_0, live["result"], live["result_low"], w_down_0 = down_step(
         act_0, finish(2), middle_0, vec_params[0]
     )
+    live["left"] = left_bases
     settle()
     chunks[4].step_y()
     chunks[5].step_x()
     result_0, result_low_0 = live["result"], live["result_low"]
     query_1, live["keyvals1"], w_in_1 = project_step(place, result_low_0, finish(3), vec_params[1])
     live["query"] = query_1
-    live["own"] = left_bases
+    live["left"] = to_owner(live["left"], wsh_count)
+    live["first"] = moment1
     settle()
     chunks[5].step_y()
-    left_own = to_owner(live.pop("own"), wsh_count)
+    live["first"] = to_owner(live["first"], wsh_count)
+    live["second"] = moment2
     keyvals_1 = keyvals_of(1)
     query_1 = live["query"]
     attn_1, summed_one_1, middle_1, mid_low_1 = mix_step(
@@ -1091,13 +1116,22 @@
         (vec_params[layer_at][None, 4 * D : 5 * D], vec_params[layer_at][None, 6 * D : 7 * D])
         for layer_at in range(LAYERS)
     ]
-    live = {"crossed": crossed}
+    live = {
+        "crossed": crossed,
+        "left": live["left"],
+        "first": live["first"],
+        "second": to_owner(live["second"], wsh_count),
+    }
     jobs = []
     vec_terms = [None] * LAYERS
 
+    every = []
+
     def settle_back():
         state = [(job.parts, job.by_y, job.by_x, job.groups) for job in jobs]
-        state, values = together(state, dict(live))
+        state, values, terms = together(state, dict(live), [one.terms for one in every])
+        for one, value in zip(every, terms):
+            one.terms = value
         for job, fields in zip(jobs, state):
             job.parts, job.by_y, job.by_x, job.groups = fields
         live.update(values)
@@ -1168,37 +1202,30 @@
 
     close_step(1, cotangent[0])
     down_1 = down_job(1)
-    live["left"] = left_own
-    live["first"] = moment1
+    feed_step(1)
     settle_back()
     down_1.first_y()
     down_1.first_x()
-    background = to_owner(live["first"], wsh_count)
-    feed_step(1)
+    up_1 = up_job(1)
     settle_back()
     down_1.second_x()
     down_1.second_y()
-    up_1 = up_job(1)
-    live["first"] = background
-    settle_back()
-    down_1.third()
     up_1.first_y()
     up_1.first_x()
     attend_step(1)
-    live["second"] = moment2
     settle_back()
     send_step()
+    down_1.third()
     up_1.second_x()
+    settle_back()
     up_1.second_y()
-    live["second"] = to_owner(live["second"], wsh_count)
-    settle_back()
     grad_flow = input_step(1)
     close_step(0, grad_flow)
     settle_back()
+    up_1.third()
     in_1 = in_job(1)
     down_0 = down_job(0)
     settle_back()
-    up_1.third()
     in_1.first_y()
     in_1.first_x()
     feed_step(0)
@@ -1219,21 +1246,28 @@
     up_0.first_y()
     up_0.first_x()
     grad_flow = input_step(0)
+    every.append(EverySum(place, jnp.stack(vec_terms)))
     settle_back()
+    every[0].step("core")
     up_0.second_x()
     up_0.second_y()
     in_0 = in_job(0)
     settle_back()
     up_0.third()
+    every[0].step("y")
     in_0.first_y()
     in_0.first_x()
     settle_back()
+    every[0].step("x")
     in_0.second_x()
     in_0.second_y()
     settle_back()
+    every[0].step("z", 1)
     in_0.third()
+    settle_back()
+    every[0].step("z", 2)
     stream_grad = grad_flow[None]
-    vec_grads = sum_everywhere(place, jnp.stack(vec_terms)) * scaling
+    vec_grads = every[0].total() * scaling
     groups = [group for job in jobs for group in job.groups]
     ids = [block for job in jobs for block in job.ids]
 
@@ -1249,33 +1283,52 @@
     arrived = lax.all_to_all(
         by_slot.reshape(ctx_count * wsh_count, rows_dev, width), ("ctx", "wsh"), 0, 0, tiled=True
     )
+    quarter_parts = []
+    for step in range(ctx_count):
+        step_y, step_core = step // CORES, step % CORES
+        to_ctx = ((place.at["y"] + step_y) % count_y) * CORES + (place.at["core"] + step_core) % CORES
+        part = lax.dynamic_index_in_dim(by_slot, to_ctx, 0, False)[:slots_dev]
+        pairs = [
+            (y * CORES + core, ((y + step_y) % count_y) * CORES + (core + step_core) % CORES)
+            for y in range(count_y)
+            for core in range(CORES)
+        ]
+        quarter_parts.append(lax.ppermute(part, "ctx", pairs) if step else part)
+    arrived, quarter_parts = together(arrived, quarter_parts)
     quarters = [(source % CORES) * count_y + source // CORES for source in range(ctx_count)]
     slot_own = jnp.minimum(lax.axis_index("wsh"), slots_dev - 1).reshape(1)
     rotated_own, update_own = rotate(
         arrived.reshape(ctx_count, BLK, width), quarters, right_bases, slot_own, live["left"], live["first"], live["second"]
     )
 
-    by_rows = after(by_slot[:, :slots_dev], arrived)
-    by_rows = lax.all_to_all(by_rows, "ctx", 0, 0, tiled=True)
-    update_own, rotated_own, by_rows = together(update_own, rotated_own, by_rows)
+    by_rows = jnp.stack(quarter_parts)
+    by_source = [
+        lax.dynamic_index_in_dim(
+            by_rows,
+            ((place.at["y"] - source // CORES) % count_y) * CORES + (place.at["core"] - source % CORES) % CORES,
+            0,
+            False,
+        )
+        for source in range(ctx_count)
+    ]
+    by_source = jnp.stack([by_source[quarters.index(quarter)] for quarter in range(ctx_count)])
+    block_grads = by_source.transpose(1, 2, 0, 3).reshape(slots_dev, rows_dev, BLK).astype(F32)
     update = from_owner(update_own, wsh_count, slots_dev)
-    by_rows = by_rows.reshape(count_y, CORES, slots_dev, rows_dev, width)
-    block_grads = by_rows.transpose(2, 3, 1, 0, 4).reshape(slots_dev, rows_dev, BLK).astype(F32)
-    update, rotated_own, block_grads = together(update, rotated_own, block_grads)
-    update = update.astype(F32)
-
-    new_master = master - LR_BLOCK * update
-    master_low = new_master.astype(BF16)
+    update, block_grads, vec_grads = together(update, block_grads, vec_grads)
+    master_low = (master - LR_BLOCK * update.astype(F32)).astype(BF16)
+    master_low, update, rotated_own = together(master_low, update, rotated_own)
     parts = gather_list(place, master_low, "y")
     rotated = from_owner(rotated_own, wsh_count, slots_dev)
-    parts, rotated = together(parts, rotated)
-    rotated = rotated.astype(F32)
-    parts = parts + [place.take(value, "core", 1) for value in parts]
+    across = place.take(master_low, "core", 1)
+    new_master = master - LR_BLOCK * update.astype(F32)
+    parts = parts + [across] + [place.take(value, "core", 1) for value in parts[1:]]
     owner_ctx, owner_at = owner_flat // slots_dev, owner_flat % slots_dev
     step_y = (owner_ctx // CORES - place.at["y"]) % count_y
     step_core = (owner_ctx % CORES - place.at["core"]) % CORES
     table = jnp.stack([step_core * count_y + step_y, owner_at]).astype(jnp.int32)
     new_weights = pick(parts, table).reshape(LAYERS, NBLK, rows_dev, BLK)
+    new_weights, new_master, rotated = together(new_weights, new_master, rotated)
+    rotated = rotated.astype(F32)
 
     new_moment1 = DECAY_RATE * moment1 + (1.0 - DECAY_RATE) * rotated
     new_moment2 = DECAY_RATE * moment2 + (1.0 - DECAY_RATE) * rotated * rotated

time: 1100 us -> 1080 us (0.982)
  waiting for transfers between devices: 504 us -> 476 us
  local copies, waits for them, and re-layouts: 78.7 us -> 92.1 us
    ppermute x2 -> x5, waiting for transfers between devices: 15.6 us -> 101 us  [the longest x2 62.3 us: step(): self.terms = [value, lax.ppermute(value, 'wsh', swap)]]
    all_to_all x2, waiting for transfers between devices: 49.2 us -> 6.24 us  [from_owner(): return lax.all_to_all(cut, 'wsh', 0, 0, tiled=True)[:slots]]
    all_to_all x1, waiting for transfers between devices: 44.9 us -> 8.72 us  [on_device(): lax.all_to_all(by_slot.reshape(ctx_count * wsh_count, rows_dev, width), (...]
    all_to_all x12, waiting for transfers between devices: 59 us -> 37.3 us  [swap_z(): lax.all_to_all(values, 'wsh', 0, 0, tiled=True, axis_index_groups=lines)]
    unnamed x232 -> x222, local copies, waits for them, and re-layouts: 33.4 us -> 42.1 us
    another operation x12 -> x11, other arithmetic: 23.1 us -> 20.2 us  [step_y(): self.held = [jnp.stack(self.held)]]
  transfers between devices with their start and end apart: 97 -> 99, of which waited for: 54 -> 49; matrix products, arithmetic and copies ran while one was open for 8% -> 9% of each run, Pallas kernels for 22% -> 24%
where the time goes in v4:
time: 1080 us; the launch traced here: 1070 us
  waiting for transfers between devices  476 us (44%)
  Pallas kernels  273 us (25%)
  starting transfers between devices  146 us (14%)
  local copies, waits for them, and re-layouts  92.1 us (9%)
  other arithmetic  77.5 us (7%)
    ppermute x76, waiting for transfers between devices, take(): return lax.ppermute(value, name, pairs)  324 us
    ppermute x2, waiting for transfers between devices, step(): self.terms = [value, lax.ppermute(value, 'wsh', swap)]  62.3 us
    all_to_all x12, starting transfers between devices, swap_z(): lax.all_to_all(values, 'wsh', 0, 0, tiled=True, axis_index_groups=lines)  56 us
    ppermute x76, starting transfers between devices, take(): return lax.ppermute(value, name, pairs)  51.6 us
    pallas_call x6, Pallas kernels, partial_sums(): call(functools.partial(sum_kernel, counts[0] if len(sets) > 1 else None,...  47.1 us
    pallas_call x2, Pallas kernels, attend_back(): call(functools.partial(attend_back_kernel, count, count_y, tokens), (D //...  42.3 us
    unnamed x222, local copies, waits for them, and re-layouts  42.1 us
    ppermute x3, waiting for transfers between devices, on_device(): quarter_parts.append(lax.ppermute(part, 'ctx', pairs) if step else part)  38.4 us
  transfers between devices with their start and end apart: 99, of which 49 were waited for; matrix products, arithmetic and copies ran while one was open for 9% of the time, Pallas kernels for 24%

profile of v4, /device:TPU:0, one launch (start us, length us, event | category | flops | bytes accessed | tf_op | source)
XLA Modules:
  0.0 1067.6 jit_solution(4633144384192836475)
XLA Ops:
  35.2 15.6 %all-to-all-done = bf16[4,6,64,512]{3,2,1,0:T(8,128)(2,1)S(1)} async-done(((bf16[4,6,64,512]{3,2,1,0:T(8,128)(2,1)}), bf16[4,6,64,512]{3,2,1,0:T(8,128)(2,1)S(1)}, u32[]{:S(2)}, u32[]{:S(2)}) %all-to-all-start) | async-done | bytes 1572896 | tf_op jit(solution)/shard_map/all_to_all | solution.py:82
  57.3 34.0 %collective-permute-done = bf16[4,6,64,512]{3,2,1,0:T(8,128)(2,1)} collective-permute-done((bf16[4,6,64,512]{3,2,1,0:T(8,128)(2,1)S(1)}, bf16[4,6,64,512]{3,2,1,0:T(8,128)(2,1)}, u32[]{:S(2)}, u32[]{:S(2)}) %collective-permute-start) | collective-permute-done | bytes 1572896 | tf_op jit(solution)/shard_map/ppermute | solution.py:69
  106.6 23.1 %collective-permute-done.1.refs_4_ = bf16[2,4,2,64,512]{4,3,2,1,0:T(8,128)(2,1)} collective-permute-done((bf16[2,4,2,64,512]{4,3,2,1,0:T(8,128)(2,1)S(1)}, bf16[2,4,2,64,512]{4,3,2,1,0:T(8,128)(2,1)}, u32[]{:S(2)}, u32[]{:S(2)}) %collective-permute-start.1) | collective-permute-done | bytes 1048608 | tf_op jit(solution)/shard_map/ppermute | solution.py:69
  129.7 8.9 collective-permute-done.3
  154.2 9.1 project.2
  163.8 14.8 %collective-permute-done.4.refs_4_ = bf16[2,4,2,64,512]{4,3,2,1,0:T(8,128)(2,1)S(1)} collective-permute-done((bf16[2,4,2,64,512]{4,3,2,1,0:T(8,128)(2,1)S(1)}, bf16[2,4,2,64,512]{4,3,2,1,0:T(8,128)(2,1)S(1)}, u32[]{:S(2)}, u32[]{:S(2)}) %collective-permute-start.4) | collective-permute-done | bytes 1048608 | tf_op jit(solution)/shard_map/ppermute | solution.py:69
  185.3 15.1 %collective-permute-done.8.refs_1_.refs_5_ = bf16[256,2048]{1,0:T(8,128)(2,1)} collective-permute-done((bf16[256,2048]{1,0:T(8,128)(2,1)}, bf16[256,2048]{1,0:T(8,128)(2,1)}, u32[]{:S(2)}, u32[]{:S(2)}) %collective-permute-start.8) | collective-permute-done | bytes 1048608 | tf_op jit(solution)/shard_map/ppermute | solution.py:69
  217.7 14.3 %attend.2.attn.refs_4_ = bf16[256,1024]{1,0:T(8,128)(2,1)} custom-call(bf16[256,1024]{1,0:T(8,128)(2,1)} %get-tuple-element.454.query, f32[1024,256]{1,0:T(8,128)} %compare_select_fusion.mask, bf16[256,2048]{1,0:T(8,128)(2,1)} %get-tuple-element.455.refs_0_.refs_4_, bf16[256,2048]{1,0:T(8,128)(2,1)} %collective-permute-done.8.refs_1_.refs_5_, ...), custom_call_target="tpu_custom_call" | custom-call | flops 280000000 | tf_op jit(solution)/shard_map/attend/pallas_call | solution.py:336
  237.1 11.5 %up.2 = (f32[256,4096]{1,0:T(8,128)}, bf16[256,4096]{1,0:T(8,128)(2,1)}, bf16[4,1024,1024]{2,1,0:T(8,128)(2,1)}) custom-call(s32[3]{0:T(128)} %pad_add_fusion.1.where, bf16[256,1024]{1,0:T(8,128)(2,1)} %get-tuple-element.459.middle_low.refs_0_, f32[4,1,1024]{2,1,0:T(1,128)} %bitcast.189, bf16[2,4,6,64,512]{4,3,2,1,0:T(8,128)(2,1)} %copy-done.2, ...), custom_call_target="tpu_custom_call" | custom-call | flops 160000000 | tf_op jit(solution)/shard_map/up/pallas_call | solution.py:438
  262.9 11.2 %down.2 = (f32[256,1024]{1,0:T(8,128)}, f32[256,1024]{1,0:T(8,128)}, bf16[256,1024]{1,0:T(8,128)(2,1)}, bf16[4,1024,1024]{2,1,0:T(8,128)(2,1)}) custom-call(s32[3]{0:T(128)} %pad_add_fusion.1.where, bf16[256,4096]{1,0:T(8,128)(2,1)} %get-tuple-element.468.act.refs_0_, f32[256,1024]{1,0:T(8,128)} %get-tuple-element.469.middle, ...), custom_call_target="tpu_custom_call" | custom-call | flops 160000000 | tf_op jit(solution)/shard_map/down/pallas_call | solution.py:478
  274.1 12.0 %collective-permute-done.15.refs_4_ = bf16[2,4,2,64,512]{4,3,2,1,0:T(8,128)(2,1)} collective-permute-done((bf16[2,4,2,64,512]{4,3,2,1,0:T(8,128)(2,1)S(1)}, bf16[2,4,2,64,512]{4,3,2,1,0:T(8,128)(2,1)}, u32[]{:S(2)}, u32[]{:S(2)}) %collective-permute-start.15) | collective-permute-done | bytes 1048608 | tf_op jit(solution)/shard_map/ppermute | solution.py:69
  308.0 9.3 project.3
  318.3 12.0 %collective-permute-done.19.refs_4_ = bf16[2,4,2,64,512]{4,3,2,1,0:T(8,128)(2,1)} collective-permute-done((bf16[2,4,2,64,512]{4,3,2,1,0:T(8,128)(2,1)}, bf16[2,4,2,64,512]{4,3,2,1,0:T(8,128)(2,1)}, u32[]{:S(2)}, u32[]{:S(2)}) %collective-permute-start.19) | collective-permute-done | bytes 1048608 | tf_op jit(solution)/shard_map/ppermute | solution.py:69
  330.3 14.8 %collective-permute-done.21 = bf16[4,4,64,512]{3,2,1,0:T(8,128)(2,1)} collective-permute-done((bf16[4,4,64,512]{3,2,1,0:T(8,128)(2,1)}, bf16[4,4,64,512]{3,2,1,0:T(8,128)(2,1)}, u32[]{:S(2)}, u32[]{:S(2)}) %collective-permute-start.21) | collective-permute-done | bytes 1048608 | tf_op jit(solution)/shard_map/ppermute | solution.py:69
  368.0 14.3 %attend.3.attn.refs_4_ = bf16[256,1024]{1,0:T(8,128)(2,1)} custom-call(bf16[256,1024]{1,0:T(8,128)(2,1)} %get-tuple-element.488.query, f32[1024,256]{1,0:T(8,128)} %compare_select_fusion.mask, bf16[256,2048]{1,0:T(8,128)(2,1)} %get-tuple-element.489.refs_0_.refs_4_, bf16[256,2048]{1,0:T(8,128)(2,1)} %collective-permute-done.23.refs_1_.refs_5_, ...), custom_call_target="tpu_custom_call" | custom-call | flops 280000000 | tf_op jit(solution)/shard_map/attend/pallas_call | solution.py:336
  387.6 11.7 %up.3 = (f32[256,4096]{1,0:T(8,128)}, bf16[256,4096]{1,0:T(8,128)(2,1)}, bf16[4,1024,1024]{2,1,0:T(8,128)(2,1)}) custom-call(s32[3]{0:T(128)} %pad_add_fusion.1.where, bf16[256,1024]{1,0:T(8,128)(2,1)} %get-tuple-element.493.middle_low.refs_0_, f32[4,1,1024]{2,1,0:T(1,128)} %bitcast.188, bf16[2,4,6,64,512]{4,3,2,1,0:T(8,128)(2,1)} %copy-done.4, ...), custom_call_target="tpu_custom_call" | custom-call | flops 160000000 | tf_op jit(solution)/shard_map/up/pallas_call | solution.py:438
  399.3 7.8 collective-permute-done.25.refs_4_
  423.4 11.9 %down.3 = (f32[256,1024]{1,0:T(8,128)}, f32[256,1024]{1,0:T(8,128)}, bf16[256,1024]{1,0:T(8,128)(2,1)}, bf16[4,1024,1024]{2,1,0:T(8,128)(2,1)}) custom-call(s32[3]{0:T(128)} %pad_add_fusion.1.where, bf16[256,4096]{1,0:T(8,128)(2,1)} %get-tuple-element.500.act.refs_0_, f32[256,1024]{1,0:T(8,128)} %get-tuple-element.501.middle, ...), custom_call_target="tpu_custom_call" | custom-call | flops 160000000 | tf_op jit(solution)/shard_map/down/pallas_call | solution.py:478
  439.4 15.1 %feed_back.2 = (bf16[256,4096]{1,0:T(8,128)(2,1)}, bf16[256,1024]{1,0:T(8,128)(2,1)}, bf16[256,1024]{1,0:T(8,128)(2,1)}, f32[256,1024]{1,0:T(8,128)}, f32[8,1024]{1,0:T(8,128)}, /*index=5*/f32[4,1,1024]{2,1,0:T(1,128)}) custom-call(f32[256,1024]{1,0:T(8,128)} %get-tuple-element.512.grad_two, bf16[256,1024]{1,0:T(8,128)(2,1)} %get-tuple-element.507.refs_2_.ffn_low, ...), custom_call_target="tpu_custom_call" | custom-call | flops 300000000 | tf_op jit(solution)/shard_map/feed_back/pallas_call | solution.py:559
  454.5 7.8 partial_sums.6
  468.1 7.6 partial_sums.7
  475.7 12.6 %collective-permute-done.35 = bf16[2,4,2,128,256]{4,3,2,1,0:T(8,128)(2,1)} collective-permute-done((bf16[2,4,2,128,256]{4,3,2,1,0:T(8,128)(2,1)}, bf16[2,4,2,128,256]{4,3,2,1,0:T(8,128)(2,1)}, u32[]{:S(2)}, u32[]{:S(2)}) %collective-permute-start.35) | collective-permute-done | bytes 1048608 | tf_op jit(solution)/shard_map/ppermute | solution.py:69
  495.1 21.2 %attend_back.2 = (bf16[256,1024]{1,0:T(8,128)(2,1)}, bf16[2,2,256,1024]{3,2,1,0:T(8,128)(2,1)}, bf16[2,2,256,1024]{3,2,1,0:T(8,128)(2,1)}) custom-call(bf16[256,1024]{1,0:T(8,128)(2,1)} %get-tuple-element.488.query, bf16[256,1024]{1,0:T(8,128)(2,1)} %get-tuple-element.556.grad, f32[1024,256]{1,0:T(8,128)} %compare_select_fusion.mask, ...), custom_call_target="tpu_custom_call" | custom-call | flops 420000000 | tf_op jit(solution)/shard_map/attend_back/pallas_call | solution.py:386
  516.4 11.2 %collective-permute-done.39 = bf16[4,2,128,256]{3,2,1,0:T(8,128)(2,1)S(1)} collective-permute-done((bf16[4,2,128,256]{3,2,1,0:T(8,128)(2,1)S(1)}, bf16[4,2,128,256]{3,2,1,0:T(8,128)(2,1)S(1)}, u32[]{:S(2)}, u32[]{:S(2)}) %collective-permute-start.39) | collective-permute-done | bytes 524320 | tf_op jit(solution)/shard_map/ppermute | solution.py:69
  544.0 13.3 %collective-permute-done.42 = bf16[4,2,128,256]{3,2,1,0:T(8,128)(2,1)} collective-permute-done((bf16[4,2,128,256]{3,2,1,0:T(8,128)(2,1)S(1)}, bf16[4,2,128,256]{3,2,1,0:T(8,128)(2,1)}, u32[]{:S(2)}, u32[]{:S(2)}) %collective-permute-start.42) | collective-permute-done | bytes 524320 | tf_op jit(solution)/shard_map/ppermute | solution.py:69
  570.2 7.8 input_back.2
  591.7 7.7 partial_sums.9
  600.2 8.1 partial_sums.8
  608.4 7.0 all-to-all-done.10.refs_1_
  617.2 15.3 %feed_back.3 = (bf16[256,4096]{1,0:T(8,128)(2,1)}, bf16[256,1024]{1,0:T(8,128)(2,1)}, bf16[256,1024]{1,0:T(8,128)(2,1)}, f32[256,1024]{1,0:T(8,128)}, f32[8,1024]{1,0:T(8,128)}, /*index=5*/f32[4,1,1024]{2,1,0:T(1,128)}) custom-call(f32[256,1024]{1,0:T(8,128)} %get-tuple-element.651.grad_two, bf16[256,1024]{1,0:T(8,128)(2,1)} %get-tuple-element.652.refs_2_.ffn_low, ...), custom_call_target="tpu_custom_call" | custom-call | flops 300000000 | tf_op jit(solution)/shard_map/feed_back/pallas_call | solution.py:559
  632.6 7.5 collective-permute-done.49
  647.6 21.1 %attend_back.3 = (bf16[256,1024]{1,0:T(8,128)(2,1)}, bf16[2,2,256,1024]{3,2,1,0:T(8,128)(2,1)}, bf16[2,2,256,1024]{3,2,1,0:T(8,128)(2,1)}) custom-call(bf16[256,1024]{1,0:T(8,128)(2,1)} %get-tuple-element.454.query, bf16[256,1024]{1,0:T(8,128)(2,1)} %get-tuple-element.678.grad, f32[1024,256]{1,0:T(8,128)} %compare_select_fusion.mask, ...), custom_call_target="tpu_custom_call" | custom-call | flops 420000000 | tf_op jit(solution)/shard_map/attend_back/pallas_call | solution.py:386
  668.7 8.1 collective-permute-done.52
  699.3 7.7 partial_sums.10
  707.9 24.5 %collective-permute-done.56 = bf16[4,2,128,256]{3,2,1,0:T(8,128)(2,1)} collective-permute-done((bf16[4,2,128,256]{3,2,1,0:T(8,128)(2,1)S(1)}, bf16[4,2,128,256]{3,2,1,0:T(8,128)(2,1)}, u32[]{:S(2)}, u32[]{:S(2)}) %collective-permute-start.56) | collective-permute-done | bytes 524320 | tf_op jit(solution)/shard_map/ppermute | solution.py:69
  745.5 7.8 input_back.3
  754.1 13.1 %collective-permute-done.60 = bf16[2,4,2,128,256]{4,3,2,1,0:T(8,128)(2,1)S(1)} collective-permute-done((bf16[2,4,2,128,256]{4,3,2,1,0:T(8,128)(2,1)}, bf16[2,4,2,128,256]{4,3,2,1,0:T(8,128)(2,1)S(1)}, u32[]{:S(2)}, u32[]{:S(2)}) %collective-permute-start.60) | collective-permute-done | bytes 1048608 | tf_op jit(solution)/shard_map/ppermute | solution.py:69
  775.4 8.1 partial_sums.11
  795.6 23.7 %collective-permute-done.69 = f32[2,12288]{1,0:T(2,128)S(1)} collective-permute-done((f32[2,12288]{1,0:T(2,128)S(1)}, f32[2,12288]{1,0:T(2,128)S(1)}, u32[]{:S(2)}, u32[]{:S(2)}) %collective-permute-start.69) | collective-permute-done | bytes 98336 | tf_op jit(solution)/shard_map/ppermute | solution.py:69
  827.0 9.9 collective-permute-done.72
  846.9 12.8 %collective-permute-done.73 = f32[2,12288]{1,0:T(2,128)S(1)} collective-permute-done((f32[2,12288]{1,0:T(2,128)S(1)}, f32[2,12288]{1,0:T(2,128)S(1)}, u32[]{:S(2)}, u32[]{:S(2)}) %collective-permute-start.73) | collective-permute-done | bytes 98336 | tf_op jit(solution)/shard_map/ppermute | solution.py:954
  879.8 29.5 %collective-permute-done.75 = bf16[6,128,256]{2,1,0:T(8,128)(2,1)S(1)} collective-permute-done((bf16[6,128,256]{2,1,0:T(8,128)(2,1)S(1)}, bf16[6,128,256]{2,1,0:T(8,128)(2,1)S(1)}, u32[]{:S(2)}, u32[]{:S(2)}) %collective-permute-start.75) | collective-permute-done | bytes 393248 | tf_op jit(solution)/shard_map/ppermute | solution.py:1296
  909.4 8.8 collective-permute-done.76
  918.2 8.7 all-to-all-done.15
  926.9 16.3 %rotate.1 = (bf16[1024,1024]{1,0:T(8,128)(2,1)}, bf16[1024,1024]{1,0:T(8,128)(2,1)}) custom-call(s32[1]{0:T(128)} %bitcast.58.where, bf16[4,1024,256]{2,1,0:T(8,128)(2,1)} %bitcast.84.grads, f32[6,1024,1024]{2,1,0:T(8,128)} %right.1, bf16[1024,1024]{1,0:T(8,128)(2,1)} %bitcast.28.left, bf16[1024,1024]{1,0:T(8,128)(2,1)} %bitcast.32.first, ...), custom_call_target="tpu_custom_call" | custom-call | flops 320000000 | tf_op jit(solution)/shard_map/rotate/pallas_call | solution.py:841
  950.5 49.5 %collective-permute-done.77 = f32[2,12288]{1,0:T(2,128)S(1)} collective-permute-done((f32[2,12288]{1,0:T(2,128)S(1)}, f32[2,12288]{1,0:T(2,128)S(1)}, u32[]{:S(2)}, u32[]{:S(2)}) %collective-permute-start.77) | collective-permute-done | bytes 98336 | tf_op jit(solution)/shard_map/ppermute | solution.py:954
  1020.8 20.8 %collective-permute-done.78.refs_1_ = bf16[6,128,1024]{2,1,0:T(8,128)(2,1)} collective-permute-done((bf16[6,128,1024]{2,1,0:T(8,128)(2,1)S(1)}, bf16[6,128,1024]{2,1,0:T(8,128)(2,1)}, u32[]{:S(2)}, u32[]{:S(2)}) %collective-permute-start.78) | collective-permute-done | bytes 1572896 | tf_op jit(solution)/shard_map/ppermute | solution.py:69
  1046.4 7.4 pick.1
  (539 shorter events, 393.6 us)
Async XLA Ops:
  7.5 43.3 %all-to-all-start = ((bf16[4,6,64,512]{3,2,1,0:T(8,128)(2,1)}), bf16[4,6,64,512]{3,2,1,0:T(8,128)(2,1)S(1)}, u32[]{:S(2)}, u32[]{:S(2)}) async-start(bf16[4,6,64,512]{3,2,1,0:T(8,128)(2,1)} %broadcast_in_dim.31), calls=%async_computation | async-start | bytes 3145728 | tf_op jit(solution)/shard_map/all_to_all | solution.py:82
  52.2 40.0 %all-to-all-start.1 = ((bf16[4,6,64,512]{3,2,1,0:T(8,128)(2,1)}), bf16[4,6,64,512]{3,2,1,0:T(8,128)(2,1)S(1)}, u32[]{:S(2)}, u32[]{:S(2)}) async-start(bf16[4,6,64,512]{3,2,1,0:T(8,128)(2,1)} %broadcast_in_dim.32), calls=%async_computation.1 | async-start | bytes 3145728 | tf_op jit(solution)/shard_map/all_to_all | solution.py:82
  55.8 35.5 %collective-permute-start = (bf16[4,6,64,512]{3,2,1,0:T(8,128)(2,1)S(1)}, bf16[4,6,64,512]{3,2,1,0:T(8,128)(2,1)}, u32[]{:S(2)}, u32[]{:S(2)}) collective-permute-start(bf16[4,6,64,512]{3,2,1,0:T(8,128)(2,1)S(1)} %all-to-all-done), channel_id=1, source_target_pairs={{1,0},{0,1},{3,2},{2,3},{5,4},{4,5},{7,6},{6,7},{9,8},{8,9},{11,10... | collective-permute-start | bytes 4718600 | tf_op jit(solution)/shard_map/ppermute | solution.py:69
  95.6 43.8 %collective-permute-start.2 = (bf16[2,4,6,64,512]{4,3,2,1,0:T(8,128)(2,1)S(1)}, bf16[2,4,6,64,512]{4,3,2,1,0:T(8,128)(2,1)}, u32[]{:S(2)}, u32[]{:S(2)}) collective-permute-start(bf16[2,4,6,64,512]{4,3,2,1,0:T(8,128)(2,1)S(1)} %pad_maximum_fusion.refs_0_.refs_2_), channel_id=1, source_target_pairs={{8,0},{0,8},{24,16},{16,24},{9,1},{1,9},{25,17},{17,25},{10,2},{2,... | collective-permute-start | bytes 9437192 | tf_op jit(solution)/shard_map/ppermute | solution.py:69
  97.8 41.6 %all-to-all-start.2 = ((bf16[4,6,64,512]{3,2,1,0:T(8,128)(2,1)}), bf16[4,6,64,512]{3,2,1,0:T(8,128)(2,1)}, u32[]{:S(2)}, u32[]{:S(2)}) async-start(bf16[4,6,64,512]{3,2,1,0:T(8,128)(2,1)} %broadcast_in_dim.33), calls=%async_computation.2 | async-start | bytes 3145728 | tf_op jit(solution)/shard_map/all_to_all | solution.py:82
  102.2 36.4 %collective-permute-start.3 = (bf16[4,6,64,512]{3,2,1,0:T(8,128)(2,1)}, bf16[4,6,64,512]{3,2,1,0:T(8,128)(2,1)}, u32[]{:S(2)}, u32[]{:S(2)}) collective-permute-start(bf16[4,6,64,512]{3,2,1,0:T(8,128)(2,1)} %copy-done.11), channel_id=1, source_target_pairs={{1,0},{0,1},{3,2},{2,3},{5,4},{4,5},{7,6},{6,7},{9,8},{8,9},{11,10... | collective-permute-start | bytes 4718600 | tf_op jit(solution)/shard_map/ppermute | solution.py:69
  141.6 58.9 %collective-permute-start.5 = (bf16[2,4,6,64,512]{4,3,2,1,0:T(8,128)(2,1)S(1)}, bf16[2,4,6,64,512]{4,3,2,1,0:T(8,128)(2,1)}, u32[]{:S(2)}, u32[]{:S(2)}) collective-permute-start(bf16[2,4,6,64,512]{4,3,2,1,0:T(8,128)(2,1)S(1)} %pad_maximum_fusion.1.refs_0_.refs_2_), channel_id=1, source_target_pairs={{8,0},{0,8},{24,16},{16,24},{9,1},{1,9},{25,17},{17,25},{10,2},{2,... | collective-permute-start | bytes 9437192 | tf_op jit(solution)/shard_map/ppermute | solution.py:69
  143.8 56.7 %all-to-all-start.3 = ((bf16[4,6,64,512]{3,2,1,0:T(8,128)(2,1)}), bf16[4,6,64,512]{3,2,1,0:T(8,128)(2,1)}, u32[]{:S(2)}, u32[]{:S(2)}) async-start(bf16[4,6,64,512]{3,2,1,0:T(8,128)(2,1)} %broadcast_in_dim.34), calls=%async_computation.3 | async-start | bytes 3145728 | tf_op jit(solution)/shard_map/all_to_all | solution.py:82
  148.2 37.1 %collective-permute-start.6 = (bf16[4,6,64,512]{3,2,1,0:T(8,128)(2,1)}, bf16[4,6,64,512]{3,2,1,0:T(8,128)(2,1)}, u32[]{:S(2)}, u32[]{:S(2)}) collective-permute-start(bf16[4,6,64,512]{3,2,1,0:T(8,128)(2,1)} %all-to-all-done.2), channel_id=1, source_target_pairs={{1,0},{0,1},{3,2},{2,3},{5,4},{4,5},{7,6},{6,7},{9,8},{8,9},{11,10... | collective-permute-start | bytes 4718600 | tf_op jit(solution)/shard_map/ppermute | solution.py:69
  163.2 37.2 %collective-permute-start.8 = (bf16[256,2048]{1,0:T(8,128)(2,1)}, bf16[256,2048]{1,0:T(8,128)(2,1)}, u32[]{:S(2)}, u32[]{:S(2)}) collective-permute-start(bf16[256,2048]{1,0:T(8,128)(2,1)} %get-tuple-element.455.refs_0_.refs_4_), channel_id=1, source_target_pairs={{16,0},{24,8},{0,16},{8,24},{17,1},{25,9},{1,17},{9,25},{18,2},{26... | collective-permute-start | bytes 3145736 | tf_op jit(solution)/shard_map/ppermute | solution.py:69
  163.8 36.7 %collective-permute-start.9 = (bf16[256,2048]{1,0:T(8,128)(2,1)}, bf16[256,2048]{1,0:T(8,128)(2,1)}, u32[]{:S(2)}, u32[]{:S(2)}) collective-permute-start(bf16[256,2048]{1,0:T(8,128)(2,1)} %get-tuple-element.455.refs_0_.refs_4_), channel_id=1, source_target_pairs={{8,0},{0,8},{24,16},{16,24},{9,1},{1,9},{25,17},{17,25},{10,2},{2,... | collective-permute-start | bytes 3145736 | tf_op jit(solution)/shard_map/ppermute | solution.py:69
  202.7 45.9 %collective-permute-start.11 = (bf16[2,4,6,64,512]{4,3,2,1,0:T(8,128)(2,1)S(1)}, bf16[2,4,6,64,512]{4,3,2,1,0:T(8,128)(2,1)}, u32[]{:S(2)}, u32[]{:S(2)}) collective-permute-start(bf16[2,4,6,64,512]{4,3,2,1,0:T(8,128)(2,1)S(1)} %pad_maximum_fusion.2.refs_0_.refs_2_), channel_id=1, source_target_pairs={{8,0},{0,8},{24,16},{16,24},{9,1},{1,9},{25,17},{17,25},{10,2},{2,... | collective-permute-start | bytes 9437192 | tf_op jit(solution)/shard_map/ppermute | solution.py:69
  204.9 43.8 %all-to-all-start.4 = ((bf16[4,6,64,512]{3,2,1,0:T(8,128)(2,1)}), bf16[4,6,64,512]{3,2,1,0:T(8,128)(2,1)}, u32[]{:S(2)}, u32[]{:S(2)}) async-start(bf16[4,6,64,512]{3,2,1,0:T(8,128)(2,1)} %broadcast_in_dim.36), calls=%async_computation.4 | async-start | bytes 3145728 | tf_op jit(solution)/shard_map/all_to_all | solution.py:82
  210.3 38.3 %collective-permute-start.12 = (bf16[4,6,64,512]{3,2,1,0:T(8,128)(2,1)}, bf16[4,6,64,512]{3,2,1,0:T(8,128)(2,1)}, u32[]{:S(2)}, u32[]{:S(2)}) collective-permute-start(bf16[4,6,64,512]{3,2,1,0:T(8,128)(2,1)} %all-to-all-done.3), channel_id=1, source_target_pairs={{1,0},{0,1},{3,2},{2,3},{5,4},{4,5},{7,6},{6,7},{9,8},{8,9},{11,10... | collective-permute-start | bytes 4718600 | tf_op jit(solution)/shard_map/ppermute | solution.py:69
  213.9 34.7 %collective-permute-start.10 = (bf16[2,4,2,64,512]{4,3,2,1,0:T(8,128)(2,1)S(1)}, bf16[2,4,2,64,512]{4,3,2,1,0:T(8,128)(2,1)}, u32[]{:S(2)}, u32[]{:S(2)}) collective-permute-start(bf16[2,4,2,64,512]{4,3,2,1,0:T(8,128)(2,1)S(1)} %fusion.5), channel_id=1, source_target_pairs={{16,0},{24,8},{0,16},{8,24},{17,1},{25,9},{1,17},{9,25},{18,2},{26... | collective-permute-start | bytes 3145736 | tf_op jit(solution)/shard_map/ppermute | solution.py:69
  250.9 37.2 %collective-permute-start.16 = (bf16[2,4,6,64,512]{4,3,2,1,0:T(8,128)(2,1)S(1)}, bf16[2,4,6,64,512]{4,3,2,1,0:T(8,128)(2,1)}, u32[]{:S(2)}, u32[]{:S(2)}) collective-permute-start(bf16[2,4,6,64,512]{4,3,2,1,0:T(8,128)(2,1)S(1)} %pad_maximum_fusion.3.refs_0_.refs_2_), channel_id=1, source_target_pairs={{8,0},{0,8},{24,16},{16,24},{9,1},{1,9},{25,17},{17,25},{10,2},{2,... | collective-permute-start | bytes 9437192 | tf_op jit(solution)/shard_map/ppermute | solution.py:69
  251.0 37.1 %collective-permute-start.17 = (bf16[4,6,64,512]{3,2,1,0:T(8,128)(2,1)}, bf16[4,6,64,512]{3,2,1,0:T(8,128)(2,1)}, u32[]{:S(2)}, u32[]{:S(2)}) collective-permute-start(bf16[4,6,64,512]{3,2,1,0:T(8,128)(2,1)} %all-to-all-done.4), channel_id=1, source_target_pairs={{1,0},{0,1},{3,2},{2,3},{5,4},{4,5},{7,6},{6,7},{9,8},{8,9},{11,10... | collective-permute-start | bytes 4718600 | tf_op jit(solution)/shard_map/ppermute | solution.py:69
  253.6 34.5 %all-to-all-start.5 = ((bf16[4,4,64,512]{3,2,1,0:T(8,128)(2,1)}), bf16[4,4,64,512]{3,2,1,0:T(8,128)(2,1)}, u32[]{:S(2)}, u32[]{:S(2)}) async-start(bf16[4,4,64,512]{3,2,1,0:T(8,128)(2,1)} %broadcast_in_dim.39), calls=%async_computation.5 | async-start | bytes 2097152 | tf_op jit(solution)/shard_map/all_to_all | solution.py:82
  291.8 59.6 %all-to-all-start.6 = ((bf16[8,128,1024]{2,1,0:T(8,128)(2,1)}), bf16[8,128,1024]{2,1,0:T(8,128)(2,1)}, u32[]{:S(2)}, u32[]{:S(2)}) async-start(bf16[8,128,1024]{2,1,0:T(8,128)(2,1)} %pad.10), calls=%async_computation.6 | async-start | bytes 4194304 | tf_op jit(solution)/shard_map/all_to_all | solution.py:972
  300.0 51.4 %collective-permute-start.20 = (bf16[2,4,6,64,512]{4,3,2,1,0:T(8,128)(2,1)S(1)}, bf16[2,4,6,64,512]{4,3,2,1,0:T(8,128)(2,1)}, u32[]{:S(2)}, u32[]{:S(2)}) collective-permute-start(bf16[2,4,6,64,512]{4,3,2,1,0:T(8,128)(2,1)S(1)} %pad_maximum_fusion.4.refs_0_.refs_2_), channel_id=1, source_target_pairs={{8,0},{0,8},{24,16},{16,24},{9,1},{1,9},{25,17},{17,25},{10,2},{2,... | collective-permute-start | bytes 9437192 | tf_op jit(solution)/shard_map/ppermute | solution.py:69
  304.4 40.7 %collective-permute-start.21 = (bf16[4,4,64,512]{3,2,1,0:T(8,128)(2,1)}, bf16[4,4,64,512]{3,2,1,0:T(8,128)(2,1)}, u32[]{:S(2)}, u32[]{:S(2)}) collective-permute-start(bf16[4,4,64,512]{3,2,1,0:T(8,128)(2,1)} %all-to-all-done.5), channel_id=1, source_target_pairs={{1,0},{0,1},{3,2},{2,3},{5,4},{4,5},{7,6},{6,7},{9,8},{8,9},{11,10... | collective-permute-start | bytes 3145736 | tf_op jit(solution)/shard_map/ppermute | solution.py:69
  317.4 34.0 %collective-permute-start.23 = (bf16[256,2048]{1,0:T(8,128)(2,1)}, bf16[256,2048]{1,0:T(8,128)(2,1)}, u32[]{:S(2)}, u32[]{:S(2)}) collective-permute-start(bf16[256,2048]{1,0:T(8,128)(2,1)} %get-tuple-element.489.refs_0_.refs_4_), channel_id=1, source_target_pairs={{16,0},{24,8},{0,16},{8,24},{17,1},{25,9},{1,17},{9,25},{18,2},{26... | collective-permute-start | bytes 3145736 | tf_op jit(solution)/shard_map/ppermute | solution.py:69
  318.3 33.1 %collective-permute-start.24 = (bf16[256,2048]{1,0:T(8,128)(2,1)}, bf16[256,2048]{1,0:T(8,128)(2,1)}, u32[]{:S(2)}, u32[]{:S(2)}) collective-permute-start(bf16[256,2048]{1,0:T(8,128)(2,1)} %get-tuple-element.489.refs_0_.refs_4_), channel_id=1, source_target_pairs={{8,0},{0,8},{24,16},{16,24},{9,1},{1,9},{25,17},{17,25},{10,2},{2,... | collective-permute-start | bytes 3145736 | tf_op jit(solution)/shard_map/ppermute | solution.py:69
  353.2 53.9 %all-to-all-start.7 = ((bf16[8,128,1024]{2,1,0:T(8,128)(2,1)}), bf16[8,128,1024]{2,1,0:T(8,128)(2,1)}, u32[]{:S(2)}, u32[]{:S(2)}) async-start(bf16[8,128,1024]{2,1,0:T(8,128)(2,1)} %pad.11), calls=%async_computation.7 | async-start | bytes 4194304 | tf_op jit(solution)/shard_map/all_to_all | solution.py:972
  361.0 46.2 %collective-permute-start.25 = (bf16[2,4,4,64,512]{4,3,2,1,0:T(8,128)(2,1)S(1)}, bf16[2,4,4,64,512]{4,3,2,1,0:T(8,128)(2,1)}, u32[]{:S(2)}, u32[]{:S(2)}) collective-permute-start(bf16[2,4,4,64,512]{4,3,2,1,0:T(8,128)(2,1)S(1)} %pad_maximum_fusion.5.refs_0_.refs_2_), channel_id=1, source_target_pairs={{16,0},{24,8},{0,16},{8,24},{17,1},{25,9},{1,17},{9,25},{18,2},{26... | collective-permute-start | bytes 6291464 | tf_op jit(solution)/shard_map/ppermute | solution.py:69
  361.5 45.6 %collective-permute-start.26 = (bf16[2,4,4,64,512]{4,3,2,1,0:T(8,128)(2,1)S(1)}, bf16[2,4,4,64,512]{4,3,2,1,0:T(8,128)(2,1)}, u32[]{:S(2)}, u32[]{:S(2)}) collective-permute-start(bf16[2,4,4,64,512]{4,3,2,1,0:T(8,128)(2,1)S(1)} %pad_maximum_fusion.5.refs_0_.refs_2_), channel_id=1, source_target_pairs={{8,0},{0,8},{24,16},{16,24},{9,1},{1,9},{25,17},{17,25},{10,2},{2,... | collective-permute-start | bytes 6291464 | tf_op jit(solution)/shard_map/ppermute | solution.py:69
  409.0 53.3 %all-to-all-start.8 = ((bf16[8,128,1024]{2,1,0:T(8,128)(2,1)}), bf16[8,128,1024]{2,1,0:T(8,128)(2,1)}, u32[]{:S(2)}, u32[]{:S(2)}) async-start(bf16[8,128,1024]{2,1,0:T(8,128)(2,1)} %pad.12), calls=%async_computation.8 | async-start | bytes 4194304 | tf_op jit(solution)/shard_map/all_to_all | solution.py:972
  415.5 46.8 %collective-permute-start.33 = (bf16[256,4096]{1,0:T(8,128)(2,1)}, bf16[256,4096]{1,0:T(8,128)(2,1)}, u32[]{:S(2)}, u32[]{:S(2)}) collective-permute-start(bf16[256,4096]{1,0:T(8,128)(2,1)} %get-tuple-element.468.act.refs_0_), channel_id=1, source_target_pairs={{8,0},{0,8},{24,16},{16,24},{9,1},{1,9},{25,17},{17,25},{10,2},{2,... | collective-permute-start | bytes 6291464 | tf_op jit(solution)/shard_map/ppermute | solution.py:69
  416.0 38.5 %collective-permute-start.30 = (bf16[256,4096]{1,0:T(8,128)(2,1)}, bf16[256,4096]{1,0:T(8,128)(2,1)}, u32[]{:S(2)}, u32[]{:S(2)}) collective-permute-start(bf16[256,4096]{1,0:T(8,128)(2,1)} %get-tuple-element.500.act.refs_0_), channel_id=1, source_target_pairs={{8,0},{0,8},{24,16},{16,24},{9,1},{1,9},{25,17},{17,25},{10,2},{2,... | collective-permute-start | bytes 6291464 | tf_op jit(solution)/shard_map/ppermute | solution.py:69
  417.3 44.9 %collective-permute-start.32 = (bf16[256,3072]{1,0:T(8,128)(2,1)}, bf16[256,3072]{1,0:T(8,128)(2,1)S(1)}, u32[]{:S(2)}, u32[]{:S(2)}) collective-permute-start(bf16[256,3072]{1,0:T(8,128)(2,1)} %pad_maximum_fusion.6), channel_id=1, source_target_pairs={{8,0},{0,8},{24,16},{16,24},{9,1},{1,9},{25,17},{17,25},{10,2},{2,... | collective-permute-start | bytes 4718600 | tf_op jit(solution)/shard_map/ppermute | solution.py:69
  419.1 43.2 %collective-permute-start.34 = (bf16[256,3072]{1,0:T(8,128)(2,1)}, bf16[256,3072]{1,0:T(8,128)(2,1)S(1)}, u32[]{:S(2)}, u32[]{:S(2)}) collective-permute-start(bf16[256,3072]{1,0:T(8,128)(2,1)} %pad_maximum_fusion.7), channel_id=1, source_target_pairs={{8,0},{0,8},{24,16},{16,24},{9,1},{1,9},{25,17},{17,25},{10,2},{2,... | collective-permute-start | bytes 4718600 | tf_op jit(solution)/shard_map/ppermute | solution.py:69
  492.3 35.2 %collective-permute-start.40 = (bf16[2,4,2,128,256]{4,3,2,1,0:T(8,128)(2,1)S(1)}, bf16[2,4,2,128,256]{4,3,2,1,0:T(8,128)(2,1)S(1)}, u32[]{:S(2)}, u32[]{:S(2)}) collective-permute-start(bf16[2,4,2,128,256]{4,3,2,1,0:T(8,128)(2,1)S(1)} %copy-done.91), channel_id=1, source_target_pairs={{16,0},{24,8},{0,16},{8,24},{17,1},{25,9},{1,17},{9,25},{18,2},{26... | collective-permute-start | bytes 3145736 | tf_op jit(solution)/shard_map/ppermute | solution.py:69
  493.8 33.7 %collective-permute-start.41 = (bf16[2,4,2,128,256]{4,3,2,1,0:T(8,128)(2,1)S(1)}, bf16[2,4,2,128,256]{4,3,2,1,0:T(8,128)(2,1)S(1)}, u32[]{:S(2)}, u32[]{:S(2)}) collective-permute-start(bf16[2,4,2,128,256]{4,3,2,1,0:T(8,128)(2,1)S(1)} %copy-done.90), channel_id=1, source_target_pairs={{1,0},{0,1},{3,2},{2,3},{5,4},{4,5},{7,6},{6,7},{9,8},{8,9},{11,10... | collective-permute-start | bytes 3145736 | tf_op jit(solution)/shard_map/ppermute | solution.py:69
  494.5 33.0 %collective-permute-start.39 = (bf16[4,2,128,256]{3,2,1,0:T(8,128)(2,1)S(1)}, bf16[4,2,128,256]{3,2,1,0:T(8,128)(2,1)S(1)}, u32[]{:S(2)}, u32[]{:S(2)}) collective-permute-start(bf16[4,2,128,256]{3,2,1,0:T(8,128)(2,1)S(1)} %get-tuple-element.904), channel_id=1, source_target_pairs={{16,0},{24,8},{0,16},{8,24},{17,1},{25,9},{1,17},{9,25},{18,2},{26... | collective-permute-start | bytes 1572872 | tf_op jit(solution)/shard_map/ppermute | solution.py:69
  642.3 34.5 %collective-permute-start.53 = (bf16[2,4,2,128,256]{4,3,2,1,0:T(8,128)(2,1)S(1)}, bf16[2,4,2,128,256]{4,3,2,1,0:T(8,128)(2,1)S(1)}, u32[]{:S(2)}, u32[]{:S(2)}) collective-permute-start(bf16[2,4,2,128,256]{4,3,2,1,0:T(8,128)(2,1)S(1)} %copy-done.89), channel_id=1, source_target_pairs={{16,0},{24,8},{0,16},{8,24},{17,1},{25,9},{1,17},{9,25},{18,2},{26... | collective-permute-start | bytes 3145736 | tf_op jit(solution)/shard_map/ppermute | solution.py:69
  643.0 33.8 %collective-permute-start.54 = (bf16[2,4,2,128,256]{4,3,2,1,0:T(8,128)(2,1)S(1)}, bf16[2,4,2,128,256]{4,3,2,1,0:T(8,128)(2,1)S(1)}, u32[]{:S(2)}, u32[]{:S(2)}) collective-permute-start(bf16[2,4,2,128,256]{4,3,2,1,0:T(8,128)(2,1)S(1)} %copy-done.88), channel_id=1, source_target_pairs={{1,0},{0,1},{3,2},{2,3},{5,4},{4,5},{7,6},{6,7},{9,8},{8,9},{11,10... | collective-permute-start | bytes 3145736 | tf_op jit(solution)/shard_map/ppermute | solution.py:69
  644.7 32.1 %collective-permute-start.52 = (bf16[4,2,128,256]{3,2,1,0:T(8,128)(2,1)S(1)}, bf16[4,2,128,256]{3,2,1,0:T(8,128)(2,1)S(1)}, u32[]{:S(2)}, u32[]{:S(2)}) collective-permute-start(bf16[4,2,128,256]{3,2,1,0:T(8,128)(2,1)S(1)} %get-tuple-element.896), channel_id=1, source_target_pairs={{16,0},{24,8},{0,16},{8,24},{17,1},{25,9},{1,17},{9,25},{18,2},{26... | collective-permute-start | bytes 1572872 | tf_op jit(solution)/shard_map/ppermute | solution.py:69
  684.1 48.3 %all-to-all-start.11 = ((bf16[4,4,128,256]{3,2,1,0:T(8,128)(2,1)}), bf16[4,4,128,256]{3,2,1,0:T(8,128)(2,1)S(1)}, u32[]{:S(2)}, u32[]{:S(2)}) async-start(bf16[4,4,128,256]{3,2,1,0:T(8,128)(2,1)} %pad_maximum_fusion.11), calls=%async_computation.11 | async-start | bytes 2097152 | tf_op jit(solution)/shard_map/all_to_all | solution.py:82
  696.0 36.4 %collective-permute-start.59 = (bf16[2,256,1024]{2,1,0:T(8,128)(2,1)}, bf16[2,256,1024]{2,1,0:T(8,128)(2,1)}, u32[]{:S(2)}, u32[]{:S(2)}) collective-permute-start(bf16[2,256,1024]{2,1,0:T(8,128)(2,1)} %get-tuple-element.870), channel_id=1, source_target_pairs={{16,0},{24,8},{0,16},{8,24},{17,1},{25,9},{1,17},{9,25},{18,2},{26... | collective-permute-start | bytes 3145736 | tf_op jit(solution)/shard_map/ppermute | solution.py:69
  698.0 34.4 %collective-permute-start.56 = (bf16[4,2,128,256]{3,2,1,0:T(8,128)(2,1)S(1)}, bf16[4,2,128,256]{3,2,1,0:T(8,128)(2,1)}, u32[]{:S(2)}, u32[]{:S(2)}) collective-permute-start(bf16[4,2,128,256]{3,2,1,0:T(8,128)(2,1)S(1)} %get-tuple-element.892), channel_id=1, source_target_pairs={{16,0},{24,8},{0,16},{8,24},{17,1},{25,9},{1,17},{9,25},{18,2},{26... | collective-permute-start | bytes 1572872 | tf_op jit(solution)/shard_map/ppermute | solution.py:69
  787.7 32.7 %all-to-all-start.13 = ((bf16[4,4,128,256]{3,2,1,0:T(8,128)(2,1)}), bf16[4,4,128,256]{3,2,1,0:T(8,128)(2,1)S(1)}, u32[]{:S(2)}, u32[]{:S(2)}) async-start(bf16[4,4,128,256]{3,2,1,0:T(8,128)(2,1)} %pad_maximum_fusion.13), calls=%async_computation.13 | async-start | bytes 2097152 | tf_op jit(solution)/shard_map/all_to_all | solution.py:82
  873.1 53.8 %all-to-all-start.15 = ((bf16[32,128,256]{2,1,0:T(8,128)(2,1)}), bf16[32,128,256]{2,1,0:T(8,128)(2,1)}, u32[]{:S(2)}, u32[]{:S(2)}) async-start(bf16[32,128,256]{2,1,0:T(8,128)(2,1)} %bitcast.170), calls=%async_computation.15 | async-start | bytes 4194304 | tf_op jit(solution)/shard_map/all_to_all | solution.py:1283
  878.1 31.2 %collective-permute-start.75 = (bf16[6,128,256]{2,1,0:T(8,128)(2,1)S(1)}, bf16[6,128,256]{2,1,0:T(8,128)(2,1)S(1)}, u32[]{:S(2)}, u32[]{:S(2)}) collective-permute-start(bf16[6,128,256]{2,1,0:T(8,128)(2,1)S(1)} %get-tuple-element.875), channel_id=1, source_target_pairs={{0,16},{8,24},{16,0},{24,8},{1,17},{9,25},{17,1},{25,9},{2,18},{10... | collective-permute-start | bytes 1179656 | tf_op jit(solution)/shard_map/ppermute | solution.py:1296
  879.8 38.4 %collective-permute-start.76 = (bf16[6,128,256]{2,1,0:T(8,128)(2,1)S(1)}, bf16[6,128,256]{2,1,0:T(8,128)(2,1)S(1)}, u32[]{:S(2)}, u32[]{:S(2)}) collective-permute-start(bf16[6,128,256]{2,1,0:T(8,128)(2,1)S(1)} %get-tuple-element.874), channel_id=1, source_target_pairs={{0,24},{8,16},{16,8},{24,0},{1,25},{9,17},{17,9},{25,1},{2,26},{10... | collective-permute-start | bytes 1179656 | tf_op jit(solution)/shard_map/ppermute | solution.py:1296
  943.2 59.9 %all-to-all-start.16 = ((bf16[8,128,1024]{2,1,0:T(8,128)(2,1)}), bf16[8,128,1024]{2,1,0:T(8,128)(2,1)}, u32[]{:S(2)}, u32[]{:S(2)}) async-start(bf16[8,128,1024]{2,1,0:T(8,128)(2,1)} %bitcast.182), calls=%async_computation.16 | async-start | bytes 4194304 | tf_op jit(solution)/shard_map/all_to_all | solution.py:977
  947.6 52.4 %collective-permute-start.77 = (f32[2,12288]{1,0:T(2,128)S(1)}, f32[2,12288]{1,0:T(2,128)S(1)}, u32[]{:S(2)}, u32[]{:S(2)}) collective-permute-start(f32[2,12288]{1,0:T(2,128)S(1)} %add.465), channel_id=1, source_target_pairs={{0,4},{1,5},{2,6},{3,7},{4,0},{5,1},{6,2},{7,3},{8,12},{9,13},{10,... | collective-permute-start | bytes 294920 | tf_op jit(solution)/shard_map/ppermute | solution.py:954
  1006.2 35.5 %collective-permute-start.78 = (bf16[6,128,1024]{2,1,0:T(8,128)(2,1)S(1)}, bf16[6,128,1024]{2,1,0:T(8,128)(2,1)}, u32[]{:S(2)}, u32[]{:S(2)}) collective-permute-start(bf16[6,128,1024]{2,1,0:T(8,128)(2,1)S(1)} %subtract_convert_fusion.refs_0_), channel_id=1, source_target_pairs={{16,0},{24,8},{0,16},{8,24},{17,1},{25,9},{1,17},{9,25},{18,2},{26... | collective-permute-start | bytes 4718600 | tf_op jit(solution)/shard_map/ppermute | solution.py:69
  1007.5 52.5 %all-to-all-start.17 = ((bf16[8,128,1024]{2,1,0:T(8,128)(2,1)}), bf16[8,128,1024]{2,1,0:T(8,128)(2,1)}, u32[]{:S(2)}, u32[]{:S(2)}) async-start(bf16[8,128,1024]{2,1,0:T(8,128)(2,1)} %bitcast.181), calls=%async_computation.17 | async-start | bytes 4194304 | tf_op jit(solution)/shard_map/all_to_all | solution.py:977
  (144 other events, 2277.5 us)

commit v5 on v4

--- a/solution.py
+++ b/solution.py
@@ -261,7 +261,7 @@
 
     @pl.when(pl.program_id(0) == 0)
     def _():
-        query[...] = value()
+        query[...] = value() * HEAD_DIM ** (-0.5)
 
     @pl.when((pl.program_id(0) > 0) & (pl.program_id(0) < 3))
     def _():
@@ -289,7 +289,7 @@
 
 def head_probs(query_h, keys_h, masks):
     scores = [
-        dot_t(key, query_h) * HEAD_DIM ** (-0.5) + mask for key, mask in zip(keys_h, masks)
+        dot_t(key, query_h) + mask for key, mask in zip(keys_h, masks)
     ]
     peak = functools.reduce(
         jnp.maximum, [jnp.max(score, axis=0, keepdims=True) for score in scores]
@@ -367,14 +367,14 @@
         for spot in range(count):
             grad_score = (probs[spot] * (grad_probs[spot] - inner)).astype(BF16)
             flow_q = flow_q + dot_tt(keys_h[spot], grad_score)
-            grads_k[spot].append(dot(grad_score, query_h) * scale)
+            grads_k[spot].append(dot(grad_score, query_h))
             grads_v[spot].append(dot(probs[spot].astype(BF16), grad_h))
         grads_q.append(flow_q * scale)
     grad_q[...] = jnp.concatenate(grads_q, axis=0).T.astype(BF16)
     for spot in range(count):
         out = mine if spot < count_y else other
-        out[0, spot % count_y] = jnp.concatenate(grads_k[spot], axis=1).astype(BF16)
-        out[1, spot % count_y] = jnp.concatenate(grads_v[spot], axis=1).astype(BF16)
+        out[spot % count_y, 0] = jnp.concatenate(grads_k[spot], axis=1).astype(BF16)
+        out[spot % count_y, 1] = jnp.concatenate(grads_v[spot], axis=1).astype(BF16)
 
 
 def attend_back(query, keyvals, grad, mask):
@@ -382,7 +382,7 @@
     count = len(keyvals)
     count_y = count // CORES
     pair = 2 * HEAD_DIM
-    part = pl.BlockSpec((2, count_y, tokens, pair), lambda i: (0, 0, 0, i))
+    part = pl.BlockSpec((count_y, 2, tokens, pair), lambda i: (0, 0, 0, i))
     return call(
         functools.partial(attend_back_kernel, count, count_y, tokens),
         (D // pair,),
@@ -390,7 +390,7 @@
         + [fixed(mask.shape)]
         + pair_specs(tokens, count),
         [pl.BlockSpec((tokens, pair), lambda i: (0, i)), part, part],
-        [shaped((tokens, D), BF16)] + [shaped((2, count_y, tokens, D), BF16)] * 2,
+        [shaped((tokens, D), BF16)] + [shaped((count_y, 2, tokens, D), BF16)] * 2,
         cost=21.0,
         name="attend_back",
     )(query, grad, mask, *keyvals, *keyvals)
@@ -640,37 +640,47 @@
     return down(act_low, chunk, middle, jnp.stack([parts[3], parts[6], parts[7]]))
 
 
-def sum_kernel(count_one, first_half, sizes, where, *refs):
+def sum_kernel(count_one, first_half, sizes, turned, where, *refs):
     sets = (refs[:4], refs[4:8]) if count_one is not None else (refs[:4],)
-    outs, product = refs[4 * len(sets) : -1], refs[-1]
+    outs, shared, product = refs[4 * len(sets) : -2], refs[-2], refs[-1]
     x_at, y_at = where[1], where[2]
     extent_z, extent_x, extent_y, rows = sizes
+    cols = BLK // (CORES * extent_y)
     spot = pl.program_id(0)
 
+    def both(mine, other):
+        return jnp.concatenate([mine[...], other[...]], axis=0)
+
+    def share(left_mine, left_other, right_mine, right_other):
+        shared[...] = (both(right_mine, right_other) if turned else both(left_mine, left_other)).T
+
     def multiply(left_mine, left_other, right_mine, right_other):
-        left = jnp.concatenate([left_mine[...], left_other[...]], axis=0)
-        right = jnp.concatenate([right_mine[...], right_other[...]], axis=0)
-        product[...] = dot_tt(left, right)
-
+        value = both(left_mine, left_other) if turned else both(right_mine, right_other)
+        product[...] = dot(shared[...], value).astype(BF16)
+
+    pl.when(spot == 0)(lambda: share(*sets[0]))
     if len(sets) == 1:
         multiply(*sets[0])
     else:
+        pl.when(spot == count_one)(lambda: share(*sets[1]))
         pl.when(spot < count_one)(lambda: multiply(*sets[0]))
         pl.when(spot >= count_one)(lambda: multiply(*sets[1]))
-    cols = product.shape[1] // extent_y
 
     def put(y_first):
         for step_y in range(extent_y):
             from_col = pl.multiple_of(lax.rem(y_at + step_y, extent_y) * cols, cols)
             for step_x in range(extent_x):
-                for step_z in range(extent_z):
-                    row_block = step_z * extent_x + lax.rem(x_at + step_x, extent_x)
+                for z in range(extent_z):
+                    row_block = z * extent_x + lax.rem(x_at + step_x, extent_x)
                     from_row = pl.multiple_of(row_block * rows, rows)
-                    value = product[pl.ds(from_row, rows), pl.ds(from_col, cols)].astype(BF16)
+                    if turned:
+                        value = product[pl.ds(from_col, cols), pl.ds(from_row, rows)]
+                    else:
+                        value = product[pl.ds(from_row, rows), pl.ds(from_col, cols)]
                     if y_first:
-                        outs[step_y][step_x, step_z, 0] = value
+                        outs[step_y][step_x, z, 0] = value
                     else:
-                        outs[extent_y + step_x][step_y, step_z, 0] = value
+                        outs[extent_y + step_x][step_y, z, 0] = value
 
     pl.when(spot < first_half)(lambda: put(True))
     pl.when(spot >= first_half)(lambda: put(False))
@@ -708,8 +718,10 @@
             )
         ] * 2
         start += amount
-    part_y = (extent_x, extent_z, 1, rows, cols)
-    part_x = (extent_y, extent_z, 1, rows, cols)
+    turned = sets[0][0].shape[1] > BLK
+    tile = (cols, rows) if turned else (rows, cols)
+    part_y = (extent_x, extent_z, 1) + tile
+    part_x = (extent_y, extent_z, 1) + tile
     spec_y = pl.BlockSpec(part_y, lambda i, where: (0, 0, jnp.minimum(i, first_half - 1), 0, 0))
     spec_x = pl.BlockSpec(part_x, lambda i, where: (0, 0, jnp.maximum(i - first_half, 0), 0, 0))
     outs = call(
@@ -718,13 +730,17 @@
             counts[0] if len(sets) > 1 else None,
             first_half,
             (extent_z, extent_x, extent_y, rows),
+            turned,
         ),
         (count,),
         specs,
         [spec_y] * extent_y + [spec_x] * extent_x,
-        [shaped((extent_x, extent_z, first_half, rows, cols), BF16)] * extent_y
-        + [shaped((extent_y, extent_z, count - first_half, rows, cols), BF16)] * extent_x,
-        scratch=[pltpu.VMEM((BLK, half), F32)],
+        [shaped((extent_x, extent_z, first_half) + tile, BF16)] * extent_y
+        + [shaped((extent_y, extent_z, count - first_half) + tile, BF16)] * extent_x,
+        scratch=[
+            pltpu.VMEM((half if turned else BLK, 2 * tokens), BF16),
+            pltpu.VMEM((half, BLK) if turned else (BLK, half), BF16),
+        ],
         prefetch=1,
         cost=8.0,
         name="partial_sums",
@@ -736,6 +752,7 @@
     def __init__(self, place, ids, sets):
         self.place = place
         self.ids = ids
+        self.turned = False
         if (BLK // (CORES * place.size["y"])) % 128:
             self.plain = True
             self.parts = self.by_y = self.by_x = ()
@@ -743,6 +760,7 @@
         else:
             self.plain = False
             sets = [(one[0], one[1], one[2], place.take(one[2], "core", 1), one[3]) for one in sets]
+            self.turned = sets[0][0].shape[1] > BLK
             self.parts = partial_sums(place, sets)
             self.by_y = self.by_x = ()
             self.groups = ()
@@ -773,13 +791,14 @@
             self.groups = [self.place.swap_z(both.astype(BF16))]
 
 
-def route_kernel(count, slots, scaling, spots, *refs):
-    parts, (out, total) = refs[:count], refs[count:]
+def route_kernel(turned, slots, scaling, spots, *refs):
+    parts, (out, total) = refs[: len(turned)], refs[len(turned) :]
     at = 0
-    for part in parts:
+    for part, turn in zip(parts, turned):
         for block in range(part.shape[1]):
             value = sum(part[addend, block].astype(F32) for addend in range(part.shape[0]))
-            total[at] = (value * scaling).astype(BF16)
+            value = value * scaling
+            total[at] = (value.T if turn else value).astype(BF16)
             at += 1
     total[at] = jnp.zeros(total.shape[1:], BF16)
     for ctx in range(out.shape[0]):
@@ -790,12 +809,12 @@
                 out[ctx, spot] = total[at]
 
 
-def route(groups, spots, slots, wsh_count, scaling):
-    rows, cols = groups[0].shape[2:]
+def route(groups, turned, spots, slots, wsh_count, rows, scaling):
+    cols = groups[0].shape[2] * groups[0].shape[3] // rows
     blocks = sum(group.shape[1] for group in groups)
     shape = (spots.shape[0] // slots, wsh_count, rows, cols)
     return call(
-        functools.partial(route_kernel, len(groups), slots, scaling),
+        functools.partial(route_kernel, turned, slots, scaling),
         (1,),
         [fixed(group.shape) for group in groups],
         fixed(shape),
@@ -807,16 +826,15 @@
     )(spots, *groups)
 
 
-def rotate_kernel(quarters, where, grads, right, left, first, second, rotated, update, total, low, right_low):
+def rotate_kernel(quarters, grads, right, left, first, second, rotated, update, total, low):
     step = BLK // 4
-    right_low[...] = right[0].astype(BF16)
     for at in range(4):
         rows = pl.ds(at * step, step)
         product = 0.0
         for source, quarter in enumerate(quarters):
             width = grads.shape[2]
             product = product + dot(
-                grads[source, rows, :], right_low[pl.ds(quarter * width, width), :]
+                grads[source, rows, :], right[pl.ds(quarter * width, width), :]
             )
         value = dot_tt(left[rows, :], product.astype(BF16))
         if at:
@@ -830,31 +848,24 @@
         first_new = DECAY_RATE * first[rows, :].astype(F32) + (1.0 - DECAY_RATE) * turned
         second_new = DECAY_RATE * second[rows, :].astype(F32) + (1.0 - DECAY_RATE) * turned * turned
         direction = first_new / (jnp.sqrt(second_new) + EPS_ADAM)
-        low[rows, :] = dot_t(direction.astype(BF16), right_low[...]).astype(BF16)
+        low[rows, :] = dot_t(direction.astype(BF16), right[...]).astype(BF16)
     for at in range(4):
         rows = pl.ds(at * step, step)
         update[rows, :] = dot(left[rows, :], low[...]).astype(BF16)
 
 
-def rotate(grads, quarters, right_bases, slot, left, first, second):
+def rotate(grads, quarters, right, left, first, second):
     full = fixed((BLK, BLK))
     return call(
         functools.partial(rotate_kernel, quarters),
         (1,),
-        [
-            fixed(grads.shape),
-            pl.BlockSpec((1, BLK, BLK), lambda i, where: (where[0], 0, 0)),
-            full,
-            full,
-            full,
-        ],
+        [fixed(grads.shape), full, full, full, full],
         [full, full],
         [shaped((BLK, BLK), BF16)] * 2,
-        scratch=[pltpu.VMEM((BLK, BLK), F32), pltpu.VMEM((BLK, BLK), BF16), pltpu.VMEM((BLK, BLK), BF16)],
-        prefetch=1,
+        scratch=[pltpu.VMEM((BLK, BLK), F32), pltpu.VMEM((BLK, BLK), BF16)],
         cost=16.0,
         name="rotate",
-    )(slot, grads, right_bases, left, first, second)
+    )(grads, right, left, first, second)
 
 
 def pick_kernel(count, amount, table, *refs):
@@ -966,15 +977,18 @@
     return jnp.sum((position[:, None] >= starts[None, :]).astype(jnp.int32), axis=1)
 
 
-def to_owner(rows_value, wsh_count):
+def fill_up(rows_value, wsh_count):
     slots = rows_value.shape[0]
-    padded = jnp.pad(rows_value.astype(BF16), ((0, wsh_count - slots), (0, 0), (0, 0)))
+    return jnp.pad(rows_value.astype(BF16), ((0, wsh_count - slots), (0, 0), (0, 0)))
+
+
+def to_owner(padded):
     return lax.all_to_all(padded, "wsh", 0, 0, tiled=True).reshape(BLK, BLK)
 
 
-def from_owner(whole, wsh_count, slots):
+def from_owner(whole, wsh_count):
     cut = whole.astype(BF16).reshape(wsh_count, BLK // wsh_count, BLK)
-    return lax.all_to_all(cut, "wsh", 0, 0, tiled=True)[:slots]
+    return lax.all_to_all(cut, "wsh", 0, 0, tiled=True)
 
 
 def on_device(
@@ -1043,6 +1057,11 @@
         return keyvals + [place.take(value, "core", 1) for value in keyvals[1:count_y]]
 
     kept = [{}, {}]
+    slot_own = jnp.minimum(lax.axis_index("wsh"), slots_dev - 1)
+    live["left"] = fill_up(left_bases, wsh_count)
+    live["first"] = fill_up(moment1, wsh_count)
+    live["second"] = fill_up(moment2, wsh_count)
+    live["right"] = lax.dynamic_index_in_dim(right_bases, slot_own, 0, False).astype(BF16)
     chunks[0].step_z()
     settle()
     chunks[0].step_x()
@@ -1075,19 +1094,16 @@
     summed_two_0, live["result"], live["result_low"], w_down_0 = down_step(
         act_0, finish(2), middle_0, vec_params[0]
     )
-    live["left"] = left_bases
     settle()
     chunks[4].step_y()
     chunks[5].step_x()
     result_0, result_low_0 = live["result"], live["result_low"]
     query_1, live["keyvals1"], w_in_1 = project_step(place, result_low_0, finish(3), vec_params[1])
     live["query"] = query_1
-    live["left"] = to_owner(live["left"], wsh_count)
-    live["first"] = moment1
+    live["left"] = to_owner(live["left"])
     settle()
     chunks[5].step_y()
-    live["first"] = to_owner(live["first"], wsh_count)
-    live["second"] = moment2
+    live["first"] = to_owner(live["first"])
     keyvals_1 = keyvals_of(1)
     query_1 = live["query"]
     attn_1, summed_one_1, middle_1, mid_low_1 = mix_step(
@@ -1120,7 +1136,8 @@
         "crossed": crossed,
         "left": live["left"],
         "first": live["first"],
-        "second": to_owner(live["second"], wsh_count),
+        "second": to_owner(live["second"]),
+        "right": live["right"],
     }
     jobs = []
     vec_terms = [None] * LAYERS
@@ -1178,7 +1195,7 @@
     def send_step():
         mine, other = live["pair"]
         arrived = place.take(other, "core", 1)
-        sums = [mine[:, step].astype(F32) + arrived[:, step].astype(F32) for step in range(count_y)]
+        sums = [mine[step].astype(F32) + arrived[step].astype(F32) for step in range(count_y)]
         live["kv"] = [sums[0]] + [
             place.take(sums[step].astype(BF16), "y", -step) for step in range(1, count_y)
         ]
@@ -1269,6 +1286,7 @@
     stream_grad = grad_flow[None]
     vec_grads = every[0].total() * scaling
     groups = [group for job in jobs for group in job.groups]
+    turned = [job.turned for job in jobs for group in job.groups]
     ids = [block for job in jobs for block in job.ids]
 
     owner_flat = owner_slots.reshape(-1)
@@ -1278,7 +1296,7 @@
     spots = jnp.where(
         jnp.any(picks, axis=1), jnp.argmax(picks, axis=1).astype(jnp.int32), block_count
     )
-    by_slot = route(groups, spots, slots_dev, wsh_count, scaling)
+    by_slot = route(groups, turned, spots, slots_dev, wsh_count, rows_dev, scaling)
 
     arrived = lax.all_to_all(
         by_slot.reshape(ctx_count * wsh_count, rows_dev, width), ("ctx", "wsh"), 0, 0, tiled=True
@@ -1294,13 +1312,7 @@
             for core in range(CORES)
         ]
         quarter_parts.append(lax.ppermute(part, "ctx", pairs) if step else part)
-    arrived, quarter_parts = together(arrived, quarter_parts)
     quarters = [(source % CORES) * count_y + source // CORES for source in range(ctx_count)]
-    slot_own = jnp.minimum(lax.axis_index("wsh"), slots_dev - 1).reshape(1)
-    rotated_own, update_own = rotate(
-        arrived.reshape(ctx_count, BLK, width), quarters, right_bases, slot_own, live["left"], live["first"], live["second"]
-    )
-
     by_rows = jnp.stack(quarter_parts)
     by_source = [
         lax.dynamic_index_in_dim(
@@ -1313,22 +1325,27 @@
     ]
     by_source = jnp.stack([by_source[quarters.index(quarter)] for quarter in range(ctx_count)])
     block_grads = by_source.transpose(1, 2, 0, 3).reshape(slots_dev, rows_dev, BLK).astype(F32)
-    update = from_owner(update_own, wsh_count, slots_dev)
-    update, block_grads, vec_grads = together(update, block_grads, vec_grads)
-    master_low = (master - LR_BLOCK * update.astype(F32)).astype(BF16)
+    arrived, block_grads = together(arrived, block_grads)
+    rotated_own, update_own = rotate(
+        arrived.reshape(ctx_count, BLK, width), quarters, live["right"], live["left"], live["first"], live["second"]
+    )
+
+    update = from_owner(update_own, wsh_count)
+    update, vec_grads = together(update, vec_grads)
+    master_low = (master - LR_BLOCK * update[:slots_dev].astype(F32)).astype(BF16)
     master_low, update, rotated_own = together(master_low, update, rotated_own)
     parts = gather_list(place, master_low, "y")
-    rotated = from_owner(rotated_own, wsh_count, slots_dev)
+    rotated = from_owner(rotated_own, wsh_count)
     across = place.take(master_low, "core", 1)
-    new_master = master - LR_BLOCK * update.astype(F32)
+    new_master = master - LR_BLOCK * update[:slots_dev].astype(F32)
     parts = parts + [across] + [place.take(value, "core", 1) for value in parts[1:]]
     owner_ctx, owner_at = owner_flat // slots_dev, owner_flat % slots_dev
     step_y = (owner_ctx // CORES - place.at["y"]) % count_y
     step_core = (owner_ctx % CORES - place.at["core"]) % CORES
     table = jnp.stack([step_core * count_y + step_y, owner_at]).astype(jnp.int32)
     new_weights = pick(parts, table).reshape(LAYERS, NBLK, rows_dev, BLK)
-    new_weights, new_master, rotated = together(new_weights, new_master, rotated)
-    rotated = rotated.astype(F32)
+    rotated, _ = together(rotated, (new_weights[0, 0, :8, :128], new_master[0, :8, :128]))
+    rotated = rotated[:slots_dev].astype(F32)
 
     new_moment1 = DECAY_RATE * moment1 + (1.0 - DECAY_RATE) * rotated
     new_moment2 = DECAY_RATE * moment2 + (1.0 - DECAY_RATE) * rotated * rotated

time: 1080 us -> 1060 us (0.981)
  waiting for transfers between devices: 476 us -> 458 us
    all_to_all x12, waiting for transfers between devices: 37.3 us -> 22.4 us  [swap_z(): lax.all_to_all(values, 'wsh', 0, 0, tiled=True, axis_index_groups=lines)]
    unnamed x222 -> x216, local copies, waits for them, and re-layouts: 42.1 us -> 45.6 us
  transfers between devices with their start and end apart: 99 -> 99, of which waited for: 49 -> 49; matrix products, arithmetic and copies ran while one was open for 9% -> 10% of each run, Pallas kernels for 24% -> 24%
where the time goes in v5:
time: 1060 us; the launch traced here: 1050 us
  waiting for transfers between devices  458 us (43%)
  Pallas kernels  275 us (26%)
  starting transfers between devices  145 us (14%)
  local copies, waits for them, and re-layouts  89 us (8%)
  other arithmetic  82.8 us (8%)
    ppermute x76, waiting for transfers between devices, take(): return lax.ppermute(value, name, pairs)  324 us
    ppermute x2, waiting for transfers between devices, step(): self.terms = [value, lax.ppermute(value, 'wsh', swap)]  62.3 us
    all_to_all x12, starting transfers between devices, swap_z(): lax.all_to_all(values, 'wsh', 0, 0, tiled=True, axis_index_groups=lines)  55.9 us
    ppermute x76, starting transfers between devices, take(): return lax.ppermute(value, name, pairs)  52 us
    pallas_call x6, Pallas kernels, partial_sums(): call(functools.partial(sum_kernel, counts[0] if len(sets) > 1 else None,...  49 us
    unnamed x216, local copies, waits for them, and re-layouts  45.6 us
    pallas_call x2, Pallas kernels, attend_back(): call(functools.partial(attend_back_kernel, count, count_y, tokens), (D //...  42.7 us
    ppermute x3, waiting for transfers between devices, on_device(): quarter_parts.append(lax.ppermute(part, 'ctx', pairs) if step else part)  38.5 us
  transfers between devices with their start and end apart: 99, of which 49 were waited for; matrix products, arithmetic and copies ran while one was open for 10% of the time, Pallas kernels for 24%

profile of v5, /device:TPU:0, one launch (start us, length us, event | category | flops | bytes accessed | tf_op | source)
XLA Modules:
  0.0 1052.3 jit_solution(7928094311734152378)
XLA Ops:
  57.3 34.0 %collective-permute-done = bf16[4,6,64,512]{3,2,1,0:T(8,128)(2,1)} collective-permute-done((bf16[4,6,64,512]{3,2,1,0:T(8,128)(2,1)S(1)}, bf16[4,6,64,512]{3,2,1,0:T(8,128)(2,1)}, u32[]{:S(2)}, u32[]{:S(2)}) %collective-permute-start) | collective-permute-done | bytes 1572896 | tf_op jit(solution)/shard_map/ppermute | solution.py:69
  106.6 23.1 %collective-permute-done.1.refs_4_ = bf16[2,4,2,64,512]{4,3,2,1,0:T(8,128)(2,1)} collective-permute-done((bf16[2,4,2,64,512]{4,3,2,1,0:T(8,128)(2,1)S(1)}, bf16[2,4,2,64,512]{4,3,2,1,0:T(8,128)(2,1)}, u32[]{:S(2)}, u32[]{:S(2)}) %collective-permute-start.1) | collective-permute-done | bytes 1048608 | tf_op jit(solution)/shard_map/ppermute | solution.py:69
  129.7 8.9 collective-permute-done.3
  154.1 9.1 project.2
  163.8 14.8 %collective-permute-done.4.refs_4_ = bf16[2,4,2,64,512]{4,3,2,1,0:T(8,128)(2,1)S(1)} collective-permute-done((bf16[2,4,2,64,512]{4,3,2,1,0:T(8,128)(2,1)S(1)}, bf16[2,4,2,64,512]{4,3,2,1,0:T(8,128)(2,1)S(1)}, u32[]{:S(2)}, u32[]{:S(2)}) %collective-permute-start.4) | collective-permute-done | bytes 1048608 | tf_op jit(solution)/shard_map/ppermute | solution.py:69
  185.3 15.1 %collective-permute-done.8.refs_1_.refs_5_ = bf16[256,2048]{1,0:T(8,128)(2,1)} collective-permute-done((bf16[256,2048]{1,0:T(8,128)(2,1)}, bf16[256,2048]{1,0:T(8,128)(2,1)}, u32[]{:S(2)}, u32[]{:S(2)}) %collective-permute-start.8) | collective-permute-done | bytes 1048608 | tf_op jit(solution)/shard_map/ppermute | solution.py:69
  217.9 14.3 %attend.2.attn.refs_4_ = bf16[256,1024]{1,0:T(8,128)(2,1)} custom-call(bf16[256,1024]{1,0:T(8,128)(2,1)} %get-tuple-element.499.query, f32[1024,256]{1,0:T(8,128)} %compare_select_fusion.mask, bf16[256,2048]{1,0:T(8,128)(2,1)} %get-tuple-element.500.refs_0_.refs_4_, bf16[256,2048]{1,0:T(8,128)(2,1)} %collective-permute-done.8.refs_1_.refs_5_, ...), custom_call_target="tpu_custom_call" | custom-call | flops 280000000 | tf_op jit(solution)/shard_map/attend/pallas_call | solution.py:336
  237.2 11.5 %up.2 = (f32[256,4096]{1,0:T(8,128)}, bf16[256,4096]{1,0:T(8,128)(2,1)}, bf16[4,1024,1024]{2,1,0:T(8,128)(2,1)}) custom-call(s32[3]{0:T(128)} %pad_add_fusion.1.where, bf16[256,1024]{1,0:T(8,128)(2,1)} %get-tuple-element.504.middle_low.refs_0_, f32[4,1,1024]{2,1,0:T(1,128)} %bitcast.186, bf16[2,4,6,64,512]{4,3,2,1,0:T(8,128)(2,1)} %copy-done.2, ...), custom_call_target="tpu_custom_call" | custom-call | flops 160000000 | tf_op jit(solution)/shard_map/up/pallas_call | solution.py:438
  262.7 11.3 %down.2 = (f32[256,1024]{1,0:T(8,128)}, f32[256,1024]{1,0:T(8,128)}, bf16[256,1024]{1,0:T(8,128)(2,1)}, bf16[4,1024,1024]{2,1,0:T(8,128)(2,1)}) custom-call(s32[3]{0:T(128)} %pad_add_fusion.1.where, bf16[256,4096]{1,0:T(8,128)(2,1)} %get-tuple-element.517.act.refs_0_, f32[256,1024]{1,0:T(8,128)} %get-tuple-element.520.middle, ...), custom_call_target="tpu_custom_call" | custom-call | flops 160000000 | tf_op jit(solution)/shard_map/down/pallas_call | solution.py:478
  274.0 11.9 %collective-permute-done.15.refs_4_ = bf16[2,4,2,64,512]{4,3,2,1,0:T(8,128)(2,1)} collective-permute-done((bf16[2,4,2,64,512]{4,3,2,1,0:T(8,128)(2,1)S(1)}, bf16[2,4,2,64,512]{4,3,2,1,0:T(8,128)(2,1)}, u32[]{:S(2)}, u32[]{:S(2)}) %collective-permute-start.15) | collective-permute-done | bytes 1048608 | tf_op jit(solution)/shard_map/ppermute | solution.py:69
  304.5 9.1 project.3
  314.6 12.2 %collective-permute-done.19.refs_4_ = bf16[2,4,2,64,512]{4,3,2,1,0:T(8,128)(2,1)} collective-permute-done((bf16[2,4,2,64,512]{4,3,2,1,0:T(8,128)(2,1)}, bf16[2,4,2,64,512]{4,3,2,1,0:T(8,128)(2,1)}, u32[]{:S(2)}, u32[]{:S(2)}) %collective-permute-start.19) | collective-permute-done | bytes 1048608 | tf_op jit(solution)/shard_map/ppermute | solution.py:69
  326.7 14.8 %collective-permute-done.21 = bf16[4,4,64,512]{3,2,1,0:T(8,128)(2,1)} collective-permute-done((bf16[4,4,64,512]{3,2,1,0:T(8,128)(2,1)}, bf16[4,4,64,512]{3,2,1,0:T(8,128)(2,1)}, u32[]{:S(2)}, u32[]{:S(2)}) %collective-permute-start.21) | collective-permute-done | bytes 1048608 | tf_op jit(solution)/shard_map/ppermute | solution.py:69
  364.3 14.3 %attend.3.attn.refs_4_ = bf16[256,1024]{1,0:T(8,128)(2,1)} custom-call(bf16[256,1024]{1,0:T(8,128)(2,1)} %get-tuple-element.544.query, f32[1024,256]{1,0:T(8,128)} %compare_select_fusion.mask, bf16[256,2048]{1,0:T(8,128)(2,1)} %get-tuple-element.545.refs_0_.refs_4_, bf16[256,2048]{1,0:T(8,128)(2,1)} %collective-permute-done.23.refs_1_.refs_5_, ...), custom_call_target="tpu_custom_call" | custom-call | flops 280000000 | tf_op jit(solution)/shard_map/attend/pallas_call | solution.py:336
  383.8 11.4 %up.3 = (f32[256,4096]{1,0:T(8,128)}, bf16[256,4096]{1,0:T(8,128)(2,1)}, bf16[4,1024,1024]{2,1,0:T(8,128)(2,1)}) custom-call(s32[3]{0:T(128)} %pad_add_fusion.1.where, bf16[256,1024]{1,0:T(8,128)(2,1)} %get-tuple-element.549.middle_low.refs_0_, f32[4,1,1024]{2,1,0:T(1,128)} %bitcast.185, bf16[2,4,6,64,512]{4,3,2,1,0:T(8,128)(2,1)} %copy-done.4, ...), custom_call_target="tpu_custom_call" | custom-call | flops 160000000 | tf_op jit(solution)/shard_map/up/pallas_call | solution.py:438
  395.3 8.1 collective-permute-done.25.refs_4_
  404.7 6.3 all-to-all-start.8
  419.0 11.8 %down.3 = (f32[256,1024]{1,0:T(8,128)}, f32[256,1024]{1,0:T(8,128)}, bf16[256,1024]{1,0:T(8,128)(2,1)}, bf16[4,1024,1024]{2,1,0:T(8,128)(2,1)}) custom-call(s32[3]{0:T(128)} %pad_add_fusion.1.where, bf16[256,4096]{1,0:T(8,128)(2,1)} %get-tuple-element.558.act.refs_0_, f32[256,1024]{1,0:T(8,128)} %get-tuple-element.559.middle, ...), custom_call_target="tpu_custom_call" | custom-call | flops 160000000 | tf_op jit(solution)/shard_map/down/pallas_call | solution.py:478
  434.9 15.2 %feed_back.2 = (bf16[256,4096]{1,0:T(8,128)(2,1)}, bf16[256,1024]{1,0:T(8,128)(2,1)}, bf16[256,1024]{1,0:T(8,128)(2,1)}, f32[256,1024]{1,0:T(8,128)}, f32[8,1024]{1,0:T(8,128)}, /*index=5*/f32[4,1,1024]{2,1,0:T(1,128)}) custom-call(f32[256,1024]{1,0:T(8,128)} %get-tuple-element.570.grad_two, bf16[256,1024]{1,0:T(8,128)(2,1)} %get-tuple-element.565.refs_2_.ffn_low, ...), custom_call_target="tpu_custom_call" | custom-call | flops 300000000 | tf_op jit(solution)/shard_map/feed_back/pallas_call | solution.py:559
  450.1 8.3 partial_sums.6
  464.3 7.6 partial_sums.7
  471.9 12.6 %collective-permute-done.35 = bf16[2,4,2,256,128]{4,3,2,1,0:T(8,128)(2,1)} collective-permute-done((bf16[2,4,2,256,128]{4,3,2,1,0:T(8,128)(2,1)}, bf16[2,4,2,256,128]{4,3,2,1,0:T(8,128)(2,1)}, u32[]{:S(2)}, u32[]{:S(2)}) %collective-permute-start.35) | collective-permute-done | bytes 1048608 | tf_op jit(solution)/shard_map/ppermute | solution.py:69
  491.2 21.4 %attend_back.2 = (bf16[256,1024]{1,0:T(8,128)(2,1)}, bf16[2,2,256,1024]{3,2,1,0:T(8,128)(2,1)}, bf16[2,2,256,1024]{3,2,1,0:T(8,128)(2,1)}) custom-call(bf16[256,1024]{1,0:T(8,128)(2,1)} %get-tuple-element.544.query, bf16[256,1024]{1,0:T(8,128)(2,1)} %get-tuple-element.616.grad, f32[1024,256]{1,0:T(8,128)} %compare_select_fusion.mask, ...), custom_call_target="tpu_custom_call" | custom-call | flops 420000000 | tf_op jit(solution)/shard_map/attend_back/pallas_call | solution.py:386
  512.6 11.1 %collective-permute-done.39 = bf16[4,2,256,128]{3,2,1,0:T(8,128)(2,1)S(1)} collective-permute-done((bf16[4,2,256,128]{3,2,1,0:T(8,128)(2,1)S(1)}, bf16[4,2,256,128]{3,2,1,0:T(8,128)(2,1)S(1)}, u32[]{:S(2)}, u32[]{:S(2)}) %collective-permute-start.39) | collective-permute-done | bytes 524320 | tf_op jit(solution)/shard_map/ppermute | solution.py:69
  537.3 13.3 %collective-permute-done.42 = bf16[4,2,128,256]{3,2,1,0:T(8,128)(2,1)} collective-permute-done((bf16[4,2,128,256]{3,2,1,0:T(8,128)(2,1)S(1)}, bf16[4,2,128,256]{3,2,1,0:T(8,128)(2,1)}, u32[]{:S(2)}, u32[]{:S(2)}) %collective-permute-start.42) | collective-permute-done | bytes 524320 | tf_op jit(solution)/shard_map/ppermute | solution.py:69
  550.6 6.4 all-to-all-done.9.refs_0_
  563.5 7.8 input_back.2
  584.9 8.3 partial_sums.9
  594.1 8.5 partial_sums.8
  610.5 15.2 %feed_back.3 = (bf16[256,4096]{1,0:T(8,128)(2,1)}, bf16[256,1024]{1,0:T(8,128)(2,1)}, bf16[256,1024]{1,0:T(8,128)(2,1)}, f32[256,1024]{1,0:T(8,128)}, f32[8,1024]{1,0:T(8,128)}, /*index=5*/f32[4,1,1024]{2,1,0:T(1,128)}) custom-call(f32[256,1024]{1,0:T(8,128)} %get-tuple-element.715.grad_two, bf16[256,1024]{1,0:T(8,128)(2,1)} %get-tuple-element.716.refs_2_.ffn_low, ...), custom_call_target="tpu_custom_call" | custom-call | flops 300000000 | tf_op jit(solution)/shard_map/feed_back/pallas_call | solution.py:559
  625.7 7.6 collective-permute-done.49
  640.9 21.3 %attend_back.3 = (bf16[256,1024]{1,0:T(8,128)(2,1)}, bf16[2,2,256,1024]{3,2,1,0:T(8,128)(2,1)}, bf16[2,2,256,1024]{3,2,1,0:T(8,128)(2,1)}) custom-call(bf16[256,1024]{1,0:T(8,128)(2,1)} %get-tuple-element.499.query, bf16[256,1024]{1,0:T(8,128)(2,1)} %get-tuple-element.743.grad, f32[1024,256]{1,0:T(8,128)} %compare_select_fusion.mask, ...), custom_call_target="tpu_custom_call" | custom-call | flops 420000000 | tf_op jit(solution)/shard_map/attend_back/pallas_call | solution.py:386
  662.2 7.6 collective-permute-done.52
  689.0 7.8 partial_sums.10
  697.5 24.6 %collective-permute-done.56 = bf16[4,2,256,128]{3,2,1,0:T(8,128)(2,1)} collective-permute-done((bf16[4,2,256,128]{3,2,1,0:T(8,128)(2,1)S(1)}, bf16[4,2,256,128]{3,2,1,0:T(8,128)(2,1)}, u32[]{:S(2)}, u32[]{:S(2)}) %collective-permute-start.56) | collective-permute-done | bytes 524320 | tf_op jit(solution)/shard_map/ppermute | solution.py:69
  734.9 7.8 input_back.3
  743.5 13.5 %collective-permute-done.60 = bf16[2,4,2,128,256]{4,3,2,1,0:T(8,128)(2,1)S(1)} collective-permute-done((bf16[2,4,2,128,256]{4,3,2,1,0:T(8,128)(2,1)}, bf16[2,4,2,128,256]{4,3,2,1,0:T(8,128)(2,1)S(1)}, u32[]{:S(2)}, u32[]{:S(2)}) %collective-permute-start.60) | collective-permute-done | bytes 1048608 | tf_op jit(solution)/shard_map/ppermute | solution.py:69
  764.9 8.5 partial_sums.11
  785.4 23.4 %collective-permute-done.69 = f32[2,12288]{1,0:T(2,128)S(1)} collective-permute-done((f32[2,12288]{1,0:T(2,128)S(1)}, f32[2,12288]{1,0:T(2,128)S(1)}, u32[]{:S(2)}, u32[]{:S(2)}) %collective-permute-start.69) | collective-permute-done | bytes 98336 | tf_op jit(solution)/shard_map/ppermute | solution.py:69
  816.5 9.9 collective-permute-done.72
  836.6 12.8 %collective-permute-done.73 = f32[2,12288]{1,0:T(2,128)S(1)} collective-permute-done((f32[2,12288]{1,0:T(2,128)S(1)}, f32[2,12288]{1,0:T(2,128)S(1)}, u32[]{:S(2)}, u32[]{:S(2)}) %collective-permute-start.73) | collective-permute-done | bytes 98336 | tf_op jit(solution)/shard_map/ppermute | solution.py:965
  849.4 6.6 all-to-all-done.14.refs_5_
  869.7 28.5 %collective-permute-done.76 = bf16[6,128,256]{2,1,0:T(8,128)(2,1)S(1)} collective-permute-done((bf16[6,128,256]{2,1,0:T(8,128)(2,1)}, bf16[6,128,256]{2,1,0:T(8,128)(2,1)S(1)}, u32[]{:S(2)}, u32[]{:S(2)}) %collective-permute-start.76) | collective-permute-done | bytes 393248 | tf_op jit(solution)/shard_map/ppermute | solution.py:1314
  898.1 10.1 collective-permute-done.75
  916.7 15.7 %rotate.1 = (bf16[1024,1024]{1,0:T(8,128)(2,1)}, bf16[1024,1024]{1,0:T(8,128)(2,1)}) custom-call(bf16[4,1024,256]{2,1,0:T(8,128)(2,1)} %bitcast.88.grads, bf16[1024,1024]{1,0:T(8,128)(2,1)} %fusion.1.right, bf16[1024,1024]{1,0:T(8,128)(2,1)} %bitcast.29.left, bf16[1024,1024]{1,0:T(8,128)(2,1)} %bitcast.33.first, bf16[1024,1024]{1,0:T(8,128)(2,1)} %bitcast.37.second), custom_call_target="tpu_custom_call" | custom-call | flops 320000000 | tf_op jit(solution)/shard_map/rotate/pallas_call | solution.py:859
  939.0 49.5 %collective-permute-done.77 = f32[2,12288]{1,0:T(2,128)S(1)} collective-permute-done((f32[2,12288]{1,0:T(2,128)S(1)}, f32[2,12288]{1,0:T(2,128)S(1)}, u32[]{:S(2)}, u32[]{:S(2)}) %collective-permute-start.77) | collective-permute-done | bytes 98336 | tf_op jit(solution)/shard_map/ppermute | solution.py:965
  1007.0 20.8 %collective-permute-done.78.refs_1_ = bf16[6,128,1024]{2,1,0:T(8,128)(2,1)} collective-permute-done((bf16[6,128,1024]{2,1,0:T(8,128)(2,1)}, bf16[6,128,1024]{2,1,0:T(8,128)(2,1)}, u32[]{:S(2)}, u32[]{:S(2)}) %collective-permute-start.78) | collective-permute-done | bytes 1572896 | tf_op jit(solution)/shard_map/ppermute | solution.py:69
  1032.5 7.6 pick.1
  (530 shorter events, 388.6 us)
Async XLA Ops:
  7.5 43.3 %all-to-all-start = ((bf16[4,6,64,512]{3,2,1,0:T(8,128)(2,1)}), bf16[4,6,64,512]{3,2,1,0:T(8,128)(2,1)S(1)}, u32[]{:S(2)}, u32[]{:S(2)}) async-start(bf16[4,6,64,512]{3,2,1,0:T(8,128)(2,1)} %broadcast_in_dim.31), calls=%async_computation | async-start | bytes 3145728 | tf_op jit(solution)/shard_map/all_to_all | solution.py:82
  52.2 40.0 %all-to-all-start.1 = ((bf16[4,6,64,512]{3,2,1,0:T(8,128)(2,1)}), bf16[4,6,64,512]{3,2,1,0:T(8,128)(2,1)S(1)}, u32[]{:S(2)}, u32[]{:S(2)}) async-start(bf16[4,6,64,512]{3,2,1,0:T(8,128)(2,1)} %broadcast_in_dim.32), calls=%async_computation.1 | async-start | bytes 3145728 | tf_op jit(solution)/shard_map/all_to_all | solution.py:82
  55.8 35.5 %collective-permute-start = (bf16[4,6,64,512]{3,2,1,0:T(8,128)(2,1)S(1)}, bf16[4,6,64,512]{3,2,1,0:T(8,128)(2,1)}, u32[]{:S(2)}, u32[]{:S(2)}) collective-permute-start(bf16[4,6,64,512]{3,2,1,0:T(8,128)(2,1)S(1)} %all-to-all-done), channel_id=1, source_target_pairs={{1,0},{0,1},{3,2},{2,3},{5,4},{4,5},{7,6},{6,7},{9,8},{8,9},{11,10... | collective-permute-start | bytes 4718600 | tf_op jit(solution)/shard_map/ppermute | solution.py:69
  95.6 43.7 %collective-permute-start.2 = (bf16[2,4,6,64,512]{4,3,2,1,0:T(8,128)(2,1)S(1)}, bf16[2,4,6,64,512]{4,3,2,1,0:T(8,128)(2,1)}, u32[]{:S(2)}, u32[]{:S(2)}) collective-permute-start(bf16[2,4,6,64,512]{4,3,2,1,0:T(8,128)(2,1)S(1)} %pad_maximum_fusion.refs_0_.refs_2_), channel_id=1, source_target_pairs={{8,0},{0,8},{24,16},{16,24},{9,1},{1,9},{25,17},{17,25},{10,2},{2,... | collective-permute-start | bytes 9437192 | tf_op jit(solution)/shard_map/ppermute | solution.py:69
  97.8 41.6 %all-to-all-start.2 = ((bf16[4,6,64,512]{3,2,1,0:T(8,128)(2,1)}), bf16[4,6,64,512]{3,2,1,0:T(8,128)(2,1)}, u32[]{:S(2)}, u32[]{:S(2)}) async-start(bf16[4,6,64,512]{3,2,1,0:T(8,128)(2,1)} %broadcast_in_dim.33), calls=%async_computation.2 | async-start | bytes 3145728 | tf_op jit(solution)/shard_map/all_to_all | solution.py:82
  102.1 36.4 %collective-permute-start.3 = (bf16[4,6,64,512]{3,2,1,0:T(8,128)(2,1)}, bf16[4,6,64,512]{3,2,1,0:T(8,128)(2,1)}, u32[]{:S(2)}, u32[]{:S(2)}) collective-permute-start(bf16[4,6,64,512]{3,2,1,0:T(8,128)(2,1)} %copy-done.12), channel_id=1, source_target_pairs={{1,0},{0,1},{3,2},{2,3},{5,4},{4,5},{7,6},{6,7},{9,8},{8,9},{11,10... | collective-permute-start | bytes 4718600 | tf_op jit(solution)/shard_map/ppermute | solution.py:69
  141.6 58.9 %collective-permute-start.5 = (bf16[2,4,6,64,512]{4,3,2,1,0:T(8,128)(2,1)S(1)}, bf16[2,4,6,64,512]{4,3,2,1,0:T(8,128)(2,1)}, u32[]{:S(2)}, u32[]{:S(2)}) collective-permute-start(bf16[2,4,6,64,512]{4,3,2,1,0:T(8,128)(2,1)S(1)} %pad_maximum_fusion.1.refs_0_.refs_2_), channel_id=1, source_target_pairs={{8,0},{0,8},{24,16},{16,24},{9,1},{1,9},{25,17},{17,25},{10,2},{2,... | collective-permute-start | bytes 9437192 | tf_op jit(solution)/shard_map/ppermute | solution.py:69
  143.7 56.7 %all-to-all-start.3 = ((bf16[4,6,64,512]{3,2,1,0:T(8,128)(2,1)}), bf16[4,6,64,512]{3,2,1,0:T(8,128)(2,1)}, u32[]{:S(2)}, u32[]{:S(2)}) async-start(bf16[4,6,64,512]{3,2,1,0:T(8,128)(2,1)} %broadcast_in_dim.34), calls=%async_computation.3 | async-start | bytes 3145728 | tf_op jit(solution)/shard_map/all_to_all | solution.py:82
  148.2 37.1 %collective-permute-start.6 = (bf16[4,6,64,512]{3,2,1,0:T(8,128)(2,1)}, bf16[4,6,64,512]{3,2,1,0:T(8,128)(2,1)}, u32[]{:S(2)}, u32[]{:S(2)}) collective-permute-start(bf16[4,6,64,512]{3,2,1,0:T(8,128)(2,1)} %all-to-all-done.2), channel_id=1, source_target_pairs={{1,0},{0,1},{3,2},{2,3},{5,4},{4,5},{7,6},{6,7},{9,8},{8,9},{11,10... | collective-permute-start | bytes 4718600 | tf_op jit(solution)/shard_map/ppermute | solution.py:69
  163.2 37.2 %collective-permute-start.8 = (bf16[256,2048]{1,0:T(8,128)(2,1)}, bf16[256,2048]{1,0:T(8,128)(2,1)}, u32[]{:S(2)}, u32[]{:S(2)}) collective-permute-start(bf16[256,2048]{1,0:T(8,128)(2,1)} %get-tuple-element.500.refs_0_.refs_4_), channel_id=1, source_target_pairs={{16,0},{24,8},{0,16},{8,24},{17,1},{25,9},{1,17},{9,25},{18,2},{26... | collective-permute-start | bytes 3145736 | tf_op jit(solution)/shard_map/ppermute | solution.py:69
  163.8 36.6 %collective-permute-start.9 = (bf16[256,2048]{1,0:T(8,128)(2,1)}, bf16[256,2048]{1,0:T(8,128)(2,1)}, u32[]{:S(2)}, u32[]{:S(2)}) collective-permute-start(bf16[256,2048]{1,0:T(8,128)(2,1)} %get-tuple-element.500.refs_0_.refs_4_), channel_id=1, source_target_pairs={{8,0},{0,8},{24,16},{16,24},{9,1},{1,9},{25,17},{17,25},{10,2},{2,... | collective-permute-start | bytes 3145736 | tf_op jit(solution)/shard_map/ppermute | solution.py:69
  202.7 46.1 %collective-permute-start.11 = (bf16[2,4,6,64,512]{4,3,2,1,0:T(8,128)(2,1)S(1)}, bf16[2,4,6,64,512]{4,3,2,1,0:T(8,128)(2,1)}, u32[]{:S(2)}, u32[]{:S(2)}) collective-permute-start(bf16[2,4,6,64,512]{4,3,2,1,0:T(8,128)(2,1)S(1)} %pad_maximum_fusion.2.refs_0_.refs_2_), channel_id=1, source_target_pairs={{8,0},{0,8},{24,16},{16,24},{9,1},{1,9},{25,17},{17,25},{10,2},{2,... | collective-permute-start | bytes 9437192 | tf_op jit(solution)/shard_map/ppermute | solution.py:69
  204.8 43.9 %all-to-all-start.4 = ((bf16[4,6,64,512]{3,2,1,0:T(8,128)(2,1)}), bf16[4,6,64,512]{3,2,1,0:T(8,128)(2,1)}, u32[]{:S(2)}, u32[]{:S(2)}) async-start(bf16[4,6,64,512]{3,2,1,0:T(8,128)(2,1)} %broadcast_in_dim.36), calls=%async_computation.4 | async-start | bytes 3145728 | tf_op jit(solution)/shard_map/all_to_all | solution.py:82
  210.4 38.3 %collective-permute-start.12 = (bf16[4,6,64,512]{3,2,1,0:T(8,128)(2,1)}, bf16[4,6,64,512]{3,2,1,0:T(8,128)(2,1)}, u32[]{:S(2)}, u32[]{:S(2)}) collective-permute-start(bf16[4,6,64,512]{3,2,1,0:T(8,128)(2,1)} %all-to-all-done.3), channel_id=1, source_target_pairs={{1,0},{0,1},{3,2},{2,3},{5,4},{4,5},{7,6},{6,7},{9,8},{8,9},{11,10... | collective-permute-start | bytes 4718600 | tf_op jit(solution)/shard_map/ppermute | solution.py:69
  214.1 34.7 %collective-permute-start.10 = (bf16[2,4,2,64,512]{4,3,2,1,0:T(8,128)(2,1)S(1)}, bf16[2,4,2,64,512]{4,3,2,1,0:T(8,128)(2,1)}, u32[]{:S(2)}, u32[]{:S(2)}) collective-permute-start(bf16[2,4,2,64,512]{4,3,2,1,0:T(8,128)(2,1)S(1)} %fusion.6), channel_id=1, source_target_pairs={{16,0},{24,8},{0,16},{8,24},{17,1},{25,9},{1,17},{9,25},{18,2},{26... | collective-permute-start | bytes 3145736 | tf_op jit(solution)/shard_map/ppermute | solution.py:69
  251.0 37.2 %collective-permute-start.16 = (bf16[2,4,6,64,512]{4,3,2,1,0:T(8,128)(2,1)S(1)}, bf16[2,4,6,64,512]{4,3,2,1,0:T(8,128)(2,1)}, u32[]{:S(2)}, u32[]{:S(2)}) collective-permute-start(bf16[2,4,6,64,512]{4,3,2,1,0:T(8,128)(2,1)S(1)} %pad_maximum_fusion.3.refs_0_.refs_2_), channel_id=1, source_target_pairs={{8,0},{0,8},{24,16},{16,24},{9,1},{1,9},{25,17},{17,25},{10,2},{2,... | collective-permute-start | bytes 9437192 | tf_op jit(solution)/shard_map/ppermute | solution.py:69
  251.1 37.1 %collective-permute-start.17 = (bf16[4,6,64,512]{3,2,1,0:T(8,128)(2,1)}, bf16[4,6,64,512]{3,2,1,0:T(8,128)(2,1)}, u32[]{:S(2)}, u32[]{:S(2)}) collective-permute-start(bf16[4,6,64,512]{3,2,1,0:T(8,128)(2,1)} %all-to-all-done.4), channel_id=1, source_target_pairs={{1,0},{0,1},{3,2},{2,3},{5,4},{4,5},{7,6},{6,7},{9,8},{8,9},{11,10... | collective-permute-start | bytes 4718600 | tf_op jit(solution)/shard_map/ppermute | solution.py:69
  253.8 34.5 %all-to-all-start.5 = ((bf16[4,4,64,512]{3,2,1,0:T(8,128)(2,1)}), bf16[4,4,64,512]{3,2,1,0:T(8,128)(2,1)}, u32[]{:S(2)}, u32[]{:S(2)}) async-start(bf16[4,4,64,512]{3,2,1,0:T(8,128)(2,1)} %broadcast_in_dim.39), calls=%async_computation.5 | async-start | bytes 2097152 | tf_op jit(solution)/shard_map/all_to_all | solution.py:82
  288.2 59.6 %all-to-all-start.6 = ((bf16[8,128,1024]{2,1,0:T(8,128)(2,1)}), bf16[8,128,1024]{2,1,0:T(8,128)(2,1)}, u32[]{:S(2)}, u32[]{:S(2)}) async-start(bf16[8,128,1024]{2,1,0:T(8,128)(2,1)} %pad.11), calls=%async_computation.6 | async-start | bytes 4194304 | tf_op jit(solution)/shard_map/all_to_all | solution.py:986
  296.5 51.4 %collective-permute-start.20 = (bf16[2,4,6,64,512]{4,3,2,1,0:T(8,128)(2,1)S(1)}, bf16[2,4,6,64,512]{4,3,2,1,0:T(8,128)(2,1)S(1)}, u32[]{:S(2)}, u32[]{:S(2)}) collective-permute-start(bf16[2,4,6,64,512]{4,3,2,1,0:T(8,128)(2,1)S(1)} %pad_maximum_fusion.4.refs_0_.refs_2_), channel_id=1, source_target_pairs={{8,0},{0,8},{24,16},{16,24},{9,1},{1,9},{25,17},{17,25},{10,2},{2,... | collective-permute-start | bytes 9437192 | tf_op jit(solution)/shard_map/ppermute | solution.py:69
  300.9 40.7 %collective-permute-start.21 = (bf16[4,4,64,512]{3,2,1,0:T(8,128)(2,1)}, bf16[4,4,64,512]{3,2,1,0:T(8,128)(2,1)}, u32[]{:S(2)}, u32[]{:S(2)}) collective-permute-start(bf16[4,4,64,512]{3,2,1,0:T(8,128)(2,1)} %all-to-all-done.5), channel_id=1, source_target_pairs={{1,0},{0,1},{3,2},{2,3},{5,4},{4,5},{7,6},{6,7},{9,8},{8,9},{11,10... | collective-permute-start | bytes 3145736 | tf_op jit(solution)/shard_map/ppermute | solution.py:69
  313.6 34.2 %collective-permute-start.23 = (bf16[256,2048]{1,0:T(8,128)(2,1)}, bf16[256,2048]{1,0:T(8,128)(2,1)}, u32[]{:S(2)}, u32[]{:S(2)}) collective-permute-start(bf16[256,2048]{1,0:T(8,128)(2,1)} %get-tuple-element.545.refs_0_.refs_4_), channel_id=1, source_target_pairs={{16,0},{24,8},{0,16},{8,24},{17,1},{25,9},{1,17},{9,25},{18,2},{26... | collective-permute-start | bytes 3145736 | tf_op jit(solution)/shard_map/ppermute | solution.py:69
  314.6 33.3 %collective-permute-start.24 = (bf16[256,2048]{1,0:T(8,128)(2,1)}, bf16[256,2048]{1,0:T(8,128)(2,1)}, u32[]{:S(2)}, u32[]{:S(2)}) collective-permute-start(bf16[256,2048]{1,0:T(8,128)(2,1)} %get-tuple-element.545.refs_0_.refs_4_), channel_id=1, source_target_pairs={{8,0},{0,8},{24,16},{16,24},{9,1},{1,9},{25,17},{17,25},{10,2},{2,... | collective-permute-start | bytes 3145736 | tf_op jit(solution)/shard_map/ppermute | solution.py:69
  349.5 55.1 %all-to-all-start.7 = ((bf16[8,128,1024]{2,1,0:T(8,128)(2,1)}), bf16[8,128,1024]{2,1,0:T(8,128)(2,1)}, u32[]{:S(2)}, u32[]{:S(2)}) async-start(bf16[8,128,1024]{2,1,0:T(8,128)(2,1)} %pad.10), calls=%async_computation.7 | async-start | bytes 4194304 | tf_op jit(solution)/shard_map/all_to_all | solution.py:986
  357.3 46.1 %collective-permute-start.25 = (bf16[2,4,4,64,512]{4,3,2,1,0:T(8,128)(2,1)S(1)}, bf16[2,4,4,64,512]{4,3,2,1,0:T(8,128)(2,1)S(1)}, u32[]{:S(2)}, u32[]{:S(2)}) collective-permute-start(bf16[2,4,4,64,512]{4,3,2,1,0:T(8,128)(2,1)S(1)} %pad_maximum_fusion.5.refs_0_.refs_2_), channel_id=1, source_target_pairs={{16,0},{24,8},{0,16},{8,24},{17,1},{25,9},{1,17},{9,25},{18,2},{26... | collective-permute-start | bytes 6291464 | tf_op jit(solution)/shard_map/ppermute | solution.py:69
  357.9 46.8 %collective-permute-start.26 = (bf16[2,4,4,64,512]{4,3,2,1,0:T(8,128)(2,1)S(1)}, bf16[2,4,4,64,512]{4,3,2,1,0:T(8,128)(2,1)}, u32[]{:S(2)}, u32[]{:S(2)}) collective-permute-start(bf16[2,4,4,64,512]{4,3,2,1,0:T(8,128)(2,1)S(1)} %pad_maximum_fusion.5.refs_0_.refs_2_), channel_id=1, source_target_pairs={{8,0},{0,8},{24,16},{16,24},{9,1},{1,9},{25,17},{17,25},{10,2},{2,... | collective-permute-start | bytes 6291464 | tf_op jit(solution)/shard_map/ppermute | solution.py:69
  404.7 53.8 %all-to-all-start.8 = ((bf16[8,128,1024]{2,1,0:T(8,128)(2,1)}), bf16[8,128,1024]{2,1,0:T(8,128)(2,1)}, u32[]{:S(2)}, u32[]{:S(2)}) async-start(bf16[8,128,1024]{2,1,0:T(8,128)(2,1)} %pad.12), calls=%async_computation.8 | async-start | bytes 4194304 | tf_op jit(solution)/shard_map/all_to_all | solution.py:986
  411.1 47.3 %collective-permute-start.33 = (bf16[256,4096]{1,0:T(8,128)(2,1)}, bf16[256,4096]{1,0:T(8,128)(2,1)}, u32[]{:S(2)}, u32[]{:S(2)}) collective-permute-start(bf16[256,4096]{1,0:T(8,128)(2,1)} %get-tuple-element.517.act.refs_0_), channel_id=1, source_target_pairs={{8,0},{0,8},{24,16},{16,24},{9,1},{1,9},{25,17},{17,25},{10,2},{2,... | collective-permute-start | bytes 6291464 | tf_op jit(solution)/shard_map/ppermute | solution.py:69
  411.6 38.5 %collective-permute-start.30 = (bf16[256,4096]{1,0:T(8,128)(2,1)}, bf16[256,4096]{1,0:T(8,128)(2,1)}, u32[]{:S(2)}, u32[]{:S(2)}) collective-permute-start(bf16[256,4096]{1,0:T(8,128)(2,1)} %get-tuple-element.558.act.refs_0_), channel_id=1, source_target_pairs={{8,0},{0,8},{24,16},{16,24},{9,1},{1,9},{25,17},{17,25},{10,2},{2,... | collective-permute-start | bytes 6291464 | tf_op jit(solution)/shard_map/ppermute | solution.py:69
  413.1 45.4 %collective-permute-start.32 = (bf16[256,3072]{1,0:T(8,128)(2,1)}, bf16[256,3072]{1,0:T(8,128)(2,1)S(1)}, u32[]{:S(2)}, u32[]{:S(2)}) collective-permute-start(bf16[256,3072]{1,0:T(8,128)(2,1)} %pad_maximum_fusion.6), channel_id=1, source_target_pairs={{8,0},{0,8},{24,16},{16,24},{9,1},{1,9},{25,17},{17,25},{10,2},{2,... | collective-permute-start | bytes 4718600 | tf_op jit(solution)/shard_map/ppermute | solution.py:69
  414.8 43.7 %collective-permute-start.34 = (bf16[256,3072]{1,0:T(8,128)(2,1)}, bf16[256,3072]{1,0:T(8,128)(2,1)S(1)}, u32[]{:S(2)}, u32[]{:S(2)}) collective-permute-start(bf16[256,3072]{1,0:T(8,128)(2,1)} %pad_maximum_fusion.7), channel_id=1, source_target_pairs={{8,0},{0,8},{24,16},{16,24},{9,1},{1,9},{25,17},{17,25},{10,2},{2,... | collective-permute-start | bytes 4718600 | tf_op jit(solution)/shard_map/ppermute | solution.py:69
  488.4 35.2 %collective-permute-start.40 = (bf16[2,4,2,128,256]{4,3,2,1,0:T(8,128)(2,1)S(1)}, bf16[2,4,2,128,256]{4,3,2,1,0:T(8,128)(2,1)S(1)}, u32[]{:S(2)}, u32[]{:S(2)}) collective-permute-start(bf16[2,4,2,128,256]{4,3,2,1,0:T(8,128)(2,1)S(1)} %copy-done.88), channel_id=1, source_target_pairs={{16,0},{24,8},{0,16},{8,24},{17,1},{25,9},{1,17},{9,25},{18,2},{26... | collective-permute-start | bytes 3145736 | tf_op jit(solution)/shard_map/ppermute | solution.py:69
  490.0 33.7 %collective-permute-start.41 = (bf16[2,4,2,128,256]{4,3,2,1,0:T(8,128)(2,1)S(1)}, bf16[2,4,2,128,256]{4,3,2,1,0:T(8,128)(2,1)S(1)}, u32[]{:S(2)}, u32[]{:S(2)}) collective-permute-start(bf16[2,4,2,128,256]{4,3,2,1,0:T(8,128)(2,1)S(1)} %copy-done.87), channel_id=1, source_target_pairs={{1,0},{0,1},{3,2},{2,3},{5,4},{4,5},{7,6},{6,7},{9,8},{8,9},{11,10... | collective-permute-start | bytes 3145736 | tf_op jit(solution)/shard_map/ppermute | solution.py:69
  490.6 33.0 %collective-permute-start.39 = (bf16[4,2,256,128]{3,2,1,0:T(8,128)(2,1)S(1)}, bf16[4,2,256,128]{3,2,1,0:T(8,128)(2,1)S(1)}, u32[]{:S(2)}, u32[]{:S(2)}) collective-permute-start(bf16[4,2,256,128]{3,2,1,0:T(8,128)(2,1)S(1)} %get-tuple-element.970), channel_id=1, source_target_pairs={{16,0},{24,8},{0,16},{8,24},{17,1},{25,9},{1,17},{9,25},{18,2},{26... | collective-permute-start | bytes 1572872 | tf_op jit(solution)/shard_map/ppermute | solution.py:69
  635.4 34.4 %collective-permute-start.53 = (bf16[2,4,2,256,128]{4,3,2,1,0:T(8,128)(2,1)}, bf16[2,4,2,256,128]{4,3,2,1,0:T(8,128)(2,1)S(1)}, u32[]{:S(2)}, u32[]{:S(2)}) collective-permute-start(bf16[2,4,2,256,128]{4,3,2,1,0:T(8,128)(2,1)} %get-tuple-element.739), channel_id=1, source_target_pairs={{16,0},{24,8},{0,16},{8,24},{17,1},{25,9},{1,17},{9,25},{18,2},{26... | collective-permute-start | bytes 3145736 | tf_op jit(solution)/shard_map/ppermute | solution.py:69
  636.1 33.7 %collective-permute-start.54 = (bf16[2,4,2,256,128]{4,3,2,1,0:T(8,128)(2,1)}, bf16[2,4,2,256,128]{4,3,2,1,0:T(8,128)(2,1)S(1)}, u32[]{:S(2)}, u32[]{:S(2)}) collective-permute-start(bf16[2,4,2,256,128]{4,3,2,1,0:T(8,128)(2,1)} %get-tuple-element.740), channel_id=1, source_target_pairs={{1,0},{0,1},{3,2},{2,3},{5,4},{4,5},{7,6},{6,7},{9,8},{8,9},{11,10... | collective-permute-start | bytes 3145736 | tf_op jit(solution)/shard_map/ppermute | solution.py:69
  638.0 31.8 %collective-permute-start.52 = (bf16[4,2,128,256]{3,2,1,0:T(8,128)(2,1)S(1)}, bf16[4,2,128,256]{3,2,1,0:T(8,128)(2,1)S(1)}, u32[]{:S(2)}, u32[]{:S(2)}) collective-permute-start(bf16[4,2,128,256]{3,2,1,0:T(8,128)(2,1)S(1)} %get-tuple-element.962), channel_id=1, source_target_pairs={{16,0},{24,8},{0,16},{8,24},{17,1},{25,9},{1,17},{9,25},{18,2},{26... | collective-permute-start | bytes 1572872 | tf_op jit(solution)/shard_map/ppermute | solution.py:69
  673.3 48.8 %all-to-all-start.11 = ((bf16[4,4,128,256]{3,2,1,0:T(8,128)(2,1)}), bf16[4,4,128,256]{3,2,1,0:T(8,128)(2,1)S(1)}, u32[]{:S(2)}, u32[]{:S(2)}) async-start(bf16[4,4,128,256]{3,2,1,0:T(8,128)(2,1)} %pad_maximum_fusion.11), calls=%async_computation.11 | async-start | bytes 2097152 | tf_op jit(solution)/shard_map/all_to_all | solution.py:82
  685.7 36.4 %collective-permute-start.59 = (bf16[2,256,1024]{2,1,0:T(8,128)(2,1)}, bf16[2,256,1024]{2,1,0:T(8,128)(2,1)}, u32[]{:S(2)}, u32[]{:S(2)}) collective-permute-start(bf16[2,256,1024]{2,1,0:T(8,128)(2,1)} %get-tuple-element.936), channel_id=1, source_target_pairs={{16,0},{24,8},{0,16},{8,24},{17,1},{25,9},{1,17},{9,25},{18,2},{26... | collective-permute-start | bytes 3145736 | tf_op jit(solution)/shard_map/ppermute | solution.py:69
  687.6 34.5 %collective-permute-start.56 = (bf16[4,2,256,128]{3,2,1,0:T(8,128)(2,1)S(1)}, bf16[4,2,256,128]{3,2,1,0:T(8,128)(2,1)}, u32[]{:S(2)}, u32[]{:S(2)}) collective-permute-start(bf16[4,2,256,128]{3,2,1,0:T(8,128)(2,1)S(1)} %get-tuple-element.958), channel_id=1, source_target_pairs={{16,0},{24,8},{0,16},{8,24},{17,1},{25,9},{1,17},{9,25},{18,2},{26... | collective-permute-start | bytes 1572872 | tf_op jit(solution)/shard_map/ppermute | solution.py:69
  777.2 32.6 %all-to-all-start.13 = ((bf16[4,4,128,256]{3,2,1,0:T(8,128)(2,1)}), bf16[4,4,128,256]{3,2,1,0:T(8,128)(2,1)S(1)}, u32[]{:S(2)}, u32[]{:S(2)}) async-start(bf16[4,4,128,256]{3,2,1,0:T(8,128)(2,1)} %pad_maximum_fusion.13), calls=%async_computation.13 | async-start | bytes 2097152 | tf_op jit(solution)/shard_map/all_to_all | solution.py:82
  862.9 53.8 %all-to-all-start.15 = ((bf16[32,128,256]{2,1,0:T(8,128)(2,1)}), bf16[32,128,256]{2,1,0:T(8,128)(2,1)}, u32[]{:S(2)}, u32[]{:S(2)}) async-start(bf16[32,128,256]{2,1,0:T(8,128)(2,1)} %bitcast.168), calls=%async_computation.15 | async-start | bytes 4194304 | tf_op jit(solution)/shard_map/all_to_all | solution.py:1301
  869.3 38.9 %collective-permute-start.75 = (bf16[6,128,256]{2,1,0:T(8,128)(2,1)}, bf16[6,128,256]{2,1,0:T(8,128)(2,1)S(1)}, u32[]{:S(2)}, u32[]{:S(2)}) collective-permute-start(bf16[6,128,256]{2,1,0:T(8,128)(2,1)} %get-tuple-element.944), channel_id=1, source_target_pairs={{0,16},{8,24},{16,0},{24,8},{1,17},{9,25},{17,1},{25,9},{2,18},{10... | collective-permute-start | bytes 1179656 | tf_op jit(solution)/shard_map/ppermute | solution.py:1314
  869.6 38.6 %collective-permute-start.74 = (bf16[6,128,256]{2,1,0:T(8,128)(2,1)S(1)}, bf16[6,128,256]{2,1,0:T(8,128)(2,1)S(1)}, u32[]{:S(2)}, u32[]{:S(2)}) collective-permute-start(bf16[6,128,256]{2,1,0:T(8,128)(2,1)S(1)} %get-tuple-element.945), channel_id=1, source_target_pairs={{0,8},{8,0},{16,24},{24,16},{1,9},{9,1},{17,25},{25,17},{2,10},{10... | collective-permute-start | bytes 1179656 | tf_op jit(solution)/shard_map/ppermute | solution.py:1314
  932.4 56.2 %all-to-all-start.16 = ((bf16[8,128,1024]{2,1,0:T(8,128)(2,1)}), bf16[8,128,1024]{2,1,0:T(8,128)(2,1)S(1)}, u32[]{:S(2)}, u32[]{:S(2)}) async-start(bf16[8,128,1024]{2,1,0:T(8,128)(2,1)} %bitcast.180), calls=%async_computation.16 | async-start | bytes 4194304 | tf_op jit(solution)/shard_map/all_to_all | solution.py:991
  936.1 52.4 %collective-permute-start.77 = (f32[2,12288]{1,0:T(2,128)S(1)}, f32[2,12288]{1,0:T(2,128)S(1)}, u32[]{:S(2)}, u32[]{:S(2)}) collective-permute-start(f32[2,12288]{1,0:T(2,128)S(1)} %add.470), channel_id=1, source_target_pairs={{0,4},{1,5},{2,6},{3,7},{4,0},{5,1},{6,2},{7,3},{8,12},{9,13},{10,... | collective-permute-start | bytes 294920 | tf_op jit(solution)/shard_map/ppermute | solution.py:965
  992.3 35.4 %collective-permute-start.78 = (bf16[6,128,1024]{2,1,0:T(8,128)(2,1)}, bf16[6,128,1024]{2,1,0:T(8,128)(2,1)}, u32[]{:S(2)}, u32[]{:S(2)}) collective-permute-start(bf16[6,128,1024]{2,1,0:T(8,128)(2,1)} %subtract_convert_fusion.refs_0_), channel_id=1, source_target_pairs={{16,0},{24,8},{0,16},{8,24},{17,1},{25,9},{1,17},{9,25},{18,2},{26... | collective-permute-start | bytes 4718600 | tf_op jit(solution)/shard_map/ppermute | solution.py:69
  993.7 52.1 %all-to-all-start.17 = ((bf16[8,128,1024]{2,1,0:T(8,128)(2,1)}), bf16[8,128,1024]{2,1,0:T(8,128)(2,1)}, u32[]{:S(2)}, u32[]{:S(2)}) async-start(bf16[8,128,1024]{2,1,0:T(8,128)(2,1)} %bitcast.179), calls=%async_computation.17 | async-start | bytes 4194304 | tf_op jit(solution)/shard_map/all_to_all | solution.py:991
  (141 other events, 2213.4 us)

commit v6 on v5

--- a/solution.py
+++ b/solution.py
@@ -187,8 +187,8 @@
     x_at, y_at, core_at = where[0], where[1], where[2]
 
     def put(first_col, sources):
-        low_col = pl.ds(pl.multiple_of(first_col * half_cols, half_cols), half_cols)
-        high_col = pl.ds(pl.multiple_of((1 - first_col) * half_cols, half_cols), half_cols)
+        low_col = pl.ds(first_col * half_cols, half_cols)
+        high_col = pl.ds((1 - first_col) * half_cols, half_cols)
         for step_x in range(extent_x):
             for z in range(extent_z):
                 base = (z * extent_x + lax.rem(x_at + step_x, extent_x)) * 2
@@ -200,7 +200,9 @@
                 out[0, other, high_col] = sources[3][step_x, z, 0]
 
     if split:
-        pl.when(spot < split)(lambda: put(y_at, list(pieces[:2]) + list(pieces[4:])))
+        sources = list(pieces[:2]) + list(pieces[4:])
+        for y in range(2):
+            pl.when((spot < split) & (y_at == y))(functools.partial(put, y, sources))
         pl.when(spot >= split)(lambda: put(0, pieces[:4]))
     else:
         put(0, pieces[:4])
@@ -287,7 +289,7 @@
     )(chunk.where(), x_low, bias, *pieces)
 
 
-def head_probs(query_h, keys_h, masks):
+def head_weights(query_h, keys_h, masks):
     scores = [
         dot_t(key, query_h) + mask for key, mask in zip(keys_h, masks)
     ]
@@ -296,8 +298,7 @@
     )
     scores = [jnp.exp(score - peak) for score in scores]
     total = sum(jnp.sum(score, axis=0, keepdims=True) for score in scores)
-    inverse = 1.0 / total
-    return [score * inverse for score in scores]
+    return scores, 1.0 / total
 
 
 def dot_tt(left, right):
@@ -313,10 +314,11 @@
     masks = [mask[pl.ds(spot * tokens, tokens), :] for spot in range(count)]
     mixed = []
     for head in range(2):
-        probs = head_probs(head_of(query, head), [head_of(key, head) for key in keys], masks)
-        mixed.append(
-            sum(dot_tt(head_of(value, head), prob.astype(BF16)) for value, prob in zip(values, probs))
+        weights, inverse = head_weights(head_of(query, head), [head_of(key, head) for key in keys], masks)
+        total = sum(
+            dot_tt(head_of(value, head), weight.astype(BF16)) for value, weight in zip(values, weights)
         )
+        mixed.append(total * inverse)
     out[...] = jnp.concatenate(mixed, axis=0).T.astype(BF16)
 
 
@@ -357,7 +359,8 @@
         query_h = head_of(query, head)
         grad_h = head_of(grad, head)
         keys_h = [head_of(key, head) for key in keys]
-        probs = head_probs(query_h, keys_h, masks)
+        weights, inverse = head_weights(query_h, keys_h, masks)
+        probs = [weight * inverse for weight in weights]
         grad_probs = [dot_t(head_of(value, head), grad_h) for value in values]
         inner = sum(
             jnp.sum(prob * grad_prob, axis=0, keepdims=True)
@@ -586,7 +589,7 @@
 
     @pl.when(spot > 0)
     def _():
-        joined[...] = sum(part[0].astype(F32) for part in parts).astype(BF16)
+        joined[...] = sum(part[0, 0].astype(F32) for part in parts).astype(BF16)
 
     low = joined[...]
     sums[0] = column_sum(low.astype(F32))
@@ -604,7 +607,7 @@
         functools.partial(input_back_kernel, len(parts)),
         (3,),
         [full, full, pl.BlockSpec((1, BLK, BLK), lambda i: (i, 0, 0))]
-        + [pl.BlockSpec((1, tokens, D), lambda i: (jnp.maximum(i - 1, 0), 0, 0))] * len(parts),
+        + [pl.BlockSpec((1, 1, tokens, D), lambda i: (0, jnp.maximum(i - 1, 0), 0, 0))] * len(parts),
         [pl.BlockSpec((tokens, D), lambda i: (0, i)), full, pl.BlockSpec((1, 1, D), lambda i: (i, 0, 0))],
         [shaped((tokens, 3 * D), BF16), shaped((tokens, D), F32), shaped((3, 1, D), F32)],
         scratch=[pltpu.VMEM((tokens, D), F32)],
@@ -617,27 +620,35 @@
     return [value] + [place.take(value, axis, step) for step in range(1, place.size[axis])]
 
 
-def project_step(place, carried_low, chunk, vector):
+def vector_sets(vector):
     parts = vector_parts(vector)
-    bias_in = jnp.stack([parts[0], jnp.zeros((D,), F32), parts[1]])[:, None]
-    query, keyval, w_in = project(carried_low, chunk, bias_in)
+    return {
+        "project": jnp.stack([parts[0], jnp.zeros((D,), F32), parts[1]])[:, None],
+        "mix": jnp.stack([parts[2], parts[4], parts[5]]),
+        "up": parts[8].reshape(FF // BLK, 1, BLK),
+        "down": jnp.stack([parts[3], parts[6], parts[7]]),
+        "gain_one": parts[4][None],
+        "gain_two": parts[6][None],
+    }
+
+
+def project_step(place, carried_low, chunk, vectors):
+    query, keyval, w_in = project(carried_low, chunk, vectors["project"])
     keyvals = [keyval, *gather_list(place, keyval, "y")[1:], place.take(keyval, "core", 1)]
     return query, keyvals, w_in
 
 
-def mix_step(query, keyvals, carried, w_in, vector, mask):
-    parts = vector_parts(vector)
+def mix_step(query, keyvals, carried, w_in, vectors, mask):
     attn_low = attend(query, keyvals, mask)
-    return attn_low, *mix(attn_low, w_in, carried, jnp.stack([parts[2], parts[4], parts[5]]))
-
-
-def up_step(mid_low, chunk, vector):
-    return up(mid_low, chunk, vector[8 * D :].reshape(FF // BLK, 1, BLK))
-
-
-def down_step(act_low, chunk, middle, vector):
-    parts = vector_parts(vector)
-    return down(act_low, chunk, middle, jnp.stack([parts[3], parts[6], parts[7]]))
+    return attn_low, *mix(attn_low, w_in, carried, vectors["mix"])
+
+
+def up_step(mid_low, chunk, vectors):
+    return up(mid_low, chunk, vectors["up"])
+
+
+def down_step(act_low, chunk, middle, vectors):
+    return down(act_low, chunk, middle, vectors["down"])
 
 
 def sum_kernel(count_one, first_half, sizes, turned, where, *refs):
@@ -666,13 +677,12 @@
         pl.when(spot < count_one)(lambda: multiply(*sets[0]))
         pl.when(spot >= count_one)(lambda: multiply(*sets[1]))
 
-    def put(y_first):
+    def put(y_first, x, y):
         for step_y in range(extent_y):
-            from_col = pl.multiple_of(lax.rem(y_at + step_y, extent_y) * cols, cols)
+            from_col = (y + step_y) % extent_y * cols
             for step_x in range(extent_x):
                 for z in range(extent_z):
-                    row_block = z * extent_x + lax.rem(x_at + step_x, extent_x)
-                    from_row = pl.multiple_of(row_block * rows, rows)
+                    from_row = (z * extent_x + (x + step_x) % extent_x) * rows
                     if turned:
                         value = product[pl.ds(from_col, cols), pl.ds(from_row, rows)]
                     else:
@@ -682,8 +692,11 @@
                     else:
                         outs[extent_y + step_x][step_y, z, 0] = value
 
-    pl.when(spot < first_half)(lambda: put(True))
-    pl.when(spot >= first_half)(lambda: put(False))
+    for x in range(extent_x):
+        for y in range(extent_y):
+            here = (x_at == x) & (y_at == y)
+            pl.when(here & (spot < first_half))(functools.partial(put, True, x, y))
+            pl.when(here & (spot >= first_half))(functools.partial(put, False, x, y))
 
 
 def partial_sums(place, sets):
@@ -1027,7 +1040,7 @@
     chunks = [
         Gathering(place, weights[layer_at, first : first + 4], split_count)
         for layer_at, first, split_count in (
-            (0, 0, 2),
+            (0, 0, 3),
             (0, 4, 2),
             (0, 8, 2),
             (1, 0, 2),
@@ -1058,15 +1071,23 @@
 
     kept = [{}, {}]
     slot_own = jnp.minimum(lax.axis_index("wsh"), slots_dev - 1)
-    live["left"] = fill_up(left_bases, wsh_count)
-    live["first"] = fill_up(moment1, wsh_count)
-    live["second"] = fill_up(moment2, wsh_count)
-    live["right"] = lax.dynamic_index_in_dim(right_bases, slot_own, 0, False).astype(BF16)
+    live["bases"] = (left_bases, right_bases)
+    live["moments"] = (moment1, moment2)
     chunks[0].step_z()
     settle()
+    left_rows, right_all = live.pop("bases")
+    live["mask"] = mask
+    live["vectors"] = [vector_sets(vec_params[layer_at]) for layer_at in range(LAYERS)]
+    live["left"] = fill_up(left_rows, wsh_count)
+    live["right"] = lax.dynamic_index_in_dim(right_all, slot_own, 0, False).astype(BF16)
     chunks[0].step_x()
     chunks[1].step_z()
     settle()
+    first_rows, second_rows = live.pop("moments")
+    mask = live.pop("mask")
+    vectors = live.pop("vectors")
+    live["first"] = fill_up(first_rows, wsh_count)
+    live["second"] = fill_up(second_rows, wsh_count)
     chunks[0].step_y()
     chunks[1].step_x()
     chunks[2].step_z()
@@ -1074,7 +1095,7 @@
     chunks[1].step_y()
     chunks[2].step_x()
     chunks[3].step_z()
-    query_0, live["keyvals0"], w_in_0 = project_step(place, stream_in[0], finish(0), vec_params[0])
+    query_0, live["keyvals0"], w_in_0 = project_step(place, stream_in[0], finish(0), vectors[0])
     live["query"] = query_0
     settle()
     chunks[2].step_y()
@@ -1083,22 +1104,22 @@
     keyvals_0 = keyvals_of(0)
     query_0 = live["query"]
     attn_0, summed_one_0, middle_0, mid_low_0 = mix_step(
-        query_0, keyvals_0, stream_in[0], w_in_0, vec_params[0], mask
+        query_0, keyvals_0, stream_in[0], w_in_0, vectors[0], mask
     )
-    hidden_0, live["act"], w_up_0 = up_step(mid_low_0, finish(1), vec_params[0])
+    hidden_0, live["act"], w_up_0 = up_step(mid_low_0, finish(1), vectors[0])
     settle()
     chunks[3].step_y()
     chunks[4].step_x()
     chunks[5].step_z()
     act_0 = live["act"]
     summed_two_0, live["result"], live["result_low"], w_down_0 = down_step(
-        act_0, finish(2), middle_0, vec_params[0]
+        act_0, finish(2), middle_0, vectors[0]
     )
     settle()
     chunks[4].step_y()
     chunks[5].step_x()
     result_0, result_low_0 = live["result"], live["result_low"]
-    query_1, live["keyvals1"], w_in_1 = project_step(place, result_low_0, finish(3), vec_params[1])
+    query_1, live["keyvals1"], w_in_1 = project_step(place, result_low_0, finish(3), vectors[1])
     live["query"] = query_1
     live["left"] = to_owner(live["left"])
     settle()
@@ -1107,12 +1128,12 @@
     keyvals_1 = keyvals_of(1)
     query_1 = live["query"]
     attn_1, summed_one_1, middle_1, mid_low_1 = mix_step(
-        query_1, keyvals_1, result_0, w_in_1, vec_params[1], mask
+        query_1, keyvals_1, result_0, w_in_1, vectors[1], mask
     )
-    hidden_1, live["act"], w_up_1 = up_step(mid_low_1, finish(4), vec_params[1])
+    hidden_1, live["act"], w_up_1 = up_step(mid_low_1, finish(4), vectors[1])
     settle()
     act_1 = live["act"]
-    summed_two_1, _, result_low_1, w_down_1 = down_step(act_1, finish(5), middle_1, vec_params[1])
+    summed_two_1, _, result_low_1, w_down_1 = down_step(act_1, finish(5), middle_1, vectors[1])
     stream_out = result_low_1[None]
 
     blocks = [(w_in_0, w_up_0, w_down_0), (w_in_1, w_up_1, w_down_1)]
@@ -1129,8 +1150,7 @@
     queries = [query_0, query_1]
     keyvals_all = [keyvals_0, keyvals_1]
     gains = [
-        (vec_params[layer_at][None, 4 * D : 5 * D], vec_params[layer_at][None, 6 * D : 7 * D])
-        for layer_at in range(LAYERS)
+        (vectors[layer_at]["gain_one"], vectors[layer_at]["gain_two"]) for layer_at in range(LAYERS)
     ]
     live = {
         "crossed": crossed,
@@ -1195,9 +1215,9 @@
     def send_step():
         mine, other = live["pair"]
         arrived = place.take(other, "core", 1)
-        sums = [mine[step].astype(F32) + arrived[step].astype(F32) for step in range(count_y)]
-        live["kv"] = [sums[0]] + [
-            place.take(sums[step].astype(BF16), "y", -step) for step in range(1, count_y)
+        live["kv"] = [mine, arrived] + [
+            place.take((mine[step].astype(F32) + arrived[step].astype(F32)).astype(BF16), "y", -step)[None]
+            for step in range(1, count_y)
         ]
 
     def input_step(layer_at):

time: 1060 us -> 1050 us (level)
    all_to_all x12, waiting for transfers between devices: 22.4 us -> 46.4 us  [swap_z(): lax.all_to_all(values, 'wsh', 0, 0, tiled=True, axis_index_groups=lines)]
    ppermute x76, waiting for transfers between devices: 324 us -> 306 us  [take(): return lax.ppermute(value, name, pairs)]
    unnamed x216 -> x218, local copies, waits for them, and re-layouts: 45.6 us -> 38.9 us
  transfers between devices with their start and end apart: 99 -> 99, of which waited for: 49 -> 52; matrix products, arithmetic and copies ran while one was open for 10% -> 8% of each run, Pallas kernels for 24% -> 24%
where the time goes in v6:
time: 1050 us; the launch traced here: 1040 us
  waiting for transfers between devices  464 us (44%)
  Pallas kernels  275 us (26%)
  starting transfers between devices  141 us (13%)
  local copies, waits for them, and re-layouts  78.6 us (7%)
  other arithmetic  78 us (7%)
    ppermute x76, waiting for transfers between devices, take(): return lax.ppermute(value, name, pairs)  306 us
    ppermute x2, waiting for transfers between devices, step(): self.terms = [value, lax.ppermute(value, 'wsh', swap)]  62.3 us
    all_to_all x12, starting transfers between devices, swap_z(): lax.all_to_all(values, 'wsh', 0, 0, tiled=True, axis_index_groups=lines)  56 us
    ppermute x76, starting transfers between devices, take(): return lax.ppermute(value, name, pairs)  50.4 us
    pallas_call x6, Pallas kernels, partial_sums(): call(functools.partial(sum_kernel, counts[0] if len(sets) > 1 else None,...  48.8 us
    all_to_all x12, waiting for transfers between devices, swap_z(): lax.all_to_all(values, 'wsh', 0, 0, tiled=True, axis_index_groups=lines)  46.4 us
    pallas_call x2, Pallas kernels, attend_back(): call(functools.partial(attend_back_kernel, count, count_y, tokens), (D //...  42.6 us
    unnamed x218, local copies, waits for them, and re-layouts  38.9 us
  transfers between devices with their start and end apart: 99, of which 52 were waited for; matrix products, arithmetic and copies ran while one was open for 8% of the time, Pallas kernels for 24%

profile of v6, /device:TPU:0, one launch (start us, length us, event | category | flops | bytes accessed | tf_op | source)
XLA Modules:
  0.0 1039.8 jit_solution(7712833799029224468)
XLA Ops:
  7.4 6.3 all-to-all-start
  25.1 19.9 %all-to-all-done = bf16[4,5,64,512]{3,2,1,0:T(8,128)(2,1)S(1)} async-done(((bf16[4,5,64,512]{3,2,1,0:T(8,128)(2,1)}), bf16[4,5,64,512]{3,2,1,0:T(8,128)(2,1)S(1)}, u32[]{:S(2)}, u32[]{:S(2)}) %all-to-all-start) | async-done | bytes 1310752 | tf_op jit(solution)/shard_map/all_to_all | solution.py:82
  64.6 19.0 %collective-permute-done = bf16[4,5,64,512]{3,2,1,0:T(8,128)(2,1)} collective-permute-done((bf16[4,5,64,512]{3,2,1,0:T(8,128)(2,1)S(1)}, bf16[4,5,64,512]{3,2,1,0:T(8,128)(2,1)}, u32[]{:S(2)}, u32[]{:S(2)}) %collective-permute-start) | collective-permute-done | bytes 1310752 | tf_op jit(solution)/shard_map/ppermute | solution.py:69
  108.5 26.7 %collective-permute-done.1.refs_4_ = bf16[2,4,3,64,512]{4,3,2,1,0:T(8,128)(2,1)} collective-permute-done((bf16[2,4,3,64,512]{4,3,2,1,0:T(8,128)(2,1)S(1)}, bf16[2,4,3,64,512]{4,3,2,1,0:T(8,128)(2,1)}, u32[]{:S(2)}, u32[]{:S(2)}) %collective-permute-start.1) | collective-permute-done | bytes 1572896 | tf_op jit(solution)/shard_map/ppermute | solution.py:69
  150.2 10.0 project.2
  161.8 14.0 %collective-permute-done.4.refs_4_ = bf16[2,4,2,64,512]{4,3,2,1,0:T(8,128)(2,1)S(1)} collective-permute-done((bf16[2,4,2,64,512]{4,3,2,1,0:T(8,128)(2,1)S(1)}, bf16[2,4,2,64,512]{4,3,2,1,0:T(8,128)(2,1)S(1)}, u32[]{:S(2)}, u32[]{:S(2)}) %collective-permute-start.4) | collective-permute-done | bytes 1048608 | tf_op jit(solution)/shard_map/ppermute | solution.py:69
  182.6 14.0 %collective-permute-done.8.refs_1_.refs_5_ = bf16[256,2048]{1,0:T(8,128)(2,1)} collective-permute-done((bf16[256,2048]{1,0:T(8,128)(2,1)}, bf16[256,2048]{1,0:T(8,128)(2,1)}, u32[]{:S(2)}, u32[]{:S(2)}) %collective-permute-start.8) | collective-permute-done | bytes 1048608 | tf_op jit(solution)/shard_map/ppermute | solution.py:69
  210.7 13.8 %attend.2.attn.refs_4_ = bf16[256,1024]{1,0:T(8,128)(2,1)} custom-call(bf16[256,1024]{1,0:T(8,128)(2,1)} %get-tuple-element.515.query, f32[1024,256]{1,0:T(8,128)} %compare_select_fusion.mask, bf16[256,2048]{1,0:T(8,128)(2,1)} %get-tuple-element.517.refs_0_.refs_4_, bf16[256,2048]{1,0:T(8,128)(2,1)} %collective-permute-done.8.refs_1_.refs_5_, ...), custom_call_target="tpu_custom_call" | custom-call | flops 280000000 | tf_op jit(solution)/shard_map/attend/pallas_call | solution.py:338
  229.6 11.5 %up.2 = (f32[256,4096]{1,0:T(8,128)}, bf16[256,4096]{1,0:T(8,128)(2,1)}, bf16[4,1024,1024]{2,1,0:T(8,128)(2,1)}) custom-call(s32[3]{0:T(128)} %pad_add_fusion.1.where, bf16[256,1024]{1,0:T(8,128)(2,1)} %get-tuple-element.522.middle_low.refs_0_, f32[4,1,1024]{2,1,0:T(1,128)} %bitcast.183, bf16[2,4,6,64,512]{4,3,2,1,0:T(8,128)(2,1)} %copy-done.1, ...), custom_call_target="tpu_custom_call" | custom-call | flops 160000000 | tf_op jit(solution)/shard_map/up/pallas_call | solution.py:441
  255.6 11.3 %down.2 = (f32[256,1024]{1,0:T(8,128)}, f32[256,1024]{1,0:T(8,128)}, bf16[256,1024]{1,0:T(8,128)(2,1)}, bf16[4,1024,1024]{2,1,0:T(8,128)(2,1)}) custom-call(s32[3]{0:T(128)} %pad_add_fusion.1.where, bf16[256,4096]{1,0:T(8,128)(2,1)} %get-tuple-element.536.act.refs_0_, f32[256,1024]{1,0:T(8,128)} %get-tuple-element.539.middle, ...), custom_call_target="tpu_custom_call" | custom-call | flops 160000000 | tf_op jit(solution)/shard_map/down/pallas_call | solution.py:481
  266.8 11.9 %collective-permute-done.15.refs_4_ = bf16[2,4,2,64,512]{4,3,2,1,0:T(8,128)(2,1)} collective-permute-done((bf16[2,4,2,64,512]{4,3,2,1,0:T(8,128)(2,1)S(1)}, bf16[2,4,2,64,512]{4,3,2,1,0:T(8,128)(2,1)}, u32[]{:S(2)}, u32[]{:S(2)}) %collective-permute-start.15) | collective-permute-done | bytes 1048608 | tf_op jit(solution)/shard_map/ppermute | solution.py:69
  297.2 9.1 project.3
  307.0 11.9 %collective-permute-done.19.refs_4_ = bf16[2,4,2,64,512]{4,3,2,1,0:T(8,128)(2,1)} collective-permute-done((bf16[2,4,2,64,512]{4,3,2,1,0:T(8,128)(2,1)}, bf16[2,4,2,64,512]{4,3,2,1,0:T(8,128)(2,1)}, u32[]{:S(2)}, u32[]{:S(2)}) %collective-permute-start.19) | collective-permute-done | bytes 1048608 | tf_op jit(solution)/shard_map/ppermute | solution.py:69
  318.9 15.4 %collective-permute-done.21 = bf16[4,4,64,512]{3,2,1,0:T(8,128)(2,1)} collective-permute-done((bf16[4,4,64,512]{3,2,1,0:T(8,128)(2,1)}, bf16[4,4,64,512]{3,2,1,0:T(8,128)(2,1)}, u32[]{:S(2)}, u32[]{:S(2)}) %collective-permute-start.21) | collective-permute-done | bytes 1048608 | tf_op jit(solution)/shard_map/ppermute | solution.py:69
  356.5 13.7 %attend.3.attn.refs_4_ = bf16[256,1024]{1,0:T(8,128)(2,1)} custom-call(bf16[256,1024]{1,0:T(8,128)(2,1)} %get-tuple-element.565.query, f32[1024,256]{1,0:T(8,128)} %compare_select_fusion.mask, bf16[256,2048]{1,0:T(8,128)(2,1)} %get-tuple-element.566.refs_0_.refs_4_, bf16[256,2048]{1,0:T(8,128)(2,1)} %collective-permute-done.23.refs_1_.refs_5_, ...), custom_call_target="tpu_custom_call" | custom-call | flops 280000000 | tf_op jit(solution)/shard_map/attend/pallas_call | solution.py:338
  375.5 11.5 %up.3 = (f32[256,4096]{1,0:T(8,128)}, bf16[256,4096]{1,0:T(8,128)(2,1)}, bf16[4,1024,1024]{2,1,0:T(8,128)(2,1)}) custom-call(s32[3]{0:T(128)} %pad_add_fusion.1.where, bf16[256,1024]{1,0:T(8,128)(2,1)} %get-tuple-element.571.middle_low.refs_0_, f32[4,1,1024]{2,1,0:T(1,128)} %bitcast.182, bf16[2,4,6,64,512]{4,3,2,1,0:T(8,128)(2,1)} %copy-done.3, ...), custom_call_target="tpu_custom_call" | custom-call | flops 160000000 | tf_op jit(solution)/shard_map/up/pallas_call | solution.py:441
  387.0 8.3 collective-permute-done.25.refs_4_
  410.7 11.9 %down.3 = (f32[256,1024]{1,0:T(8,128)}, f32[256,1024]{1,0:T(8,128)}, bf16[256,1024]{1,0:T(8,128)(2,1)}, bf16[4,1024,1024]{2,1,0:T(8,128)(2,1)}) custom-call(s32[3]{0:T(128)} %pad_add_fusion.1.where, bf16[256,4096]{1,0:T(8,128)(2,1)} %get-tuple-element.581.act.refs_0_, f32[256,1024]{1,0:T(8,128)} %get-tuple-element.582.middle, ...), custom_call_target="tpu_custom_call" | custom-call | flops 160000000 | tf_op jit(solution)/shard_map/down/pallas_call | solution.py:481
  426.6 15.1 %feed_back.2 = (bf16[256,4096]{1,0:T(8,128)(2,1)}, bf16[256,1024]{1,0:T(8,128)(2,1)}, bf16[256,1024]{1,0:T(8,128)(2,1)}, f32[256,1024]{1,0:T(8,128)}, f32[8,1024]{1,0:T(8,128)}, /*index=5*/f32[4,1,1024]{2,1,0:T(1,128)}) custom-call(f32[256,1024]{1,0:T(8,128)} %get-tuple-element.595.grad_two, bf16[256,1024]{1,0:T(8,128)(2,1)} %get-tuple-element.590.refs_2_.ffn_low, ...), custom_call_target="tpu_custom_call" | custom-call | flops 300000000 | tf_op jit(solution)/shard_map/feed_back/pallas_call | solution.py:562
  441.8 8.1 partial_sums.6
  455.7 7.7 partial_sums.7
  463.4 12.5 %collective-permute-done.35 = bf16[2,4,2,256,128]{4,3,2,1,0:T(8,128)(2,1)} collective-permute-done((bf16[2,4,2,256,128]{4,3,2,1,0:T(8,128)(2,1)}, bf16[2,4,2,256,128]{4,3,2,1,0:T(8,128)(2,1)}, u32[]{:S(2)}, u32[]{:S(2)}) %collective-permute-start.35) | collective-permute-done | bytes 1048608 | tf_op jit(solution)/shard_map/ppermute | solution.py:69
  482.8 21.4 %attend_back.2 = (bf16[256,1024]{1,0:T(8,128)(2,1)}, bf16[2,2,256,1024]{3,2,1,0:T(8,128)(2,1)}, bf16[2,2,256,1024]{3,2,1,0:T(8,128)(2,1)}) custom-call(bf16[256,1024]{1,0:T(8,128)(2,1)} %get-tuple-element.565.query, bf16[256,1024]{1,0:T(8,128)(2,1)} %get-tuple-element.642.grad, f32[1024,256]{1,0:T(8,128)} %compare_select_fusion.mask, ...), custom_call_target="tpu_custom_call" | custom-call | flops 420000000 | tf_op jit(solution)/shard_map/attend_back/pallas_call | solution.py:389
  504.2 10.9 %collective-permute-done.39 = bf16[4,2,256,128]{3,2,1,0:T(8,128)(2,1)S(1)} collective-permute-done((bf16[4,2,256,128]{3,2,1,0:T(8,128)(2,1)S(1)}, bf16[4,2,256,128]{3,2,1,0:T(8,128)(2,1)S(1)}, u32[]{:S(2)}, u32[]{:S(2)}) %collective-permute-start.39) | collective-permute-done | bytes 524320 | tf_op jit(solution)/shard_map/ppermute | solution.py:69
  527.3 13.2 %collective-permute-done.42 = bf16[4,2,128,256]{3,2,1,0:T(8,128)(2,1)S(1)} collective-permute-done((bf16[4,2,128,256]{3,2,1,0:T(8,128)(2,1)S(1)}, bf16[4,2,128,256]{3,2,1,0:T(8,128)(2,1)S(1)}, u32[]{:S(2)}, u32[]{:S(2)}) %collective-permute-start.42) | collective-permute-done | bytes 524320 | tf_op jit(solution)/shard_map/ppermute | solution.py:69
  540.5 8.0 all-to-all-done.9.refs_0_
  553.5 7.9 input_back.2
  574.5 8.2 partial_sums.9
  583.4 8.5 partial_sums.8
  600.0 15.2 %feed_back.3 = (bf16[256,4096]{1,0:T(8,128)(2,1)}, bf16[256,1024]{1,0:T(8,128)(2,1)}, bf16[256,1024]{1,0:T(8,128)(2,1)}, f32[256,1024]{1,0:T(8,128)}, f32[8,1024]{1,0:T(8,128)}, /*index=5*/f32[4,1,1024]{2,1,0:T(1,128)}) custom-call(f32[256,1024]{1,0:T(8,128)} %get-tuple-element.743.grad_two, bf16[256,1024]{1,0:T(8,128)(2,1)} %get-tuple-element.744.refs_2_.ffn_low, ...), custom_call_target="tpu_custom_call" | custom-call | flops 300000000 | tf_op jit(solution)/shard_map/feed_back/pallas_call | solution.py:562
  615.2 7.5 collective-permute-done.49
  630.4 21.2 %attend_back.3 = (bf16[256,1024]{1,0:T(8,128)(2,1)}, bf16[2,2,256,1024]{3,2,1,0:T(8,128)(2,1)}, bf16[2,2,256,1024]{3,2,1,0:T(8,128)(2,1)}) custom-call(bf16[256,1024]{1,0:T(8,128)(2,1)} %get-tuple-element.515.query, bf16[256,1024]{1,0:T(8,128)(2,1)} %get-tuple-element.772.grad, f32[1024,256]{1,0:T(8,128)} %compare_select_fusion.mask, ...), custom_call_target="tpu_custom_call" | custom-call | flops 420000000 | tf_op jit(solution)/shard_map/attend_back/pallas_call | solution.py:389
  651.6 8.0 collective-permute-done.52
  675.7 7.8 partial_sums.10
  684.3 25.3 %collective-permute-done.56 = bf16[4,2,256,128]{3,2,1,0:T(8,128)(2,1)} collective-permute-done((bf16[4,2,256,128]{3,2,1,0:T(8,128)(2,1)S(1)}, bf16[4,2,256,128]{3,2,1,0:T(8,128)(2,1)}, u32[]{:S(2)}, u32[]{:S(2)}) %collective-permute-start.56) | collective-permute-done | bytes 524320 | tf_op jit(solution)/shard_map/ppermute | solution.py:69
  722.7 7.9 input_back.3
  731.4 13.1 %collective-permute-done.60 = bf16[2,4,2,128,256]{4,3,2,1,0:T(8,128)(2,1)S(1)} collective-permute-done((bf16[2,4,2,128,256]{4,3,2,1,0:T(8,128)(2,1)}, bf16[2,4,2,128,256]{4,3,2,1,0:T(8,128)(2,1)S(1)}, u32[]{:S(2)}, u32[]{:S(2)}) %collective-permute-start.60) | collective-permute-done | bytes 1048608 | tf_op jit(solution)/shard_map/ppermute | solution.py:69
  752.6 8.5 partial_sums.11
  772.9 23.7 %collective-permute-done.69 = f32[2,12288]{1,0:T(2,128)S(1)} collective-permute-done((f32[2,12288]{1,0:T(2,128)S(1)}, f32[2,12288]{1,0:T(2,128)S(1)}, u32[]{:S(2)}, u32[]{:S(2)}) %collective-permute-start.69) | collective-permute-done | bytes 98336 | tf_op jit(solution)/shard_map/ppermute | solution.py:69
  804.3 9.9 collective-permute-done.72
  824.3 12.8 %collective-permute-done.73 = f32[2,12288]{1,0:T(2,128)S(1)} collective-permute-done((f32[2,12288]{1,0:T(2,128)S(1)}, f32[2,12288]{1,0:T(2,128)S(1)}, u32[]{:S(2)}, u32[]{:S(2)}) %collective-permute-start.73) | collective-permute-done | bytes 98336 | tf_op jit(solution)/shard_map/ppermute | solution.py:978
  837.1 6.6 all-to-all-done.14.refs_5_
  857.2 28.2 %collective-permute-done.76 = bf16[6,128,256]{2,1,0:T(8,128)(2,1)S(1)} collective-permute-done((bf16[6,128,256]{2,1,0:T(8,128)(2,1)}, bf16[6,128,256]{2,1,0:T(8,128)(2,1)S(1)}, u32[]{:S(2)}, u32[]{:S(2)}) %collective-permute-start.76) | collective-permute-done | bytes 393248 | tf_op jit(solution)/shard_map/ppermute | solution.py:1334
  885.4 10.2 collective-permute-done.75
  904.2 15.7 %rotate.1 = (bf16[1024,1024]{1,0:T(8,128)(2,1)}, bf16[1024,1024]{1,0:T(8,128)(2,1)}) custom-call(bf16[4,1024,256]{2,1,0:T(8,128)(2,1)} %bitcast.88.grads, bf16[1024,1024]{1,0:T(8,128)(2,1)} %fusion.1.right, bf16[1024,1024]{1,0:T(8,128)(2,1)} %bitcast.30.left, bf16[1024,1024]{1,0:T(8,128)(2,1)} %bitcast.33.first, bf16[1024,1024]{1,0:T(8,128)(2,1)} %bitcast.37.second), custom_call_target="tpu_custom_call" | custom-call | flops 320000000 | tf_op jit(solution)/shard_map/rotate/pallas_call | solution.py:872
  926.8 49.5 %collective-permute-done.77 = f32[2,12288]{1,0:T(2,128)S(1)} collective-permute-done((f32[2,12288]{1,0:T(2,128)S(1)}, f32[2,12288]{1,0:T(2,128)S(1)}, u32[]{:S(2)}, u32[]{:S(2)}) %collective-permute-start.77) | collective-permute-done | bytes 98336 | tf_op jit(solution)/shard_map/ppermute | solution.py:978
  994.6 21.0 %collective-permute-done.78.refs_1_ = bf16[6,128,1024]{2,1,0:T(8,128)(2,1)} collective-permute-done((bf16[6,128,1024]{2,1,0:T(8,128)(2,1)}, bf16[6,128,1024]{2,1,0:T(8,128)(2,1)}, u32[]{:S(2)}, u32[]{:S(2)}) %collective-permute-start.78) | collective-permute-done | bytes 1572896 | tf_op jit(solution)/shard_map/ppermute | solution.py:69
  1020.3 7.6 pick.1
  (532 shorter events, 375.8 us)
Async XLA Ops:
  7.4 37.7 %all-to-all-start = ((bf16[4,5,64,512]{3,2,1,0:T(8,128)(2,1)}), bf16[4,5,64,512]{3,2,1,0:T(8,128)(2,1)S(1)}, u32[]{:S(2)}, u32[]{:S(2)}) async-start(bf16[4,5,64,512]{3,2,1,0:T(8,128)(2,1)} %broadcast_in_dim.35), calls=%async_computation | async-start | bytes 2621440 | tf_op jit(solution)/shard_map/all_to_all | solution.py:82
  47.6 40.0 %all-to-all-start.1 = ((bf16[4,6,64,512]{3,2,1,0:T(8,128)(2,1)}), bf16[4,6,64,512]{3,2,1,0:T(8,128)(2,1)S(1)}, u32[]{:S(2)}, u32[]{:S(2)}) async-start(bf16[4,6,64,512]{3,2,1,0:T(8,128)(2,1)} %broadcast_in_dim.36), calls=%async_computation.1 | async-start | bytes 3145728 | tf_op jit(solution)/shard_map/all_to_all | solution.py:82
  90.8 45.6 %collective-permute-start.2 = (bf16[2,4,5,64,512]{4,3,2,1,0:T(8,128)(2,1)S(1)}, bf16[2,4,5,64,512]{4,3,2,1,0:T(8,128)(2,1)}, u32[]{:S(2)}, u32[]{:S(2)}) collective-permute-start(bf16[2,4,5,64,512]{4,3,2,1,0:T(8,128)(2,1)S(1)} %pad_maximum_fusion.4.refs_0_.refs_2_), channel_id=1, source_target_pairs={{8,0},{0,8},{24,16},{16,24},{9,1},{1,9},{25,17},{17,25},{10,2},{2,... | collective-permute-start | bytes 7864328 | tf_op jit(solution)/shard_map/ppermute | solution.py:69
  92.8 43.6 %all-to-all-start.2 = ((bf16[4,6,64,512]{3,2,1,0:T(8,128)(2,1)}), bf16[4,6,64,512]{3,2,1,0:T(8,128)(2,1)}, u32[]{:S(2)}, u32[]{:S(2)}) async-start(bf16[4,6,64,512]{3,2,1,0:T(8,128)(2,1)} %broadcast_in_dim.41), calls=%async_computation.2 | async-start | bytes 3145728 | tf_op jit(solution)/shard_map/all_to_all | solution.py:82
  98.8 36.4 %collective-permute-start.1 = (bf16[2,4,3,64,512]{4,3,2,1,0:T(8,128)(2,1)S(1)}, bf16[2,4,3,64,512]{4,3,2,1,0:T(8,128)(2,1)}, u32[]{:S(2)}, u32[]{:S(2)}) collective-permute-start(bf16[2,4,3,64,512]{4,3,2,1,0:T(8,128)(2,1)S(1)} %fusion.2), channel_id=1, source_target_pairs={{16,0},{24,8},{0,16},{8,24},{17,1},{25,9},{1,17},{9,25},{18,2},{26... | collective-permute-start | bytes 4718600 | tf_op jit(solution)/shard_map/ppermute | solution.py:69
  100.4 36.0 %collective-permute-start.3 = (bf16[4,6,64,512]{3,2,1,0:T(8,128)(2,1)S(1)}, bf16[4,6,64,512]{3,2,1,0:T(8,128)(2,1)}, u32[]{:S(2)}, u32[]{:S(2)}) collective-permute-start(bf16[4,6,64,512]{3,2,1,0:T(8,128)(2,1)S(1)} %copy-done.12), channel_id=1, source_target_pairs={{1,0},{0,1},{3,2},{2,3},{5,4},{4,5},{7,6},{6,7},{9,8},{8,9},{11,10... | collective-permute-start | bytes 4718600 | tf_op jit(solution)/shard_map/ppermute | solution.py:69
  138.7 57.9 %collective-permute-start.5 = (bf16[2,4,6,64,512]{4,3,2,1,0:T(8,128)(2,1)S(1)}, bf16[2,4,6,64,512]{4,3,2,1,0:T(8,128)(2,1)}, u32[]{:S(2)}, u32[]{:S(2)}) collective-permute-start(bf16[2,4,6,64,512]{4,3,2,1,0:T(8,128)(2,1)S(1)} %pad_maximum_fusion.refs_0_.refs_2_), channel_id=1, source_target_pairs={{8,0},{0,8},{24,16},{16,24},{9,1},{1,9},{25,17},{17,25},{10,2},{2,... | collective-permute-start | bytes 9437192 | tf_op jit(solution)/shard_map/ppermute | solution.py:69
  140.8 41.8 %all-to-all-start.3 = ((bf16[4,6,64,512]{3,2,1,0:T(8,128)(2,1)}), bf16[4,6,64,512]{3,2,1,0:T(8,128)(2,1)}, u32[]{:S(2)}, u32[]{:S(2)}) async-start(bf16[4,6,64,512]{3,2,1,0:T(8,128)(2,1)} %broadcast_in_dim.42), calls=%async_computation.3 | async-start | bytes 3145728 | tf_op jit(solution)/shard_map/all_to_all | solution.py:82
  145.6 36.1 %collective-permute-start.6 = (bf16[4,6,64,512]{3,2,1,0:T(8,128)(2,1)}, bf16[4,6,64,512]{3,2,1,0:T(8,128)(2,1)}, u32[]{:S(2)}, u32[]{:S(2)}) collective-permute-start(bf16[4,6,64,512]{3,2,1,0:T(8,128)(2,1)} %all-to-all-done.2), channel_id=1, source_target_pairs={{1,0},{0,1},{3,2},{2,3},{5,4},{4,5},{7,6},{6,7},{9,8},{8,9},{11,10... | collective-permute-start | bytes 4718600 | tf_op jit(solution)/shard_map/ppermute | solution.py:69
  160.2 36.4 %collective-permute-start.8 = (bf16[256,2048]{1,0:T(8,128)(2,1)}, bf16[256,2048]{1,0:T(8,128)(2,1)}, u32[]{:S(2)}, u32[]{:S(2)}) collective-permute-start(bf16[256,2048]{1,0:T(8,128)(2,1)} %get-tuple-element.517.refs_0_.refs_4_), channel_id=1, source_target_pairs={{16,0},{24,8},{0,16},{8,24},{17,1},{25,9},{1,17},{9,25},{18,2},{26... | collective-permute-start | bytes 3145736 | tf_op jit(solution)/shard_map/ppermute | solution.py:69
  161.8 34.8 %collective-permute-start.9 = (bf16[256,2048]{1,0:T(8,128)(2,1)}, bf16[256,2048]{1,0:T(8,128)(2,1)}, u32[]{:S(2)}, u32[]{:S(2)}) collective-permute-start(bf16[256,2048]{1,0:T(8,128)(2,1)} %get-tuple-element.517.refs_0_.refs_4_), channel_id=1, source_target_pairs={{8,0},{0,8},{24,16},{16,24},{9,1},{1,9},{25,17},{17,25},{10,2},{2,... | collective-permute-start | bytes 3145736 | tf_op jit(solution)/shard_map/ppermute | solution.py:69
  198.8 44.4 %collective-permute-start.11 = (bf16[2,4,6,64,512]{4,3,2,1,0:T(8,128)(2,1)S(1)}, bf16[2,4,6,64,512]{4,3,2,1,0:T(8,128)(2,1)}, u32[]{:S(2)}, u32[]{:S(2)}) collective-permute-start(bf16[2,4,6,64,512]{4,3,2,1,0:T(8,128)(2,1)S(1)} %pad_maximum_fusion.1.refs_0_.refs_2_), channel_id=1, source_target_pairs={{8,0},{0,8},{24,16},{16,24},{9,1},{1,9},{25,17},{17,25},{10,2},{2,... | collective-permute-start | bytes 9437192 | tf_op jit(solution)/shard_map/ppermute | solution.py:69
  201.0 42.2 %all-to-all-start.4 = ((bf16[4,6,64,512]{3,2,1,0:T(8,128)(2,1)}), bf16[4,6,64,512]{3,2,1,0:T(8,128)(2,1)}, u32[]{:S(2)}, u32[]{:S(2)}) async-start(bf16[4,6,64,512]{3,2,1,0:T(8,128)(2,1)} %broadcast_in_dim.43), calls=%async_computation.4 | async-start | bytes 3145728 | tf_op jit(solution)/shard_map/all_to_all | solution.py:82
  206.3 36.1 %collective-permute-start.12 = (bf16[4,6,64,512]{3,2,1,0:T(8,128)(2,1)}, bf16[4,6,64,512]{3,2,1,0:T(8,128)(2,1)}, u32[]{:S(2)}, u32[]{:S(2)}) collective-permute-start(bf16[4,6,64,512]{3,2,1,0:T(8,128)(2,1)} %all-to-all-done.3), channel_id=1, source_target_pairs={{1,0},{0,1},{3,2},{2,3},{5,4},{4,5},{7,6},{6,7},{9,8},{8,9},{11,10... | collective-permute-start | bytes 4718600 | tf_op jit(solution)/shard_map/ppermute | solution.py:69
  208.7 32.4 %collective-permute-start.10 = (bf16[2,4,2,64,512]{4,3,2,1,0:T(8,128)(2,1)S(1)}, bf16[2,4,2,64,512]{4,3,2,1,0:T(8,128)(2,1)}, u32[]{:S(2)}, u32[]{:S(2)}) collective-permute-start(bf16[2,4,2,64,512]{4,3,2,1,0:T(8,128)(2,1)S(1)} %fusion.7), channel_id=1, source_target_pairs={{16,0},{24,8},{0,16},{8,24},{17,1},{25,9},{1,17},{9,25},{18,2},{26... | collective-permute-start | bytes 3145736 | tf_op jit(solution)/shard_map/ppermute | solution.py:69
  245.4 37.2 %collective-permute-start.16 = (bf16[2,4,6,64,512]{4,3,2,1,0:T(8,128)(2,1)S(1)}, bf16[2,4,6,64,512]{4,3,2,1,0:T(8,128)(2,1)}, u32[]{:S(2)}, u32[]{:S(2)}) collective-permute-start(bf16[2,4,6,64,512]{4,3,2,1,0:T(8,128)(2,1)S(1)} %pad_maximum_fusion.2.refs_0_.refs_2_), channel_id=1, source_target_pairs={{8,0},{0,8},{24,16},{16,24},{9,1},{1,9},{25,17},{17,25},{10,2},{2,... | collective-permute-start | bytes 9437192 | tf_op jit(solution)/shard_map/ppermute | solution.py:69
  245.5 37.1 %collective-permute-start.17 = (bf16[4,6,64,512]{3,2,1,0:T(8,128)(2,1)}, bf16[4,6,64,512]{3,2,1,0:T(8,128)(2,1)}, u32[]{:S(2)}, u32[]{:S(2)}) collective-permute-start(bf16[4,6,64,512]{3,2,1,0:T(8,128)(2,1)} %all-to-all-done.4), channel_id=1, source_target_pairs={{1,0},{0,1},{3,2},{2,3},{5,4},{4,5},{7,6},{6,7},{9,8},{8,9},{11,10... | collective-permute-start | bytes 4718600 | tf_op jit(solution)/shard_map/ppermute | solution.py:69
  247.4 35.2 %all-to-all-start.5 = ((bf16[4,4,64,512]{3,2,1,0:T(8,128)(2,1)}), bf16[4,4,64,512]{3,2,1,0:T(8,128)(2,1)}, u32[]{:S(2)}, u32[]{:S(2)}) async-start(bf16[4,4,64,512]{3,2,1,0:T(8,128)(2,1)} %broadcast_in_dim.44), calls=%async_computation.5 | async-start | bytes 2097152 | tf_op jit(solution)/shard_map/all_to_all | solution.py:82
  282.6 57.4 %all-to-all-start.6 = ((bf16[8,128,1024]{2,1,0:T(8,128)(2,1)}), bf16[8,128,1024]{2,1,0:T(8,128)(2,1)}, u32[]{:S(2)}, u32[]{:S(2)}) async-start(bf16[8,128,1024]{2,1,0:T(8,128)(2,1)} %pad.10), calls=%async_computation.6 | async-start | bytes 4194304 | tf_op jit(solution)/shard_map/all_to_all | solution.py:999
  289.2 50.8 %collective-permute-start.20 = (bf16[2,4,6,64,512]{4,3,2,1,0:T(8,128)(2,1)S(1)}, bf16[2,4,6,64,512]{4,3,2,1,0:T(8,128)(2,1)S(1)}, u32[]{:S(2)}, u32[]{:S(2)}) collective-permute-start(bf16[2,4,6,64,512]{4,3,2,1,0:T(8,128)(2,1)S(1)} %pad_maximum_fusion.3.refs_0_.refs_2_), channel_id=1, source_target_pairs={{8,0},{0,8},{24,16},{16,24},{9,1},{1,9},{25,17},{17,25},{10,2},{2,... | collective-permute-start | bytes 9437192 | tf_op jit(solution)/shard_map/ppermute | solution.py:69
  293.1 41.2 %collective-permute-start.21 = (bf16[4,4,64,512]{3,2,1,0:T(8,128)(2,1)}, bf16[4,4,64,512]{3,2,1,0:T(8,128)(2,1)}, u32[]{:S(2)}, u32[]{:S(2)}) collective-permute-start(bf16[4,4,64,512]{3,2,1,0:T(8,128)(2,1)} %all-to-all-done.5), channel_id=1, source_target_pairs={{1,0},{0,1},{3,2},{2,3},{5,4},{4,5},{7,6},{6,7},{9,8},{8,9},{11,10... | collective-permute-start | bytes 3145736 | tf_op jit(solution)/shard_map/ppermute | solution.py:69
  306.3 33.7 %collective-permute-start.23 = (bf16[256,2048]{1,0:T(8,128)(2,1)}, bf16[256,2048]{1,0:T(8,128)(2,1)}, u32[]{:S(2)}, u32[]{:S(2)}) collective-permute-start(bf16[256,2048]{1,0:T(8,128)(2,1)} %get-tuple-element.566.refs_0_.refs_4_), channel_id=1, source_target_pairs={{16,0},{24,8},{0,16},{8,24},{17,1},{25,9},{1,17},{9,25},{18,2},{26... | collective-permute-start | bytes 3145736 | tf_op jit(solution)/shard_map/ppermute | solution.py:69
  307.0 33.1 %collective-permute-start.24 = (bf16[256,2048]{1,0:T(8,128)(2,1)}, bf16[256,2048]{1,0:T(8,128)(2,1)}, u32[]{:S(2)}, u32[]{:S(2)}) collective-permute-start(bf16[256,2048]{1,0:T(8,128)(2,1)} %get-tuple-element.566.refs_0_.refs_4_), channel_id=1, source_target_pairs={{8,0},{0,8},{24,16},{16,24},{9,1},{1,9},{25,17},{17,25},{10,2},{2,... | collective-permute-start | bytes 3145736 | tf_op jit(solution)/shard_map/ppermute | solution.py:69
  341.7 54.9 %all-to-all-start.7 = ((bf16[8,128,1024]{2,1,0:T(8,128)(2,1)}), bf16[8,128,1024]{2,1,0:T(8,128)(2,1)}, u32[]{:S(2)}, u32[]{:S(2)}) async-start(bf16[8,128,1024]{2,1,0:T(8,128)(2,1)} %pad.11), calls=%async_computation.7 | async-start | bytes 4194304 | tf_op jit(solution)/shard_map/all_to_all | solution.py:999
  349.3 46.0 %collective-permute-start.25 = (bf16[2,4,4,64,512]{4,3,2,1,0:T(8,128)(2,1)S(1)}, bf16[2,4,4,64,512]{4,3,2,1,0:T(8,128)(2,1)S(1)}, u32[]{:S(2)}, u32[]{:S(2)}) collective-permute-start(bf16[2,4,4,64,512]{4,3,2,1,0:T(8,128)(2,1)S(1)} %pad_maximum_fusion.5.refs_0_.refs_2_), channel_id=1, source_target_pairs={{16,0},{24,8},{0,16},{8,24},{17,1},{25,9},{1,17},{9,25},{18,2},{26... | collective-permute-start | bytes 6291464 | tf_op jit(solution)/shard_map/ppermute | solution.py:69
  350.0 46.5 %collective-permute-start.26 = (bf16[2,4,4,64,512]{4,3,2,1,0:T(8,128)(2,1)S(1)}, bf16[2,4,4,64,512]{4,3,2,1,0:T(8,128)(2,1)}, u32[]{:S(2)}, u32[]{:S(2)}) collective-permute-start(bf16[2,4,4,64,512]{4,3,2,1,0:T(8,128)(2,1)S(1)} %pad_maximum_fusion.5.refs_0_.refs_2_), channel_id=1, source_target_pairs={{8,0},{0,8},{24,16},{16,24},{9,1},{1,9},{25,17},{17,25},{10,2},{2,... | collective-permute-start | bytes 6291464 | tf_op jit(solution)/shard_map/ppermute | solution.py:69
  396.6 53.3 %all-to-all-start.8 = ((bf16[8,128,1024]{2,1,0:T(8,128)(2,1)}), bf16[8,128,1024]{2,1,0:T(8,128)(2,1)}, u32[]{:S(2)}, u32[]{:S(2)}) async-start(bf16[8,128,1024]{2,1,0:T(8,128)(2,1)} %pad.12), calls=%async_computation.8 | async-start | bytes 4194304 | tf_op jit(solution)/shard_map/all_to_all | solution.py:999
  402.8 47.1 %collective-permute-start.33 = (bf16[256,4096]{1,0:T(8,128)(2,1)}, bf16[256,4096]{1,0:T(8,128)(2,1)}, u32[]{:S(2)}, u32[]{:S(2)}) collective-permute-start(bf16[256,4096]{1,0:T(8,128)(2,1)} %get-tuple-element.536.act.refs_0_), channel_id=1, source_target_pairs={{8,0},{0,8},{24,16},{16,24},{9,1},{1,9},{25,17},{17,25},{10,2},{2,... | collective-permute-start | bytes 6291464 | tf_op jit(solution)/shard_map/ppermute | solution.py:69
  403.3 38.4 %collective-permute-start.30 = (bf16[256,4096]{1,0:T(8,128)(2,1)}, bf16[256,4096]{1,0:T(8,128)(2,1)}, u32[]{:S(2)}, u32[]{:S(2)}) collective-permute-start(bf16[256,4096]{1,0:T(8,128)(2,1)} %get-tuple-element.581.act.refs_0_), channel_id=1, source_target_pairs={{8,0},{0,8},{24,16},{16,24},{9,1},{1,9},{25,17},{17,25},{10,2},{2,... | collective-permute-start | bytes 6291464 | tf_op jit(solution)/shard_map/ppermute | solution.py:69
  404.8 45.1 %collective-permute-start.32 = (bf16[256,3072]{1,0:T(8,128)(2,1)}, bf16[256,3072]{1,0:T(8,128)(2,1)S(1)}, u32[]{:S(2)}, u32[]{:S(2)}) collective-permute-start(bf16[256,3072]{1,0:T(8,128)(2,1)} %pad_maximum_fusion.6), channel_id=1, source_target_pairs={{8,0},{0,8},{24,16},{16,24},{9,1},{1,9},{25,17},{17,25},{10,2},{2,... | collective-permute-start | bytes 4718600 | tf_op jit(solution)/shard_map/ppermute | solution.py:69
  406.5 43.4 %collective-permute-start.34 = (bf16[256,3072]{1,0:T(8,128)(2,1)}, bf16[256,3072]{1,0:T(8,128)(2,1)S(1)}, u32[]{:S(2)}, u32[]{:S(2)}) collective-permute-start(bf16[256,3072]{1,0:T(8,128)(2,1)} %pad_maximum_fusion.7), channel_id=1, source_target_pairs={{8,0},{0,8},{24,16},{16,24},{9,1},{1,9},{25,17},{17,25},{10,2},{2,... | collective-permute-start | bytes 4718600 | tf_op jit(solution)/shard_map/ppermute | solution.py:69
  480.0 35.1 %collective-permute-start.40 = (bf16[2,4,2,128,256]{4,3,2,1,0:T(8,128)(2,1)S(1)}, bf16[2,4,2,128,256]{4,3,2,1,0:T(8,128)(2,1)S(1)}, u32[]{:S(2)}, u32[]{:S(2)}) collective-permute-start(bf16[2,4,2,128,256]{4,3,2,1,0:T(8,128)(2,1)S(1)} %copy-done.91), channel_id=1, source_target_pairs={{16,0},{24,8},{0,16},{8,24},{17,1},{25,9},{1,17},{9,25},{18,2},{26... | collective-permute-start | bytes 3145736 | tf_op jit(solution)/shard_map/ppermute | solution.py:69
  481.4 33.8 %collective-permute-start.41 = (bf16[2,4,2,128,256]{4,3,2,1,0:T(8,128)(2,1)S(1)}, bf16[2,4,2,128,256]{4,3,2,1,0:T(8,128)(2,1)S(1)}, u32[]{:S(2)}, u32[]{:S(2)}) collective-permute-start(bf16[2,4,2,128,256]{4,3,2,1,0:T(8,128)(2,1)S(1)} %copy-done.90), channel_id=1, source_target_pairs={{1,0},{0,1},{3,2},{2,3},{5,4},{4,5},{7,6},{6,7},{9,8},{8,9},{11,10... | collective-permute-start | bytes 3145736 | tf_op jit(solution)/shard_map/ppermute | solution.py:69
  482.0 33.1 %collective-permute-start.39 = (bf16[4,2,256,128]{3,2,1,0:T(8,128)(2,1)S(1)}, bf16[4,2,256,128]{3,2,1,0:T(8,128)(2,1)S(1)}, u32[]{:S(2)}, u32[]{:S(2)}) collective-permute-start(bf16[4,2,256,128]{3,2,1,0:T(8,128)(2,1)S(1)} %get-tuple-element.996), channel_id=1, source_target_pairs={{16,0},{24,8},{0,16},{8,24},{17,1},{25,9},{1,17},{9,25},{18,2},{26... | collective-permute-start | bytes 1572872 | tf_op jit(solution)/shard_map/ppermute | solution.py:69
  625.0 34.5 %collective-permute-start.53 = (bf16[2,4,2,256,128]{4,3,2,1,0:T(8,128)(2,1)S(1)}, bf16[2,4,2,256,128]{4,3,2,1,0:T(8,128)(2,1)S(1)}, u32[]{:S(2)}, u32[]{:S(2)}) collective-permute-start(bf16[2,4,2,256,128]{4,3,2,1,0:T(8,128)(2,1)S(1)} %copy-done.89), channel_id=1, source_target_pairs={{16,0},{24,8},{0,16},{8,24},{17,1},{25,9},{1,17},{9,25},{18,2},{26... | collective-permute-start | bytes 3145736 | tf_op jit(solution)/shard_map/ppermute | solution.py:69
  625.7 33.8 %collective-permute-start.54 = (bf16[2,4,2,256,128]{4,3,2,1,0:T(8,128)(2,1)S(1)}, bf16[2,4,2,256,128]{4,3,2,1,0:T(8,128)(2,1)S(1)}, u32[]{:S(2)}, u32[]{:S(2)}) collective-permute-start(bf16[2,4,2,256,128]{4,3,2,1,0:T(8,128)(2,1)S(1)} %copy-done.88), channel_id=1, source_target_pairs={{1,0},{0,1},{3,2},{2,3},{5,4},{4,5},{7,6},{6,7},{9,8},{8,9},{11,10... | collective-permute-start | bytes 3145736 | tf_op jit(solution)/shard_map/ppermute | solution.py:69
  627.4 32.1 %collective-permute-start.52 = (bf16[4,2,128,256]{3,2,1,0:T(8,128)(2,1)S(1)}, bf16[4,2,128,256]{3,2,1,0:T(8,128)(2,1)S(1)}, u32[]{:S(2)}, u32[]{:S(2)}) collective-permute-start(bf16[4,2,128,256]{3,2,1,0:T(8,128)(2,1)S(1)} %get-tuple-element.988), channel_id=1, source_target_pairs={{16,0},{24,8},{0,16},{8,24},{17,1},{25,9},{1,17},{9,25},{18,2},{26... | collective-permute-start | bytes 1572872 | tf_op jit(solution)/shard_map/ppermute | solution.py:69
  663.0 46.6 %all-to-all-start.11 = ((bf16[4,4,128,256]{3,2,1,0:T(8,128)(2,1)}), bf16[4,4,128,256]{3,2,1,0:T(8,128)(2,1)S(1)}, u32[]{:S(2)}, u32[]{:S(2)}) async-start(bf16[4,4,128,256]{3,2,1,0:T(8,128)(2,1)} %pad_maximum_fusion.11), calls=%async_computation.11 | async-start | bytes 2097152 | tf_op jit(solution)/shard_map/all_to_all | solution.py:82
  673.2 36.4 %collective-permute-start.59 = (bf16[2,256,1024]{2,1,0:T(8,128)(2,1)}, bf16[2,256,1024]{2,1,0:T(8,128)(2,1)S(1)}, u32[]{:S(2)}, u32[]{:S(2)}) collective-permute-start(bf16[2,256,1024]{2,1,0:T(8,128)(2,1)} %fusion.4), channel_id=1, source_target_pairs={{16,0},{24,8},{0,16},{8,24},{17,1},{25,9},{1,17},{9,25},{18,2},{26... | collective-permute-start | bytes 3145736 | tf_op jit(solution)/shard_map/ppermute | solution.py:69
  674.2 35.3 %collective-permute-start.56 = (bf16[4,2,256,128]{3,2,1,0:T(8,128)(2,1)S(1)}, bf16[4,2,256,128]{3,2,1,0:T(8,128)(2,1)}, u32[]{:S(2)}, u32[]{:S(2)}) collective-permute-start(bf16[4,2,256,128]{3,2,1,0:T(8,128)(2,1)S(1)} %get-tuple-element.984), channel_id=1, source_target_pairs={{16,0},{24,8},{0,16},{8,24},{17,1},{25,9},{1,17},{9,25},{18,2},{26... | collective-permute-start | bytes 1572872 | tf_op jit(solution)/shard_map/ppermute | solution.py:69
  764.9 32.6 %all-to-all-start.13 = ((bf16[4,4,128,256]{3,2,1,0:T(8,128)(2,1)}), bf16[4,4,128,256]{3,2,1,0:T(8,128)(2,1)S(1)}, u32[]{:S(2)}, u32[]{:S(2)}) async-start(bf16[4,4,128,256]{3,2,1,0:T(8,128)(2,1)} %pad_maximum_fusion.13), calls=%async_computation.13 | async-start | bytes 2097152 | tf_op jit(solution)/shard_map/all_to_all | solution.py:82
  850.6 53.7 %all-to-all-start.15 = ((bf16[32,128,256]{2,1,0:T(8,128)(2,1)}), bf16[32,128,256]{2,1,0:T(8,128)(2,1)}, u32[]{:S(2)}, u32[]{:S(2)}) async-start(bf16[32,128,256]{2,1,0:T(8,128)(2,1)} %bitcast.164), calls=%async_computation.15 | async-start | bytes 4194304 | tf_op jit(solution)/shard_map/all_to_all | solution.py:1321
  856.6 38.9 %collective-permute-start.75 = (bf16[6,128,256]{2,1,0:T(8,128)(2,1)}, bf16[6,128,256]{2,1,0:T(8,128)(2,1)S(1)}, u32[]{:S(2)}, u32[]{:S(2)}) collective-permute-start(bf16[6,128,256]{2,1,0:T(8,128)(2,1)} %get-tuple-element.970), channel_id=1, source_target_pairs={{0,16},{8,24},{16,0},{24,8},{1,17},{9,25},{17,1},{25,9},{2,18},{10... | collective-permute-start | bytes 1179656 | tf_op jit(solution)/shard_map/ppermute | solution.py:1334
  857.0 38.6 %collective-permute-start.74 = (bf16[6,128,256]{2,1,0:T(8,128)(2,1)S(1)}, bf16[6,128,256]{2,1,0:T(8,128)(2,1)S(1)}, u32[]{:S(2)}, u32[]{:S(2)}) collective-permute-start(bf16[6,128,256]{2,1,0:T(8,128)(2,1)S(1)} %get-tuple-element.971), channel_id=1, source_target_pairs={{0,8},{8,0},{16,24},{24,16},{1,9},{9,1},{17,25},{25,17},{2,10},{10... | collective-permute-start | bytes 1179656 | tf_op jit(solution)/shard_map/ppermute | solution.py:1334
  920.0 56.4 %all-to-all-start.16 = ((bf16[8,128,1024]{2,1,0:T(8,128)(2,1)}), bf16[8,128,1024]{2,1,0:T(8,128)(2,1)S(1)}, u32[]{:S(2)}, u32[]{:S(2)}) async-start(bf16[8,128,1024]{2,1,0:T(8,128)(2,1)} %bitcast.176), calls=%async_computation.16 | async-start | bytes 4194304 | tf_op jit(solution)/shard_map/all_to_all | solution.py:1004
  923.9 52.4 %collective-permute-start.77 = (f32[2,12288]{1,0:T(2,128)S(1)}, f32[2,12288]{1,0:T(2,128)S(1)}, u32[]{:S(2)}, u32[]{:S(2)}) collective-permute-start(f32[2,12288]{1,0:T(2,128)S(1)} %add.454), channel_id=1, source_target_pairs={{0,4},{1,5},{2,6},{3,7},{4,0},{5,1},{6,2},{7,3},{8,12},{9,13},{10,... | collective-permute-start | bytes 294920 | tf_op jit(solution)/shard_map/ppermute | solution.py:978
  980.1 35.4 %collective-permute-start.78 = (bf16[6,128,1024]{2,1,0:T(8,128)(2,1)}, bf16[6,128,1024]{2,1,0:T(8,128)(2,1)}, u32[]{:S(2)}, u32[]{:S(2)}) collective-permute-start(bf16[6,128,1024]{2,1,0:T(8,128)(2,1)} %subtract_convert_fusion.refs_0_), channel_id=1, source_target_pairs={{16,0},{24,8},{0,16},{8,24},{17,1},{25,9},{1,17},{9,25},{18,2},{26... | collective-permute-start | bytes 4718600 | tf_op jit(solution)/shard_map/ppermute | solution.py:69
  981.4 51.9 %all-to-all-start.17 = ((bf16[8,128,1024]{2,1,0:T(8,128)(2,1)}), bf16[8,128,1024]{2,1,0:T(8,128)(2,1)}, u32[]{:S(2)}, u32[]{:S(2)}) async-start(bf16[8,128,1024]{2,1,0:T(8,128)(2,1)} %bitcast.175), calls=%async_computation.17 | async-start | bytes 4194304 | tf_op jit(solution)/shard_map/all_to_all | solution.py:1004
  (144 other events, 1579.1 us)

commit v7 on v6

--- a/solution.py
+++ b/solution.py
@@ -772,7 +772,10 @@
             self.groups = [sum_job_plain(place, one[0], one[2], "y")[None] for one in sets]
         else:
             self.plain = False
-            sets = [(one[0], one[1], one[2], place.take(one[2], "core", 1), one[3]) for one in sets]
+            sets = [
+                (*one[:3], place.take(one[2], "core", 1) if one[4] is None else one[4], one[3])
+                for one in sets
+            ]
             self.turned = sets[0][0].shape[1] > BLK
             self.parts = partial_sums(place, sets)
             self.by_y = self.by_x = ()
@@ -1173,14 +1176,14 @@
             job.parts, job.by_y, job.by_x, job.groups = fields
         live.update(values)
 
-    def begin(layer_at, first_block, *sets):
+    def begin(layer_at, first_block, *sets, right_other=None):
         ids = [layer_at * NBLK + first_block + spot for spot in range(4)]
         jobs.append(
             Summing(
                 place,
                 ids,
                 [
-                    (lefts[layer_at][spot], live["crossed"][layer_at][spot // 3], right, spot % 3)
+                    (lefts[layer_at][spot], live["crossed"][layer_at][spot // 3], right, spot % 3, right_other)
                     for spot, right in sets
                 ],
             )
@@ -1190,8 +1193,8 @@
     def close_step(layer_at, flow):
         live["two"], live["ffn"], live["sums_two"] = close(flow, summed[layer_at][1], gains[layer_at][1])
 
-    def down_job(layer_at):
-        return begin(layer_at, 8, (3, live["ffn"]))
+    def down_job(layer_at, right_other=None):
+        return begin(layer_at, 8, (3, live["ffn"]), right_other=right_other)
 
     def in_job(layer_at):
         return begin(layer_at, 0, (0, live["joined"]), (1, live["branch_in"]))
@@ -1259,13 +1262,14 @@
     grad_flow = input_step(1)
     close_step(0, grad_flow)
     settle_back()
+    in_1 = in_job(1)
+    live["ffn_other"] = place.take(live["ffn"], "core", 1)
+    settle_back()
     up_1.third()
-    in_1 = in_job(1)
-    down_0 = down_job(0)
-    settle_back()
     in_1.first_y()
     in_1.first_x()
     feed_step(0)
+    down_0 = down_job(0, live.pop("ffn_other"))
     settle_back()
     in_1.second_x()
     in_1.second_y()

time: 1050 us -> 1040 us (level)
  transfers between devices with their start and end apart: 99 -> 99, of which waited for: 52 -> 50; matrix products, arithmetic and copies ran while one was open for 8% -> 8% of each run, Pallas kernels for 24% -> 24%
where the time goes in v7:
time: 1040 us; the launch traced here: 1030 us
  waiting for transfers between devices  454 us (44%)
  Pallas kernels  275 us (26%)
  starting transfers between devices  143 us (14%)
  local copies, waits for them, and re-layouts  80.3 us (8%)
  other arithmetic  79.7 us (8%)
    ppermute x76, waiting for transfers between devices, take(): return lax.ppermute(value, name, pairs)  302 us
    ppermute x2, waiting for transfers between devices, step(): self.terms = [value, lax.ppermute(value, 'wsh', swap)]  62.4 us
    all_to_all x12, starting transfers between devices, swap_z(): lax.all_to_all(values, 'wsh', 0, 0, tiled=True, axis_index_groups=lines)  57.1 us
    ppermute x76, starting transfers between devices, take(): return lax.ppermute(value, name, pairs)  50.5 us
    pallas_call x6, Pallas kernels, partial_sums(): call(functools.partial(sum_kernel, counts[0] if len(sets) > 1 else None,...  48.8 us
    pallas_call x2, Pallas kernels, attend_back(): call(functools.partial(attend_back_kernel, count, count_y, tokens), (D //...  42.6 us
    unnamed x218, local copies, waits for them, and re-layouts  40.5 us
    all_to_all x12, waiting for transfers between devices, swap_z(): lax.all_to_all(values, 'wsh', 0, 0, tiled=True, axis_index_groups=lines)  40.4 us
  transfers between devices with their start and end apart: 99, of which 50 were waited for; matrix products, arithmetic and copies ran while one was open for 8% of the time, Pallas kernels for 24%

profile of v7, /device:TPU:0, one launch (start us, length us, event | category | flops | bytes accessed | tf_op | source)
XLA Modules:
  0.0 1034.0 jit_solution(15987331561640212552)
XLA Ops:
  7.4 6.3 all-to-all-start
  25.1 19.9 %all-to-all-done = bf16[4,5,64,512]{3,2,1,0:T(8,128)(2,1)S(1)} async-done(((bf16[4,5,64,512]{3,2,1,0:T(8,128)(2,1)}), bf16[4,5,64,512]{3,2,1,0:T(8,128)(2,1)S(1)}, u32[]{:S(2)}, u32[]{:S(2)}) %all-to-all-start) | async-done | bytes 1310752 | tf_op jit(solution)/shard_map/all_to_all | solution.py:82
  64.6 19.0 %collective-permute-done = bf16[4,5,64,512]{3,2,1,0:T(8,128)(2,1)} collective-permute-done((bf16[4,5,64,512]{3,2,1,0:T(8,128)(2,1)S(1)}, bf16[4,5,64,512]{3,2,1,0:T(8,128)(2,1)}, u32[]{:S(2)}, u32[]{:S(2)}) %collective-permute-start) | collective-permute-done | bytes 1310752 | tf_op jit(solution)/shard_map/ppermute | solution.py:69
  108.5 26.7 %collective-permute-done.1.refs_4_ = bf16[2,4,3,64,512]{4,3,2,1,0:T(8,128)(2,1)} collective-permute-done((bf16[2,4,3,64,512]{4,3,2,1,0:T(8,128)(2,1)S(1)}, bf16[2,4,3,64,512]{4,3,2,1,0:T(8,128)(2,1)}, u32[]{:S(2)}, u32[]{:S(2)}) %collective-permute-start.1) | collective-permute-done | bytes 1572896 | tf_op jit(solution)/shard_map/ppermute | solution.py:69
  150.2 10.0 project.2
  161.8 14.0 %collective-permute-done.4.refs_4_ = bf16[2,4,2,64,512]{4,3,2,1,0:T(8,128)(2,1)S(1)} collective-permute-done((bf16[2,4,2,64,512]{4,3,2,1,0:T(8,128)(2,1)S(1)}, bf16[2,4,2,64,512]{4,3,2,1,0:T(8,128)(2,1)S(1)}, u32[]{:S(2)}, u32[]{:S(2)}) %collective-permute-start.4) | collective-permute-done | bytes 1048608 | tf_op jit(solution)/shard_map/ppermute | solution.py:69
  182.6 14.0 %collective-permute-done.8.refs_1_.refs_5_ = bf16[256,2048]{1,0:T(8,128)(2,1)} collective-permute-done((bf16[256,2048]{1,0:T(8,128)(2,1)}, bf16[256,2048]{1,0:T(8,128)(2,1)}, u32[]{:S(2)}, u32[]{:S(2)}) %collective-permute-start.8) | collective-permute-done | bytes 1048608 | tf_op jit(solution)/shard_map/ppermute | solution.py:69
  210.5 13.8 %attend.2.attn.refs_4_ = bf16[256,1024]{1,0:T(8,128)(2,1)} custom-call(bf16[256,1024]{1,0:T(8,128)(2,1)} %get-tuple-element.516.query, f32[1024,256]{1,0:T(8,128)} %compare_select_fusion.mask, bf16[256,2048]{1,0:T(8,128)(2,1)} %get-tuple-element.518.refs_0_.refs_4_, bf16[256,2048]{1,0:T(8,128)(2,1)} %collective-permute-done.8.refs_1_.refs_5_, ...), custom_call_target="tpu_custom_call" | custom-call | flops 280000000 | tf_op jit(solution)/shard_map/attend/pallas_call | solution.py:338
  229.3 11.5 %up.2 = (f32[256,4096]{1,0:T(8,128)}, bf16[256,4096]{1,0:T(8,128)(2,1)}, bf16[4,1024,1024]{2,1,0:T(8,128)(2,1)}) custom-call(s32[3]{0:T(128)} %pad_add_fusion.1.where, bf16[256,1024]{1,0:T(8,128)(2,1)} %get-tuple-element.523.middle_low.refs_0_, f32[4,1,1024]{2,1,0:T(1,128)} %bitcast.183, bf16[2,4,6,64,512]{4,3,2,1,0:T(8,128)(2,1)} %copy-done.1, ...), custom_call_target="tpu_custom_call" | custom-call | flops 160000000 | tf_op jit(solution)/shard_map/up/pallas_call | solution.py:441
  255.3 11.3 %down.2 = (f32[256,1024]{1,0:T(8,128)}, f32[256,1024]{1,0:T(8,128)}, bf16[256,1024]{1,0:T(8,128)(2,1)}, bf16[4,1024,1024]{2,1,0:T(8,128)(2,1)}) custom-call(s32[3]{0:T(128)} %pad_add_fusion.1.where, bf16[256,4096]{1,0:T(8,128)(2,1)} %get-tuple-element.537.act.refs_0_, f32[256,1024]{1,0:T(8,128)} %get-tuple-element.540.middle, ...), custom_call_target="tpu_custom_call" | custom-call | flops 160000000 | tf_op jit(solution)/shard_map/down/pallas_call | solution.py:481
  266.6 11.9 %collective-permute-done.15.refs_4_ = bf16[2,4,2,64,512]{4,3,2,1,0:T(8,128)(2,1)} collective-permute-done((bf16[2,4,2,64,512]{4,3,2,1,0:T(8,128)(2,1)S(1)}, bf16[2,4,2,64,512]{4,3,2,1,0:T(8,128)(2,1)}, u32[]{:S(2)}, u32[]{:S(2)}) %collective-permute-start.15) | collective-permute-done | bytes 1048608 | tf_op jit(solution)/shard_map/ppermute | solution.py:69
  297.0 9.1 project.3
  306.8 11.9 %collective-permute-done.19.refs_4_ = bf16[2,4,2,64,512]{4,3,2,1,0:T(8,128)(2,1)} collective-permute-done((bf16[2,4,2,64,512]{4,3,2,1,0:T(8,128)(2,1)}, bf16[2,4,2,64,512]{4,3,2,1,0:T(8,128)(2,1)}, u32[]{:S(2)}, u32[]{:S(2)}) %collective-permute-start.19) | collective-permute-done | bytes 1048608 | tf_op jit(solution)/shard_map/ppermute | solution.py:69
  318.7 15.4 %collective-permute-done.21 = bf16[4,4,64,512]{3,2,1,0:T(8,128)(2,1)} collective-permute-done((bf16[4,4,64,512]{3,2,1,0:T(8,128)(2,1)}, bf16[4,4,64,512]{3,2,1,0:T(8,128)(2,1)}, u32[]{:S(2)}, u32[]{:S(2)}) %collective-permute-start.21) | collective-permute-done | bytes 1048608 | tf_op jit(solution)/shard_map/ppermute | solution.py:69
  356.2 13.7 %attend.3.attn.refs_4_ = bf16[256,1024]{1,0:T(8,128)(2,1)} custom-call(bf16[256,1024]{1,0:T(8,128)(2,1)} %get-tuple-element.566.query, f32[1024,256]{1,0:T(8,128)} %compare_select_fusion.mask, bf16[256,2048]{1,0:T(8,128)(2,1)} %get-tuple-element.567.refs_0_.refs_4_, bf16[256,2048]{1,0:T(8,128)(2,1)} %collective-permute-done.23.refs_1_.refs_5_, ...), custom_call_target="tpu_custom_call" | custom-call | flops 280000000 | tf_op jit(solution)/shard_map/attend/pallas_call | solution.py:338
  375.2 11.5 %up.3 = (f32[256,4096]{1,0:T(8,128)}, bf16[256,4096]{1,0:T(8,128)(2,1)}, bf16[4,1024,1024]{2,1,0:T(8,128)(2,1)}) custom-call(s32[3]{0:T(128)} %pad_add_fusion.1.where, bf16[256,1024]{1,0:T(8,128)(2,1)} %get-tuple-element.572.middle_low.refs_0_, f32[4,1,1024]{2,1,0:T(1,128)} %bitcast.182, bf16[2,4,6,64,512]{4,3,2,1,0:T(8,128)(2,1)} %copy-done.3, ...), custom_call_target="tpu_custom_call" | custom-call | flops 160000000 | tf_op jit(solution)/shard_map/up/pallas_call | solution.py:441
  386.7 8.3 collective-permute-done.25.refs_4_
  396.3 6.3 all-to-all-start.8
  410.7 11.9 %down.3 = (f32[256,1024]{1,0:T(8,128)}, f32[256,1024]{1,0:T(8,128)}, bf16[256,1024]{1,0:T(8,128)(2,1)}, bf16[4,1024,1024]{2,1,0:T(8,128)(2,1)}) custom-call(s32[3]{0:T(128)} %pad_add_fusion.1.where, bf16[256,4096]{1,0:T(8,128)(2,1)} %get-tuple-element.582.act.refs_0_, f32[256,1024]{1,0:T(8,128)} %get-tuple-element.583.middle, ...), custom_call_target="tpu_custom_call" | custom-call | flops 160000000 | tf_op jit(solution)/shard_map/down/pallas_call | solution.py:481
  426.6 15.1 %feed_back.2 = (bf16[256,4096]{1,0:T(8,128)(2,1)}, bf16[256,1024]{1,0:T(8,128)(2,1)}, bf16[256,1024]{1,0:T(8,128)(2,1)}, f32[256,1024]{1,0:T(8,128)}, f32[8,1024]{1,0:T(8,128)}, /*index=5*/f32[4,1,1024]{2,1,0:T(1,128)}) custom-call(f32[256,1024]{1,0:T(8,128)} %get-tuple-element.596.grad_two, bf16[256,1024]{1,0:T(8,128)(2,1)} %get-tuple-element.591.refs_2_.ffn_low, ...), custom_call_target="tpu_custom_call" | custom-call | flops 300000000 | tf_op jit(solution)/shard_map/feed_back/pallas_call | solution.py:562
  441.7 8.1 partial_sums.6
  455.7 7.7 partial_sums.7
  463.3 12.5 %collective-permute-done.35 = bf16[2,4,2,256,128]{4,3,2,1,0:T(8,128)(2,1)} collective-permute-done((bf16[2,4,2,256,128]{4,3,2,1,0:T(8,128)(2,1)}, bf16[2,4,2,256,128]{4,3,2,1,0:T(8,128)(2,1)}, u32[]{:S(2)}, u32[]{:S(2)}) %collective-permute-start.35) | collective-permute-done | bytes 1048608 | tf_op jit(solution)/shard_map/ppermute | solution.py:69
  482.7 21.4 %attend_back.2 = (bf16[256,1024]{1,0:T(8,128)(2,1)}, bf16[2,2,256,1024]{3,2,1,0:T(8,128)(2,1)}, bf16[2,2,256,1024]{3,2,1,0:T(8,128)(2,1)}) custom-call(bf16[256,1024]{1,0:T(8,128)(2,1)} %get-tuple-element.566.query, bf16[256,1024]{1,0:T(8,128)(2,1)} %get-tuple-element.643.grad, f32[1024,256]{1,0:T(8,128)} %compare_select_fusion.mask, ...), custom_call_target="tpu_custom_call" | custom-call | flops 420000000 | tf_op jit(solution)/shard_map/attend_back/pallas_call | solution.py:389
  504.1 11.0 %collective-permute-done.39 = bf16[4,2,256,128]{3,2,1,0:T(8,128)(2,1)S(1)} collective-permute-done((bf16[4,2,256,128]{3,2,1,0:T(8,128)(2,1)S(1)}, bf16[4,2,256,128]{3,2,1,0:T(8,128)(2,1)S(1)}, u32[]{:S(2)}, u32[]{:S(2)}) %collective-permute-start.39) | collective-permute-done | bytes 524320 | tf_op jit(solution)/shard_map/ppermute | solution.py:69
  527.3 13.2 %collective-permute-done.42 = bf16[4,2,128,256]{3,2,1,0:T(8,128)(2,1)S(1)} collective-permute-done((bf16[4,2,128,256]{3,2,1,0:T(8,128)(2,1)S(1)}, bf16[4,2,128,256]{3,2,1,0:T(8,128)(2,1)S(1)}, u32[]{:S(2)}, u32[]{:S(2)}) %collective-permute-start.42) | collective-permute-done | bytes 524320 | tf_op jit(solution)/shard_map/ppermute | solution.py:69
  540.5 8.0 all-to-all-done.9.refs_0_
  553.5 7.9 input_back.2
  572.3 8.6 partial_sums.8
  589.4 8.1 partial_sums.9
  597.5 15.3 %feed_back.3 = (bf16[256,4096]{1,0:T(8,128)(2,1)}, bf16[256,1024]{1,0:T(8,128)(2,1)}, bf16[256,1024]{1,0:T(8,128)(2,1)}, f32[256,1024]{1,0:T(8,128)}, f32[8,1024]{1,0:T(8,128)}, /*index=5*/f32[4,1,1024]{2,1,0:T(1,128)}) custom-call(f32[256,1024]{1,0:T(8,128)} %get-tuple-element.746.grad_two, bf16[256,1024]{1,0:T(8,128)(2,1)} %get-tuple-element.740.refs_2_.ffn_low, ...), custom_call_target="tpu_custom_call" | custom-call | flops 300000000 | tf_op jit(solution)/shard_map/feed_back/pallas_call | solution.py:562
  621.9 21.2 %attend_back.3 = (bf16[256,1024]{1,0:T(8,128)(2,1)}, bf16[2,2,256,1024]{3,2,1,0:T(8,128)(2,1)}, bf16[2,2,256,1024]{3,2,1,0:T(8,128)(2,1)}) custom-call(bf16[256,1024]{1,0:T(8,128)(2,1)} %get-tuple-element.516.query, bf16[256,1024]{1,0:T(8,128)(2,1)} %get-tuple-element.774.grad, f32[1024,256]{1,0:T(8,128)} %compare_select_fusion.mask, ...), custom_call_target="tpu_custom_call" | custom-call | flops 420000000 | tf_op jit(solution)/shard_map/attend_back/pallas_call | solution.py:389
  643.1 9.8 collective-permute-done.52
  670.2 7.8 partial_sums.10
  678.9 25.0 %collective-permute-done.56 = bf16[4,2,256,128]{3,2,1,0:T(8,128)(2,1)} collective-permute-done((bf16[4,2,256,128]{3,2,1,0:T(8,128)(2,1)S(1)}, bf16[4,2,256,128]{3,2,1,0:T(8,128)(2,1)}, u32[]{:S(2)}, u32[]{:S(2)}) %collective-permute-start.56) | collective-permute-done | bytes 524320 | tf_op jit(solution)/shard_map/ppermute | solution.py:69
  717.3 7.9 input_back.3
  726.1 12.6 %collective-permute-done.60 = bf16[2,4,2,128,256]{4,3,2,1,0:T(8,128)(2,1)S(1)} collective-permute-done((bf16[2,4,2,128,256]{4,3,2,1,0:T(8,128)(2,1)}, bf16[2,4,2,128,256]{4,3,2,1,0:T(8,128)(2,1)S(1)}, u32[]{:S(2)}, u32[]{:S(2)}) %collective-permute-start.60) | collective-permute-done | bytes 1048608 | tf_op jit(solution)/shard_map/ppermute | solution.py:69
  747.0 8.5 partial_sums.11
  767.0 23.9 %collective-permute-done.69 = f32[2,12288]{1,0:T(2,128)S(1)} collective-permute-done((f32[2,12288]{1,0:T(2,128)S(1)}, f32[2,12288]{1,0:T(2,128)S(1)}, u32[]{:S(2)}, u32[]{:S(2)}) %collective-permute-start.69) | collective-permute-done | bytes 98336 | tf_op jit(solution)/shard_map/ppermute | solution.py:69
  798.6 9.9 collective-permute-done.72
  818.4 12.9 %collective-permute-done.73 = f32[2,12288]{1,0:T(2,128)S(1)} collective-permute-done((f32[2,12288]{1,0:T(2,128)S(1)}, f32[2,12288]{1,0:T(2,128)S(1)}, u32[]{:S(2)}, u32[]{:S(2)}) %collective-permute-start.73) | collective-permute-done | bytes 98336 | tf_op jit(solution)/shard_map/ppermute | solution.py:981
  831.3 6.6 all-to-all-done.14.refs_5_
  851.5 28.2 %collective-permute-done.76 = bf16[6,128,256]{2,1,0:T(8,128)(2,1)S(1)} collective-permute-done((bf16[6,128,256]{2,1,0:T(8,128)(2,1)}, bf16[6,128,256]{2,1,0:T(8,128)(2,1)S(1)}, u32[]{:S(2)}, u32[]{:S(2)}) %collective-permute-start.76) | collective-permute-done | bytes 393248 | tf_op jit(solution)/shard_map/ppermute | solution.py:1338
  879.7 10.2 collective-permute-done.75
  898.5 15.7 %rotate.1 = (bf16[1024,1024]{1,0:T(8,128)(2,1)}, bf16[1024,1024]{1,0:T(8,128)(2,1)}) custom-call(bf16[4,1024,256]{2,1,0:T(8,128)(2,1)} %bitcast.88.grads, bf16[1024,1024]{1,0:T(8,128)(2,1)} %fusion.1.right, bf16[1024,1024]{1,0:T(8,128)(2,1)} %bitcast.30.left, bf16[1024,1024]{1,0:T(8,128)(2,1)} %bitcast.33.first, bf16[1024,1024]{1,0:T(8,128)(2,1)} %bitcast.37.second), custom_call_target="tpu_custom_call" | custom-call | flops 320000000 | tf_op jit(solution)/shard_map/rotate/pallas_call | solution.py:875
  921.0 49.5 %collective-permute-done.77 = f32[2,12288]{1,0:T(2,128)S(1)} collective-permute-done((f32[2,12288]{1,0:T(2,128)S(1)}, f32[2,12288]{1,0:T(2,128)S(1)}, u32[]{:S(2)}, u32[]{:S(2)}) %collective-permute-start.77) | collective-permute-done | bytes 98336 | tf_op jit(solution)/shard_map/ppermute | solution.py:981
  988.8 20.9 %collective-permute-done.78.refs_1_ = bf16[6,128,1024]{2,1,0:T(8,128)(2,1)} collective-permute-done((bf16[6,128,1024]{2,1,0:T(8,128)(2,1)}, bf16[6,128,1024]{2,1,0:T(8,128)(2,1)}, u32[]{:S(2)}, u32[]{:S(2)}) %collective-permute-start.78) | collective-permute-done | bytes 1572896 | tf_op jit(solution)/shard_map/ppermute | solution.py:69
  1014.5 7.6 pick.1
  (532 shorter events, 369.8 us)
Async XLA Ops:
  7.4 37.7 %all-to-all-start = ((bf16[4,5,64,512]{3,2,1,0:T(8,128)(2,1)}), bf16[4,5,64,512]{3,2,1,0:T(8,128)(2,1)S(1)}, u32[]{:S(2)}, u32[]{:S(2)}) async-start(bf16[4,5,64,512]{3,2,1,0:T(8,128)(2,1)} %broadcast_in_dim.35), calls=%async_computation | async-start | bytes 2621440 | tf_op jit(solution)/shard_map/all_to_all | solution.py:82
  47.6 40.0 %all-to-all-start.1 = ((bf16[4,6,64,512]{3,2,1,0:T(8,128)(2,1)}), bf16[4,6,64,512]{3,2,1,0:T(8,128)(2,1)S(1)}, u32[]{:S(2)}, u32[]{:S(2)}) async-start(bf16[4,6,64,512]{3,2,1,0:T(8,128)(2,1)} %broadcast_in_dim.36), calls=%async_computation.1 | async-start | bytes 3145728 | tf_op jit(solution)/shard_map/all_to_all | solution.py:82
  90.8 45.6 %collective-permute-start.2 = (bf16[2,4,5,64,512]{4,3,2,1,0:T(8,128)(2,1)S(1)}, bf16[2,4,5,64,512]{4,3,2,1,0:T(8,128)(2,1)}, u32[]{:S(2)}, u32[]{:S(2)}) collective-permute-start(bf16[2,4,5,64,512]{4,3,2,1,0:T(8,128)(2,1)S(1)} %pad_maximum_fusion.4.refs_0_.refs_2_), channel_id=1, source_target_pairs={{8,0},{0,8},{24,16},{16,24},{9,1},{1,9},{25,17},{17,25},{10,2},{2,... | collective-permute-start | bytes 7864328 | tf_op jit(solution)/shard_map/ppermute | solution.py:69
  92.8 43.6 %all-to-all-start.2 = ((bf16[4,6,64,512]{3,2,1,0:T(8,128)(2,1)}), bf16[4,6,64,512]{3,2,1,0:T(8,128)(2,1)}, u32[]{:S(2)}, u32[]{:S(2)}) async-start(bf16[4,6,64,512]{3,2,1,0:T(8,128)(2,1)} %broadcast_in_dim.41), calls=%async_computation.2 | async-start | bytes 3145728 | tf_op jit(solution)/shard_map/all_to_all | solution.py:82
  98.8 36.4 %collective-permute-start.1 = (bf16[2,4,3,64,512]{4,3,2,1,0:T(8,128)(2,1)S(1)}, bf16[2,4,3,64,512]{4,3,2,1,0:T(8,128)(2,1)}, u32[]{:S(2)}, u32[]{:S(2)}) collective-permute-start(bf16[2,4,3,64,512]{4,3,2,1,0:T(8,128)(2,1)S(1)} %fusion.2), channel_id=1, source_target_pairs={{16,0},{24,8},{0,16},{8,24},{17,1},{25,9},{1,17},{9,25},{18,2},{26... | collective-permute-start | bytes 4718600 | tf_op jit(solution)/shard_map/ppermute | solution.py:69
  100.4 36.0 %collective-permute-start.3 = (bf16[4,6,64,512]{3,2,1,0:T(8,128)(2,1)S(1)}, bf16[4,6,64,512]{3,2,1,0:T(8,128)(2,1)}, u32[]{:S(2)}, u32[]{:S(2)}) collective-permute-start(bf16[4,6,64,512]{3,2,1,0:T(8,128)(2,1)S(1)} %copy-done.12), channel_id=1, source_target_pairs={{1,0},{0,1},{3,2},{2,3},{5,4},{4,5},{7,6},{6,7},{9,8},{8,9},{11,10... | collective-permute-start | bytes 4718600 | tf_op jit(solution)/shard_map/ppermute | solution.py:69
  138.7 57.9 %collective-permute-start.5 = (bf16[2,4,6,64,512]{4,3,2,1,0:T(8,128)(2,1)S(1)}, bf16[2,4,6,64,512]{4,3,2,1,0:T(8,128)(2,1)}, u32[]{:S(2)}, u32[]{:S(2)}) collective-permute-start(bf16[2,4,6,64,512]{4,3,2,1,0:T(8,128)(2,1)S(1)} %pad_maximum_fusion.refs_0_.refs_2_), channel_id=1, source_target_pairs={{8,0},{0,8},{24,16},{16,24},{9,1},{1,9},{25,17},{17,25},{10,2},{2,... | collective-permute-start | bytes 9437192 | tf_op jit(solution)/shard_map/ppermute | solution.py:69
  140.8 41.8 %all-to-all-start.3 = ((bf16[4,6,64,512]{3,2,1,0:T(8,128)(2,1)}), bf16[4,6,64,512]{3,2,1,0:T(8,128)(2,1)}, u32[]{:S(2)}, u32[]{:S(2)}) async-start(bf16[4,6,64,512]{3,2,1,0:T(8,128)(2,1)} %broadcast_in_dim.42), calls=%async_computation.3 | async-start | bytes 3145728 | tf_op jit(solution)/shard_map/all_to_all | solution.py:82
  145.6 36.1 %collective-permute-start.6 = (bf16[4,6,64,512]{3,2,1,0:T(8,128)(2,1)}, bf16[4,6,64,512]{3,2,1,0:T(8,128)(2,1)}, u32[]{:S(2)}, u32[]{:S(2)}) collective-permute-start(bf16[4,6,64,512]{3,2,1,0:T(8,128)(2,1)} %all-to-all-done.2), channel_id=1, source_target_pairs={{1,0},{0,1},{3,2},{2,3},{5,4},{4,5},{7,6},{6,7},{9,8},{8,9},{11,10... | collective-permute-start | bytes 4718600 | tf_op jit(solution)/shard_map/ppermute | solution.py:69
  160.2 36.4 %collective-permute-start.8 = (bf16[256,2048]{1,0:T(8,128)(2,1)}, bf16[256,2048]{1,0:T(8,128)(2,1)}, u32[]{:S(2)}, u32[]{:S(2)}) collective-permute-start(bf16[256,2048]{1,0:T(8,128)(2,1)} %get-tuple-element.518.refs_0_.refs_4_), channel_id=1, source_target_pairs={{16,0},{24,8},{0,16},{8,24},{17,1},{25,9},{1,17},{9,25},{18,2},{26... | collective-permute-start | bytes 3145736 | tf_op jit(solution)/shard_map/ppermute | solution.py:69
  161.8 34.8 %collective-permute-start.9 = (bf16[256,2048]{1,0:T(8,128)(2,1)}, bf16[256,2048]{1,0:T(8,128)(2,1)}, u32[]{:S(2)}, u32[]{:S(2)}) collective-permute-start(bf16[256,2048]{1,0:T(8,128)(2,1)} %get-tuple-element.518.refs_0_.refs_4_), channel_id=1, source_target_pairs={{8,0},{0,8},{24,16},{16,24},{9,1},{1,9},{25,17},{17,25},{10,2},{2,... | collective-permute-start | bytes 3145736 | tf_op jit(solution)/shard_map/ppermute | solution.py:69
  198.8 44.1 %collective-permute-start.11 = (bf16[2,4,6,64,512]{4,3,2,1,0:T(8,128)(2,1)S(1)}, bf16[2,4,6,64,512]{4,3,2,1,0:T(8,128)(2,1)}, u32[]{:S(2)}, u32[]{:S(2)}) collective-permute-start(bf16[2,4,6,64,512]{4,3,2,1,0:T(8,128)(2,1)S(1)} %pad_maximum_fusion.1.refs_0_.refs_2_), channel_id=1, source_target_pairs={{8,0},{0,8},{24,16},{16,24},{9,1},{1,9},{25,17},{17,25},{10,2},{2,... | collective-permute-start | bytes 9437192 | tf_op jit(solution)/shard_map/ppermute | solution.py:69
  201.0 42.0 %all-to-all-start.4 = ((bf16[4,6,64,512]{3,2,1,0:T(8,128)(2,1)}), bf16[4,6,64,512]{3,2,1,0:T(8,128)(2,1)}, u32[]{:S(2)}, u32[]{:S(2)}) async-start(bf16[4,6,64,512]{3,2,1,0:T(8,128)(2,1)} %broadcast_in_dim.43), calls=%async_computation.4 | async-start | bytes 3145728 | tf_op jit(solution)/shard_map/all_to_all | solution.py:82
  206.0 36.1 %collective-permute-start.12 = (bf16[4,6,64,512]{3,2,1,0:T(8,128)(2,1)}, bf16[4,6,64,512]{3,2,1,0:T(8,128)(2,1)}, u32[]{:S(2)}, u32[]{:S(2)}) collective-permute-start(bf16[4,6,64,512]{3,2,1,0:T(8,128)(2,1)} %all-to-all-done.3), channel_id=1, source_target_pairs={{1,0},{0,1},{3,2},{2,3},{5,4},{4,5},{7,6},{6,7},{9,8},{8,9},{11,10... | collective-permute-start | bytes 4718600 | tf_op jit(solution)/shard_map/ppermute | solution.py:69
  208.5 32.4 %collective-permute-start.10 = (bf16[2,4,2,64,512]{4,3,2,1,0:T(8,128)(2,1)S(1)}, bf16[2,4,2,64,512]{4,3,2,1,0:T(8,128)(2,1)}, u32[]{:S(2)}, u32[]{:S(2)}) collective-permute-start(bf16[2,4,2,64,512]{4,3,2,1,0:T(8,128)(2,1)S(1)} %fusion.7), channel_id=1, source_target_pairs={{16,0},{24,8},{0,16},{8,24},{17,1},{25,9},{1,17},{9,25},{18,2},{26... | collective-permute-start | bytes 3145736 | tf_op jit(solution)/shard_map/ppermute | solution.py:69
  245.2 37.2 %collective-permute-start.16 = (bf16[2,4,6,64,512]{4,3,2,1,0:T(8,128)(2,1)S(1)}, bf16[2,4,6,64,512]{4,3,2,1,0:T(8,128)(2,1)}, u32[]{:S(2)}, u32[]{:S(2)}) collective-permute-start(bf16[2,4,6,64,512]{4,3,2,1,0:T(8,128)(2,1)S(1)} %pad_maximum_fusion.2.refs_0_.refs_2_), channel_id=1, source_target_pairs={{8,0},{0,8},{24,16},{16,24},{9,1},{1,9},{25,17},{17,25},{10,2},{2,... | collective-permute-start | bytes 9437192 | tf_op jit(solution)/shard_map/ppermute | solution.py:69
  245.2 37.1 %collective-permute-start.17 = (bf16[4,6,64,512]{3,2,1,0:T(8,128)(2,1)}, bf16[4,6,64,512]{3,2,1,0:T(8,128)(2,1)}, u32[]{:S(2)}, u32[]{:S(2)}) collective-permute-start(bf16[4,6,64,512]{3,2,1,0:T(8,128)(2,1)} %all-to-all-done.4), channel_id=1, source_target_pairs={{1,0},{0,1},{3,2},{2,3},{5,4},{4,5},{7,6},{6,7},{9,8},{8,9},{11,10... | collective-permute-start | bytes 4718600 | tf_op jit(solution)/shard_map/ppermute | solution.py:69
  247.2 35.2 %all-to-all-start.5 = ((bf16[4,4,64,512]{3,2,1,0:T(8,128)(2,1)}), bf16[4,4,64,512]{3,2,1,0:T(8,128)(2,1)}, u32[]{:S(2)}, u32[]{:S(2)}) async-start(bf16[4,4,64,512]{3,2,1,0:T(8,128)(2,1)} %broadcast_in_dim.44), calls=%async_computation.5 | async-start | bytes 2097152 | tf_op jit(solution)/shard_map/all_to_all | solution.py:82
  282.4 57.4 %all-to-all-start.6 = ((bf16[8,128,1024]{2,1,0:T(8,128)(2,1)}), bf16[8,128,1024]{2,1,0:T(8,128)(2,1)}, u32[]{:S(2)}, u32[]{:S(2)}) async-start(bf16[8,128,1024]{2,1,0:T(8,128)(2,1)} %pad.10), calls=%async_computation.6 | async-start | bytes 4194304 | tf_op jit(solution)/shard_map/all_to_all | solution.py:1002
  288.9 50.8 %collective-permute-start.20 = (bf16[2,4,6,64,512]{4,3,2,1,0:T(8,128)(2,1)S(1)}, bf16[2,4,6,64,512]{4,3,2,1,0:T(8,128)(2,1)S(1)}, u32[]{:S(2)}, u32[]{:S(2)}) collective-permute-start(bf16[2,4,6,64,512]{4,3,2,1,0:T(8,128)(2,1)S(1)} %pad_maximum_fusion.3.refs_0_.refs_2_), channel_id=1, source_target_pairs={{8,0},{0,8},{24,16},{16,24},{9,1},{1,9},{25,17},{17,25},{10,2},{2,... | collective-permute-start | bytes 9437192 | tf_op jit(solution)/shard_map/ppermute | solution.py:69
  292.9 41.2 %collective-permute-start.21 = (bf16[4,4,64,512]{3,2,1,0:T(8,128)(2,1)}, bf16[4,4,64,512]{3,2,1,0:T(8,128)(2,1)}, u32[]{:S(2)}, u32[]{:S(2)}) collective-permute-start(bf16[4,4,64,512]{3,2,1,0:T(8,128)(2,1)} %all-to-all-done.5), channel_id=1, source_target_pairs={{1,0},{0,1},{3,2},{2,3},{5,4},{4,5},{7,6},{6,7},{9,8},{8,9},{11,10... | collective-permute-start | bytes 3145736 | tf_op jit(solution)/shard_map/ppermute | solution.py:69
  306.0 33.7 %collective-permute-start.23 = (bf16[256,2048]{1,0:T(8,128)(2,1)}, bf16[256,2048]{1,0:T(8,128)(2,1)}, u32[]{:S(2)}, u32[]{:S(2)}) collective-permute-start(bf16[256,2048]{1,0:T(8,128)(2,1)} %get-tuple-element.567.refs_0_.refs_4_), channel_id=1, source_target_pairs={{16,0},{24,8},{0,16},{8,24},{17,1},{25,9},{1,17},{9,25},{18,2},{26... | collective-permute-start | bytes 3145736 | tf_op jit(solution)/shard_map/ppermute | solution.py:69
  306.7 33.1 %collective-permute-start.24 = (bf16[256,2048]{1,0:T(8,128)(2,1)}, bf16[256,2048]{1,0:T(8,128)(2,1)}, u32[]{:S(2)}, u32[]{:S(2)}) collective-permute-start(bf16[256,2048]{1,0:T(8,128)(2,1)} %get-tuple-element.567.refs_0_.refs_4_), channel_id=1, source_target_pairs={{8,0},{0,8},{24,16},{16,24},{9,1},{1,9},{25,17},{17,25},{10,2},{2,... | collective-permute-start | bytes 3145736 | tf_op jit(solution)/shard_map/ppermute | solution.py:69
  341.4 54.9 %all-to-all-start.7 = ((bf16[8,128,1024]{2,1,0:T(8,128)(2,1)}), bf16[8,128,1024]{2,1,0:T(8,128)(2,1)}, u32[]{:S(2)}, u32[]{:S(2)}) async-start(bf16[8,128,1024]{2,1,0:T(8,128)(2,1)} %pad.11), calls=%async_computation.7 | async-start | bytes 4194304 | tf_op jit(solution)/shard_map/all_to_all | solution.py:1002
  349.0 46.0 %collective-permute-start.25 = (bf16[2,4,4,64,512]{4,3,2,1,0:T(8,128)(2,1)S(1)}, bf16[2,4,4,64,512]{4,3,2,1,0:T(8,128)(2,1)S(1)}, u32[]{:S(2)}, u32[]{:S(2)}) collective-permute-start(bf16[2,4,4,64,512]{4,3,2,1,0:T(8,128)(2,1)S(1)} %pad_maximum_fusion.5.refs_0_.refs_2_), channel_id=1, source_target_pairs={{16,0},{24,8},{0,16},{8,24},{17,1},{25,9},{1,17},{9,25},{18,2},{26... | collective-permute-start | bytes 6291464 | tf_op jit(solution)/shard_map/ppermute | solution.py:69
  349.8 46.5 %collective-permute-start.26 = (bf16[2,4,4,64,512]{4,3,2,1,0:T(8,128)(2,1)S(1)}, bf16[2,4,4,64,512]{4,3,2,1,0:T(8,128)(2,1)}, u32[]{:S(2)}, u32[]{:S(2)}) collective-permute-start(bf16[2,4,4,64,512]{4,3,2,1,0:T(8,128)(2,1)S(1)} %pad_maximum_fusion.5.refs_0_.refs_2_), channel_id=1, source_target_pairs={{8,0},{0,8},{24,16},{16,24},{9,1},{1,9},{25,17},{17,25},{10,2},{2,... | collective-permute-start | bytes 6291464 | tf_op jit(solution)/shard_map/ppermute | solution.py:69
  396.3 53.5 %all-to-all-start.8 = ((bf16[8,128,1024]{2,1,0:T(8,128)(2,1)}), bf16[8,128,1024]{2,1,0:T(8,128)(2,1)}, u32[]{:S(2)}, u32[]{:S(2)}) async-start(bf16[8,128,1024]{2,1,0:T(8,128)(2,1)} %pad.12), calls=%async_computation.8 | async-start | bytes 4194304 | tf_op jit(solution)/shard_map/all_to_all | solution.py:1002
  402.8 47.1 %collective-permute-start.33 = (bf16[256,4096]{1,0:T(8,128)(2,1)}, bf16[256,4096]{1,0:T(8,128)(2,1)}, u32[]{:S(2)}, u32[]{:S(2)}) collective-permute-start(bf16[256,4096]{1,0:T(8,128)(2,1)} %get-tuple-element.537.act.refs_0_), channel_id=1, source_target_pairs={{8,0},{0,8},{24,16},{16,24},{9,1},{1,9},{25,17},{17,25},{10,2},{2,... | collective-permute-start | bytes 6291464 | tf_op jit(solution)/shard_map/ppermute | solution.py:69
  403.3 38.4 %collective-permute-start.30 = (bf16[256,4096]{1,0:T(8,128)(2,1)}, bf16[256,4096]{1,0:T(8,128)(2,1)}, u32[]{:S(2)}, u32[]{:S(2)}) collective-permute-start(bf16[256,4096]{1,0:T(8,128)(2,1)} %get-tuple-element.582.act.refs_0_), channel_id=1, source_target_pairs={{8,0},{0,8},{24,16},{16,24},{9,1},{1,9},{25,17},{17,25},{10,2},{2,... | collective-permute-start | bytes 6291464 | tf_op jit(solution)/shard_map/ppermute | solution.py:69
  404.7 45.1 %collective-permute-start.32 = (bf16[256,3072]{1,0:T(8,128)(2,1)}, bf16[256,3072]{1,0:T(8,128)(2,1)S(1)}, u32[]{:S(2)}, u32[]{:S(2)}) collective-permute-start(bf16[256,3072]{1,0:T(8,128)(2,1)} %pad_maximum_fusion.6), channel_id=1, source_target_pairs={{8,0},{0,8},{24,16},{16,24},{9,1},{1,9},{25,17},{17,25},{10,2},{2,... | collective-permute-start | bytes 4718600 | tf_op jit(solution)/shard_map/ppermute | solution.py:69
  406.4 43.4 %collective-permute-start.34 = (bf16[256,3072]{1,0:T(8,128)(2,1)}, bf16[256,3072]{1,0:T(8,128)(2,1)S(1)}, u32[]{:S(2)}, u32[]{:S(2)}) collective-permute-start(bf16[256,3072]{1,0:T(8,128)(2,1)} %pad_maximum_fusion.7), channel_id=1, source_target_pairs={{8,0},{0,8},{24,16},{16,24},{9,1},{1,9},{25,17},{17,25},{10,2},{2,... | collective-permute-start | bytes 4718600 | tf_op jit(solution)/shard_map/ppermute | solution.py:69
  480.0 35.1 %collective-permute-start.40 = (bf16[2,4,2,128,256]{4,3,2,1,0:T(8,128)(2,1)S(1)}, bf16[2,4,2,128,256]{4,3,2,1,0:T(8,128)(2,1)S(1)}, u32[]{:S(2)}, u32[]{:S(2)}) collective-permute-start(bf16[2,4,2,128,256]{4,3,2,1,0:T(8,128)(2,1)S(1)} %copy-done.91), channel_id=1, source_target_pairs={{16,0},{24,8},{0,16},{8,24},{17,1},{25,9},{1,17},{9,25},{18,2},{26... | collective-permute-start | bytes 3145736 | tf_op jit(solution)/shard_map/ppermute | solution.py:69
  481.3 33.8 %collective-permute-start.41 = (bf16[2,4,2,128,256]{4,3,2,1,0:T(8,128)(2,1)S(1)}, bf16[2,4,2,128,256]{4,3,2,1,0:T(8,128)(2,1)S(1)}, u32[]{:S(2)}, u32[]{:S(2)}) collective-permute-start(bf16[2,4,2,128,256]{4,3,2,1,0:T(8,128)(2,1)S(1)} %copy-done.90), channel_id=1, source_target_pairs={{1,0},{0,1},{3,2},{2,3},{5,4},{4,5},{7,6},{6,7},{9,8},{8,9},{11,10... | collective-permute-start | bytes 3145736 | tf_op jit(solution)/shard_map/ppermute | solution.py:69
  482.0 33.1 %collective-permute-start.39 = (bf16[4,2,256,128]{3,2,1,0:T(8,128)(2,1)S(1)}, bf16[4,2,256,128]{3,2,1,0:T(8,128)(2,1)S(1)}, u32[]{:S(2)}, u32[]{:S(2)}) collective-permute-start(bf16[4,2,256,128]{3,2,1,0:T(8,128)(2,1)S(1)} %get-tuple-element.998), channel_id=1, source_target_pairs={{16,0},{24,8},{0,16},{8,24},{17,1},{25,9},{1,17},{9,25},{18,2},{26... | collective-permute-start | bytes 1572872 | tf_op jit(solution)/shard_map/ppermute | solution.py:69
  617.3 35.6 %collective-permute-start.53 = (bf16[2,4,2,256,128]{4,3,2,1,0:T(8,128)(2,1)}, bf16[2,4,2,256,128]{4,3,2,1,0:T(8,128)(2,1)S(1)}, u32[]{:S(2)}, u32[]{:S(2)}) collective-permute-start(bf16[2,4,2,256,128]{4,3,2,1,0:T(8,128)(2,1)} %get-tuple-element.770), channel_id=1, source_target_pairs={{16,0},{24,8},{0,16},{8,24},{17,1},{25,9},{1,17},{9,25},{18,2},{26... | collective-permute-start | bytes 3145736 | tf_op jit(solution)/shard_map/ppermute | solution.py:69
  618.1 34.8 %collective-permute-start.54 = (bf16[2,4,2,256,128]{4,3,2,1,0:T(8,128)(2,1)}, bf16[2,4,2,256,128]{4,3,2,1,0:T(8,128)(2,1)S(1)}, u32[]{:S(2)}, u32[]{:S(2)}) collective-permute-start(bf16[2,4,2,256,128]{4,3,2,1,0:T(8,128)(2,1)} %get-tuple-element.771), channel_id=1, source_target_pairs={{1,0},{0,1},{3,2},{2,3},{5,4},{4,5},{7,6},{6,7},{9,8},{8,9},{11,10... | collective-permute-start | bytes 3145736 | tf_op jit(solution)/shard_map/ppermute | solution.py:69
  619.5 33.4 %collective-permute-start.52 = (bf16[4,2,128,256]{3,2,1,0:T(8,128)(2,1)S(1)}, bf16[4,2,128,256]{3,2,1,0:T(8,128)(2,1)S(1)}, u32[]{:S(2)}, u32[]{:S(2)}) collective-permute-start(bf16[4,2,128,256]{3,2,1,0:T(8,128)(2,1)S(1)} %get-tuple-element.990), channel_id=1, source_target_pairs={{16,0},{24,8},{0,16},{8,24},{17,1},{25,9},{1,17},{9,25},{18,2},{26... | collective-permute-start | bytes 1572872 | tf_op jit(solution)/shard_map/ppermute | solution.py:69
  656.4 47.5 %all-to-all-start.11 = ((bf16[4,4,128,256]{3,2,1,0:T(8,128)(2,1)}), bf16[4,4,128,256]{3,2,1,0:T(8,128)(2,1)S(1)}, u32[]{:S(2)}, u32[]{:S(2)}) async-start(bf16[4,4,128,256]{3,2,1,0:T(8,128)(2,1)} %pad_maximum_fusion.11), calls=%async_computation.11 | async-start | bytes 2097152 | tf_op jit(solution)/shard_map/all_to_all | solution.py:82
  667.7 36.2 %collective-permute-start.59 = (bf16[2,256,1024]{2,1,0:T(8,128)(2,1)}, bf16[2,256,1024]{2,1,0:T(8,128)(2,1)S(1)}, u32[]{:S(2)}, u32[]{:S(2)}) collective-permute-start(bf16[2,256,1024]{2,1,0:T(8,128)(2,1)} %fusion.4), channel_id=1, source_target_pairs={{16,0},{24,8},{0,16},{8,24},{17,1},{25,9},{1,17},{9,25},{18,2},{26... | collective-permute-start | bytes 3145736 | tf_op jit(solution)/shard_map/ppermute | solution.py:69
  668.8 35.1 %collective-permute-start.56 = (bf16[4,2,256,128]{3,2,1,0:T(8,128)(2,1)S(1)}, bf16[4,2,256,128]{3,2,1,0:T(8,128)(2,1)}, u32[]{:S(2)}, u32[]{:S(2)}) collective-permute-start(bf16[4,2,256,128]{3,2,1,0:T(8,128)(2,1)S(1)} %get-tuple-element.986), channel_id=1, source_target_pairs={{16,0},{24,8},{0,16},{8,24},{17,1},{25,9},{1,17},{9,25},{18,2},{26... | collective-permute-start | bytes 1572872 | tf_op jit(solution)/shard_map/ppermute | solution.py:69
  759.3 32.6 %all-to-all-start.13 = ((bf16[4,4,128,256]{3,2,1,0:T(8,128)(2,1)}), bf16[4,4,128,256]{3,2,1,0:T(8,128)(2,1)S(1)}, u32[]{:S(2)}, u32[]{:S(2)}) async-start(bf16[4,4,128,256]{3,2,1,0:T(8,128)(2,1)} %pad_maximum_fusion.13), calls=%async_computation.13 | async-start | bytes 2097152 | tf_op jit(solution)/shard_map/all_to_all | solution.py:82
  844.8 53.7 %all-to-all-start.15 = ((bf16[32,128,256]{2,1,0:T(8,128)(2,1)}), bf16[32,128,256]{2,1,0:T(8,128)(2,1)}, u32[]{:S(2)}, u32[]{:S(2)}) async-start(bf16[32,128,256]{2,1,0:T(8,128)(2,1)} %bitcast.164), calls=%async_computation.15 | async-start | bytes 4194304 | tf_op jit(solution)/shard_map/all_to_all | solution.py:1325
  850.9 38.9 %collective-permute-start.75 = (bf16[6,128,256]{2,1,0:T(8,128)(2,1)}, bf16[6,128,256]{2,1,0:T(8,128)(2,1)S(1)}, u32[]{:S(2)}, u32[]{:S(2)}) collective-permute-start(bf16[6,128,256]{2,1,0:T(8,128)(2,1)} %get-tuple-element.972), channel_id=1, source_target_pairs={{0,16},{8,24},{16,0},{24,8},{1,17},{9,25},{17,1},{25,9},{2,18},{10... | collective-permute-start | bytes 1179656 | tf_op jit(solution)/shard_map/ppermute | solution.py:1338
  851.3 38.6 %collective-permute-start.74 = (bf16[6,128,256]{2,1,0:T(8,128)(2,1)S(1)}, bf16[6,128,256]{2,1,0:T(8,128)(2,1)S(1)}, u32[]{:S(2)}, u32[]{:S(2)}) collective-permute-start(bf16[6,128,256]{2,1,0:T(8,128)(2,1)S(1)} %get-tuple-element.973), channel_id=1, source_target_pairs={{0,8},{8,0},{16,24},{24,16},{1,9},{9,1},{17,25},{25,17},{2,10},{10... | collective-permute-start | bytes 1179656 | tf_op jit(solution)/shard_map/ppermute | solution.py:1338
  914.3 56.4 %all-to-all-start.16 = ((bf16[8,128,1024]{2,1,0:T(8,128)(2,1)}), bf16[8,128,1024]{2,1,0:T(8,128)(2,1)S(1)}, u32[]{:S(2)}, u32[]{:S(2)}) async-start(bf16[8,128,1024]{2,1,0:T(8,128)(2,1)} %bitcast.176), calls=%async_computation.16 | async-start | bytes 4194304 | tf_op jit(solution)/shard_map/all_to_all | solution.py:1007
  918.1 52.4 %collective-permute-start.77 = (f32[2,12288]{1,0:T(2,128)S(1)}, f32[2,12288]{1,0:T(2,128)S(1)}, u32[]{:S(2)}, u32[]{:S(2)}) collective-permute-start(f32[2,12288]{1,0:T(2,128)S(1)} %add.454), channel_id=1, source_target_pairs={{0,4},{1,5},{2,6},{3,7},{4,0},{5,1},{6,2},{7,3},{8,12},{9,13},{10,... | collective-permute-start | bytes 294920 | tf_op jit(solution)/shard_map/ppermute | solution.py:981
  974.3 35.4 %collective-permute-start.78 = (bf16[6,128,1024]{2,1,0:T(8,128)(2,1)}, bf16[6,128,1024]{2,1,0:T(8,128)(2,1)}, u32[]{:S(2)}, u32[]{:S(2)}) collective-permute-start(bf16[6,128,1024]{2,1,0:T(8,128)(2,1)} %subtract_convert_fusion.refs_0_), channel_id=1, source_target_pairs={{16,0},{24,8},{0,16},{8,24},{17,1},{25,9},{1,17},{9,25},{18,2},{26... | collective-permute-start | bytes 4718600 | tf_op jit(solution)/shard_map/ppermute | solution.py:69
  975.6 51.9 %all-to-all-start.17 = ((bf16[8,128,1024]{2,1,0:T(8,128)(2,1)}), bf16[8,128,1024]{2,1,0:T(8,128)(2,1)}, u32[]{:S(2)}, u32[]{:S(2)}) async-start(bf16[8,128,1024]{2,1,0:T(8,128)(2,1)} %bitcast.175), calls=%async_computation.17 | async-start | bytes 4194304 | tf_op jit(solution)/shard_map/all_to_all | solution.py:1007
  (144 other events, 1551.2 us)
